TPU v7x, 128 devices: a whole 4x4x4 slice. The times are simulated.
128 devices in a mesh: prow: 16 (over y, x), pcol: 8 (over z, core).
Axes of the slice: x: 4, y: 4, z: 4, core: 2. Of those that a mesh axis runs over, the one named last changes fastest.
Arguments:
- front: float32 [2, 4096, 4, 2048], P(None, 'prow', None, 'pcol')
- partials: float32 [128, 128, 8, 256], P(('prow', 'pcol')), may hold values from -6 to 6
- targets: int32 [128, 128, 8], P(('prow', 'pcol')), may hold values from 0 to 2047
- counts: int32 [128, 128], P(('prow', 'pcol')), may hold values from 0 to 8, as said below
- local_picks: int32 [2, 16, 256], replicated, may hold values from 0 to 511, as said below
- level_picks: int32 [2, 4, 16, 256], replicated, may hold values from 0 to 511, as said below
- order: int32 [2, 256], replicated, may hold values from 0 to 255, as said below
Outputs:
- factored: float32 [2, 4096, 4, 2048], P(None, 'prow', None, 'pcol')
Inputs may be any that keep to these rules, and one draw needn't show every extreme that they name: `targets`: code c names local row c // 4 and local tile column c % 4 of the owner's block; codes of unused slots are arbitrary and ignored. `counts`: in every draw some owner receives 8 rows from every source. For panel k, row p of local_picks names 256 different local rows of prow index p, none of them a winner of an earlier panel. `level_picks`: each list names 256 different positions; at level l the lists of indices that differ only in bits 0 .. l are equal. `order`: each row is a permutation.
All inputs are finite; a program needn't handle non-finite values.
Results may differ from a plain program's by a relative error of at most 0.0001.
Values sent between devices are 32-bit elements; how exact they have to be, the bound alone decides.
No kernel may reach another device: no remote copies, remote signals or barrier semaphores. Data moves between devices by JAX's collectives and lax.ppermute only.
A program may use at most 64 MiB of HBM per device.

v0:
```python
import jax
import jax.numpy as jnp
from jax import lax
from jax.sharding import PartitionSpec as P

PANELS = 2


def partner_2(x, axis, stride):
    return lax.ppermute(x, axis, [(i, i ^ 1 << stride) for i in range(lax.axis_size(axis))])


def spread(x, axis, root):
    mine = lax.axis_index(axis) == root
    return lax.psum(jnp.where(mine, x, jnp.zeros_like(x)), axis)


def winner_rows(chosen_rows, levels, final_order, prow_size, tile_width):
    device_ids = jnp.arange(prow_size, dtype=jnp.int32)
    candidates = (
        chosen_rows // tile_width * prow_size + device_ids[:, None]
    ) * tile_width + chosen_rows % tile_width
    for level_id in range(levels.shape[0]):
        partner = device_ids ^ 1 << level_id
        lower_side = jnp.minimum(device_ids, partner)
        upper_side = jnp.maximum(device_ids, partner)
        joined = jnp.concatenate([candidates[lower_side], candidates[upper_side]], axis=1)
        candidates = jnp.take_along_axis(joined, levels[level_id], axis=1)
    return candidates[0][final_order]


def newton_inverse(diag_block):
    identity = jnp.eye(diag_block.shape[0], dtype=jnp.float32)
    approx = identity / jnp.diagonal(diag_block)[:, None]
    for refine in range(2):
        approx = jnp.dot(
            approx,
            2.0 * identity - jnp.dot(diag_block, approx, precision=lax.Precision.HIGHEST),
            precision=lax.Precision.HIGHEST,
        )
    return approx


def body(front, partials, targets, counts, local_picks, level_picks, order):
    tiles_r = front.shape[0]
    tile_width = front.shape[1]
    tiles_c = front.shape[2]
    rows_local = tiles_r * tile_width
    cols_local = tiles_c * tile_width
    prow_size = lax.axis_size("prow")
    pcol_size = lax.axis_size("pcol")
    row_index = lax.axis_index("prow")
    col_index = lax.axis_index("pcol")
    slot_count = partials.shape[2]
    occupied = jnp.arange(slot_count, dtype=jnp.int32)[None, None, :] < counts[:, :, None]
    partial_rows = jnp.where(occupied[..., None], partials, jnp.float32(0.0))
    target_codes = jnp.where(occupied, targets, 0)
    partial_rows, target_codes = (
        lax.all_to_all(partial_rows, ("prow", "pcol"), split_axis=1, concat_axis=0, tiled=True),
        lax.all_to_all(target_codes, ("prow", "pcol"), split_axis=1, concat_axis=0, tiled=True),
    )
    partial_rows = partial_rows.reshape(-1, tile_width)
    target_codes = target_codes.reshape(-1)
    tiled = front.reshape(rows_local, tiles_c, tile_width)
    tiled = tiled.at[target_codes // tiles_c, target_codes % tiles_c].add(partial_rows)
    matrix = tiled.reshape(rows_local, cols_local)
    local_rows = jnp.arange(rows_local, dtype=jnp.int32)
    global_rows = (
        local_rows // tile_width * prow_size + row_index
    ) * tile_width + local_rows % tile_width
    local_cols = jnp.arange(cols_local, dtype=jnp.int32)
    global_cols = (
        local_cols // tile_width * pcol_size + col_index
    ) * tile_width + local_cols % tile_width
    tile_global = jnp.arange(tiles_c, dtype=jnp.int32) * pcol_size + col_index
    retired = jnp.zeros((rows_local,), dtype=bool)
    identity = jnp.eye(tile_width, dtype=jnp.float32)
    for panel_id in range(PANELS):
        winners = winner_rows(
            local_picks[panel_id], level_picks[panel_id], order[panel_id], prow_size, tile_width
        )
        is_winner = global_rows[:, None] == winners[None, :]
        retired = retired | jnp.any(is_winner, axis=1)
        own_picks = lax.dynamic_index_in_dim(local_picks[panel_id], row_index, 0, keepdims=False)
        candidates = matrix[own_picks]
        for level_id in range(level_picks.shape[1]):
            partner_rows = partner_2(candidates, "prow", level_id)
            upper_bit = row_index >> level_id & 1
            leading = jnp.where(upper_bit == 1, partner_rows, candidates)
            second = jnp.where(upper_bit == 1, candidates, partner_rows)
            joined = jnp.concatenate([leading, second], axis=0)
            chosen = lax.dynamic_index_in_dim(
                level_picks[panel_id, level_id], row_index, 0, keepdims=False
            )
            candidates = joined[chosen]
        pivots = candidates[order[panel_id]]
        diag_block = jnp.where(col_index == panel_id, pivots[:, :tile_width], identity)
        inverse = newton_inverse(diag_block)
        multipliers = jnp.dot(matrix[:, :tile_width], inverse, precision=lax.Precision.HIGHEST)
        multipliers = spread(multipliers, "pcol", panel_id)
        product = jnp.dot(multipliers, pivots, precision=lax.Precision.HIGHEST)
        active = jnp.logical_not(retired)
        trailing = global_cols >= (panel_id + 1) * tile_width
        matrix = matrix - jnp.where(active[:, None] & trailing[None, :], product, jnp.float32(0.0))
        in_panel = tile_global == panel_id
        blocked = matrix.reshape(rows_local, tiles_c, tile_width)
        blocked = jnp.where(
            active[:, None, None] & in_panel[None, :, None], multipliers[:, None, :], blocked
        )
        matrix = blocked.reshape(rows_local, cols_local)
    return matrix.reshape(front.shape)


def solution(mesh):
    placed = (
        P(None, "prow", None, "pcol"),
        P(("prow", "pcol"), None, None, None),
        P(("prow", "pcol"), None, None),
        P(("prow", "pcol"), None),
        P(),
        P(),
        P(),
    )
    return jax.shard_map(
        body, mesh=mesh, in_specs=placed, out_specs=P(None, "prow", None, "pcol"), check_vma=False
    )
```

profile of v0, /device:TPU:65, one launch (start us, length us, event | category | flops | bytes accessed | tf_op | source)
XLA Modules:
  0.0 659.4 jit_solution(1097944625852958872)
XLA Ops:
  8.0 10.4 %all-to-all-start = ((s32[1,128,8]{2,0,1:T(1,128)}), s32[1,128,8]{2,0,1:T(1,128)S(1)}, u32[]{:S(2)}, u32[]{:S(2)}) async-start(s32[1,128,8]{2,0,1:T(1,128)} %copy.17), calls=%async_computation | async-start | bytes 131072 | tf_op jit(solution)/shard_map/all_to_all | solution.py:60
  19.1 1.5 fusion.83
  24.6 32.8 %gather_fusion.36 = s32[4096]{0:T(1024)S(1)} fusion(s32[16,512]{1,0:T(8,128)S(1)} %pad_add_fusion.4, s32[4096]{0:T(1024)S(1)} %bitcast.255), kind=kCustom, calls=%fused_computation.4.clone | custom fusion | bytes 65536 | tf_op jit(solution)/shard_map/jit(take_along_axis)/gather | solution.py:28
  57.4 32.8 %gather_fusion.32 = s32[4096]{0:T(1024)S(1)} fusion(s32[16,512]{1,0:T(8,128)S(1)} %pad_add_fusion, s32[4096]{0:T(1024)S(1)} %bitcast.256), kind=kCustom, calls=%fused_computation.clone | custom fusion | bytes 65536 | tf_op jit(solution)/shard_map/jit(take_along_axis)/gather | solution.py:28
  92.7 9.8 %all-to-all-start.1 = ((f32[1,128,8,256]{3,2,0,1:T(8,128)}), f32[1,128,8,256]{3,2,0,1:T(8,128)S(1)}, u32[]{:S(2)}, u32[]{:S(2)}) async-start(f32[1,128,8,256]{3,2,0,1:T(8,128)} %bitcast_select_fusion), calls=%async_computation.1 | async-start | bytes 2097152 | tf_op jit(solution)/shard_map/all_to_all | solution.py:59
  103.1 3.0 reshape.869
  107.7 11.0 %all-to-all-done.1 = f32[1,128,8,256]{3,2,0,1:T(8,128)S(1)} async-done(((f32[1,128,8,256]{3,2,0,1:T(8,128)}), f32[1,128,8,256]{3,2,0,1:T(8,128)S(1)}, u32[]{:S(2)}, u32[]{:S(2)}) %all-to-all-start.1) | async-done | bytes 1048608 | tf_op jit(solution)/shard_map/all_to_all | solution.py:59
  118.7 9.0 %scatter_custom_fusion = f32[2048,256]{1,0:T(8,128)} fusion(f32[2048,256]{1,0:T(8,128)} %reshape.869, s32[1024]{0:T(1024)S(1)} %broadcast_select_fusion.17, f32[1,128,8,256]{3,2,0,1:T(8,128)S(1)} %all-to-all-done.1), kind=kCustom, calls=%fused_computation.57 | custom fusion | flops 262144 | bytes 3145728
  127.7 1.8 reshape.866
  132.7 32.8 %gather_fusion.33 = s32[4096]{0:T(1024)S(1)} fusion(s32[16,512]{1,0:T(8,128)S(1)} %pad_add_fusion.1, s32[4096]{0:T(1024)S(1)} %bitcast.257), kind=kCustom, calls=%fused_computation.1.clone | custom fusion | bytes 65536 | tf_op jit(solution)/shard_map/jit(take_along_axis)/gather | solution.py:28
  167.0 1.5 pad_maximum_fusion
  168.4 3.2 gather_fusion.19
  171.6 2.8 collective-permute-start.1
  177.1 32.8 %gather_fusion.34 = s32[4096]{0:T(1024)S(1)} fusion(s32[16,512]{1,0:T(8,128)S(1)} %pad_add_fusion.2, s32[4096]{0:T(1024)S(1)} %bitcast.258), kind=kCustom, calls=%fused_computation.2.clone | custom fusion | bytes 65536 | tf_op jit(solution)/shard_map/jit(take_along_axis)/gather | solution.py:28
  209.9 32.8 %gather_fusion.37 = s32[4096]{0:T(1024)S(1)} fusion(s32[16,512]{1,0:T(8,128)S(1)} %pad_add_fusion.5, s32[4096]{0:T(1024)S(1)} %bitcast.259), kind=kCustom, calls=%fused_computation.5.clone | custom fusion | bytes 65536 | tf_op jit(solution)/shard_map/jit(take_along_axis)/gather | solution.py:28
  244.9 1.5 pad_maximum_fusion.1
  246.3 3.2 gather_fusion.20
  252.5 32.8 %gather_fusion.38 = s32[4096]{0:T(1024)S(1)} fusion(s32[16,512]{1,0:T(8,128)S(1)} %pad_add_fusion.6, s32[4096]{0:T(1024)S(1)} %bitcast.260), kind=kCustom, calls=%fused_computation.6.clone | custom fusion | bytes 65536 | tf_op jit(solution)/shard_map/jit(take_along_axis)/gather | solution.py:28
  286.5 32.8 %gather_fusion.35 = s32[4096]{0:T(1024)S(1)} fusion(s32[16,512]{1,0:T(8,128)S(1)} %pad_add_fusion.3, s32[4096]{0:T(1024)S(1)} %bitcast.261), kind=kCustom, calls=%fused_computation.3.clone | custom fusion | bytes 65536 | tf_op jit(solution)/shard_map/jit(take_along_axis)/gather | solution.py:28
  319.3 32.8 %gather_fusion.39 = s32[4096]{0:T(1024)S(1)} fusion(s32[16,512]{1,0:T(8,128)S(1)} %pad_add_fusion.7, s32[4096]{0:T(1024)S(1)} %bitcast.262), kind=kCustom, calls=%fused_computation.7.clone | custom fusion | bytes 65536 | tf_op jit(solution)/shard_map/jit(take_along_axis)/gather | solution.py:28
  354.3 1.5 pad_maximum_fusion.2
  355.7 3.2 gather_fusion.21
  358.9 1.9 collective-permute-start.3
  360.9 1.9 gather_fusion.8
  362.8 1.9 gather_fusion.17
  365.9 18.5 %collective-permute-done.3 = f32[256,1024]{1,0:T(8,128)} collective-permute-done((f32[256,1024]{1,0:T(8,128)S(1)}, f32[256,1024]{1,0:T(8,128)}, u32[]{:S(2)}, u32[]{:S(2)}) %collective-permute-start.3) | collective-permute-done | bytes 1048608 | tf_op jit(solution)/shard_map/ppermute | solution.py:10
  384.3 1.4 broadcast_select_fusion.16
  385.7 1.5 pad_maximum_fusion.3
  387.2 3.2 gather_fusion.22
  390.4 2.0 gather_fusion.23
  393.4 2.3 gather_fusion.24
  399.0 1.6 broadcast_in_dim.63
  400.9 55.2 %all-reduce.3.cloned.1.call-done = f32[512,256]{1,0:T(8,128)} async-done(((f32[512,256]{1,0:T(8,128)}), f32[512,256]{1,0:T(8,128)}) %all-reduce.3.cloned.1.call-update) | async-done | bytes 524304 | tf_op jit(solution)/shard_map/psum | solution.py:15
  458.9 3.7 subtract_select_fusion
  462.6 3.2 gather_fusion.25
  467.0 23.4 %collective-permute-done.4 = f32[256,1024]{1,0:T(8,128)S(1)} collective-permute-done((f32[256,1024]{1,0:T(8,128)S(1)}, f32[256,1024]{1,0:T(8,128)S(1)}, u32[]{:S(2)}, u32[]{:S(2)}) %collective-permute-start.4) | collective-permute-done | bytes 1048608 | tf_op jit(solution)/shard_map/ppermute | solution.py:10
  491.8 3.0 collective-permute-start.5
  494.8 22.5 %collective-permute-done.5 = f32[256,1024]{1,0:T(8,128)S(1)} collective-permute-done((f32[256,1024]{1,0:T(8,128)S(1)}, f32[256,1024]{1,0:T(8,128)S(1)}, u32[]{:S(2)}, u32[]{:S(2)}) %collective-permute-start.5) | collective-permute-done | bytes 1048608 | tf_op jit(solution)/shard_map/ppermute | solution.py:10
  520.1 21.6 %collective-permute-done.6 = f32[256,1024]{1,0:T(8,128)S(1)} collective-permute-done((f32[256,1024]{1,0:T(8,128)S(1)}, f32[256,1024]{1,0:T(8,128)S(1)}, u32[]{:S(2)}, u32[]{:S(2)}) %collective-permute-start.6) | collective-permute-done | bytes 1048608 | tf_op jit(solution)/shard_map/ppermute | solution.py:10
  543.1 2.8 collective-permute-start.7
  545.9 20.6 %collective-permute-done.7 = f32[256,1024]{1,0:T(8,128)S(1)} collective-permute-done((f32[256,1024]{1,0:T(8,128)S(1)}, f32[256,1024]{1,0:T(8,128)S(1)}, u32[]{:S(2)}, u32[]{:S(2)}) %collective-permute-start.7) | collective-permute-done | bytes 1048608 | tf_op jit(solution)/shard_map/ppermute | solution.py:10
  566.8 1.5 pad_maximum_fusion.7
  568.3 3.2 gather_fusion.29
  572.6 2.3 gather_fusion.31
  578.2 65.0 %all-reduce.5.cloned.1.call-done = f32[512,256]{1,0:T(8,128)} async-done(((f32[512,256]{1,0:T(8,128)}), f32[512,256]{1,0:T(8,128)}) %all-reduce.5.cloned.1.call-update) | async-done | bytes 524304 | tf_op jit(solution)/shard_map/psum | solution.py:15
  643.1 4.4 select_subtract_fusion
  647.5 2.3 reshape.867
  649.8 2.6 broadcast_select_fusion
  (176 shorter events, 46.1 us)
Async XLA Ops:
  8.0 84.7 %all-to-all-start = ((s32[1,128,8]{2,0,1:T(1,128)}), s32[1,128,8]{2,0,1:T(1,128)S(1)}, u32[]{:S(2)}, u32[]{:S(2)}) async-start(s32[1,128,8]{2,0,1:T(1,128)} %copy.17), calls=%async_computation | async-start | bytes 131072 | tf_op jit(solution)/shard_map/all_to_all | solution.py:60
  57.4 32.8 %copy-start.5 = (f32[1,128,8,256]{3,2,1,0:T(8,128)S(1)}, f32[1,128,8,256]{3,2,1,0:T(8,128)}, u32[]{:S(2)}) copy-start(f32[1,128,8,256]{3,2,1,0:T(8,128)} %param.10) | copy-start | bytes 3145732
  90.2 1.2 copy-start.4
  90.2 1.8 copy-start.6
  92.7 26.0 %all-to-all-start.1 = ((f32[1,128,8,256]{3,2,0,1:T(8,128)}), f32[1,128,8,256]{3,2,0,1:T(8,128)S(1)}, u32[]{:S(2)}, u32[]{:S(2)}) async-start(f32[1,128,8,256]{3,2,0,1:T(8,128)} %bitcast_select_fusion), calls=%async_computation.1 | async-start | bytes 2097152 | tf_op jit(solution)/shard_map/all_to_all | solution.py:59
  102.4 353.7 %all-reduce.3.cloned.1.call-start = ((), (), s32[]{:S(2)}) async-start(), calls=%async_computation.2 | async-start | bytes 1048576 | tf_op jit(solution)/shard_map/psum | solution.py:15
  103.1 4.5 copy-start.14
  103.1 4.6 copy-start.13
  130.6 35.0 %collective-permute-start = (f32[256,1024]{1,0:T(8,128)S(1)}, f32[256,1024]{1,0:T(8,128)}, u32[]{:S(2)}, u32[]{:S(2)}) collective-permute-start(f32[256,1024]{1,0:T(8,128)S(1)} %gather_fusion.18), channel_id=1, source_target_pairs={{0,8},{8,0},{16,24},{24,16},{32,40},{40,32},{48,56},{56,48},{64,72... | collective-permute-start | bytes 3145736 | tf_op jit(solution)/shard_map/ppermute | solution.py:10
  131.4 0.6 copy-start.9
  132.1 0.6 copy-start.10
  132.7 32.8 %copy-start.11 = (s32[256,1]{0,1:T(1,128)S(1)}, s32[256,1]{0,1:T(1,128)}, u32[]{:S(2)}) copy-start(s32[256,1]{0,1:T(1,128)} %get-tuple-element.64) | copy-start | bytes 3076
  165.5 10.3 %copy-start.7 = (s32[1024]{0:T(1024)}, s32[1024]{0:T(1024)S(1)}, u32[]{:S(2)}) copy-start(s32[1024]{0:T(1024)S(1)} %pad_clamp_fusion.15) | copy-start | bytes 12292
  171.6 71.9 %collective-permute-start.1 = (f32[256,1024]{1,0:T(8,128)S(1)}, f32[256,1024]{1,0:T(8,128)}, u32[]{:S(2)}, u32[]{:S(2)}) collective-permute-start(f32[256,1024]{1,0:T(8,128)S(1)} %gather_fusion.19), channel_id=1, source_target_pairs={{0,16},{8,24},{16,0},{24,8},{32,48},{40,56},{48,32},{56,40},{64,80... | collective-permute-start | bytes 3145736 | tf_op jit(solution)/shard_map/ppermute | solution.py:10
  176.4 0.6 copy-start.8
  249.5 103.4 %collective-permute-start.2 = (f32[256,1024]{1,0:T(8,128)S(1)}, f32[256,1024]{1,0:T(8,128)}, u32[]{:S(2)}, u32[]{:S(2)}) collective-permute-start(f32[256,1024]{1,0:T(8,128)S(1)} %gather_fusion.20), channel_id=1, source_target_pairs={{0,32},{8,40},{16,48},{24,56},{32,0},{40,8},{48,16},{56,24},{64,96... | collective-permute-start | bytes 3145736 | tf_op jit(solution)/shard_map/ppermute | solution.py:10
  355.7 5.1 copy-start.12
  358.9 25.4 %collective-permute-start.3 = (f32[256,1024]{1,0:T(8,128)S(1)}, f32[256,1024]{1,0:T(8,128)}, u32[]{:S(2)}, u32[]{:S(2)}) collective-permute-start(f32[256,1024]{1,0:T(8,128)S(1)} %gather_fusion.21), channel_id=1, source_target_pairs={{0,64},{8,72},{16,80},{24,88},{32,96},{40,104},{48,112},{56,120},{... | collective-permute-start | bytes 3145736 | tf_op jit(solution)/shard_map/ppermute | solution.py:10
  398.8 244.3 %all-reduce.5.cloned.1.call-start = ((), (), s32[]{:S(2)}) async-start(), calls=%async_computation.3 | async-start | bytes 1048576 | tf_op jit(solution)/shard_map/psum | solution.py:15
  457.5 1.2 copy-start.1
  457.5 1.3 copy-start.2
  465.7 24.7 %collective-permute-start.4 = (f32[256,1024]{1,0:T(8,128)S(1)}, f32[256,1024]{1,0:T(8,128)S(1)}, u32[]{:S(2)}, u32[]{:S(2)}) collective-permute-start(f32[256,1024]{1,0:T(8,128)S(1)} %gather_fusion.25), channel_id=1, source_target_pairs={{0,8},{8,0},{16,24},{24,16},{32,40},{40,32},{48,56},{56,48},{64,72... | collective-permute-start | bytes 3145736 | tf_op jit(solution)/shard_map/ppermute | solution.py:10
  491.8 25.5 %collective-permute-start.5 = (f32[256,1024]{1,0:T(8,128)S(1)}, f32[256,1024]{1,0:T(8,128)S(1)}, u32[]{:S(2)}, u32[]{:S(2)}) collective-permute-start(f32[256,1024]{1,0:T(8,128)S(1)} %gather_fusion.26), channel_id=1, source_target_pairs={{0,16},{8,24},{16,0},{24,8},{32,48},{40,56},{48,32},{56,40},{64,80... | collective-permute-start | bytes 3145736 | tf_op jit(solution)/shard_map/ppermute | solution.py:10
  518.8 22.9 %collective-permute-start.6 = (f32[256,1024]{1,0:T(8,128)S(1)}, f32[256,1024]{1,0:T(8,128)S(1)}, u32[]{:S(2)}, u32[]{:S(2)}) collective-permute-start(f32[256,1024]{1,0:T(8,128)S(1)} %gather_fusion.27), channel_id=1, source_target_pairs={{0,32},{8,40},{16,48},{24,56},{32,0},{40,8},{48,16},{56,24},{64,96... | collective-permute-start | bytes 3145736 | tf_op jit(solution)/shard_map/ppermute | solution.py:10
  543.1 23.5 %collective-permute-start.7 = (f32[256,1024]{1,0:T(8,128)S(1)}, f32[256,1024]{1,0:T(8,128)S(1)}, u32[]{:S(2)}, u32[]{:S(2)}) collective-permute-start(f32[256,1024]{1,0:T(8,128)S(1)} %gather_fusion.28), channel_id=1, source_target_pairs={{0,64},{8,72},{16,80},{24,88},{32,96},{40,104},{48,112},{56,120},{... | collective-permute-start | bytes 3145736 | tf_op jit(solution)/shard_map/ppermute | solution.py:10
  574.9 1.7 copy-start
  647.5 2.3 copy-start.3
Sparse Core Ops, SparseCore 0:
  398.9 57.1 all-reduce.2
  578.1 64.9 all-reduce.4
where the time goes:
time: 672 us; the launch traced here: 659 us
  local copies, waits for them, and re-layouts  322 us (48%)
  waiting for transfers between devices  238 us (35%)
  other arithmetic  36.3 us (5%)
  starting transfers between devices  34.5 us (5%)
  between operations  14.7 us (2%)
  matrix products  14.1 us (2%)
    gather x16, local copies, waits for them, and re-layouts, winner_rows(): candidates = jnp.take_along_axis(joined, levels[level_id], axis=1)  262 us
    psum x2, waiting for transfers between devices, spread(): return lax.psum(jnp.where(mine, x, jnp.zeros_like(x)), axis)  120 us
    ppermute x8, waiting for transfers between devices, partner_2(): lax.ppermute(x, axis, [(i, i ^ 1 << stride) for i in range(lax.axis_size(...  107 us
    gather x8, local copies, waits for them, and re-layouts, body(): candidates = joined[chosen]  19 us
    ppermute x8, starting transfers between devices, partner_2(): lax.ppermute(x, axis, [(i, i ^ 1 << stride) for i in range(lax.axis_size(...  14.3 us
  transfers between devices with their start and end apart: 12, of which 8 were waited for; matrix products, arithmetic and copies ran while one was open for 44% of the time, Pallas kernels for 0%

commit v1 on v0

v1 whole, which is shorter than its diff:
```python
import functools

import jax
import jax.numpy as jnp
from jax import lax
from jax.experimental import pallas as pl
from jax.experimental.pallas import tpu as pltpu
from jax.sharding import PartitionSpec as P

F32 = jnp.float32
BF16 = jnp.bfloat16
VM = pl.BlockSpec(memory_space=pltpu.VMEM)
SM = pl.BlockSpec(memory_space=pltpu.SMEM)
B = 256
PARAMS = dict(compiler_params=pltpu.CompilerParams(vmem_limit_bytes=56 * 1024 * 1024))


def iota(shape, dim):
    return lax.broadcasted_iota(jnp.int32, shape, dim)


def dot(a, b):
    return jnp.dot(a, b, preferred_element_type=F32)


def halves(x):
    high = x.astype(BF16)
    return high, (x - high.astype(F32)).astype(BF16)


def dot3(a, b):
    ah, al = a
    bh, bl = b
    return dot(ah, bh) + (dot(ah, bl) + dot(al, bh))


def pick(onehot, x):
    high, low = halves(x)
    return dot(onehot, high) + dot(onehot, low)


def lookup(table, d, pos):
    n = pos.shape[1]
    hot = (iota((B, n), 0) == pos).astype(F32).astype(BF16)
    high = table // 256
    low = table - high * 256
    both = jnp.concatenate([high, low], axis=0).astype(F32).astype(BF16)
    got = dot(both, hot).astype(jnp.int32)
    rows = table.shape[0]
    values = got[:rows] * 256 + got[rows:]
    return jnp.sum(jnp.where(iota((rows, n), 0) == d, values, 0), axis=0, keepdims=True)


def index_kernel(place, local_picks, level_picks, order, own_out, active_out):
    rows = active_out.shape[1]
    p = place[0]
    retired = jnp.zeros((rows, 1), F32)
    for k in range(order.shape[0]):
        pos = order[k : k + 1, :]
        d = jnp.zeros_like(pos)
        for level in range(level_picks.shape[1] - 1, -1, -1):
            j = lookup(level_picks[k, level], d, pos)
            bit = 1 << level
            d = (d & ~bit) | jnp.where(j >= B, bit, 0)
            pos = j & (B - 1)
        r = lookup(local_picks[k], d, pos)
        own = jnp.where(d == p, r, -1)
        own_out[k * B : (k + 1) * B, :] = jnp.broadcast_to(own, (128, B)).T
        hit = (iota((rows, B), 0) == own).astype(F32)
        retired = jnp.maximum(retired, jnp.max(hit, axis=1, keepdims=True))
        active_out[k] = jnp.broadcast_to(1.0 - retired, (rows, 128))


def assemble_kernel(payload, front, own, matrix_out, pivots_out):
    sources = payload.shape[0] // 17
    groups = sources // 16
    left, right, codes = [], [], []
    for g in range(groups):
        row = jnp.zeros((1, 128), F32)
        for s in range(16 * g, 16 * g + 16):
            left.append(payload[17 * s : 17 * s + 8, :])
            right.append(payload[17 * s + 8 : 17 * s + 16, :])
            row = row + payload[17 * s + 16 : 17 * s + 17, :]
        codes.append(row)
    values = jnp.concatenate([jnp.concatenate(left, axis=0), jnp.concatenate(right, axis=0)], axis=1)
    high, low = halves(values)
    code = jnp.concatenate(codes, axis=1).astype(jnp.int32)
    rows = front.shape[0]
    count = code.shape[1]
    pivot_hot = (own[:, 0:1] == iota((own.shape[0], rows), 1)).astype(F32).astype(BF16)
    for u in range(4):
        hot = (code == iota((rows, count), 0) * 4 + u).astype(F32).astype(BF16)
        tile = front[:, u * B : (u + 1) * B] + (dot(hot, high) + dot(hot, low))
        matrix_out[:, u * B : (u + 1) * B] = tile
        pivots_out[:, u * B : (u + 1) * B] = pick(pivot_hot, tile)


def inverse_of(diag):
    eye = iota((B, B), 0) == iota((B, B), 1)
    only = jnp.where(eye, diag, 0.0)
    by_row = 1.0 / jnp.sum(only, axis=1, keepdims=True)
    by_col = 1.0 / jnp.sum(only, axis=0, keepdims=True)
    two = jnp.where(eye, 2.0, 0.0)
    x = by_row * (two - diag * by_col)
    xs = halves(x)
    return dot3(xs, halves(two - dot3(halves(diag), xs)))


def panel_kernel(place, w_own, w_other, r_own, r_other, active, half_out, tile_out):
    even = place[1] % 2 == 0
    w0 = jnp.where(even, w_own[...], w_other[...])
    w1 = jnp.where(even, w_other[...], w_own[...])
    r0 = jnp.where(even, r_own[...], r_other[...])
    r1 = jnp.where(even, r_other[...], r_own[...])
    act0 = active[0][:, 0:1]
    act1 = active[1][:, 0:1]
    inv0 = halves(inverse_of(w0[:B]))
    m0w = dot3(halves(w0[B:]), inv0)
    m0w_s = halves(m0w)
    p01 = halves(w1[:B])
    inv1 = halves(inverse_of(w1[B:] - dot3(m0w_s, p01)))
    m0 = dot3(halves(r0), inv0)
    m0a = jnp.where(act0 > 0, m0, 0.0)
    r1 = r1 - dot3(halves(m0a), p01)
    m1 = dot3(halves(r1), inv1)
    n1 = jnp.where(act1 > 0, m1, 0.0)
    n0 = m0a - dot3(halves(n1), m0w_s)
    half_out[...] = jnp.where(even, n0, n1)
    tile_out[...] = jnp.where(even, jnp.where(act0 > 0, m0, r0), jnp.where(act1 > 0, m1, r1))


def update_kernel(place, matrix, pivots, n_own, n_other, tile, out):
    even = place[1] % 2 == 0
    n0 = halves(jnp.where(even, n_own[...], n_other[...]))
    n1 = halves(jnp.where(even, n_other[...], n_own[...]))
    for u in range(4):
        cols = slice(u * B, (u + 1) * B)
        new = matrix[:, cols] - (
            dot3(n0, halves(pivots[:B, cols])) + dot3(n1, halves(pivots[B:, cols]))
        )
        if u == 0:
            new = jnp.where(place[1] < 2, tile[...], new)
        out[:, cols] = new


def call(kernel, outs, n_in, scalars=1, flops=0, moved=0):
    return pl.pallas_call(
        kernel,
        out_shape=outs,
        in_specs=[SM] * scalars + [VM] * (n_in - scalars),
        out_specs=jax.tree.map(lambda _: VM, outs),
        cost_estimate=pl.CostEstimate(flops=flops, bytes_accessed=moved, transcendentals=0),
        **PARAMS,
    )


def shaped(*shape, dtype=F32):
    return jax.ShapeDtypeStruct(shape, dtype)


def core_swap(x):
    return lax.ppermute(x, "pcol", [(i, i ^ 1) for i in range(lax.axis_size("pcol"))])


def spread_z(x, z):
    one = lax.ppermute(x, "pcol", [(0, 2), (1, 3)])
    three = lax.ppermute(x, "pcol", [(0, 6), (1, 7)])
    two = lax.ppermute(x, "pcol", [(0, 4), (1, 5)])
    return jnp.where(z == 0, x, jnp.where(z == 1, one, jnp.where(z == 2, two, three)))


def body(front, partials, targets, counts, local_picks, level_picks, order):
    rows = front.shape[0] * front.shape[1]
    cols = front.shape[2] * front.shape[3]
    p = lax.axis_index("prow")
    q = lax.axis_index("pcol")
    me = p * lax.axis_size("pcol") + q
    place = jnp.stack([p, q]).astype(jnp.int32)
    sources = partials.shape[1]
    slots = partials.shape[2]

    used = iota((sources, slots), 1) < counts[0][:, None]
    codes = jnp.where(used, targets[0], -1)
    lanes = jnp.tile(codes, (1, 16))
    code_row = jnp.where(iota((sources, 128), 1) // slots == me % 16, lanes, 0).astype(F32)
    values = partials[0].reshape(sources, slots, 2, 128).transpose(0, 2, 1, 3).reshape(sources, 16, 128)
    payload = jnp.concatenate([values, code_row[:, None, :]], axis=1).reshape(sources * 17, 1, 128)
    payload = lax.all_to_all(payload, ("prow", "pcol"), 0, 0, tiled=True).reshape(sources * 17, 128)

    own, active = call(
        index_kernel, (shaped(2 * B, 128, dtype=jnp.int32), shaped(2, rows, 128)), 4, flops=10**9, moved=10**6
    )(place, local_picks, level_picks, order)

    matrix, pivots = call(
        assemble_kernel, (shaped(rows, cols), shaped(2 * B, cols)), 3, scalars=0, flops=4 * 10**9, moved=8 * 10**6
    )(payload, front.reshape(rows, cols), own)

    r_own = matrix[:, :B]
    r_other = core_swap(r_own)
    pivots = lax.psum(pivots, "prow")
    w_own = pivots[:, :B]
    w_other = core_swap(w_own)
    half, tile = call(
        panel_kernel, (shaped(rows, B), shaped(rows, B)), 6, flops=2 * 10**9, moved=4 * 10**6
    )(place, w_own, w_other, r_own, r_other, active)
    n_own = spread_z(half, q // 2)
    n_other = core_swap(n_own)
    out = call(
        update_kernel, shaped(rows, cols), 6, flops=2 * 10**9, moved=8 * 10**6
    )(place, matrix, pivots, n_own, n_other, tile)
    return out.reshape(front.shape)


def solution(mesh):
    placed = (
        P(None, "prow", None, "pcol"),
        P(("prow", "pcol"), None, None, None),
        P(("prow", "pcol"), None, None),
        P(("prow", "pcol"), None),
        P(),
        P(),
        P(),
    )
    return jax.shard_map(
        body, mesh=mesh, in_specs=placed, out_specs=P(None, "prow", None, "pcol"), check_vma=False
    )
```

time: 672 us -> 196 us (0.29); the launches traced: 659 us -> 193 us
  local copies, waits for them, and re-layouts: 322 us -> 10.9 us
  waiting for transfers between devices: 238 us -> 124 us
  other arithmetic: 36.3 us -> 2.84 us
  Pallas kernels: 0 us -> 25.2 us
  starting transfers between devices: 34.5 us -> 17 us
  matrix products: 14.1 us -> 0 us
    gather x48 -> x0, local copies, waits for them, and re-layouts: 307 us -> none  [the longest x16 262 us: winner_rows(): candidates = jnp.take_along_axis(joined, levels[level_id], axis=1)]
    ppermute x8 -> x6, waiting for transfers between devices: 107 us -> 26.7 us  [the longest x1 23.7 us: spread_z(): two = lax.ppermute(x, 'pcol', [(0, 4), (1, 5)])]
    psum x2 -> x1, waiting for transfers between devices: 120 us -> 85.9 us  [body(): pivots = lax.psum(pivots, 'prow')]
    pallas_call x0 -> x4, Pallas kernels: none -> 25.2 us  [the longest x1 10.2 us: body(): call(assemble_kernel, (shaped(rows, cols), shaped(2 * B, cols)), 3, scala...]
    select_n x30 -> x2, other arithmetic: 15.4 us -> 0.83 us  [the longest x1 0.69 us: body(): codes = jnp.where(used, targets[0], -1)]
    dot_general x12 -> x0, matrix products: 14.1 us -> none  [the longest x2 8.06 us: body(): product = jnp.dot(multipliers, pivots, precision=lax.Precision.HIGHEST)]
    unnamed x5 -> x0, other arithmetic: 10 us -> none
    all_to_all x2 -> x1, starting transfers between devices: 20.1 us -> 10.4 us  [body(): lax.all_to_all(payload, ('prow', 'pcol'), 0, 0, tiled=True)]
  transfers between devices with their start and end apart: 12 -> 8, of which waited for: 8 -> 5; matrix products, arithmetic and copies ran while one was open for 44% -> 2% of each run, Pallas kernels for 0% -> 2%
where the time goes in v1:
time: 196 us; the launch traced here: 193 us
  waiting for transfers between devices  124 us (63%)
  Pallas kernels  25.2 us (13%)
  starting transfers between devices  17 us (9%)
  between operations  13.5 us (7%)
  local copies, waits for them, and re-layouts  10.9 us (6%)
  other arithmetic  2.84 us (1%)
    psum x1, waiting for transfers between devices, body(): pivots = lax.psum(pivots, 'prow')  85.9 us
    ppermute x1, waiting for transfers between devices, spread_z(): two = lax.ppermute(x, 'pcol', [(0, 4), (1, 5)])  23.7 us
    all_to_all x1, waiting for transfers between devices, body(): lax.all_to_all(payload, ('prow', 'pcol'), 0, 0, tiled=True)  11.2 us
    all_to_all x1, starting transfers between devices, body(): lax.all_to_all(payload, ('prow', 'pcol'), 0, 0, tiled=True)  10.4 us
    pallas_call x1, Pallas kernels, body(): call(assemble_kernel, (shaped(rows, cols), shaped(2 * B, cols)), 3, scala...  10.2 us
    pallas_call x1, Pallas kernels, body(): call(panel_kernel, (shaped(rows, B), shaped(rows, B)), 6, flops=2 * 10 **...  5.86 us
    pallas_call x1, Pallas kernels, body(): call(update_kernel, shaped(rows, cols), 6, flops=2 * 10 ** 9, moved=8 * 1...  5.79 us
    unnamed x17, local copies, waits for them, and re-layouts  4.4 us
  transfers between devices with their start and end apart: 8, of which 5 were waited for; matrix products, arithmetic and copies ran while one was open for 2% of the time, Pallas kernels for 2%

profile of v1, /device:TPU:65, one launch (start us, length us, event | category | flops | bytes accessed | tf_op | source)
XLA Modules:
  0.0 193.2 jit_solution(15620597552536640246)
XLA Ops:
  6.5 0.7 bitcast_select_fusion.1
  7.2 0.1 fusion
  7.4 0.1 copy.10
  7.5 1.3 pad_maximum_fusion
  8.8 1.1 reshape.114
  9.9 0.0 copy-start
  9.9 10.4 %all-to-all-start = ((f32[2176,1,128]{2,1,0:T(1,128)}), f32[2176,1,128]{2,1,0:T(1,128)S(1)}, u32[]{:S(2)}, u32[]{:S(2)}) async-start(f32[2176,1,128]{2,1,0:T(1,128)} %bitcast.8), calls=%async_computation | async-start | bytes 2228224 | tf_op jit(solution)/shard_map/all_to_all | solution.py:188
  20.3 0.0 all-reduce.2.cloned.1.call-start
  20.3 0.0 copy-done
  20.3 1.8 copy.12
  22.1 0.6 pad_add_fusion.place
  22.7 3.4 %shard_map.73 = (s32[512,128]{1,0:T(8,128)}, f32[2,512,128]{2,1,0:T(8,128)}) custom-call(s32[2]{0:T(128)} %pad_add_fusion.place, s32[2,16,256]{2,1,0:T(8,128)} %local_picks.1, s32[2,4,16,256]{3,2,1,0:T(8,128)} %level_picks.1, s32[2,256]{1,0:T(2,128)} %order.1), custom_call_target="tpu_custom_call" | custom-call | flops 1000000000 | bytes 1000000 | tf_op jit(solution)/shard_map/pallas_call | solution.py:190
  26.0 11.2 %all-to-all-done = f32[2176,1,128]{2,1,0:T(1,128)S(1)} async-done(((f32[2176,1,128]{2,1,0:T(1,128)}), f32[2176,1,128]{2,1,0:T(1,128)S(1)}, u32[]{:S(2)}, u32[]{:S(2)}) %all-to-all-start) | async-done | bytes 1114144 | tf_op jit(solution)/shard_map/all_to_all | solution.py:188
  37.2 0.0 copy-start.2
  37.2 1.0 copy-done.2
  38.2 10.2 %shard_map.74 = (f32[512,1024]{1,0:T(8,128)}, f32[512,1024]{1,0:T(8,128)}) custom-call(f32[2176,128]{1,0:T(8,128)} %bitcast.21, f32[512,1024]{1,0:T(8,128)} %bitcast.20, s32[512,128]{1,0:T(8,128)} %get-tuple-element.11.own), custom_call_target="tpu_custom_call" | custom-call | flops 4000000000 | bytes 8000000 | tf_op jit(solution)/shard_map/pallas_call | solution.py:194
  48.4 0.0 all-reduce.2.cloned.1.call-update
  48.4 1.1 slice.7.r_own
  49.5 0.0 copy-start.4
  49.5 0.8 collective-permute-start.1
  50.3 85.9 %all-reduce.2.cloned.1.call-done.pivots = f32[512,1024]{1,0:T(8,128)} async-done(((f32[512,1024]{1,0:T(8,128)}), f32[512,1024]{1,0:T(8,128)}) %all-reduce.2.cloned.1.call-update) | async-done | bytes 2097168 | tf_op jit(solution)/shard_map/psum | solution.py:200
  136.1 1.1 slice.8.w_own
  137.2 0.0 copy-start.5
  137.2 1.9 collective-permute-start
  139.1 0.0 collective-permute-done.1.r_other
  139.1 0.0 copy-start.6
  139.1 1.5 collective-permute-done.w_other
  140.6 0.0 copy-start.7
  140.6 0.0 copy-done.4
  140.6 0.0 copy-done.5
  140.6 0.0 copy-done.6
  140.6 0.8 copy-done.7
  141.4 5.9 %shard_map.75 = (f32[512,256]{1,0:T(8,128)}, f32[512,256]{1,0:T(8,128)}) custom-call(s32[2]{0:T(128)} %pad_add_fusion.place, f32[512,256]{1,0:T(8,128)} %copy-done.5, f32[512,256]{1,0:T(8,128)} %copy-done.7, f32[512,256]{1,0:T(8,128)} %copy-done.4, f32[512,256]{1,0:T(8,128)} %copy-done.6, f32[2,512,128]{2,1,0:T(8,128)} %get-tuple-element.14.active), custom_call_target="tpu_custom_call" | custom-call | flops 2000000000 | bytes 4000000 | tf_op jit(solution)/shard_map/pallas_call | solution.py:203
  147.3 0.7 collective-permute-start.2
  148.0 1.3 collective-permute-start.3
  149.3 0.7 collective-permute-start.4
  150.0 0.0 collective-permute-done.2
  150.0 23.7 %collective-permute-done.3 = f32[512,256]{1,0:T(8,128)S(1)} collective-permute-done((f32[512,256]{1,0:T(8,128)}, f32[512,256]{1,0:T(8,128)S(1)}, u32[]{:S(2)}, u32[]{:S(2)}) %collective-permute-start.3) | collective-permute-done | bytes 524320 | tf_op jit(solution)/shard_map/ppermute | solution.py:168
  173.7 0.0 collective-permute-done.4
  173.7 0.1 select_select_fusion.n_own
  173.8 0.0 copy-start.1
  173.8 1.3 collective-permute-start.5
  175.1 1.5 collective-permute-done.5.n_other
  176.6 0.0 copy-start.3
  176.6 0.0 copy-done.1
  176.6 0.8 copy-done.3
  177.4 5.8 %shard_map.76 = f32[512,1024]{1,0:T(8,128)} custom-call(s32[2]{0:T(128)} %pad_add_fusion.place, f32[512,1024]{1,0:T(8,128)} %get-tuple-element.12.matrix, f32[512,1024]{1,0:T(8,128)} %all-reduce.2.cloned.1.call-done.pivots, f32[512,256]{1,0:T(8,128)} %copy-done.1, f32[512,256]{1,0:T(8,128)} %copy-done.3, f32[512,256]{1,0:T(8,128)} %get-tuple-element.16.tile), custom_call_target="tpu_custom_call" | custom-call | flops 2000000000 | bytes 8000000 | tf_op jit(solution)/shard_map/pallas_call | solution.py:208
  183.2 3.2 %reshape.117 = f32[2,256,4,256]{3,2,1,0:T(4,128)} reshape(f32[512,1024]{1,0:T(8,128)} %shard_map.76) | data formatting | bytes 4194304 | tf_op jit(solution)/shard_map/reshape | solution.py:211
  (2 shorter events, 0.0 us)
Async XLA Ops:
  9.9 10.4 %copy-start = (f32[2,256,4,256]{3,2,1,0:T(4,128)S(1)}, f32[2,256,4,256]{3,2,1,0:T(4,128)}, u32[]{:S(2)}) copy-start(f32[2,256,4,256]{3,2,1,0:T(4,128)} %param.7) | copy-start | bytes 6291460
  9.9 27.3 %all-to-all-start = ((f32[2176,1,128]{2,1,0:T(1,128)}), f32[2176,1,128]{2,1,0:T(1,128)S(1)}, u32[]{:S(2)}, u32[]{:S(2)}) async-start(f32[2176,1,128]{2,1,0:T(1,128)} %bitcast.8), calls=%async_computation | async-start | bytes 2228224 | tf_op jit(solution)/shard_map/all_to_all | solution.py:188
  20.3 115.9 %all-reduce.2.cloned.1.call-start = ((), (), s32[]{:S(2)}) async-start(), calls=%async_computation.1 | async-start | bytes 4194304 | tf_op jit(solution)/shard_map/psum | solution.py:200
  37.2 1.0 copy-start.2
  49.5 91.1 %copy-start.4 = (f32[512,256]{1,0:T(8,128)}, f32[512,256]{1,0:T(8,128)S(1)}, u32[]{:S(2)}) copy-start(f32[512,256]{1,0:T(8,128)S(1)} %slice.7.r_own) | copy-start | bytes 1572868
  49.5 89.6 %collective-permute-start.1 = (f32[512,256]{1,0:T(8,128)S(1)}, f32[512,256]{1,0:T(8,128)S(1)}, u32[]{:S(2)}, u32[]{:S(2)}) collective-permute-start(f32[512,256]{1,0:T(8,128)S(1)} %slice.7.r_own), channel_id=1, source_target_pairs={{0,1},{1,0},{2,3},{3,2},{4,5},{5,4},{6,7},{7,6},{8,9},{9,8},{10,11... | collective-permute-start | bytes 1572872 | tf_op jit(solution)/shard_map/ppermute | solution.py:162
  137.2 3.4 %copy-start.5 = (f32[512,256]{1,0:T(8,128)}, f32[512,256]{1,0:T(8,128)S(1)}, u32[]{:S(2)}) copy-start(f32[512,256]{1,0:T(8,128)S(1)} %slice.8.w_own) | copy-start | bytes 1572868
  137.2 3.4 %collective-permute-start = (f32[512,256]{1,0:T(8,128)S(1)}, f32[512,256]{1,0:T(8,128)S(1)}, u32[]{:S(2)}, u32[]{:S(2)}) collective-permute-start(f32[512,256]{1,0:T(8,128)S(1)} %slice.8.w_own), channel_id=1, source_target_pairs={{0,1},{1,0},{2,3},{3,2},{4,5},{5,4},{6,7},{7,6},{8,9},{9,8},{10,11... | collective-permute-start | bytes 1572872 | tf_op jit(solution)/shard_map/ppermute | solution.py:162
  139.1 1.5 copy-start.6
  140.6 0.8 copy-start.7
  147.3 2.7 %collective-permute-start.2 = (f32[512,256]{1,0:T(8,128)}, f32[512,256]{1,0:T(8,128)S(1)}, u32[]{:S(2)}, u32[]{:S(2)}) collective-permute-start(f32[512,256]{1,0:T(8,128)} %get-tuple-element.15), channel_id=1, source_target_pairs={{0,2},{1,3},{8,10},{9,11},{16,18},{17,19},{24,26},{25,27},{32,34},... | collective-permute-start | bytes 1572872 | tf_op jit(solution)/shard_map/ppermute | solution.py:166
  148.0 25.7 %collective-permute-start.3 = (f32[512,256]{1,0:T(8,128)}, f32[512,256]{1,0:T(8,128)S(1)}, u32[]{:S(2)}, u32[]{:S(2)}) collective-permute-start(f32[512,256]{1,0:T(8,128)} %get-tuple-element.15), channel_id=1, source_target_pairs={{0,4},{1,5},{8,12},{9,13},{16,20},{17,21},{24,28},{25,29},{32,36},... | collective-permute-start | bytes 1572872 | tf_op jit(solution)/shard_map/ppermute | solution.py:168
  149.3 24.4 %collective-permute-start.4 = (f32[512,256]{1,0:T(8,128)}, f32[512,256]{1,0:T(8,128)S(1)}, u32[]{:S(2)}, u32[]{:S(2)}) collective-permute-start(f32[512,256]{1,0:T(8,128)} %get-tuple-element.15), channel_id=1, source_target_pairs={{0,6},{1,7},{8,14},{9,15},{16,22},{17,23},{24,30},{25,31},{32,38},... | collective-permute-start | bytes 1572872 | tf_op jit(solution)/shard_map/ppermute | solution.py:167
  173.8 2.8 %copy-start.1 = (f32[512,256]{1,0:T(8,128)}, f32[512,256]{1,0:T(8,128)S(1)}, u32[]{:S(2)}) copy-start(f32[512,256]{1,0:T(8,128)S(1)} %select_select_fusion.n_own) | copy-start | bytes 1572868
  173.8 2.8 %collective-permute-start.5 = (f32[512,256]{1,0:T(8,128)S(1)}, f32[512,256]{1,0:T(8,128)S(1)}, u32[]{:S(2)}, u32[]{:S(2)}) collective-permute-start(f32[512,256]{1,0:T(8,128)S(1)} %select_select_fusion.n_own), channel_id=1, source_target_pairs={{0,1},{1,0},{2,3},{3,2},{4,5},{5,4},{6,7},{7,6},{8,9},{9,8},{10,11... | collective-permute-start | bytes 1572872 | tf_op jit(solution)/shard_map/ppermute | solution.py:162
  176.6 0.8 copy-start.3
Sparse Core Ops, SparseCore 0:
  48.5 87.5 all-reduce.1

commit v2 on v1

--- a/solution.py
+++ b/solution.py
@@ -12,6 +12,7 @@
 VM = pl.BlockSpec(memory_space=pltpu.VMEM)
 SM = pl.BlockSpec(memory_space=pltpu.SMEM)
 B = 256
+KEEP = 48
 PARAMS = dict(compiler_params=pltpu.CompilerParams(vmem_limit_bytes=56 * 1024 * 1024))
 
 
@@ -51,10 +52,12 @@
     return jnp.sum(jnp.where(iota((rows, n), 0) == d, values, 0), axis=0, keepdims=True)
 
 
-def index_kernel(place, local_picks, level_picks, order, own_out, active_out):
+def index_kernel(place, local_picks, level_picks, order, own_out, active_out, give_out, slot_out, fits_out):
     rows = active_out.shape[1]
+    keep = give_out.shape[0]
     p = place[0]
     retired = jnp.zeros((rows, 1), F32)
+    owners, locals_ = [], []
     for k in range(order.shape[0]):
         pos = order[k : k + 1, :]
         d = jnp.zeros_like(pos)
@@ -69,13 +72,25 @@
         hit = (iota((rows, B), 0) == own).astype(F32)
         retired = jnp.maximum(retired, jnp.max(hit, axis=1, keepdims=True))
         active_out[k] = jnp.broadcast_to(1.0 - retired, (rows, 128))
-
-
-def assemble_kernel(payload, front, own, matrix_out, pivots_out):
+        owners.append(d)
+        locals_.append(r)
+    d = jnp.concatenate(owners, axis=1)
+    r = jnp.concatenate(locals_, axis=1)
+    n = d.shape[1]
+    d_col = jnp.broadcast_to(d, (128, n)).T[:, 0:1]
+    before = (d_col == d) & (iota((n, n), 0) < iota((n, n), 1))
+    rank = jnp.sum(before.astype(jnp.int32), axis=0, keepdims=True)
+    fits_out[0] = (jnp.max(rank) < keep).astype(jnp.int32)
+    slot_out[...] = jnp.broadcast_to(d * keep + rank, (128, n)).T
+    mine = (iota((keep, n), 0) == rank) & (d == p)
+    give = jnp.sum(jnp.where(mine, r + 1, 0), axis=1, keepdims=True) - 1
+    give_out[...] = jnp.broadcast_to(give, (keep, 128))
+
+
+def unpack(payload):
     sources = payload.shape[0] // 17
-    groups = sources // 16
     left, right, codes = [], [], []
-    for g in range(groups):
+    for g in range(sources // 16):
         row = jnp.zeros((1, 128), F32)
         for s in range(16 * g, 16 * g + 16):
             left.append(payload[17 * s : 17 * s + 8, :])
@@ -83,16 +98,55 @@
             row = row + payload[17 * s + 16 : 17 * s + 17, :]
         codes.append(row)
     values = jnp.concatenate([jnp.concatenate(left, axis=0), jnp.concatenate(right, axis=0)], axis=1)
-    high, low = halves(values)
-    code = jnp.concatenate(codes, axis=1).astype(jnp.int32)
+    return halves(values), jnp.concatenate(codes, axis=1).astype(jnp.int32)
+
+
+def hot_of(code, rows, u):
+    return (code == iota((rows, code.shape[1]), 0) * 4 + u).astype(F32).astype(BF16)
+
+
+def rows_hot(chosen, rows):
+    return (chosen[:, 0:1] == iota((chosen.shape[0], rows), 1)).astype(F32).astype(BF16)
+
+
+def assemble_kernel(payload, front, own, matrix_out, pivots_out):
+    (high, low), code = unpack(payload)
     rows = front.shape[0]
-    count = code.shape[1]
-    pivot_hot = (own[:, 0:1] == iota((own.shape[0], rows), 1)).astype(F32).astype(BF16)
+    pivot_hot = rows_hot(own, rows)
     for u in range(4):
-        hot = (code == iota((rows, count), 0) * 4 + u).astype(F32).astype(BF16)
-        tile = front[:, u * B : (u + 1) * B] + (dot(hot, high) + dot(hot, low))
-        matrix_out[:, u * B : (u + 1) * B] = tile
-        pivots_out[:, u * B : (u + 1) * B] = pick(pivot_hot, tile)
+        cols = slice(u * B, (u + 1) * B)
+        hot = hot_of(code, rows, u)
+        tile = front[:, cols] + (dot(hot, high) + dot(hot, low))
+        matrix_out[:, cols] = tile
+        pivots_out[:, cols] = pick(pivot_hot, tile)
+
+
+def first_kernel(payload, front, give, tile_out, send_out, high_out, low_out, code_out):
+    (high, low), code = unpack(payload)
+    high_out[...] = high
+    low_out[...] = low
+    code_out[...] = jnp.broadcast_to(code, code_out.shape)
+    rows = front.shape[0]
+    hot = hot_of(code, rows, 0)
+    tile = front[:, :B] + (dot(hot, high) + dot(hot, low))
+    tile_out[...] = tile
+    sent = pick(rows_hot(give, rows), tile)
+    for i in range(send_out.shape[0] // sent.shape[0]):
+        send_out[i * sent.shape[0] : (i + 1) * sent.shape[0], :] = sent
+
+
+def rest_kernel(high, low, code, front, give, rest_out, send_out):
+    rows = front.shape[0]
+    give_hot = rows_hot(give, rows)
+    keep = give.shape[0]
+    for u in range(1, 4):
+        hot = hot_of(code[0:1, :], rows, u)
+        tile = front[:, u * B : (u + 1) * B] + (dot(hot, high[...]) + dot(hot, low[...]))
+        cols = slice((u - 1) * B, u * B)
+        rest_out[:, cols] = tile
+        sent = pick(give_hot, tile)
+        for i in range(send_out.shape[0] // keep):
+            send_out[i * keep : (i + 1) * keep, cols] = sent
 
 
 def inverse_of(diag):
@@ -104,6 +158,11 @@
     x = by_row * (two - diag * by_col)
     xs = halves(x)
     return dot3(xs, halves(two - dot3(halves(diag), xs)))
+
+
+def panel_slots_kernel(place, slot, w_own, w_other, r_own, r_other, active, half_out, tile_out):
+    hot = rows_hot(slot, w_own.shape[0])
+    panel_kernel(place, pick(hot, w_own[...]), pick(hot, w_other[...]), r_own, r_other, active, half_out, tile_out)
 
 
 def panel_kernel(place, w_own, w_other, r_own, r_other, active, half_out, tile_out):
@@ -143,12 +202,38 @@
         out[:, cols] = new
 
 
-def call(kernel, outs, n_in, scalars=1, flops=0, moved=0):
+def spread_kernel(place, slot, n_own, n_other, high_out, low_out):
+    even = place[1] % 2 == 0
+    hot = rows_hot(slot, high_out.shape[1])
+    h0, l0 = halves(jnp.where(even, n_own[...], n_other[...]))
+    h1, l1 = halves(jnp.where(even, n_other[...], n_own[...]))
+    high_out[...] = (dot(h0, hot[:B]) + dot(h1, hot[B:])).astype(BF16)
+    low_out[...] = (dot(l0, hot[:B]) + dot(l1, hot[B:])).astype(BF16)
+
+
+def finish_kernel(place, first, rest, w_first, w_rest, high, low, tile, out):
+    n = (high[...], low[...])
+    half = out.shape[1]
+    for u in range(4):
+        if u == 0:
+            new = first[...] - dot3(n, halves(w_first[...]))
+            new = jnp.where(place[1] < 2, tile[...], new)
+        else:
+            cols = slice((u - 1) * B, u * B)
+            new = rest[:, cols] - dot3(n, halves(w_rest[:, cols]))
+        for t in range(out.shape[0]):
+            out[t, :, u, :] = new[t * half : (t + 1) * half]
+
+
+def call(kernel, outs, n_in, scalars=1, outs_in_smem=0, flops=0, moved=0):
+    specs = jax.tree.map(lambda _: VM, outs)
+    if outs_in_smem:
+        specs = specs[:-outs_in_smem] + (SM,) * outs_in_smem
     return pl.pallas_call(
         kernel,
         out_shape=outs,
         in_specs=[SM] * scalars + [VM] * (n_in - scalars),
-        out_specs=jax.tree.map(lambda _: VM, outs),
+        out_specs=specs,
         cost_estimate=pl.CostEstimate(flops=flops, bytes_accessed=moved, transcendentals=0),
         **PARAMS,
     )
@@ -187,28 +272,78 @@
     payload = jnp.concatenate([values, code_row[:, None, :]], axis=1).reshape(sources * 17, 1, 128)
     payload = lax.all_to_all(payload, ("prow", "pcol"), 0, 0, tiled=True).reshape(sources * 17, 128)
 
-    own, active = call(
-        index_kernel, (shaped(2 * B, 128, dtype=jnp.int32), shaped(2, rows, 128)), 4, flops=10**9, moved=10**6
+    own, active, give, slot, fits = call(
+        index_kernel,
+        (
+            shaped(2 * B, 128, dtype=jnp.int32),
+            shaped(2, rows, 128),
+            shaped(KEEP, 128, dtype=jnp.int32),
+            shaped(2 * B, 128, dtype=jnp.int32),
+            shaped(1, dtype=jnp.int32),
+        ),
+        4,
+        outs_in_smem=1,
+        flops=10**9,
+        moved=10**6,
     )(place, local_picks, level_picks, order)
-
-    matrix, pivots = call(
-        assemble_kernel, (shaped(rows, cols), shaped(2 * B, cols)), 3, scalars=0, flops=4 * 10**9, moved=8 * 10**6
-    )(payload, front.reshape(rows, cols), own)
-
-    r_own = matrix[:, :B]
-    r_other = core_swap(r_own)
-    pivots = lax.psum(pivots, "prow")
-    w_own = pivots[:, :B]
-    w_other = core_swap(w_own)
-    half, tile = call(
-        panel_kernel, (shaped(rows, B), shaped(rows, B)), 6, flops=2 * 10**9, moved=4 * 10**6
-    )(place, w_own, w_other, r_own, r_other, active)
-    n_own = spread_z(half, q // 2)
-    n_other = core_swap(n_own)
-    out = call(
-        update_kernel, shaped(rows, cols), 6, flops=2 * 10**9, moved=8 * 10**6
-    )(place, matrix, pivots, n_own, n_other, tile)
-    return out.reshape(front.shape)
+    front, own = lax.optimization_barrier((front, own))
+    flat = front.reshape(rows, cols)
+    copies = lax.axis_size("prow") * KEEP
+
+    def gather(payload, flat, own, active, give, slot, place):
+        first, send, high, low, code = call(
+            first_kernel,
+            (
+                shaped(rows, B),
+                shaped(copies, B),
+                shaped(sources * slots, B, dtype=BF16),
+                shaped(sources * slots, B, dtype=BF16),
+                shaped(8, sources * slots, dtype=jnp.int32),
+            ),
+            3,
+            scalars=0,
+            flops=10**9,
+            moved=4 * 10**6,
+        )(payload, flat, give)
+        w_first = lax.all_to_all(send, "prow", 0, 0, tiled=True)
+        r_other = core_swap(first)
+        rest, send = call(
+            rest_kernel, (shaped(rows, cols - B), shaped(copies, cols - B)), 5, scalars=0, flops=3 * 10**9, moved=8 * 10**6
+        )(high, low, code, flat, give)
+        w_rest = lax.all_to_all(send, "prow", 0, 0, tiled=True)
+        w_other = core_swap(w_first)
+        half, tile = call(
+            panel_slots_kernel, (shaped(rows, B), shaped(rows, B)), 7, flops=2 * 10**9, moved=4 * 10**6
+        )(place, slot, w_first, w_other, first, r_other, active)
+        n_own = spread_z(half, place[1] // 2)
+        n_other = core_swap(n_own)
+        high, low = call(
+            spread_kernel, (shaped(rows, copies, dtype=BF16), shaped(rows, copies, dtype=BF16)), 4, flops=10**9, moved=2 * 10**6
+        )(place, slot, n_own, n_other)
+        return call(finish_kernel, shaped(*front.shape), 8, flops=4 * 10**9, moved=8 * 10**6)(
+            place, first, rest, w_first, w_rest, high, low, tile
+        )
+
+    def add_up(payload, flat, own, active, give, slot, place):
+        matrix, pivots = call(
+            assemble_kernel, (shaped(rows, cols), shaped(2 * B, cols)), 3, scalars=0, flops=4 * 10**9, moved=8 * 10**6
+        )(payload, flat, own)
+        r_own = matrix[:, :B]
+        r_other = core_swap(r_own)
+        pivots = lax.psum(pivots, "prow")
+        w_own = pivots[:, :B]
+        w_other = core_swap(w_own)
+        half, tile = call(
+            panel_kernel, (shaped(rows, B), shaped(rows, B)), 6, flops=2 * 10**9, moved=4 * 10**6
+        )(place, w_own, w_other, r_own, r_other, active)
+        n_own = spread_z(half, place[1] // 2)
+        n_other = core_swap(n_own)
+        out = call(update_kernel, shaped(rows, cols), 6, flops=2 * 10**9, moved=8 * 10**6)(
+            place, matrix, pivots, n_own, n_other, tile
+        )
+        return out.reshape(front.shape)
+
+    return lax.cond(fits[0] == 1, gather, add_up, payload, flat, own, active, give, slot, place)
 
 
 def solution(mesh):

time: 196 us -> 133 us (0.68)
  the two profiles are of different devices: /device:TPU:65 before, /device:TPU:1 now
where the time goes in v2:
time: 133 us
  waiting for transfers between devices  38.9 us (29%)
  Pallas kernels  30.2 us (23%)
  starting transfers between devices  24.5 us (18%)
  blocking collectives  16.8 us (13%)
  between operations  14 us (11%)
  local copies, waits for them, and re-layouts  4.72 us (4%)
  other arithmetic  3.41 us (3%)
    all_to_all x1, blocking collectives, gather(): w_first = lax.all_to_all(send, 'prow', 0, 0, tiled=True)  16.8 us
    all_to_all x1, waiting for transfers between devices, body(): lax.all_to_all(payload, ('prow', 'pcol'), 0, 0, tiled=True)  15.1 us
    all_to_all x1, starting transfers between devices, body(): lax.all_to_all(payload, ('prow', 'pcol'), 0, 0, tiled=True)  11.5 us
    ppermute x1, waiting for transfers between devices, spread_z(): one = lax.ppermute(x, 'pcol', [(0, 2), (1, 3)])  11.2 us
    ppermute x1, waiting for transfers between devices, spread_z(): three = lax.ppermute(x, 'pcol', [(0, 6), (1, 7)])  7.83 us
    pallas_call x1, Pallas kernels, gather(): call(finish_kernel, shaped(*front.shape), 8, flops=4 * 10 ** 9, moved=8 *...  7.54 us
    pallas_call x1, Pallas kernels, gather(): call(panel_slots_kernel, (shaped(rows, B), shaped(rows, B)), 7, flops=2 *...  6.96 us
    pallas_call x1, Pallas kernels, gather(): call(rest_kernel, (shaped(rows, cols - B), shaped(copies, cols - B)), 5,...  6.65 us
  transfers between devices with their start and end apart: 8, of which 6 were waited for; matrix products, arithmetic and copies ran while one was open for 1% of the time, Pallas kernels for 15%

profile of v2, /device:TPU:1, one launch (start us, length us, event | category | flops | bytes accessed | tf_op | source)
XLA Modules:
  0.0 132.6 jit_solution(8748070239472906271)
XLA Ops:
  6.5 0.7 bitcast_select_fusion.1
  7.2 0.1 fusion
  7.4 0.1 copy.12
  7.5 1.3 %pad_maximum_fusion = f32[128,17,128]{2,1,0:T(8,128)S(1)} fusion(f32[128,1,128]{2,1,0:T(1,128)S(1)} %copy.12, f32[128,16,128]{2,1,0:T(8,128)} %bitcast.31), kind=kLoop, calls=%fused_computation.2 | loop fusion | flops 278528 | bytes 2228224 | tf_op jit(solution)/shard_map/concatenate | solution.py:272
  8.8 1.1 reshape.122
  9.9 11.5 %all-to-all-start.2 = ((f32[2176,1,128]{2,1,0:T(1,128)}), f32[2176,1,128]{2,1,0:T(1,128)S(1)}, u32[]{:S(2)}, u32[]{:S(2)}) async-start(f32[2176,1,128]{2,1,0:T(1,128)} %bitcast.13), calls=%async_computation.2 | async-start | bytes 2228224 | tf_op jit(solution)/shard_map/all_to_all | solution.py:273
  21.4 0.0 copy-start.1
  21.4 0.1 pad_add_fusion.place
  21.5 3.5 %shard_map.75 = (s32[512,128]{1,0:T(8,128)S(1)}, f32[2,512,128]{2,1,0:T(8,128)}, s32[48,128]{1,0:T(8,128)S(1)}, s32[512,128]{1,0:T(8,128)}, s32[1]{0:T(128)}) custom-call(s32[2]{0:T(128)S(1)} %pad_add_fusion.place, s32[2,16,256]{2,1,0:T(8,128)} %local_picks.1, s32[2,4,16,256]{3,2,1,0:T(8,128)} %level_picks.1, s32[2,256]{1,0:T(2,128)} %order.1), custom_call_target="tpu_custom_call" | custom-call | flops 1000000000 | bytes 1000000 | tf_op jit(solution)/shard_map/pallas_call | solution.py:275
  25.6 0.0 copy-done.1
  25.6 0.5 copy.14
  26.1 15.1 %all-to-all-done.2 = f32[2176,1,128]{2,1,0:T(1,128)S(1)} async-done(((f32[2176,1,128]{2,1,0:T(1,128)}), f32[2176,1,128]{2,1,0:T(1,128)S(1)}, u32[]{:S(2)}, u32[]{:S(2)}) %all-to-all-start.2) | async-done | bytes 1114144 | tf_op jit(solution)/shard_map/all_to_all | solution.py:273
  41.2 84.6 %conditional.1 = (f32[2,256,4,256]{3,2,1,0:T(4,128)}) conditional(s32[]{:T(128)} %bitcast.6, (f32[2176,128]{1,0:T(8,128)S(1)}, f32[512,1024]{1,0:T(8,128)S(1)}, s32[512,128]{1,0:T(8,128)S(1)}, s32[]{:T(128)}, s32[2]{0:T(128)S(1)}, /*index=5*/f32[2,512,128]{2,1,0:T(8,128)}) %tuple.24, (f32[2176,128]{1,0:T(8,128)S(1)}, f32[512,1024]{1,0:T(8,128)S(1)}, ...), branch_computations={%region_0.2_spmd, %region_2.3_spmd} | conditional | flops 11000393728 | bytes 71875848 | solution.py:346
  41.2 2.3 %branch_1_fun.5 = (f32[512,256]{1,0:T(8,128)}, f32[768,256]{1,0:T(8,128)}, bf16[1024,256]{1,0:T(8,128)(2,1)}, bf16[1024,256]{1,0:T(8,128)(2,1)}, s32[8,1024]{1,0:T(8,128)}) custom-call(f32[2176,128]{1,0:T(8,128)S(1)} %get-tuple-element.45.payload, f32[512,1024]{1,0:T(8,128)S(1)} %get-tuple-element.46.front, s32[48,128]{1,0:T(8,128)S(1)} %get-tuple-element.47.give), custom_call_target="tpu_custom_call" | custom-call | flops 1000000000 | bytes 4000000 | tf_op jit(solution)/shard_map/cond/branch_1_fun/pallas_call | solution.py:294
  43.5 16.8 %all_to_all.21 = f32[16,48,256]{2,1,0:T(8,128)S(1)} all-to-all(f32[16,48,256]{2,1,0:T(8,128)} %bitcast.35), channel_id=1, replica_groups=mesh['prow'=16,'pcol'=8] {'prow'}, dimensions={0} | all-to-all | bytes 1572864 | tf_op jit(solution)/shard_map/cond/branch_1_fun/all_to_all | solution.py:308
  60.3 0.0 copy-start.3
  60.3 2.1 %collective-permute-start.6 = (f32[768,256]{1,0:T(8,128)S(1)}, f32[768,256]{1,0:T(8,128)}, u32[]{:S(2)}, u32[]{:S(2)}) collective-permute-start(f32[768,256]{1,0:T(8,128)S(1)} %bitcast.32), channel_id=1, source_target_pairs={{0,1},{1,0},{2,3},{3,2},{4,5},{5,4},{6,7},{7,6},{8,9},{9,8},{10,11... | collective-permute-start | bytes 2359304 | tf_op jit(solution)/shard_map/cond/branch_1_fun/ppermute | solution.py:247
  62.4 6.7 %branch_1_fun.6 = (f32[512,768]{1,0:T(8,128)}, f32[768,768]{1,0:T(8,128)}) custom-call(bf16[1024,256]{1,0:T(8,128)(2,1)} %get-tuple-element.49.high, bf16[1024,256]{1,0:T(8,128)(2,1)} %get-tuple-element.50.low, s32[8,1024]{1,0:T(8,128)} %get-tuple-element.51.code, f32[512,1024]{1,0:T(8,128)S(1)} %get-tuple-element.46.front, s32[48,128]{1,0:T(8,128)S(1)} %get-tuple-element.47.give), custom_call_target="tpu_custom_call" | custom-call | flops 3000000000 | bytes 8000000 | tf_op jit(solution)/shard_map/cond/branch_1_fun/pallas_call | solution.py:310
  69.0 0.0 copy-done.3
  69.0 0.0 copy-start.12
  69.0 3.9 %all-to-all-start.1 = ((f32[16,48,768]{2,1,0:T(8,128)}), f32[16,48,768]{2,1,0:T(8,128)S(1)}, u32[]{:S(2)}, u32[]{:S(2)}) async-start(f32[16,48,768]{2,1,0:T(8,128)} %bitcast.25), calls=%async_computation.1 | async-start | bytes 4718592 | tf_op jit(solution)/shard_map/cond/branch_1_fun/all_to_all | solution.py:313
  72.9 0.4 collective-permute-start.7
  73.3 1.8 %collective-permute-done.7.r_other = f32[512,256]{1,0:T(8,128)S(1)} collective-permute-done((f32[512,256]{1,0:T(8,128)}, f32[512,256]{1,0:T(8,128)S(1)}, u32[]{:S(2)}, u32[]{:S(2)}) %collective-permute-start.7) | collective-permute-done | bytes 524320 | tf_op jit(solution)/shard_map/cond/branch_1_fun/ppermute | solution.py:247
  75.1 0.0 copy-start.10
  75.1 0.0 collective-permute-done.6.w_other
  75.1 0.8 copy-done.10
  75.9 0.0 copy-done.12
  75.9 7.0 %branch_1_fun.7 = (f32[512,256]{1,0:T(8,128)}, f32[512,256]{1,0:T(8,128)}) custom-call(s32[2]{0:T(128)S(1)} %get-tuple-element.44.place, s32[512,128]{1,0:T(8,128)S(1)} %copy-done.12, f32[768,256]{1,0:T(8,128)} %bitcast.33, f32[768,256]{1,0:T(8,128)} %collective-permute-done.6.w_other, f32[512,256]{1,0:T(8,128)} %get-tuple-element.48.r_own.first, ...), custom_call_target="tpu_custom_call" | custom-call | flops 2000000000 | bytes 4000000 | tf_op jit(solution)/shard_map/cond/branch_1_fun/pallas_call | solution.py:315
  82.9 2.1 %collective-permute-start.10 = (f32[512,256]{1,0:T(8,128)}, f32[512,256]{1,0:T(8,128)S(1)}, u32[]{:S(2)}, u32[]{:S(2)}) collective-permute-start(f32[512,256]{1,0:T(8,128)} %get-tuple-element.58), channel_id=1, source_target_pairs={{0,6},{1,7},{8,14},{9,15},{16,22},{17,23},{24,30},{25,31},{32,38},... | collective-permute-start | bytes 1572872 | tf_op jit(solution)/shard_map/cond/branch_1_fun/ppermute | solution.py:252
  84.9 1.3 collective-permute-start.9
  86.2 2.1 %collective-permute-start.8 = (f32[512,256]{1,0:T(8,128)}, f32[512,256]{1,0:T(8,128)}, u32[]{:S(2)}, u32[]{:S(2)}) collective-permute-start(f32[512,256]{1,0:T(8,128)} %get-tuple-element.58), channel_id=1, source_target_pairs={{0,2},{1,3},{8,10},{9,11},{16,18},{17,19},{24,26},{25,27},{32,34},... | collective-permute-start | bytes 1572872 | tf_op jit(solution)/shard_map/cond/branch_1_fun/ppermute | solution.py:251
  88.4 0.0 copy-start.13
  88.4 7.8 %collective-permute-done.10 = f32[512,256]{1,0:T(8,128)S(1)} collective-permute-done((f32[512,256]{1,0:T(8,128)}, f32[512,256]{1,0:T(8,128)S(1)}, u32[]{:S(2)}, u32[]{:S(2)}) %collective-permute-start.10) | collective-permute-done | bytes 524320 | tf_op jit(solution)/shard_map/cond/branch_1_fun/ppermute | solution.py:252
  96.2 1.3 %collective-permute-done.9 = f32[512,256]{1,0:T(8,128)S(1)} collective-permute-done((f32[512,256]{1,0:T(8,128)}, f32[512,256]{1,0:T(8,128)S(1)}, u32[]{:S(2)}, u32[]{:S(2)}) %collective-permute-start.9) | collective-permute-done | bytes 524320 | tf_op jit(solution)/shard_map/cond/branch_1_fun/ppermute | solution.py:253
  97.5 11.2 %collective-permute-done.8 = f32[512,256]{1,0:T(8,128)} collective-permute-done((f32[512,256]{1,0:T(8,128)}, f32[512,256]{1,0:T(8,128)}, u32[]{:S(2)}, u32[]{:S(2)}) %collective-permute-start.8) | collective-permute-done | bytes 524320 | tf_op jit(solution)/shard_map/cond/branch_1_fun/ppermute | solution.py:251
  108.8 1.2 select_select_fusion.1.n_own
  110.0 0.0 copy-start.7
  110.0 1.2 collective-permute-start.11
  111.2 1.5 %collective-permute-done.11.n_other = f32[512,256]{1,0:T(8,128)S(1)} collective-permute-done((f32[512,256]{1,0:T(8,128)S(1)}, f32[512,256]{1,0:T(8,128)S(1)}, u32[]{:S(2)}, u32[]{:S(2)}) %collective-permute-start.11) | collective-permute-done | bytes 524320 | tf_op jit(solution)/shard_map/cond/branch_1_fun/ppermute | solution.py:247
  112.7 0.0 copy-done.7
  112.7 0.0 copy-start.11
  112.7 0.8 copy-done.11
  113.5 0.0 copy-done.13
  113.5 3.3 %branch_1_fun.8 = (bf16[512,768]{1,0:T(8,128)(2,1)}, bf16[512,768]{1,0:T(8,128)(2,1)}) custom-call(s32[2]{0:T(128)S(1)} %get-tuple-element.44.place, s32[512,128]{1,0:T(8,128)S(1)} %copy-done.13, f32[512,256]{1,0:T(8,128)} %copy-done.7, f32[512,256]{1,0:T(8,128)} %copy-done.11), custom_call_target="tpu_custom_call" | custom-call | flops 1000000000 | bytes 2000000 | tf_op jit(solution)/shard_map/cond/branch_1_fun/pallas_call | solution.py:320
  116.8 0.0 all-to-all-done.1
  116.8 0.0 copy-start
  116.8 1.4 %copy-done = f32[16,48,768]{2,1,0:T(8,128)} copy-done((f32[16,48,768]{2,1,0:T(8,128)}, f32[16,48,768]{2,1,0:T(8,128)S(1)}, u32[]{:S(2)}) %copy-start) | copy-done | bytes 2359320 | tf_op jit(solution)/shard_map/cond
  118.3 7.5 %branch_1_fun.9 = f32[2,256,4,256]{3,2,1,0:T(4,128)} custom-call(s32[2]{0:T(128)S(1)} %get-tuple-element.44.place, f32[512,256]{1,0:T(8,128)} %get-tuple-element.48.r_own.first, f32[512,768]{1,0:T(8,128)} %get-tuple-element.52.rest, f32[768,256]{1,0:T(8,128)} %bitcast.34, f32[768,768]{1,0:T(8,128)} %bitcast.24, bf16[512,768]{1,0:T(8,128)(2,1)} %get-tuple-element.59.high, ...), custom_call_target="tpu_custom_call" | custom-call | flops 4000000000 | bytes 8000000 | tf_op jit(solution)/shard_map/cond/branch_1_fun/pallas_call | solution.py:323
  (2 shorter events, 0.0 us)
Async XLA Ops:
  9.9 31.4 %all-to-all-start.2 = ((f32[2176,1,128]{2,1,0:T(1,128)}), f32[2176,1,128]{2,1,0:T(1,128)S(1)}, u32[]{:S(2)}, u32[]{:S(2)}) async-start(f32[2176,1,128]{2,1,0:T(1,128)} %bitcast.13), calls=%async_computation.2 | async-start | bytes 2228224 | tf_op jit(solution)/shard_map/all_to_all | solution.py:273
  21.4 4.2 %copy-start.1 = (f32[2,256,4,256]{3,2,1,0:T(4,128)S(1)}, f32[2,256,4,256]{3,2,1,0:T(4,128)}, u32[]{:S(2)}) copy-start(f32[2,256,4,256]{3,2,1,0:T(4,128)} %param.9) | copy-start | bytes 6291460
  60.3 8.7 %copy-start.3 = (f32[16,48,256]{2,1,0:T(8,128)}, f32[16,48,256]{2,1,0:T(8,128)S(1)}, u32[]{:S(2)}) copy-start(f32[16,48,256]{2,1,0:T(8,128)S(1)} %all_to_all.21) | copy-start | bytes 2359300 | tf_op jit(solution)/shard_map/cond
  60.3 14.8 %collective-permute-start.6 = (f32[768,256]{1,0:T(8,128)S(1)}, f32[768,256]{1,0:T(8,128)}, u32[]{:S(2)}, u32[]{:S(2)}) collective-permute-start(f32[768,256]{1,0:T(8,128)S(1)} %bitcast.32), channel_id=1, source_target_pairs={{0,1},{1,0},{2,3},{3,2},{4,5},{5,4},{6,7},{7,6},{8,9},{9,8},{10,11... | collective-permute-start | bytes 2359304 | tf_op jit(solution)/shard_map/cond/branch_1_fun/ppermute | solution.py:247
  69.0 6.9 %copy-start.12 = (s32[512,128]{1,0:T(8,128)S(1)}, s32[512,128]{1,0:T(8,128)}, u32[]{:S(2)}) copy-start(s32[512,128]{1,0:T(8,128)} %get-tuple-element.55.slot) | copy-start | bytes 786436 | tf_op jit(solution)/shard_map/cond
  69.0 47.8 %all-to-all-start.1 = ((f32[16,48,768]{2,1,0:T(8,128)}), f32[16,48,768]{2,1,0:T(8,128)S(1)}, u32[]{:S(2)}, u32[]{:S(2)}) async-start(f32[16,48,768]{2,1,0:T(8,128)} %bitcast.25), calls=%async_computation.1 | async-start | bytes 4718592 | tf_op jit(solution)/shard_map/cond/branch_1_fun/all_to_all | solution.py:313
  72.9 2.2 %collective-permute-start.7 = (f32[512,256]{1,0:T(8,128)}, f32[512,256]{1,0:T(8,128)S(1)}, u32[]{:S(2)}, u32[]{:S(2)}) collective-permute-start(f32[512,256]{1,0:T(8,128)} %get-tuple-element.48.r_own.first), channel_id=1, source_target_pairs={{0,1},{1,0},{2,3},{3,2},{4,5},{5,4},{6,7},{7,6},{8,9},{9,8},{10,11... | collective-permute-start | bytes 1572872 | tf_op jit(solution)/shard_map/cond/branch_1_fun/ppermute | solution.py:247
  75.1 0.8 copy-start.10
  82.9 13.4 %collective-permute-start.10 = (f32[512,256]{1,0:T(8,128)}, f32[512,256]{1,0:T(8,128)S(1)}, u32[]{:S(2)}, u32[]{:S(2)}) collective-permute-start(f32[512,256]{1,0:T(8,128)} %get-tuple-element.58), channel_id=1, source_target_pairs={{0,6},{1,7},{8,14},{9,15},{16,22},{17,23},{24,30},{25,31},{32,38},... | collective-permute-start | bytes 1572872 | tf_op jit(solution)/shard_map/cond/branch_1_fun/ppermute | solution.py:252
  84.9 12.6 %collective-permute-start.9 = (f32[512,256]{1,0:T(8,128)}, f32[512,256]{1,0:T(8,128)S(1)}, u32[]{:S(2)}, u32[]{:S(2)}) collective-permute-start(f32[512,256]{1,0:T(8,128)} %get-tuple-element.58), channel_id=1, source_target_pairs={{0,4},{1,5},{8,12},{9,13},{16,20},{17,21},{24,28},{25,29},{32,36},... | collective-permute-start | bytes 1572872 | tf_op jit(solution)/shard_map/cond/branch_1_fun/ppermute | solution.py:253
  86.2 22.5 %collective-permute-start.8 = (f32[512,256]{1,0:T(8,128)}, f32[512,256]{1,0:T(8,128)}, u32[]{:S(2)}, u32[]{:S(2)}) collective-permute-start(f32[512,256]{1,0:T(8,128)} %get-tuple-element.58), channel_id=1, source_target_pairs={{0,2},{1,3},{8,10},{9,11},{16,18},{17,19},{24,26},{25,27},{32,34},... | collective-permute-start | bytes 1572872 | tf_op jit(solution)/shard_map/cond/branch_1_fun/ppermute | solution.py:251
  88.4 25.2 %copy-start.13 = (s32[512,128]{1,0:T(8,128)S(1)}, s32[512,128]{1,0:T(8,128)}, u32[]{:S(2)}) copy-start(s32[512,128]{1,0:T(8,128)} %get-tuple-element.55.slot) | copy-start | bytes 786436 | tf_op jit(solution)/shard_map/cond
  110.0 2.7 %copy-start.7 = (f32[512,256]{1,0:T(8,128)}, f32[512,256]{1,0:T(8,128)S(1)}, u32[]{:S(2)}) copy-start(f32[512,256]{1,0:T(8,128)S(1)} %select_select_fusion.1.n_own) | copy-start | bytes 1572868 | tf_op jit(solution)/shard_map/cond
  110.0 2.7 %collective-permute-start.11 = (f32[512,256]{1,0:T(8,128)S(1)}, f32[512,256]{1,0:T(8,128)S(1)}, u32[]{:S(2)}, u32[]{:S(2)}) collective-permute-start(f32[512,256]{1,0:T(8,128)S(1)} %select_select_fusion.1.n_own), channel_id=1, source_target_pairs={{0,1},{1,0},{2,3},{3,2},{4,5},{5,4},{6,7},{7,6},{8,9},{9,8},{10,11... | collective-permute-start | bytes 1572872 | tf_op jit(solution)/shard_map/cond/branch_1_fun/ppermute | solution.py:247
  112.7 0.8 copy-start.11
  116.8 1.4 %copy-start = (f32[16,48,768]{2,1,0:T(8,128)}, f32[16,48,768]{2,1,0:T(8,128)S(1)}, u32[]{:S(2)}) copy-start(f32[16,48,768]{2,1,0:T(8,128)S(1)} %all-to-all-done.1) | copy-start | bytes 7077892 | tf_op jit(solution)/shard_map/cond

commit v3 on v2

--- a/solution.py
+++ b/solution.py
@@ -13,7 +13,7 @@
 SM = pl.BlockSpec(memory_space=pltpu.SMEM)
 B = 256
 KEEP = 48
-PARAMS = dict(compiler_params=pltpu.CompilerParams(vmem_limit_bytes=56 * 1024 * 1024))
+PARAMS = dict(compiler_params=pltpu.CompilerParams(vmem_limit_bytes=24 * 1024 * 1024))
 
 
 def iota(shape, dim):
@@ -87,6 +87,20 @@
     give_out[...] = jnp.broadcast_to(give, (keep, 128))
 
 
+def pack_kernel(place, partials, targets, counts, out):
+    sources, slots = targets.shape
+    limit = jnp.broadcast_to(counts[...], (sources, sources)).T
+    lane = iota((sources, 128), 1)
+    row = jnp.full((sources, 128), -1, jnp.int32)
+    for j in range(slots):
+        row = jnp.where((lane % slots == j) & (limit > j), jnp.broadcast_to(targets[:, j : j + 1], (sources, 128)), row)
+    row = jnp.where(lane // slots == place[2] % 16, row, 0).astype(F32)
+    for s in range(sources):
+        out[17 * s : 17 * s + 8, :] = partials[s, :, :128]
+        out[17 * s + 8 : 17 * s + 16, :] = partials[s, :, 128:]
+        out[17 * s + 16 : 17 * s + 17, :] = row[s : s + 1, :]
+
+
 def unpack(payload):
     sources = payload.shape[0] // 17
     left, right, codes = [], [], []
@@ -135,18 +149,20 @@
         send_out[i * sent.shape[0] : (i + 1) * sent.shape[0], :] = sent
 
 
-def rest_kernel(high, low, code, front, give, rest_out, send_out):
+def rest_kernel(high, low, code, front, give, rest_out, send_out, done_out):
     rows = front.shape[0]
     give_hot = rows_hot(give, rows)
-    keep = give.shape[0]
     for u in range(1, 4):
         hot = hot_of(code[0:1, :], rows, u)
         tile = front[:, u * B : (u + 1) * B] + (dot(hot, high[...]) + dot(hot, low[...]))
         cols = slice((u - 1) * B, u * B)
         rest_out[:, cols] = tile
-        sent = pick(give_hot, tile)
-        for i in range(send_out.shape[0] // keep):
-            send_out[i * keep : (i + 1) * keep, cols] = sent
+        send_out[:, cols] = pick(give_hot, tile)
+    done_out[...] = jnp.zeros_like(done_out)
+
+
+def sort_kernel(slot, gathered, done, out):
+    out[...] = pick(rows_hot(slot, gathered.shape[0]), gathered[...])
 
 
 def inverse_of(diag):
@@ -158,11 +174,6 @@
     x = by_row * (two - diag * by_col)
     xs = halves(x)
     return dot3(xs, halves(two - dot3(halves(diag), xs)))
-
-
-def panel_slots_kernel(place, slot, w_own, w_other, r_own, r_other, active, half_out, tile_out):
-    hot = rows_hot(slot, w_own.shape[0])
-    panel_kernel(place, pick(hot, w_own[...]), pick(hot, w_other[...]), r_own, r_other, active, half_out, tile_out)
 
 
 def panel_kernel(place, w_own, w_other, r_own, r_other, active, half_out, tile_out):
@@ -202,22 +213,26 @@
         out[:, cols] = new
 
 
-def spread_kernel(place, slot, n_own, n_other, high_out, low_out):
-    even = place[1] % 2 == 0
+def spread_kernel(place, slot, n_early, n_late, o_early, o_late, first, w_first, tile, high_out, low_out, first_out):
+    q = place[1]
+    even = q % 2 == 0
+    n_own = jnp.where((q < 3) | (q == 7), n_early[...], n_late[...])
+    n_other = jnp.where((q < 2) | (q == 3) | (q == 6), o_early[...], o_late[...])
     hot = rows_hot(slot, high_out.shape[1])
-    h0, l0 = halves(jnp.where(even, n_own[...], n_other[...]))
-    h1, l1 = halves(jnp.where(even, n_other[...], n_own[...]))
+    h0, l0 = halves(jnp.where(even, n_own, n_other))
+    h1, l1 = halves(jnp.where(even, n_other, n_own))
     high_out[...] = (dot(h0, hot[:B]) + dot(h1, hot[B:])).astype(BF16)
     low_out[...] = (dot(l0, hot[:B]) + dot(l1, hot[B:])).astype(BF16)
-
-
-def finish_kernel(place, first, rest, w_first, w_rest, high, low, tile, out):
+    new = first[...] - (dot3((h0, l0), halves(w_first[:B])) + dot3((h1, l1), halves(w_first[B:])))
+    first_out[...] = jnp.where(q < 2, tile[...], new)
+
+
+def finish_kernel(first, rest, w_rest, high, low, out):
     n = (high[...], low[...])
     half = out.shape[1]
     for u in range(4):
         if u == 0:
-            new = first[...] - dot3(n, halves(w_first[...]))
-            new = jnp.where(place[1] < 2, tile[...], new)
+            new = first[...]
         else:
             cols = slice((u - 1) * B, u * B)
             new = rest[:, cols] - dot3(n, halves(w_rest[:, cols]))
@@ -260,16 +275,13 @@
     p = lax.axis_index("prow")
     q = lax.axis_index("pcol")
     me = p * lax.axis_size("pcol") + q
-    place = jnp.stack([p, q]).astype(jnp.int32)
+    place = jnp.stack([p, q, me]).astype(jnp.int32)
     sources = partials.shape[1]
     slots = partials.shape[2]
 
-    used = iota((sources, slots), 1) < counts[0][:, None]
-    codes = jnp.where(used, targets[0], -1)
-    lanes = jnp.tile(codes, (1, 16))
-    code_row = jnp.where(iota((sources, 128), 1) // slots == me % 16, lanes, 0).astype(F32)
-    values = partials[0].reshape(sources, slots, 2, 128).transpose(0, 2, 1, 3).reshape(sources, 16, 128)
-    payload = jnp.concatenate([values, code_row[:, None, :]], axis=1).reshape(sources * 17, 1, 128)
+    payload = call(pack_kernel, shaped(sources * 17, 128), 4, flops=10**6, moved=2 * 10**6)(
+        place, partials[0], targets[0], counts
+    ).reshape(sources * 17, 1, 128)
     payload = lax.all_to_all(payload, ("prow", "pcol"), 0, 0, tiled=True).reshape(sources * 17, 128)
 
     own, active, give, slot, fits = call(
@@ -307,21 +319,35 @@
         )(payload, flat, give)
         w_first = lax.all_to_all(send, "prow", 0, 0, tiled=True)
         r_other = core_swap(first)
-        rest, send = call(
-            rest_kernel, (shaped(rows, cols - B), shaped(copies, cols - B)), 5, scalars=0, flops=3 * 10**9, moved=8 * 10**6
+        rest, send, done = call(
+            rest_kernel,
+            (shaped(rows, cols - B), shaped(KEEP, cols - B), shaped(8, 128)),
+            5,
+            scalars=0,
+            flops=3 * 10**9,
+            moved=6 * 10**6,
         )(high, low, code, flat, give)
-        w_rest = lax.all_to_all(send, "prow", 0, 0, tiled=True)
+        w_rest = lax.all_gather(send, "prow", axis=0, tiled=True)
+        w_first = call(sort_kernel, shaped(2 * B, B), 3, scalars=0, flops=10**9, moved=10**6)(slot, w_first, done)
         w_other = core_swap(w_first)
         half, tile = call(
-            panel_slots_kernel, (shaped(rows, B), shaped(rows, B)), 7, flops=2 * 10**9, moved=4 * 10**6
-        )(place, slot, w_first, w_other, first, r_other, active)
-        n_own = spread_z(half, place[1] // 2)
-        n_other = core_swap(n_own)
-        high, low = call(
-            spread_kernel, (shaped(rows, copies, dtype=BF16), shaped(rows, copies, dtype=BF16)), 4, flops=10**9, moved=2 * 10**6
-        )(place, slot, n_own, n_other)
-        return call(finish_kernel, shaped(*front.shape), 8, flops=4 * 10**9, moved=8 * 10**6)(
-            place, first, rest, w_first, w_rest, high, low, tile
+            panel_kernel, (shaped(rows, B), shaped(rows, B)), 6, flops=2 * 10**9, moved=4 * 10**6
+        )(place, w_first, w_other, first, r_other, active)
+        q = place[1]
+        step = lax.ppermute(half, "pcol", [(0, 2), (1, 7)])
+        n_early = jnp.where((q == 2) | (q == 7), step, half)
+        n_late = lax.ppermute(n_early, "pcol", [(1, 3), (0, 6), (2, 4), (7, 5)])
+        o_early = lax.ppermute(n_early, "pcol", [(0, 1), (1, 0), (2, 3), (7, 6)])
+        o_late = lax.ppermute(n_late, "pcol", [(3, 2), (6, 7), (4, 5), (5, 4)])
+        high, low, first = call(
+            spread_kernel,
+            (shaped(rows, copies, dtype=BF16), shaped(rows, copies, dtype=BF16), shaped(rows, B)),
+            9,
+            flops=10**9,
+            moved=4 * 10**6,
+        )(place, slot, n_early, n_late, o_early, o_late, first, w_first, tile)
+        return call(finish_kernel, shaped(*front.shape), 5, scalars=0, flops=4 * 10**9, moved=8 * 10**6)(
+            first, rest, w_rest, high, low
         )
 
     def add_up(payload, flat, own, active, give, slot, place):

time: 133 us -> 118 us (0.89)
  the two profiles are of different devices: /device:TPU:1 before, /device:TPU:65 now
where the time goes in v3:
time: 118 us
  waiting for transfers between devices  44.7 us (38%)
  starting transfers between devices  24.2 us (21%)
  Pallas kernels  24.1 us (20%)
  between operations  14.1 us (12%)
  local copies, waits for them, and re-layouts  10.5 us (9%)
    ppermute x1, waiting for transfers between devices, gather(): n_late = lax.ppermute(n_early, 'pcol', [(1, 3), (0, 6), (2, 4), (7, 5)])  17.6 us
    all_to_all x1, waiting for transfers between devices, gather(): w_first = lax.all_to_all(send, 'prow', 0, 0, tiled=True)  12.7 us
    all_to_all x1, waiting for transfers between devices, body(): lax.all_to_all(payload, ('prow', 'pcol'), 0, 0, tiled=True)  11.3 us
    all_to_all x1, starting transfers between devices, body(): lax.all_to_all(payload, ('prow', 'pcol'), 0, 0, tiled=True)  10.8 us
    cond x12, local copies, waits for them, and re-layouts  6.05 us
    unnamed x14, local copies, waits for them, and re-layouts  4.44 us
    pallas_call x1, Pallas kernels, gather(): call(panel_kernel, (shaped(rows, B), shaped(rows, B)), 6, flops=2 * 10 **...  4.42 us
    pallas_call x1, Pallas kernels, gather(): call(rest_kernel, (shaped(rows, cols - B), shaped(KEEP, cols - B), shaped...  4.29 us
  transfers between devices with their start and end apart: 9, of which 5 were waited for; matrix products, arithmetic and copies ran while one was open for 2% of the time, Pallas kernels for 9%

profile of v3, /device:TPU:65, one launch (start us, length us, event | category | flops | bytes accessed | tf_op | source)
XLA Modules:
  0.0 117.8 jit_solution(10598828759199797546)
XLA Ops:
  6.5 0.8 copy.11
  7.3 0.1 pad_add_fusion.place
  7.4 0.0 copy-start.4
  7.4 1.2 %copy-done.4 = f32[1,128,8,256]{3,2,1,0:T(8,128)S(1)} copy-done((f32[1,128,8,256]{3,2,1,0:T(8,128)S(1)}, f32[1,128,8,256]{3,2,1,0:T(8,128)}, u32[]{:S(2)}) %copy-start.4) | copy-done | bytes 1048600
  8.6 0.0 copy-start.5
  8.6 0.7 copy-done.5
  9.3 0.0 copy-start.11
  9.3 1.8 %shard_map.76 = f32[2176,128]{1,0:T(8,128)} custom-call(s32[3]{0:T(128)S(1)} %pad_add_fusion.place, f32[128,8,256]{2,1,0:T(8,128)S(1)} %bitcast.15, s32[128,8]{1,0:T(8,128)S(1)} %bitcast.17, s32[1,128]{1,0:T(1,128)S(1)} %copy-done.5), custom_call_target="tpu_custom_call" | custom-call | flops 1000000 | bytes 2000000 | tf_op jit(solution)/shard_map/pallas_call | solution.py:282
  11.1 10.8 %all-to-all-start.1 = ((f32[2176,1,128]{2,1,0:T(1,128)}), f32[2176,1,128]{2,1,0:T(1,128)}, u32[]{:S(2)}, u32[]{:S(2)}) async-start(f32[2176,1,128]{2,1,0:T(1,128)} %bitcast.9), calls=%async_computation.1 | async-start | bytes 2228224 | tf_op jit(solution)/shard_map/all_to_all | solution.py:285
  21.8 0.0 copy-done.11
  21.8 0.0 copy-done.12
  21.9 0.0 copy-done.13
  21.9 0.0 copy-start.16
  21.9 2.9 %shard_map.75 = (s32[512,128]{1,0:T(8,128)S(1)}, f32[2,512,128]{2,1,0:T(8,128)}, s32[48,128]{1,0:T(8,128)S(1)}, s32[512,128]{1,0:T(8,128)S(1)}, s32[1]{0:T(128)}) custom-call(s32[3]{0:T(128)S(1)} %pad_add_fusion.place, s32[2,16,256]{2,1,0:T(8,128)S(1)} %copy-done.12, s32[2,4,16,256]{3,2,1,0:T(8,128)S(1)} %copy-done.11, s32[2,256]{1,0:T(2,128)S(1)} %copy-done.13), custom_call_target="tpu_custom_call" | custom-call | flops 1000000000 | bytes 1000000 | tf_op jit(solution)/shard_map/pallas_call | solution.py:287
  24.8 0.0 copy-done.16
  24.8 1.8 %copy.13 = f32[64,8,4,256]{3,1,2,0:T(8,128)} copy(f32[64,8,4,256]{3,2,1,0:T(4,128)S(1)} %bitcast.18) | data formatting | bytes 4194304
  27.2 11.3 %all-to-all-done.1 = f32[2176,1,128]{2,1,0:T(1,128)} async-done(((f32[2176,1,128]{2,1,0:T(1,128)}), f32[2176,1,128]{2,1,0:T(1,128)}, u32[]{:S(2)}, u32[]{:S(2)}) %all-to-all-start.1) | async-done | bytes 1114144 | tf_op jit(solution)/shard_map/all_to_all | solution.py:285
  38.5 72.5 %conditional.1 = (f32[2,256,4,256]{3,2,1,0:T(4,128)}) conditional(s32[]{:T(128)} %bitcast.5, (f32[2176,128]{1,0:T(8,128)}, f32[512,1024]{1,0:T(8,128)}, s32[512,128]{1,0:T(8,128)S(1)}, s32[]{:T(128)}, s32[3]{0:T(128)S(1)}, /*index=5*/f32[2,512,128]{2,1,0:T(8,128)}) %tuple.23, (s32[]{:T(128)}, f32[2176,128]{1,0:T(8,128)}, f32[512,1024]{1,0:T(8,128)}, ...), branch_computations={%region_0.2_spmd, %region_2.3_spmd} | conditional | flops 12000131072 | bytes 91828088 | solution.py:372
  38.5 0.0 all-gather.2.cloned.1.call-start
  38.5 4.1 %branch_1_fun.6 = (f32[512,256]{1,0:T(8,128)S(1)}, f32[768,256]{1,0:T(8,128)}, bf16[1024,256]{1,0:T(8,128)(2,1)S(1)}, bf16[1024,256]{1,0:T(8,128)(2,1)S(1)}, s32[8,1024]{1,0:T(8,128)S(1)}) custom-call(f32[2176,128]{1,0:T(8,128)} %get-tuple-element.47.payload, f32[512,1024]{1,0:T(8,128)} %get-tuple-element.48.front, s32[48,128]{1,0:T(8,128)S(1)} %get-tuple-element.49.give), custom_call_target="tpu_custom_call" | custom-call | flops 1000000000 | bytes 4000000 | tf_op jit(solution)/shard_map/cond/branch_1_fun/pallas_call | solution.py:306
  42.5 0.0 copy-done.17
  42.5 4.3 %branch_1_fun.7 = (f32[512,768]{1,0:T(8,128)S(1)}, f32[48,768]{1,0:T(8,128)}, f32[8,128]{1,0:T(8,128)S(1)}) custom-call(bf16[1024,256]{1,0:T(8,128)(2,1)S(1)} %get-tuple-element.51.high, bf16[1024,256]{1,0:T(8,128)(2,1)S(1)} %get-tuple-element.52.low, s32[8,1024]{1,0:T(8,128)S(1)} %get-tuple-element.53.code, f32[512,1024]{1,0:T(8,128)S(1)} %copy-done.17, ...), custom_call_target="tpu_custom_call" | custom-call | flops 3000000000 | bytes 6000000 | tf_op jit(solution)/shard_map/cond/branch_1_fun/pallas_call | solution.py:322
  46.8 1.1 copy-done.14
  48.0 0.0 all-gather.2.cloned.1.call-update
  48.0 3.7 %all-to-all-start = ((f32[16,48,256]{2,1,0:T(8,128)}), f32[16,48,256]{2,1,0:T(8,128)S(1)}, u32[]{:S(2)}, u32[]{:S(2)}) async-start(f32[16,48,256]{2,1,0:T(8,128)} %bitcast), calls=%async_computation | async-start | bytes 1572864 | tf_op jit(solution)/shard_map/cond/branch_1_fun/all_to_all | solution.py:320
  51.8 1.2 collective-permute-start.7
  52.9 12.7 %all-to-all-done = f32[16,48,256]{2,1,0:T(8,128)S(1)} async-done(((f32[16,48,256]{2,1,0:T(8,128)}), f32[16,48,256]{2,1,0:T(8,128)S(1)}, u32[]{:S(2)}, u32[]{:S(2)}) %all-to-all-start) | async-done | bytes 786464 | tf_op jit(solution)/shard_map/cond/branch_1_fun/all_to_all | solution.py:320
  65.7 0.7 branch_1_fun.8.w_own.w_first
  66.4 2.7 %collective-permute-start.6 = (f32[512,256]{1,0:T(8,128)S(1)}, f32[512,256]{1,0:T(8,128)S(1)}, u32[]{:S(2)}, u32[]{:S(2)}) collective-permute-start(f32[512,256]{1,0:T(8,128)S(1)} %branch_1_fun.8.w_own.w_first), channel_id=1, source_target_pairs={{0,1},{1,0},{2,3},{3,2},{4,5},{5,4},{6,7},{7,6},{8,9},{9,8},{10,11... | collective-permute-start | bytes 1572872 | tf_op jit(solution)/shard_map/cond/branch_1_fun/ppermute | solution.py:262
  69.0 0.0 collective-permute-done.7.r_other
  69.0 1.5 %collective-permute-done.6.w_other = f32[512,256]{1,0:T(8,128)S(1)} collective-permute-done((f32[512,256]{1,0:T(8,128)S(1)}, f32[512,256]{1,0:T(8,128)S(1)}, u32[]{:S(2)}, u32[]{:S(2)}) %collective-permute-start.6) | collective-permute-done | bytes 524320 | tf_op jit(solution)/shard_map/cond/branch_1_fun/ppermute | solution.py:262
  70.6 4.4 %branch_1_fun.9 = (f32[512,256]{1,0:T(8,128)S(1)}, f32[512,256]{1,0:T(8,128)S(1)}) custom-call(s32[3]{0:T(128)S(1)} %get-tuple-element.44.place, f32[512,256]{1,0:T(8,128)S(1)} %branch_1_fun.8.w_own.w_first, f32[512,256]{1,0:T(8,128)S(1)} %collective-permute-done.6.w_other, f32[512,256]{1,0:T(8,128)S(1)} %get-tuple-element.55.r_own.first, ...), custom_call_target="tpu_custom_call" | custom-call | flops 2000000000 | bytes 4000000 | tf_op jit(solution)/shard_map/cond/branch_1_fun/pallas_call | solution.py:333
  75.0 0.7 collective-permute-start.8
  75.7 0.0 collective-permute-done.8
  75.7 0.1 broadcast_select_fusion.n_early
  75.8 1.3 %collective-permute-start.9 = (f32[512,256]{1,0:T(8,128)S(1)}, f32[512,256]{1,0:T(8,128)S(1)}, u32[]{:S(2)}, u32[]{:S(2)}) collective-permute-start(f32[512,256]{1,0:T(8,128)S(1)} %broadcast_select_fusion.n_early), channel_id=1, source_target_pairs={{1,3},{0,6},{2,4},{7,5},{9,11},{8,14},{10,12},{15,13},{17,19},{16,... | collective-permute-start | bytes 1572872 | tf_op jit(solution)/shard_map/cond/branch_1_fun/ppermute | solution.py:339
  77.1 0.7 collective-permute-start.10
  77.8 17.6 %collective-permute-done.9.n_late = f32[512,256]{1,0:T(8,128)S(1)} collective-permute-done((f32[512,256]{1,0:T(8,128)S(1)}, f32[512,256]{1,0:T(8,128)S(1)}, u32[]{:S(2)}, u32[]{:S(2)}) %collective-permute-start.9) | collective-permute-done | bytes 524320 | tf_op jit(solution)/shard_map/cond/branch_1_fun/ppermute | solution.py:339
  95.4 3.1 %collective-permute-start.11 = (f32[512,256]{1,0:T(8,128)S(1)}, f32[512,256]{1,0:T(8,128)S(1)}, u32[]{:S(2)}, u32[]{:S(2)}) collective-permute-start(f32[512,256]{1,0:T(8,128)S(1)} %collective-permute-done.9.n_late), channel_id=1, source_target_pairs={{3,2},{6,7},{4,5},{5,4},{11,10},{14,15},{12,13},{13,12},{19,18},{2... | collective-permute-start | bytes 1572872 | tf_op jit(solution)/shard_map/cond/branch_1_fun/ppermute | solution.py:341
  98.6 0.0 collective-permute-done.10.o_early
  98.6 1.5 %collective-permute-done.11.o_late = f32[512,256]{1,0:T(8,128)S(1)} collective-permute-done((f32[512,256]{1,0:T(8,128)S(1)}, f32[512,256]{1,0:T(8,128)S(1)}, u32[]{:S(2)}, u32[]{:S(2)}) %collective-permute-start.11) | collective-permute-done | bytes 524320 | tf_op jit(solution)/shard_map/cond/branch_1_fun/ppermute | solution.py:341
  100.1 2.1 %branch_1_fun.10 = (bf16[512,768]{1,0:T(8,128)(2,1)S(1)}, bf16[512,768]{1,0:T(8,128)(2,1)S(1)}, f32[512,256]{1,0:T(8,128)S(1)}) custom-call(s32[3]{0:T(128)S(1)} %get-tuple-element.44.place, s32[512,128]{1,0:T(8,128)S(1)} %get-tuple-element.45.slot, f32[512,256]{1,0:T(8,128)S(1)} %broadcast_select_fusion.n_early, ...), custom_call_target="tpu_custom_call" | custom-call | flops 1000000000 | bytes 4000000 | tf_op jit(solution)/shard_map/cond/branch_1_fun/pallas_call | solution.py:342
  102.2 0.0 copy-start.9
  102.2 0.8 copy-done.9
  103.0 1.7 %copy-done.6 = f32[768,768]{1,0:T(8,128)S(1)} copy-done((f32[768,768]{1,0:T(8,128)S(1)}, f32[768,768]{1,0:T(8,128)}, u32[]{:S(2)}) %copy-start.6) | copy-done | bytes 2359320 | tf_op jit(solution)/shard_map/cond
  104.7 1.0 copy-done.10
  105.7 1.4 %copy-done.15 = f32[512,768]{1,0:T(8,128)S(1)} copy-done((f32[512,768]{1,0:T(8,128)S(1)}, f32[512,768]{1,0:T(8,128)}, u32[]{:S(2)}) %copy-start.15) | copy-done | bytes 1572888 | tf_op jit(solution)/shard_map/cond
  107.2 3.8 %branch_1_fun.11 = f32[2,256,4,256]{3,2,1,0:T(4,128)} custom-call(f32[512,256]{1,0:T(8,128)S(1)} %copy-done.10, f32[512,768]{1,0:T(8,128)S(1)} %copy-done.15, f32[768,768]{1,0:T(8,128)S(1)} %copy-done.6, bf16[512,768]{1,0:T(8,128)(2,1)S(1)} %get-tuple-element.62.high, bf16[512,768]{1,0:T(8,128)(2,1)S(1)} %get-tuple-element.63.low), custom_call_target="tpu_custom_call" | custom-call | flops 4000000000 | bytes 8000000 | tf_op jit(solution)/shard_map/cond/branch_1_fun/pallas_call | solution.py:349
  (8 shorter events, 0.0 us)
Async XLA Ops:
  7.4 1.2 %copy-start.4 = (f32[1,128,8,256]{3,2,1,0:T(8,128)S(1)}, f32[1,128,8,256]{3,2,1,0:T(8,128)}, u32[]{:S(2)}) copy-start(f32[1,128,8,256]{3,2,1,0:T(8,128)} %param.10) | copy-start | bytes 3145732
  8.6 0.7 copy-start.5
  9.3 12.6 %copy-start.11 = (s32[2,4,16,256]{3,2,1,0:T(8,128)S(1)}, s32[2,4,16,256]{3,2,1,0:T(8,128)}, u32[]{:S(2)}) copy-start(s32[2,4,16,256]{3,2,1,0:T(8,128)} %level_picks.1) | copy-start | bytes 393220
  9.3 12.6 %copy-start.12 = (s32[2,16,256]{2,1,0:T(8,128)S(1)}, s32[2,16,256]{2,1,0:T(8,128)}, u32[]{:S(2)}) copy-start(s32[2,16,256]{2,1,0:T(8,128)} %local_picks.1) | copy-start | bytes 98308
  9.3 12.6 %copy-start.13 = (s32[2,256]{1,0:T(2,128)S(1)}, s32[2,256]{1,0:T(2,128)}, u32[]{:S(2)}) copy-start(s32[2,256]{1,0:T(2,128)} %order.1) | copy-start | bytes 6148
  11.1 27.4 %all-to-all-start.1 = ((f32[2176,1,128]{2,1,0:T(1,128)}), f32[2176,1,128]{2,1,0:T(1,128)}, u32[]{:S(2)}, u32[]{:S(2)}) async-start(f32[2176,1,128]{2,1,0:T(1,128)} %bitcast.9), calls=%async_computation.1 | async-start | bytes 2228224 | tf_op jit(solution)/shard_map/all_to_all | solution.py:285
  21.9 2.9 %copy-start.16 = (f32[2,256,4,256]{3,2,1,0:T(4,128)S(1)}, f32[2,256,4,256]{3,2,1,0:T(4,128)}, u32[]{:S(2)}) copy-start(f32[2,256,4,256]{3,2,1,0:T(4,128)} %param.9) | copy-start | bytes 6291460
  38.5 4.1 %copy-start.17 = (f32[512,1024]{1,0:T(8,128)S(1)}, f32[512,1024]{1,0:T(8,128)}, u32[]{:S(2)}) copy-start(f32[512,1024]{1,0:T(8,128)} %get-tuple-element.48.front) | copy-start | bytes 6291460 | tf_op jit(solution)/shard_map/cond
  38.5 64.6 %all-gather.2.cloned.1.call-start = ((), (), s32[]{:S(2)}) async-start(), calls=%async_computation.3 | async-start | bytes 2506752 | tf_op jit(solution)/shard_map/cond/branch_1_fun/all_gather | solution.py:330
  46.8 1.1 copy-start.14
  48.0 17.6 %all-to-all-start = ((f32[16,48,256]{2,1,0:T(8,128)}), f32[16,48,256]{2,1,0:T(8,128)S(1)}, u32[]{:S(2)}, u32[]{:S(2)}) async-start(f32[16,48,256]{2,1,0:T(8,128)} %bitcast), calls=%async_computation | async-start | bytes 1572864 | tf_op jit(solution)/shard_map/cond/branch_1_fun/all_to_all | solution.py:320
  51.8 17.3 %collective-permute-start.7 = (f32[512,256]{1,0:T(8,128)S(1)}, f32[512,256]{1,0:T(8,128)S(1)}, u32[]{:S(2)}, u32[]{:S(2)}) collective-permute-start(f32[512,256]{1,0:T(8,128)S(1)} %get-tuple-element.55.r_own.first), channel_id=1, source_target_pairs={{0,1},{1,0},{2,3},{3,2},{4,5},{5,4},{6,7},{7,6},{8,9},{9,8},{10,11... | collective-permute-start | bytes 1572872 | tf_op jit(solution)/shard_map/cond/branch_1_fun/ppermute | solution.py:262
  66.4 4.2 %collective-permute-start.6 = (f32[512,256]{1,0:T(8,128)S(1)}, f32[512,256]{1,0:T(8,128)S(1)}, u32[]{:S(2)}, u32[]{:S(2)}) collective-permute-start(f32[512,256]{1,0:T(8,128)S(1)} %branch_1_fun.8.w_own.w_first), channel_id=1, source_target_pairs={{0,1},{1,0},{2,3},{3,2},{4,5},{5,4},{6,7},{7,6},{8,9},{9,8},{10,11... | collective-permute-start | bytes 1572872 | tf_op jit(solution)/shard_map/cond/branch_1_fun/ppermute | solution.py:262
  75.0 0.7 collective-permute-start.8
  75.8 19.6 %collective-permute-start.9 = (f32[512,256]{1,0:T(8,128)S(1)}, f32[512,256]{1,0:T(8,128)S(1)}, u32[]{:S(2)}, u32[]{:S(2)}) collective-permute-start(f32[512,256]{1,0:T(8,128)S(1)} %broadcast_select_fusion.n_early), channel_id=1, source_target_pairs={{1,3},{0,6},{2,4},{7,5},{9,11},{8,14},{10,12},{15,13},{17,19},{16,... | collective-permute-start | bytes 1572872 | tf_op jit(solution)/shard_map/cond/branch_1_fun/ppermute | solution.py:339
  77.1 21.5 %collective-permute-start.10 = (f32[512,256]{1,0:T(8,128)S(1)}, f32[512,256]{1,0:T(8,128)S(1)}, u32[]{:S(2)}, u32[]{:S(2)}) collective-permute-start(f32[512,256]{1,0:T(8,128)S(1)} %broadcast_select_fusion.n_early), channel_id=1, source_target_pairs={{0,1},{1,0},{2,3},{7,6},{8,9},{9,8},{10,11},{15,14},{16,17},{17,16... | collective-permute-start | bytes 1572872 | tf_op jit(solution)/shard_map/cond/branch_1_fun/ppermute | solution.py:340
  95.4 4.7 %collective-permute-start.11 = (f32[512,256]{1,0:T(8,128)S(1)}, f32[512,256]{1,0:T(8,128)S(1)}, u32[]{:S(2)}, u32[]{:S(2)}) collective-permute-start(f32[512,256]{1,0:T(8,128)S(1)} %collective-permute-done.9.n_late), channel_id=1, source_target_pairs={{3,2},{6,7},{4,5},{5,4},{11,10},{14,15},{12,13},{13,12},{19,18},{2... | collective-permute-start | bytes 1572872 | tf_op jit(solution)/shard_map/cond/branch_1_fun/ppermute | solution.py:341
  102.2 0.8 copy-start.9
  103.0 1.7 %copy-start.6 = (f32[768,768]{1,0:T(8,128)S(1)}, f32[768,768]{1,0:T(8,128)}, u32[]{:S(2)}) copy-start(f32[768,768]{1,0:T(8,128)} %all-gather.2.cloned.1.call-done.w_rest) | copy-start | bytes 7077892 | tf_op jit(solution)/shard_map/cond
  104.7 1.0 copy-start.10
  105.7 1.4 %copy-start.15 = (f32[512,768]{1,0:T(8,128)S(1)}, f32[512,768]{1,0:T(8,128)}, u32[]{:S(2)}) copy-start(f32[512,768]{1,0:T(8,128)} %copy-done.14) | copy-start | bytes 4718596 | tf_op jit(solution)/shard_map/cond
Sparse Core Ops, SparseCore 0:
  48.1 46.0 all-gather.1

commit v4 on v3

--- a/solution.py
+++ b/solution.py
@@ -13,7 +13,7 @@
 SM = pl.BlockSpec(memory_space=pltpu.SMEM)
 B = 256
 KEEP = 48
-PARAMS = dict(compiler_params=pltpu.CompilerParams(vmem_limit_bytes=24 * 1024 * 1024))
+PARAMS = dict(compiler_params=pltpu.CompilerParams(vmem_limit_bytes=14 * 1024 * 1024))
 
 
 def iota(shape, dim):
@@ -83,18 +83,16 @@
     fits_out[0] = (jnp.max(rank) < keep).astype(jnp.int32)
     slot_out[...] = jnp.broadcast_to(d * keep + rank, (128, n)).T
     mine = (iota((keep, n), 0) == rank) & (d == p)
-    give = jnp.sum(jnp.where(mine, r + 1, 0), axis=1, keepdims=True) - 1
+    give = jnp.sum(jnp.where(mine, r + 2, 0), axis=1, keepdims=True) - 2
     give_out[...] = jnp.broadcast_to(give, (keep, 128))
 
 
 def pack_kernel(place, partials, targets, counts, out):
-    sources, slots = targets.shape
-    limit = jnp.broadcast_to(counts[...], (sources, sources)).T
-    lane = iota((sources, 128), 1)
-    row = jnp.full((sources, 128), -1, jnp.int32)
-    for j in range(slots):
-        row = jnp.where((lane % slots == j) & (limit > j), jnp.broadcast_to(targets[:, j : j + 1], (sources, 128)), row)
-    row = jnp.where(lane // slots == place[2] % 16, row, 0).astype(F32)
+    slots, sources = targets.shape
+    codes = jnp.where(iota((slots, sources), 0) < counts[...], targets[...], -1)
+    codes = jnp.concatenate([codes] * (128 // slots), axis=0)
+    codes = jnp.where(iota(codes.shape, 0) // slots == place[2] % (128 // slots), codes, 0)
+    row = codes.astype(F32).T
     for s in range(sources):
         out[17 * s : 17 * s + 8, :] = partials[s, :, :128]
         out[17 * s + 8 : 17 * s + 16, :] = partials[s, :, 128:]
@@ -135,33 +133,37 @@
         pivots_out[:, cols] = pick(pivot_hot, tile)
 
 
-def first_kernel(payload, front, give, tile_out, send_out, high_out, low_out, code_out):
+def front_kernel(front, give, out):
+    keep = give.shape[0]
+    hot = rows_hot(give, front.shape[0])
+    for u in range(4):
+        out[u * keep : (u + 1) * keep, :] = pick(hot, front[:, u * B : (u + 1) * B])
+
+
+def lead_kernel(payload, front_rows, give, send_first, send_rest):
     (high, low), code = unpack(payload)
-    high_out[...] = high
-    low_out[...] = low
-    code_out[...] = jnp.broadcast_to(code, code_out.shape)
-    rows = front.shape[0]
-    hot = hot_of(code, rows, 0)
-    tile = front[:, :B] + (dot(hot, high) + dot(hot, low))
-    tile_out[...] = tile
-    sent = pick(rows_hot(give, rows), tile)
-    for i in range(send_out.shape[0] // sent.shape[0]):
-        send_out[i * sent.shape[0] : (i + 1) * sent.shape[0], :] = sent
-
-
-def rest_kernel(high, low, code, front, give, rest_out, send_out, done_out):
-    rows = front.shape[0]
-    give_hot = rows_hot(give, rows)
+    keep = give.shape[0]
+    chosen = give[:, 0:1] * 4
+    hot = jnp.concatenate([(chosen + u == code).astype(F32) for u in range(4)], axis=0).astype(BF16)
+    sums = front_rows[...] + (dot(hot, high) + dot(hot, low))
+    for i in range(send_first.shape[0] // keep):
+        send_first[i * keep : (i + 1) * keep, :] = sums[:keep]
     for u in range(1, 4):
-        hot = hot_of(code[0:1, :], rows, u)
-        tile = front[:, u * B : (u + 1) * B] + (dot(hot, high[...]) + dot(hot, low[...]))
-        cols = slice((u - 1) * B, u * B)
-        rest_out[:, cols] = tile
-        send_out[:, cols] = pick(give_hot, tile)
-    done_out[...] = jnp.zeros_like(done_out)
-
-
-def sort_kernel(slot, gathered, done, out):
+        send_rest[:, (u - 1) * B : u * B] = sums[u * keep : (u + 1) * keep]
+
+
+def tiles_kernel(payload, front, first_out, rest_out):
+    (high, low), code = unpack(payload)
+    for u in range(4):
+        hot = hot_of(code, front.shape[0], u)
+        tile = front[:, u * B : (u + 1) * B] + (dot(hot, high) + dot(hot, low))
+        if u == 0:
+            first_out[...] = tile
+        else:
+            rest_out[:, (u - 1) * B : u * B] = tile
+
+
+def sort_kernel(slot, gathered, out):
     out[...] = pick(rows_hot(slot, gathered.shape[0]), gathered[...])
 
 
@@ -280,7 +282,7 @@
     slots = partials.shape[2]
 
     payload = call(pack_kernel, shaped(sources * 17, 128), 4, flops=10**6, moved=2 * 10**6)(
-        place, partials[0], targets[0], counts
+        place, partials[0], targets[0].T, counts
     ).reshape(sources * 17, 1, 128)
     payload = lax.all_to_all(payload, ("prow", "pcol"), 0, 0, tiled=True).reshape(sources * 17, 128)
 
@@ -302,33 +304,19 @@
     flat = front.reshape(rows, cols)
     copies = lax.axis_size("prow") * KEEP
 
-    def gather(payload, flat, own, active, give, slot, place):
-        first, send, high, low, code = call(
-            first_kernel,
-            (
-                shaped(rows, B),
-                shaped(copies, B),
-                shaped(sources * slots, B, dtype=BF16),
-                shaped(sources * slots, B, dtype=BF16),
-                shaped(8, sources * slots, dtype=jnp.int32),
-            ),
-            3,
-            scalars=0,
-            flops=10**9,
-            moved=4 * 10**6,
-        )(payload, flat, give)
-        w_first = lax.all_to_all(send, "prow", 0, 0, tiled=True)
+    front_rows = call(front_kernel, shaped(4 * KEEP, B), 2, scalars=0, flops=10**8, moved=3 * 10**6)(flat, give)
+
+    def gather(payload, flat, own, active, give, slot, place, front_rows):
+        send_first, send_rest = call(
+            lead_kernel, (shaped(copies, B), shaped(KEEP, cols - B)), 3, scalars=0, flops=10**8, moved=2 * 10**6
+        )(payload, front_rows, give)
+        w_first = lax.all_to_all(send_first, "prow", 0, 0, tiled=True)
+        w_rest = lax.all_gather(send_rest, "prow", axis=0, tiled=True)
+        first, rest = call(
+            tiles_kernel, (shaped(rows, B), shaped(rows, cols - B)), 2, scalars=0, flops=4 * 10**9, moved=6 * 10**6
+        )(payload, flat)
         r_other = core_swap(first)
-        rest, send, done = call(
-            rest_kernel,
-            (shaped(rows, cols - B), shaped(KEEP, cols - B), shaped(8, 128)),
-            5,
-            scalars=0,
-            flops=3 * 10**9,
-            moved=6 * 10**6,
-        )(high, low, code, flat, give)
-        w_rest = lax.all_gather(send, "prow", axis=0, tiled=True)
-        w_first = call(sort_kernel, shaped(2 * B, B), 3, scalars=0, flops=10**9, moved=10**6)(slot, w_first, done)
+        w_first = call(sort_kernel, shaped(2 * B, B), 2, scalars=0, flops=10**8, moved=10**6)(slot, w_first)
         w_other = core_swap(w_first)
         half, tile = call(
             panel_kernel, (shaped(rows, B), shaped(rows, B)), 6, flops=2 * 10**9, moved=4 * 10**6
@@ -350,7 +338,7 @@
             first, rest, w_rest, high, low
         )
 
-    def add_up(payload, flat, own, active, give, slot, place):
+    def add_up(payload, flat, own, active, give, slot, place, front_rows):
         matrix, pivots = call(
             assemble_kernel, (shaped(rows, cols), shaped(2 * B, cols)), 3, scalars=0, flops=4 * 10**9, moved=8 * 10**6
         )(payload, flat, own)
@@ -369,7 +357,7 @@
         )
         return out.reshape(front.shape)
 
-    return lax.cond(fits[0] == 1, gather, add_up, payload, flat, own, active, give, slot, place)
+    return lax.cond(fits[0] == 1, gather, add_up, payload, flat, own, active, give, slot, place, front_rows)
 
 
 def solution(mesh):

time: 118 us -> 111 us (0.941)
  waiting for transfers between devices: 44.7 us -> 38.9 us
    all_to_all x1, waiting for transfers between devices: 12.7 us -> 7.23 us  [gather(): w_first = lax.all_to_all(send_first, 'prow', 0, 0, tiled=True)]
    unnamed x14 -> x17, local copies, waits for them, and re-layouts: 4.44 us -> 3.77 us
    pallas_call x3 -> x4, Pallas kernels: 9.05 us -> 8.79 us  [the longest x1 4.33 us: gather(): call(tiles_kernel, (shaped(rows, B), shaped(rows, cols - B)), 2, scalars=...]
  transfers between devices with their start and end apart: 9 -> 9, of which waited for: 5 -> 5; matrix products, arithmetic and copies ran while one was open for 2% -> 0% of each run, Pallas kernels for 9% -> 14%
where the time goes in v4:
time: 111 us; the launch traced here: 110 us
  waiting for transfers between devices  38.9 us (35%)
  Pallas kernels  23.8 us (21%)
  starting transfers between devices  23.6 us (21%)
  between operations  14.1 us (13%)
  local copies, waits for them, and re-layouts  9.83 us (9%)
    ppermute x1, waiting for transfers between devices, gather(): n_late = lax.ppermute(n_early, 'pcol', [(1, 3), (0, 6), (2, 4), (7, 5)])  17.7 us
    all_to_all x1, waiting for transfers between devices, body(): lax.all_to_all(payload, ('prow', 'pcol'), 0, 0, tiled=True)  10.8 us
    all_to_all x1, starting transfers between devices, body(): lax.all_to_all(payload, ('prow', 'pcol'), 0, 0, tiled=True)  10.4 us
    all_to_all x1, waiting for transfers between devices, gather(): w_first = lax.all_to_all(send_first, 'prow', 0, 0, tiled=True)  7.23 us
    cond x12, local copies, waits for them, and re-layouts  6.06 us
    pallas_call x1, Pallas kernels, gather(): call(panel_kernel, (shaped(rows, B), shaped(rows, B)), 6, flops=2 * 10 **...  4.42 us
    pallas_call x1, Pallas kernels, gather(): call(tiles_kernel, (shaped(rows, B), shaped(rows, cols - B)), 2, scalars=...  4.33 us
    pallas_call x1, Pallas kernels, gather(): call(finish_kernel, shaped(*front.shape), 5, scalars=0, flops=4 * 10 ** 9...  3.79 us
  transfers between devices with their start and end apart: 9, of which 5 were waited for; matrix products, arithmetic and copies ran while one was open for 0% of the time, Pallas kernels for 14%

profile of v4, /device:TPU:65, one launch (start us, length us, event | category | flops | bytes accessed | tf_op | source)
XLA Modules:
  0.0 110.4 jit_solution(17568266477694726942)
XLA Ops:
  6.5 0.1 pad_add_fusion.place
  6.6 1.2 %copy-done.4 = f32[1,128,8,256]{3,2,1,0:T(8,128)S(1)} copy-done((f32[1,128,8,256]{3,2,1,0:T(8,128)S(1)}, f32[1,128,8,256]{3,2,1,0:T(8,128)}, u32[]{:S(2)}) %copy-start.4) | copy-done | bytes 1048600
  7.8 0.7 copy-done.5
  8.5 0.7 copy-done.6
  9.2 1.6 %shard_map.76 = f32[2176,128]{1,0:T(8,128)} custom-call(s32[3]{0:T(128)S(1)} %pad_add_fusion.place, f32[128,8,256]{2,1,0:T(8,128)S(1)} %bitcast.18, s32[8,128]{1,0:T(8,128)S(1)} %bitcast.19, s32[1,128]{1,0:T(1,128)S(1)} %copy-done.6), custom_call_target="tpu_custom_call" | custom-call | flops 1000000 | bytes 2000000 | tf_op jit(solution)/shard_map/pallas_call | solution.py:284
  10.8 10.4 %all-to-all-start.1 = ((f32[2176,1,128]{2,1,0:T(1,128)}), f32[2176,1,128]{2,1,0:T(1,128)S(1)}, u32[]{:S(2)}, u32[]{:S(2)}) async-start(f32[2176,1,128]{2,1,0:T(1,128)} %bitcast.10), calls=%async_computation.1 | async-start | bytes 2228224 | tf_op jit(solution)/shard_map/all_to_all | solution.py:287
  21.2 0.0 copy-done.12
  21.2 0.0 copy-done.13
  21.2 0.0 copy-done.14
  21.2 0.0 copy-start.19
  21.2 3.0 %shard_map.75 = (s32[512,128]{1,0:T(8,128)}, f32[2,512,128]{2,1,0:T(8,128)}, s32[48,128]{1,0:T(8,128)S(1)}, s32[512,128]{1,0:T(8,128)S(1)}, s32[1]{0:T(128)}) custom-call(s32[3]{0:T(128)S(1)} %pad_add_fusion.place, s32[2,16,256]{2,1,0:T(8,128)S(1)} %copy-done.13, s32[2,4,16,256]{3,2,1,0:T(8,128)S(1)} %copy-done.12, s32[2,256]{1,0:T(2,128)S(1)} %copy-done.14), custom_call_target="tpu_custom_call" | custom-call | flops 1000000000 | bytes 1000000 | tf_op jit(solution)/shard_map/pallas_call | solution.py:289
  24.2 0.0 copy-done.19
  24.2 0.5 copy.11
  24.7 0.0 copy-start.17
  25.3 0.7 copy-done.17
  26.1 1.2 %shard_map.77 = f32[192,256]{1,0:T(8,128)} custom-call(f32[512,1024]{1,0:T(8,128)S(1)} %bitcast.20, s32[48,128]{1,0:T(8,128)S(1)} %get-tuple-element.75.give), custom_call_target="tpu_custom_call" | custom-call | flops 100000000 | bytes 3000000 | tf_op jit(solution)/shard_map/pallas_call | solution.py:307
  27.3 10.8 %all-to-all-done.1 = f32[2176,1,128]{2,1,0:T(1,128)S(1)} async-done(((f32[2176,1,128]{2,1,0:T(1,128)}), f32[2176,1,128]{2,1,0:T(1,128)S(1)}, u32[]{:S(2)}, u32[]{:S(2)}) %all-to-all-start.1) | async-done | bytes 1114144 | tf_op jit(solution)/shard_map/all_to_all | solution.py:287
  38.1 65.4 %conditional.1 = (f32[2,256,4,256]{3,2,1,0:T(4,128)}) conditional(s32[]{:T(128)} %bitcast.5, (f32[2176,128]{1,0:T(8,128)S(1)}, f32[512,1024]{1,0:T(8,128)}, s32[512,128]{1,0:T(8,128)}, s32[]{:T(128)}, s32[3]{0:T(128)S(1)}, /*index=5*/f32[2,512,128]{2,1,0:T(8,128)}) %tuple.25, (s32[]{:T(128)}, f32[2176,128]{1,0:T(8,128)S(1)}, f32[192,256]{1,0:T(8,128)}, ...), branch_computations={%region_0.2_spmd, %region_2.3_spmd} | conditional | flops 11200131072 | bytes 91828088 | solution.py:360
  38.1 0.0 all-gather.2.cloned.1.call-start
  38.1 2.5 %branch_1_fun.6 = (f32[768,256]{1,0:T(8,128)}, f32[48,768]{1,0:T(8,128)}) custom-call(f32[2176,128]{1,0:T(8,128)S(1)} %get-tuple-element.49.payload, f32[192,256]{1,0:T(8,128)} %get-tuple-element.50.front_rows, s32[48,128]{1,0:T(8,128)S(1)} %get-tuple-element.51.give), custom_call_target="tpu_custom_call" | custom-call | flops 100000000 | bytes 2000000 | tf_op jit(solution)/shard_map/cond/branch_1_fun/pallas_call | solution.py:310
  40.7 0.0 all-gather.2.cloned.1.call-update
  40.7 0.0 copy-done.18
  40.7 3.7 %all-to-all-start = ((f32[16,48,256]{2,1,0:T(8,128)}), f32[16,48,256]{2,1,0:T(8,128)S(1)}, u32[]{:S(2)}, u32[]{:S(2)}) async-start(f32[16,48,256]{2,1,0:T(8,128)} %bitcast), calls=%async_computation | async-start | bytes 1572864 | tf_op jit(solution)/shard_map/cond/branch_1_fun/all_to_all | solution.py:313
  44.5 4.3 %branch_1_fun.8 = (f32[512,256]{1,0:T(8,128)S(1)}, f32[512,768]{1,0:T(8,128)S(1)}) custom-call(f32[2176,128]{1,0:T(8,128)} %copy-done.18, f32[512,1024]{1,0:T(8,128)} %get-tuple-element.53.front), custom_call_target="tpu_custom_call" | custom-call | flops 4000000000 | bytes 6000000 | tf_op jit(solution)/shard_map/cond/branch_1_fun/pallas_call | solution.py:315
  48.8 0.0 copy-start.15
  48.8 1.1 %copy-done.15 = f32[512,768]{1,0:T(8,128)} copy-done((f32[512,768]{1,0:T(8,128)}, f32[512,768]{1,0:T(8,128)S(1)}, u32[]{:S(2)}) %copy-start.15) | copy-done | bytes 1572888 | tf_op jit(solution)/shard_map/cond
  49.9 1.1 collective-permute-start.7
  51.0 7.2 %all-to-all-done = f32[16,48,256]{2,1,0:T(8,128)S(1)} async-done(((f32[16,48,256]{2,1,0:T(8,128)}), f32[16,48,256]{2,1,0:T(8,128)S(1)}, u32[]{:S(2)}, u32[]{:S(2)}) %all-to-all-start) | async-done | bytes 786464 | tf_op jit(solution)/shard_map/cond/branch_1_fun/all_to_all | solution.py:313
  58.3 0.7 branch_1_fun.7.w_own.w_first
  59.0 2.6 %collective-permute-start.6 = (f32[512,256]{1,0:T(8,128)S(1)}, f32[512,256]{1,0:T(8,128)S(1)}, u32[]{:S(2)}, u32[]{:S(2)}) collective-permute-start(f32[512,256]{1,0:T(8,128)S(1)} %branch_1_fun.7.w_own.w_first), channel_id=1, source_target_pairs={{0,1},{1,0},{2,3},{3,2},{4,5},{5,4},{6,7},{7,6},{8,9},{9,8},{10,11... | collective-permute-start | bytes 1572872 | tf_op jit(solution)/shard_map/cond/branch_1_fun/ppermute | solution.py:264
  61.6 0.0 collective-permute-done.7.r_other
  61.6 1.5 %collective-permute-done.6.w_other = f32[512,256]{1,0:T(8,128)S(1)} collective-permute-done((f32[512,256]{1,0:T(8,128)S(1)}, f32[512,256]{1,0:T(8,128)S(1)}, u32[]{:S(2)}, u32[]{:S(2)}) %collective-permute-start.6) | collective-permute-done | bytes 524320 | tf_op jit(solution)/shard_map/cond/branch_1_fun/ppermute | solution.py:264
  63.1 4.4 %branch_1_fun.9 = (f32[512,256]{1,0:T(8,128)S(1)}, f32[512,256]{1,0:T(8,128)S(1)}) custom-call(s32[3]{0:T(128)S(1)} %get-tuple-element.46.place, f32[512,256]{1,0:T(8,128)S(1)} %branch_1_fun.7.w_own.w_first, f32[512,256]{1,0:T(8,128)S(1)} %collective-permute-done.6.w_other, f32[512,256]{1,0:T(8,128)S(1)} %get-tuple-element.54.r_own.first, ...), custom_call_target="tpu_custom_call" | custom-call | flops 2000000000 | bytes 4000000 | tf_op jit(solution)/shard_map/cond/branch_1_fun/pallas_call | solution.py:321
  67.5 0.7 collective-permute-start.8
  68.2 0.0 collective-permute-done.8
  68.2 0.1 broadcast_select_fusion.n_early
  68.3 1.3 %collective-permute-start.9 = (f32[512,256]{1,0:T(8,128)S(1)}, f32[512,256]{1,0:T(8,128)S(1)}, u32[]{:S(2)}, u32[]{:S(2)}) collective-permute-start(f32[512,256]{1,0:T(8,128)S(1)} %broadcast_select_fusion.n_early), channel_id=1, source_target_pairs={{1,3},{0,6},{2,4},{7,5},{9,11},{8,14},{10,12},{15,13},{17,19},{16,... | collective-permute-start | bytes 1572872 | tf_op jit(solution)/shard_map/cond/branch_1_fun/ppermute | solution.py:327
  69.6 0.7 collective-permute-start.10
  70.3 17.7 %collective-permute-done.9.n_late = f32[512,256]{1,0:T(8,128)S(1)} collective-permute-done((f32[512,256]{1,0:T(8,128)S(1)}, f32[512,256]{1,0:T(8,128)S(1)}, u32[]{:S(2)}, u32[]{:S(2)}) %collective-permute-start.9) | collective-permute-done | bytes 524320 | tf_op jit(solution)/shard_map/cond/branch_1_fun/ppermute | solution.py:327
  88.1 3.1 %collective-permute-start.11 = (f32[512,256]{1,0:T(8,128)S(1)}, f32[512,256]{1,0:T(8,128)S(1)}, u32[]{:S(2)}, u32[]{:S(2)}) collective-permute-start(f32[512,256]{1,0:T(8,128)S(1)} %collective-permute-done.9.n_late), channel_id=1, source_target_pairs={{3,2},{6,7},{4,5},{5,4},{11,10},{14,15},{12,13},{13,12},{19,18},{2... | collective-permute-start | bytes 1572872 | tf_op jit(solution)/shard_map/cond/branch_1_fun/ppermute | solution.py:329
  91.2 0.0 collective-permute-done.10.o_early
  91.2 1.5 %collective-permute-done.11.o_late = f32[512,256]{1,0:T(8,128)S(1)} collective-permute-done((f32[512,256]{1,0:T(8,128)S(1)}, f32[512,256]{1,0:T(8,128)S(1)}, u32[]{:S(2)}, u32[]{:S(2)}) %collective-permute-start.11) | collective-permute-done | bytes 524320 | tf_op jit(solution)/shard_map/cond/branch_1_fun/ppermute | solution.py:329
  92.7 2.1 %branch_1_fun.10 = (bf16[512,768]{1,0:T(8,128)(2,1)S(1)}, bf16[512,768]{1,0:T(8,128)(2,1)S(1)}, f32[512,256]{1,0:T(8,128)S(1)}) custom-call(s32[3]{0:T(128)S(1)} %get-tuple-element.46.place, s32[512,128]{1,0:T(8,128)S(1)} %get-tuple-element.47.slot, f32[512,256]{1,0:T(8,128)S(1)} %broadcast_select_fusion.n_early, ...), custom_call_target="tpu_custom_call" | custom-call | flops 1000000000 | bytes 4000000 | tf_op jit(solution)/shard_map/cond/branch_1_fun/pallas_call | solution.py:330
  94.8 0.8 copy-done.10
  95.6 1.7 %copy-done.7 = f32[768,768]{1,0:T(8,128)S(1)} copy-done((f32[768,768]{1,0:T(8,128)S(1)}, f32[768,768]{1,0:T(8,128)}, u32[]{:S(2)}) %copy-start.7) | copy-done | bytes 2359320 | tf_op jit(solution)/shard_map/cond
  97.3 1.0 copy-done.11
  98.4 1.4 %copy-done.16 = f32[512,768]{1,0:T(8,128)S(1)} copy-done((f32[512,768]{1,0:T(8,128)S(1)}, f32[512,768]{1,0:T(8,128)}, u32[]{:S(2)}) %copy-start.16) | copy-done | bytes 1572888 | tf_op jit(solution)/shard_map/cond
  99.8 3.8 %branch_1_fun.11 = f32[2,256,4,256]{3,2,1,0:T(4,128)} custom-call(f32[512,256]{1,0:T(8,128)S(1)} %copy-done.11, f32[512,768]{1,0:T(8,128)S(1)} %copy-done.16, f32[768,768]{1,0:T(8,128)S(1)} %copy-done.7, bf16[512,768]{1,0:T(8,128)(2,1)S(1)} %get-tuple-element.61.high, bf16[512,768]{1,0:T(8,128)(2,1)S(1)} %get-tuple-element.62.low), custom_call_target="tpu_custom_call" | custom-call | flops 4000000000 | bytes 8000000 | tf_op jit(solution)/shard_map/cond/branch_1_fun/pallas_call | solution.py:337
  (12 shorter events, 0.0 us)
Async XLA Ops:
  6.6 1.2 %copy-start.4 = (f32[1,128,8,256]{3,2,1,0:T(8,128)S(1)}, f32[1,128,8,256]{3,2,1,0:T(8,128)}, u32[]{:S(2)}) copy-start(f32[1,128,8,256]{3,2,1,0:T(8,128)} %param.10) | copy-start | bytes 3145732
  7.8 0.7 copy-start.5
  8.5 0.7 copy-start.6
  9.2 12.0 %copy-start.12 = (s32[2,4,16,256]{3,2,1,0:T(8,128)S(1)}, s32[2,4,16,256]{3,2,1,0:T(8,128)}, u32[]{:S(2)}) copy-start(s32[2,4,16,256]{3,2,1,0:T(8,128)} %level_picks.1) | copy-start | bytes 393220
  9.2 12.0 %copy-start.13 = (s32[2,16,256]{2,1,0:T(8,128)S(1)}, s32[2,16,256]{2,1,0:T(8,128)}, u32[]{:S(2)}) copy-start(s32[2,16,256]{2,1,0:T(8,128)} %local_picks.1) | copy-start | bytes 98308
  9.2 12.0 %copy-start.14 = (s32[2,256]{1,0:T(2,128)S(1)}, s32[2,256]{1,0:T(2,128)}, u32[]{:S(2)}) copy-start(s32[2,256]{1,0:T(2,128)} %order.1) | copy-start | bytes 6148
  10.8 27.3 %all-to-all-start.1 = ((f32[2176,1,128]{2,1,0:T(1,128)}), f32[2176,1,128]{2,1,0:T(1,128)S(1)}, u32[]{:S(2)}, u32[]{:S(2)}) async-start(f32[2176,1,128]{2,1,0:T(1,128)} %bitcast.10), calls=%async_computation.1 | async-start | bytes 2228224 | tf_op jit(solution)/shard_map/all_to_all | solution.py:287
  21.2 3.0 %copy-start.19 = (f32[2,256,4,256]{3,2,1,0:T(4,128)S(1)}, f32[2,256,4,256]{3,2,1,0:T(4,128)}, u32[]{:S(2)}) copy-start(f32[2,256,4,256]{3,2,1,0:T(4,128)} %param.9) | copy-start | bytes 6291460
  24.7 1.3 %copy-start.17 = (f32[64,8,4,256]{3,1,2,0:T(8,128)}, f32[64,8,4,256]{3,1,2,0:T(8,128)S(1)}, u32[]{:S(2)}) copy-start(f32[64,8,4,256]{3,1,2,0:T(8,128)S(1)} %copy.11) | copy-start | bytes 6291460
  38.1 2.6 %copy-start.18 = (f32[2176,128]{1,0:T(8,128)}, f32[2176,128]{1,0:T(8,128)S(1)}, u32[]{:S(2)}) copy-start(f32[2176,128]{1,0:T(8,128)S(1)} %get-tuple-element.49.payload) | copy-start | bytes 3342340 | tf_op jit(solution)/shard_map/cond
  38.1 57.5 %all-gather.2.cloned.1.call-start = ((), (), s32[]{:S(2)}) async-start(), calls=%async_computation.3 | async-start | bytes 2506752 | tf_op jit(solution)/shard_map/cond/branch_1_fun/all_gather | solution.py:314
  40.7 17.6 %all-to-all-start = ((f32[16,48,256]{2,1,0:T(8,128)}), f32[16,48,256]{2,1,0:T(8,128)S(1)}, u32[]{:S(2)}, u32[]{:S(2)}) async-start(f32[16,48,256]{2,1,0:T(8,128)} %bitcast), calls=%async_computation | async-start | bytes 1572864 | tf_op jit(solution)/shard_map/cond/branch_1_fun/all_to_all | solution.py:313
  48.8 1.1 %copy-start.15 = (f32[512,768]{1,0:T(8,128)}, f32[512,768]{1,0:T(8,128)S(1)}, u32[]{:S(2)}) copy-start(f32[512,768]{1,0:T(8,128)S(1)} %get-tuple-element.59.rest) | copy-start | bytes 4718596 | tf_op jit(solution)/shard_map/cond
  49.9 11.6 %collective-permute-start.7 = (f32[512,256]{1,0:T(8,128)S(1)}, f32[512,256]{1,0:T(8,128)S(1)}, u32[]{:S(2)}, u32[]{:S(2)}) collective-permute-start(f32[512,256]{1,0:T(8,128)S(1)} %get-tuple-element.54.r_own.first), channel_id=1, source_target_pairs={{0,1},{1,0},{2,3},{3,2},{4,5},{5,4},{6,7},{7,6},{8,9},{9,8},{10,11... | collective-permute-start | bytes 1572872 | tf_op jit(solution)/shard_map/cond/branch_1_fun/ppermute | solution.py:264
  59.0 4.1 %collective-permute-start.6 = (f32[512,256]{1,0:T(8,128)S(1)}, f32[512,256]{1,0:T(8,128)S(1)}, u32[]{:S(2)}, u32[]{:S(2)}) collective-permute-start(f32[512,256]{1,0:T(8,128)S(1)} %branch_1_fun.7.w_own.w_first), channel_id=1, source_target_pairs={{0,1},{1,0},{2,3},{3,2},{4,5},{5,4},{6,7},{7,6},{8,9},{9,8},{10,11... | collective-permute-start | bytes 1572872 | tf_op jit(solution)/shard_map/cond/branch_1_fun/ppermute | solution.py:264
  67.5 0.7 collective-permute-start.8
  68.3 19.7 %collective-permute-start.9 = (f32[512,256]{1,0:T(8,128)S(1)}, f32[512,256]{1,0:T(8,128)S(1)}, u32[]{:S(2)}, u32[]{:S(2)}) collective-permute-start(f32[512,256]{1,0:T(8,128)S(1)} %broadcast_select_fusion.n_early), channel_id=1, source_target_pairs={{1,3},{0,6},{2,4},{7,5},{9,11},{8,14},{10,12},{15,13},{17,19},{16,... | collective-permute-start | bytes 1572872 | tf_op jit(solution)/shard_map/cond/branch_1_fun/ppermute | solution.py:327
  69.6 21.5 %collective-permute-start.10 = (f32[512,256]{1,0:T(8,128)S(1)}, f32[512,256]{1,0:T(8,128)S(1)}, u32[]{:S(2)}, u32[]{:S(2)}) collective-permute-start(f32[512,256]{1,0:T(8,128)S(1)} %broadcast_select_fusion.n_early), channel_id=1, source_target_pairs={{0,1},{1,0},{2,3},{7,6},{8,9},{9,8},{10,11},{15,14},{16,17},{17,16... | collective-permute-start | bytes 1572872 | tf_op jit(solution)/shard_map/cond/branch_1_fun/ppermute | solution.py:328
  88.1 4.6 %collective-permute-start.11 = (f32[512,256]{1,0:T(8,128)S(1)}, f32[512,256]{1,0:T(8,128)S(1)}, u32[]{:S(2)}, u32[]{:S(2)}) collective-permute-start(f32[512,256]{1,0:T(8,128)S(1)} %collective-permute-done.9.n_late), channel_id=1, source_target_pairs={{3,2},{6,7},{4,5},{5,4},{11,10},{14,15},{12,13},{13,12},{19,18},{2... | collective-permute-start | bytes 1572872 | tf_op jit(solution)/shard_map/cond/branch_1_fun/ppermute | solution.py:329
  94.8 0.8 copy-start.10
  95.6 1.7 %copy-start.7 = (f32[768,768]{1,0:T(8,128)S(1)}, f32[768,768]{1,0:T(8,128)}, u32[]{:S(2)}) copy-start(f32[768,768]{1,0:T(8,128)} %all-gather.2.cloned.1.call-done.w_rest) | copy-start | bytes 7077892 | tf_op jit(solution)/shard_map/cond
  97.3 1.0 copy-start.11
  98.3 1.4 %copy-start.16 = (f32[512,768]{1,0:T(8,128)S(1)}, f32[512,768]{1,0:T(8,128)}, u32[]{:S(2)}) copy-start(f32[512,768]{1,0:T(8,128)} %copy-done.15) | copy-start | bytes 4718596 | tf_op jit(solution)/shard_map/cond
Sparse Core Ops, SparseCore 0:
  41.3 45.5 all-gather.1

commit v5 on v4

--- a/solution.py
+++ b/solution.py
@@ -10,10 +10,13 @@
 F32 = jnp.float32
 BF16 = jnp.bfloat16
 VM = pl.BlockSpec(memory_space=pltpu.VMEM)
+HBM = pl.BlockSpec(memory_space=pltpu.HBM)
 SM = pl.BlockSpec(memory_space=pltpu.SMEM)
 B = 256
 KEEP = 48
 PARAMS = dict(compiler_params=pltpu.CompilerParams(vmem_limit_bytes=14 * 1024 * 1024))
+
+ALONE = dict(compiler_params=pltpu.CompilerParams(vmem_limit_bytes=63 * 1024 * 1024))
 
 
 def iota(shape, dim):
@@ -87,16 +90,34 @@
     give_out[...] = jnp.broadcast_to(give, (keep, 128))
 
 
-def pack_kernel(place, partials, targets, counts, out):
+def pack_kernel(place, partials_hbm, targets_hbm, counts_hbm, out, partials, targets, counts, sems):
     slots, sources = targets.shape
+    parts = sems.shape[0] - 2
+    step = sources // parts
+    small = [
+        pltpu.make_async_copy(targets_hbm, targets, sems.at[parts]),
+        pltpu.make_async_copy(counts_hbm, counts, sems.at[parts + 1]),
+    ]
+    large = [
+        pltpu.make_async_copy(
+            partials_hbm.at[i * step : (i + 1) * step], partials.at[i * step : (i + 1) * step], sems.at[i]
+        )
+        for i in range(parts)
+    ]
+    for copy in small + large:
+        copy.start()
+    for copy in small:
+        copy.wait()
     codes = jnp.where(iota((slots, sources), 0) < counts[...], targets[...], -1)
     codes = jnp.concatenate([codes] * (128 // slots), axis=0)
     codes = jnp.where(iota(codes.shape, 0) // slots == place[2] % (128 // slots), codes, 0)
     row = codes.astype(F32).T
-    for s in range(sources):
-        out[17 * s : 17 * s + 8, :] = partials[s, :, :128]
-        out[17 * s + 8 : 17 * s + 16, :] = partials[s, :, 128:]
-        out[17 * s + 16 : 17 * s + 17, :] = row[s : s + 1, :]
+    for i in range(parts):
+        large[i].wait()
+        for s in range(i * step, (i + 1) * step):
+            out[17 * s : 17 * s + 8, :] = partials[s, :, :128]
+            out[17 * s + 8 : 17 * s + 16, :] = partials[s, :, 128:]
+            out[17 * s + 16 : 17 * s + 17, :] = row[s : s + 1, :]
 
 
 def unpack(payload):
@@ -148,8 +169,9 @@
     sums = front_rows[...] + (dot(hot, high) + dot(hot, low))
     for i in range(send_first.shape[0] // keep):
         send_first[i * keep : (i + 1) * keep, :] = sums[:keep]
-    for u in range(1, 4):
-        send_rest[:, (u - 1) * B : u * B] = sums[u * keep : (u + 1) * keep]
+    for i in range(send_rest.shape[0] // keep):
+        for u in range(1, 4):
+            send_rest[i * keep : (i + 1) * keep, (u - 1) * B : u * B] = sums[u * keep : (u + 1) * keep]
 
 
 def tiles_kernel(payload, front, first_out, rest_out):
@@ -215,31 +237,74 @@
         out[:, cols] = new
 
 
-def spread_kernel(place, slot, n_early, n_late, o_early, o_late, first, w_first, tile, high_out, low_out, first_out):
+def finish_kernel(
+    place, slot_hbm, n_early, n_late, o_early, o_late, first_hbm, w_first_hbm, tile_hbm, rest_hbm, w_rest_hbm, out_hbm,
+    slot, n_own, n_other, first, w_first, tile, rest, w_rest, out, sems
+):
     q = place[1]
     even = q % 2 == 0
-    n_own = jnp.where((q < 3) | (q == 7), n_early[...], n_late[...])
-    n_other = jnp.where((q < 2) | (q == 3) | (q == 6), o_early[...], o_late[...])
-    hot = rows_hot(slot, high_out.shape[1])
-    h0, l0 = halves(jnp.where(even, n_own, n_other))
-    h1, l1 = halves(jnp.where(even, n_other, n_own))
-    high_out[...] = (dot(h0, hot[:B]) + dot(h1, hot[B:])).astype(BF16)
-    low_out[...] = (dot(l0, hot[:B]) + dot(l1, hot[B:])).astype(BF16)
+    own_early = (q < 3) | (q == 7)
+    other_early = (q < 2) | (q == 3) | (q == 6)
+    copy = pltpu.make_async_copy
+
+    @pl.when(own_early)
+    def _():
+        copy(n_early, n_own, sems.at[0]).start()
+
+    @pl.when(jnp.logical_not(own_early))
+    def _():
+        copy(n_late, n_own, sems.at[0]).start()
+
+    @pl.when(other_early)
+    def _():
+        copy(o_early, n_other, sems.at[1]).start()
+
+    @pl.when(jnp.logical_not(other_early))
+    def _():
+        copy(o_late, n_other, sems.at[1]).start()
+
+    moves = [
+        copy(slot_hbm, slot, sems.at[2]),
+        copy(first_hbm, first, sems.at[3]),
+        copy(w_first_hbm, w_first, sems.at[4]),
+        copy(tile_hbm, tile, sems.at[5]),
+        copy(rest_hbm, rest, sems.at[6]),
+        copy(w_rest_hbm, w_rest, sems.at[7]),
+    ]
+    for move in moves:
+        move.start()
+    copy(n_early, n_own, sems.at[0]).wait()
+    copy(o_early, n_other, sems.at[1]).wait()
+    h0, l0 = halves(jnp.where(even, n_own[...], n_other[...]))
+    h1, l1 = halves(jnp.where(even, n_other[...], n_own[...]))
+    for move in moves[1:4]:
+        move.wait()
+    rows = first.shape[0]
+    half = out.shape[1]
     new = first[...] - (dot3((h0, l0), halves(w_first[:B])) + dot3((h1, l1), halves(w_first[B:])))
-    first_out[...] = jnp.where(q < 2, tile[...], new)
-
-
-def finish_kernel(first, rest, w_rest, high, low, out):
-    n = (high[...], low[...])
-    half = out.shape[1]
-    for u in range(4):
-        if u == 0:
-            new = first[...]
-        else:
-            cols = slice((u - 1) * B, u * B)
-            new = rest[:, cols] - dot3(n, halves(w_rest[:, cols]))
-        for t in range(out.shape[0]):
-            out[t, :, u, :] = new[t * half : (t + 1) * half]
+    new = jnp.where(q < 2, tile[...], new)
+    for t in range(rows // half):
+        out[t, :, 0, :] = new[t * half : (t + 1) * half]
+    moves[0].wait()
+    hot = rows_hot(slot, w_rest.shape[0])
+    high = (dot(h0, hot[:B]) + dot(h1, hot[B:])).astype(BF16)
+    low = (dot(l0, hot[:B]) + dot(l1, hot[B:])).astype(BF16)
+    for move in moves[4:]:
+        move.wait()
+    w = [halves(w_rest[:, u * B : (u + 1) * B]) for u in range(3)]
+    block = half // 2
+    sent = []
+    for i in range(rows // block):
+        t, at = i * block // half, i * block % half
+        span = slice(i * block, (i + 1) * block)
+        n = (high[span], low[span])
+        for u in range(1, 4):
+            out[t, at : at + block, u, :] = rest[span, (u - 1) * B : u * B] - dot3(n, w[u - 1])
+        done = copy(out.at[t, at : at + block], out_hbm.at[t, at : at + block], sems.at[8 + i])
+        done.start()
+        sent.append(done)
+    for done in sent:
+        done.wait()
 
 
 def call(kernel, outs, n_in, scalars=1, outs_in_smem=0, flops=0, moved=0):
@@ -281,9 +346,20 @@
     sources = partials.shape[1]
     slots = partials.shape[2]
 
-    payload = call(pack_kernel, shaped(sources * 17, 128), 4, flops=10**6, moved=2 * 10**6)(
-        place, partials[0], targets[0].T, counts
-    ).reshape(sources * 17, 1, 128)
+    payload = pl.pallas_call(
+        pack_kernel,
+        out_shape=shaped(sources * 17, 128),
+        in_specs=[SM, HBM, HBM, HBM],
+        out_specs=VM,
+        scratch_shapes=[
+            pltpu.VMEM((sources, slots, B), F32),
+            pltpu.VMEM((slots, sources), jnp.int32),
+            pltpu.VMEM((1, sources), jnp.int32),
+            pltpu.SemaphoreType.DMA((6,)),
+        ],
+        cost_estimate=pl.CostEstimate(flops=10**6, bytes_accessed=2 * 10**6, transcendentals=0),
+        **ALONE,
+    )(place, partials[0], targets[0].T, counts).reshape(sources * 17, 1, 128)
     payload = lax.all_to_all(payload, ("prow", "pcol"), 0, 0, tiled=True).reshape(sources * 17, 128)
 
     own, active, give, slot, fits = call(
@@ -303,15 +379,16 @@
     front, own = lax.optimization_barrier((front, own))
     flat = front.reshape(rows, cols)
     copies = lax.axis_size("prow") * KEEP
+    share_rows = 2 * B // lax.axis_size("prow")
 
     front_rows = call(front_kernel, shaped(4 * KEEP, B), 2, scalars=0, flops=10**8, moved=3 * 10**6)(flat, give)
 
     def gather(payload, flat, own, active, give, slot, place, front_rows):
         send_first, send_rest = call(
-            lead_kernel, (shaped(copies, B), shaped(KEEP, cols - B)), 3, scalars=0, flops=10**8, moved=2 * 10**6
+            lead_kernel, (shaped(copies, B), shaped(copies, cols - B)), 3, scalars=0, flops=10**8, moved=2 * 10**6
         )(payload, front_rows, give)
         w_first = lax.all_to_all(send_first, "prow", 0, 0, tiled=True)
-        w_rest = lax.all_gather(send_rest, "prow", axis=0, tiled=True)
+        w_rest = lax.all_to_all(send_rest, "prow", 0, 0, tiled=True)
         first, rest = call(
             tiles_kernel, (shaped(rows, B), shaped(rows, cols - B)), 2, scalars=0, flops=4 * 10**9, moved=6 * 10**6
         )(payload, flat)
@@ -327,16 +404,26 @@
         n_late = lax.ppermute(n_early, "pcol", [(1, 3), (0, 6), (2, 4), (7, 5)])
         o_early = lax.ppermute(n_early, "pcol", [(0, 1), (1, 0), (2, 3), (7, 6)])
         o_late = lax.ppermute(n_late, "pcol", [(3, 2), (6, 7), (4, 5), (5, 4)])
-        high, low, first = call(
-            spread_kernel,
-            (shaped(rows, copies, dtype=BF16), shaped(rows, copies, dtype=BF16), shaped(rows, B)),
-            9,
-            flops=10**9,
-            moved=4 * 10**6,
-        )(place, slot, n_early, n_late, o_early, o_late, first, w_first, tile)
-        return call(finish_kernel, shaped(*front.shape), 5, scalars=0, flops=4 * 10**9, moved=8 * 10**6)(
-            first, rest, w_rest, high, low
-        )
+        return pl.pallas_call(
+            finish_kernel,
+            out_shape=shaped(*front.shape),
+            in_specs=[SM] + [HBM] * 10,
+            out_specs=HBM,
+            scratch_shapes=[
+                pltpu.VMEM((2 * B, 128), jnp.int32),
+                pltpu.VMEM((rows, B), F32),
+                pltpu.VMEM((rows, B), F32),
+                pltpu.VMEM((rows, B), F32),
+                pltpu.VMEM((2 * B, B), F32),
+                pltpu.VMEM((rows, B), F32),
+                pltpu.VMEM((rows, cols - B), F32),
+                pltpu.VMEM((copies, cols - B), F32),
+                pltpu.VMEM(front.shape, F32),
+                pltpu.SemaphoreType.DMA((12,)),
+            ],
+            cost_estimate=pl.CostEstimate(flops=4 * 10**9, bytes_accessed=8 * 10**6, transcendentals=0),
+            **ALONE,
+        )(place, slot, n_early, n_late, o_early, o_late, first, w_first, tile, rest, w_rest)
 
     def add_up(payload, flat, own, active, give, slot, place, front_rows):
         matrix, pivots = call(
@@ -344,7 +431,8 @@
         )(payload, flat, own)
         r_own = matrix[:, :B]
         r_other = core_swap(r_own)
-        pivots = lax.psum(pivots, "prow")
+        share = lax.all_to_all(pivots, "prow", 0, 0, tiled=True).reshape(-1, share_rows, cols).sum(axis=0)
+        pivots = lax.all_to_all(jnp.tile(share, (lax.axis_size("prow"), 1)), "prow", 0, 0, tiled=True)
         w_own = pivots[:, :B]
         w_other = core_swap(w_own)
         half, tile = call(

time: 111 us -> 111 us (level)
  the two profiles are of different devices: /device:TPU:65 before, /device:TPU:1 now
where the time goes in v5:
time: 111 us; the launch traced here: 110 us
  waiting for transfers between devices  47.4 us (43%)
  starting transfers between devices  30.3 us (27%)
  Pallas kernels  27.4 us (25%)
  local copies, waits for them, and re-layouts  4.08 us (4%)
    all_to_all x1, waiting for transfers between devices, gather(): w_rest = lax.all_to_all(send_rest, 'prow', 0, 0, tiled=True)  16.6 us
    all_to_all x1, waiting for transfers between devices, body(): lax.all_to_all(payload, ('prow', 'pcol'), 0, 0, tiled=True)  14.9 us
    all_to_all x1, starting transfers between devices, body(): lax.all_to_all(payload, ('prow', 'pcol'), 0, 0, tiled=True)  11.9 us
    pallas_call x1, Pallas kernels, gather(): pl.pallas_call(finish_kernel, out_shape=shaped(*front.shape), in_specs=[S...  7.86 us
    all_to_all x1, waiting for transfers between devices, gather(): w_first = lax.all_to_all(send_first, 'prow', 0, 0, tiled=True)  6.12 us
    ppermute x1, waiting for transfers between devices, gather(): step = lax.ppermute(half, 'pcol', [(0, 2), (1, 7)])  6.07 us
    all_to_all x1, starting transfers between devices, gather(): w_rest = lax.all_to_all(send_rest, 'prow', 0, 0, tiled=True)  4.57 us
    pallas_call x1, Pallas kernels, gather(): call(tiles_kernel, (shaped(rows, B), shaped(rows, cols - B)), 2, scalars=...  4.36 us
  transfers between devices with their start and end apart: 9, of which 5 were waited for; matrix products, arithmetic and copies ran while one was open for 0% of the time, Pallas kernels for 11%

profile of v5, /device:TPU:1, one launch (start us, length us, event | category | flops | bytes accessed | tf_op | source)
XLA Modules:
  0.0 110.2 jit_solution(12325473625879479623)
XLA Ops:
  0.0 0.1 pad_add_fusion.place
  0.1 2.8 %shard_map.76 = f32[2176,128]{1,0:T(8,128)} custom-call(s32[3]{0:T(128)S(1)} %pad_add_fusion.place, f32[128,8,256]{2,1,0:T(8,128)} %bitcast.30, s32[8,128]{1,0:T(8,128)} %bitcast.31, s32[1,128]{1,0:T(1,128)} %counts_hbm.1), custom_call_target="tpu_custom_call" | custom-call | flops 1000000 | bytes 2000000 | tf_op jit(solution)/shard_map/pallas_call | solution.py:349
  2.9 11.9 %all-to-all-start.4 = ((f32[2176,1,128]{2,1,0:T(1,128)}), f32[2176,1,128]{2,1,0:T(1,128)}, u32[]{:S(2)}, u32[]{:S(2)}) async-start(f32[2176,1,128]{2,1,0:T(1,128)} %bitcast.28), calls=%async_computation.4 | async-start | bytes 2228224 | tf_op jit(solution)/shard_map/all_to_all | solution.py:363
  14.8 0.0 copy-done.7
  14.8 0.0 copy-done.8
  14.8 0.0 copy-done.9
  14.9 0.0 copy-start.13
  14.9 3.1 %shard_map.75 = (s32[512,128]{1,0:T(8,128)S(1)}, f32[2,512,128]{2,1,0:T(8,128)}, s32[48,128]{1,0:T(8,128)S(1)}, s32[512,128]{1,0:T(8,128)}, s32[1]{0:T(128)}) custom-call(s32[3]{0:T(128)S(1)} %pad_add_fusion.place, s32[2,16,256]{2,1,0:T(8,128)S(1)} %copy-done.8, s32[2,4,16,256]{3,2,1,0:T(8,128)S(1)} %copy-done.7, s32[2,256]{1,0:T(2,128)S(1)} %copy-done.9), custom_call_target="tpu_custom_call" | custom-call | flops 1000000000 | bytes 1000000 | tf_op jit(solution)/shard_map/pallas_call | solution.py:365
  18.5 0.0 copy-done.13
  18.5 0.5 copy.11
  19.0 0.5 shard_map.77
  19.5 14.9 %all-to-all-done.4 = f32[2176,1,128]{2,1,0:T(1,128)} async-done(((f32[2176,1,128]{2,1,0:T(1,128)}), f32[2176,1,128]{2,1,0:T(1,128)}, u32[]{:S(2)}, u32[]{:S(2)}) %all-to-all-start.4) | async-done | bytes 1114144 | tf_op jit(solution)/shard_map/all_to_all | solution.py:363
  34.4 75.7 %conditional.1 = (f32[2,256,4,256]{3,2,1,0:T(4,128)}) conditional(s32[]{:T(128)} %bitcast.9, (f32[2176,128]{1,0:T(8,128)}, f32[512,1024]{1,0:T(8,128)S(1)}, s32[512,128]{1,0:T(8,128)S(1)}, s32[]{:T(128)}, s32[3]{0:T(128)S(1)}, /*index=5*/f32[2,512,128]{2,1,0:T(8,128)}) %tuple.19, (s32[]{:T(128)}, f32[2176,128]{1,0:T(8,128)}, ...), branch_computations={%region_0.2_spmd, %region_2.3_spmd} | conditional | flops 10200131584 | bytes 85798736 | solution.py:448
  34.4 4.1 %branch_1_fun.5 = (f32[768,256]{1,0:T(8,128)}, f32[768,768]{1,0:T(8,128)}) custom-call(f32[2176,128]{1,0:T(8,128)} %get-tuple-element.49.payload, f32[192,256]{1,0:T(8,128)S(1)} %get-tuple-element.50.front_rows, s32[48,128]{1,0:T(8,128)S(1)} %get-tuple-element.51.give), custom_call_target="tpu_custom_call" | custom-call | flops 100000000 | bytes 2000000 | tf_op jit(solution)/shard_map/cond/branch_1_fun/pallas_call | solution.py:387
  38.5 0.0 copy-done.12
  38.5 3.6 %all-to-all-start.2 = ((f32[16,48,256]{2,1,0:T(8,128)}), f32[16,48,256]{2,1,0:T(8,128)S(1)}, u32[]{:S(2)}, u32[]{:S(2)}) async-start(f32[16,48,256]{2,1,0:T(8,128)} %bitcast.2), calls=%async_computation.2 | async-start | bytes 1572864 | tf_op jit(solution)/shard_map/cond/branch_1_fun/all_to_all | solution.py:390
  42.2 0.0 copy-start.15
  42.2 4.4 %branch_1_fun.7 = (f32[512,256]{1,0:T(8,128)S(1)}, f32[512,768]{1,0:T(8,128)S(1)}) custom-call(f32[2176,128]{1,0:T(8,128)} %get-tuple-element.49.payload, f32[512,1024]{1,0:T(8,128)} %copy-done.12), custom_call_target="tpu_custom_call" | custom-call | flops 4000000000 | bytes 6000000 | tf_op jit(solution)/shard_map/cond/branch_1_fun/pallas_call | solution.py:392
  46.5 0.0 copy-start.10
  46.5 1.2 %copy-done.10 = f32[512,768]{1,0:T(8,128)} copy-done((f32[512,768]{1,0:T(8,128)}, f32[512,768]{1,0:T(8,128)S(1)}, u32[]{:S(2)}) %copy-start.10) | copy-done | bytes 1572888 | tf_op jit(solution)/shard_map/cond
  47.7 1.2 %collective-permute-start.7 = (f32[512,256]{1,0:T(8,128)S(1)}, f32[512,256]{1,0:T(8,128)S(1)}, u32[]{:S(2)}, u32[]{:S(2)}) collective-permute-start(f32[512,256]{1,0:T(8,128)S(1)} %get-tuple-element.54.r_own.first_hbm), channel_id=1, source_target_pairs={{0,1},{1,0},{2,3},{3,2},{4,5},{5,4},{6,7},{7,6},{8,9},{9,8},{10,11... | collective-permute-start | bytes 1572872 | tf_op jit(solution)/shard_map/cond/branch_1_fun/ppermute | solution.py:329
  48.9 6.1 %all-to-all-done.2 = f32[16,48,256]{2,1,0:T(8,128)S(1)} async-done(((f32[16,48,256]{2,1,0:T(8,128)}), f32[16,48,256]{2,1,0:T(8,128)S(1)}, u32[]{:S(2)}, u32[]{:S(2)}) %all-to-all-start.2) | async-done | bytes 786464 | tf_op jit(solution)/shard_map/cond/branch_1_fun/all_to_all | solution.py:390
  55.1 0.0 copy-done.15
  55.1 0.7 branch_1_fun.6.w_own.w_first_hbm
  55.8 0.0 copy-start.3
  55.8 2.5 %collective-permute-start.6 = (f32[512,256]{1,0:T(8,128)S(1)}, f32[512,256]{1,0:T(8,128)S(1)}, u32[]{:S(2)}, u32[]{:S(2)}) collective-permute-start(f32[512,256]{1,0:T(8,128)S(1)} %branch_1_fun.6.w_own.w_first_hbm), channel_id=1, source_target_pairs={{0,1},{1,0},{2,3},{3,2},{4,5},{5,4},{6,7},{7,6},{8,9},{9,8},{10,11... | collective-permute-start | bytes 1572872 | tf_op jit(solution)/shard_map/cond/branch_1_fun/ppermute | solution.py:329
  58.3 4.6 %all-to-all-start.3 = ((f32[16,48,768]{2,1,0:T(8,128)}), f32[16,48,768]{2,1,0:T(8,128)}, u32[]{:S(2)}, u32[]{:S(2)}) async-start(f32[16,48,768]{2,1,0:T(8,128)} %bitcast.4), calls=%async_computation.3 | async-start | bytes 4718592 | tf_op jit(solution)/shard_map/cond/branch_1_fun/all_to_all | solution.py:391
  62.9 0.0 collective-permute-done.7.r_other
  62.9 0.0 collective-permute-done.6.w_other
  62.9 0.0 copy-done.4
  62.9 0.0 copy-done.3
  62.9 0.0 copy-done.19
  62.9 3.9 %branch_1_fun.8 = (f32[512,256]{1,0:T(8,128)S(1)}, f32[512,256]{1,0:T(8,128)S(1)}) custom-call(s32[3]{0:T(128)S(1)} %get-tuple-element.46.place, f32[512,256]{1,0:T(8,128)S(1)} %branch_1_fun.6.w_own.w_first_hbm, f32[512,256]{1,0:T(8,128)S(1)} %collective-permute-done.6.w_other, f32[512,256]{1,0:T(8,128)S(1)} %get-tuple-element.54.r_own.first_hbm, ...), custom_call_target="tpu_custom_call" | custom-call | flops 2000000000 | bytes 4000000 | tf_op jit(solution)/shard_map/cond/branch_1_fun/pallas_call | solution.py:398
  66.8 0.8 copy-done.11
  67.6 2.1 %collective-permute-start.8 = (f32[512,256]{1,0:T(8,128)S(1)}, f32[512,256]{1,0:T(8,128)S(1)}, u32[]{:S(2)}, u32[]{:S(2)}) collective-permute-start(f32[512,256]{1,0:T(8,128)S(1)} %get-tuple-element.56), channel_id=1, source_target_pairs={{0,2},{1,7},{8,10},{9,15},{16,18},{17,23},{24,26},{25,31},{32,34},... | collective-permute-start | bytes 1572872 | tf_op jit(solution)/shard_map/cond/branch_1_fun/ppermute | solution.py:402
  69.8 6.1 %collective-permute-done.8 = f32[512,256]{1,0:T(8,128)S(1)} collective-permute-done((f32[512,256]{1,0:T(8,128)S(1)}, f32[512,256]{1,0:T(8,128)S(1)}, u32[]{:S(2)}, u32[]{:S(2)}) %collective-permute-start.8) | collective-permute-done | bytes 524320 | tf_op jit(solution)/shard_map/cond/branch_1_fun/ppermute | solution.py:402
  75.8 0.1 broadcast_select_fusion.n_early
  75.9 1.3 %collective-permute-start.9 = (f32[512,256]{1,0:T(8,128)S(1)}, f32[512,256]{1,0:T(8,128)S(1)}, u32[]{:S(2)}, u32[]{:S(2)}) collective-permute-start(f32[512,256]{1,0:T(8,128)S(1)} %broadcast_select_fusion.n_early), channel_id=1, source_target_pairs={{1,3},{0,6},{2,4},{7,5},{9,11},{8,14},{10,12},{15,13},{17,19},{16,... | collective-permute-start | bytes 1572872 | tf_op jit(solution)/shard_map/cond/branch_1_fun/ppermute | solution.py:404
  77.3 2.4 %collective-permute-start.10 = (f32[512,256]{1,0:T(8,128)S(1)}, f32[512,256]{1,0:T(8,128)S(1)}, u32[]{:S(2)}, u32[]{:S(2)}) collective-permute-start(f32[512,256]{1,0:T(8,128)S(1)} %broadcast_select_fusion.n_early), channel_id=1, source_target_pairs={{0,1},{1,0},{2,3},{7,6},{8,9},{9,8},{10,11},{15,14},{16,17},{17,16... | collective-permute-start | bytes 1572872 | tf_op jit(solution)/shard_map/cond/branch_1_fun/ppermute | solution.py:405
  79.6 3.7 %collective-permute-done.9.n_late = f32[512,256]{1,0:T(8,128)S(1)} collective-permute-done((f32[512,256]{1,0:T(8,128)S(1)}, f32[512,256]{1,0:T(8,128)S(1)}, u32[]{:S(2)}, u32[]{:S(2)}) %collective-permute-start.9) | collective-permute-done | bytes 524320 | tf_op jit(solution)/shard_map/cond/branch_1_fun/ppermute | solution.py:404
  83.3 0.7 collective-permute-start.11
  84.0 16.6 %all-to-all-done.3 = f32[16,48,768]{2,1,0:T(8,128)} async-done(((f32[16,48,768]{2,1,0:T(8,128)}), f32[16,48,768]{2,1,0:T(8,128)}, u32[]{:S(2)}, u32[]{:S(2)}) %all-to-all-start.3) | async-done | bytes 2359328 | tf_op jit(solution)/shard_map/cond/branch_1_fun/all_to_all | solution.py:391
  100.6 0.0 collective-permute-done.10.o_early
  100.6 0.0 copy-done.16
  100.6 0.0 collective-permute-done.11.o_late
  100.6 0.8 copy-done.17
  101.4 0.8 copy-done.18
  102.2 7.9 %branch_1_fun.9 = f32[2,256,4,256]{3,2,1,0:T(4,128)} custom-call(s32[3]{0:T(128)S(1)} %get-tuple-element.46.place, s32[512,128]{1,0:T(8,128)S(1)} %copy-done.15, f32[512,256]{1,0:T(8,128)} %copy-done.14, f32[512,256]{1,0:T(8,128)} %copy-done.16, f32[512,256]{1,0:T(8,128)} %copy-done.17, f32[512,256]{1,0:T(8,128)} %copy-done.18, f32[512,256]{1,0:T(8,128)} %copy-done.4, ...), custom_call_target="tpu_custom_call" | custom-call | flops 4000000000 | bytes 8000000 | tf_op jit(solution)/shard_map/cond/branch_1_fun/pallas_call | solution.py:407
  (12 shorter events, 0.0 us)
Async XLA Ops:
  0.1 14.8 %copy-start.7 = (s32[2,4,16,256]{3,2,1,0:T(8,128)S(1)}, s32[2,4,16,256]{3,2,1,0:T(8,128)}, u32[]{:S(2)}) copy-start(s32[2,4,16,256]{3,2,1,0:T(8,128)} %level_picks.1) | copy-start | bytes 393220
  0.1 14.8 %copy-start.8 = (s32[2,16,256]{2,1,0:T(8,128)S(1)}, s32[2,16,256]{2,1,0:T(8,128)}, u32[]{:S(2)}) copy-start(s32[2,16,256]{2,1,0:T(8,128)} %local_picks.1) | copy-start | bytes 98308
  0.1 14.8 %copy-start.9 = (s32[2,256]{1,0:T(2,128)S(1)}, s32[2,256]{1,0:T(2,128)}, u32[]{:S(2)}) copy-start(s32[2,256]{1,0:T(2,128)} %order.1) | copy-start | bytes 6148
  2.9 31.5 %all-to-all-start.4 = ((f32[2176,1,128]{2,1,0:T(1,128)}), f32[2176,1,128]{2,1,0:T(1,128)}, u32[]{:S(2)}, u32[]{:S(2)}) async-start(f32[2176,1,128]{2,1,0:T(1,128)} %bitcast.28), calls=%async_computation.4 | async-start | bytes 2228224 | tf_op jit(solution)/shard_map/all_to_all | solution.py:363
  14.9 3.6 %copy-start.13 = (f32[2,256,4,256]{3,2,1,0:T(4,128)S(1)}, f32[2,256,4,256]{3,2,1,0:T(4,128)}, u32[]{:S(2)}) copy-start(f32[2,256,4,256]{3,2,1,0:T(4,128)} %param.9) | copy-start | bytes 6291460
  34.4 4.1 %copy-start.12 = (f32[512,1024]{1,0:T(8,128)}, f32[512,1024]{1,0:T(8,128)S(1)}, u32[]{:S(2)}) copy-start(f32[512,1024]{1,0:T(8,128)S(1)} %get-tuple-element.53.front) | copy-start | bytes 6291460 | tf_op jit(solution)/shard_map/cond
  38.5 16.5 %all-to-all-start.2 = ((f32[16,48,256]{2,1,0:T(8,128)}), f32[16,48,256]{2,1,0:T(8,128)S(1)}, u32[]{:S(2)}, u32[]{:S(2)}) async-start(f32[16,48,256]{2,1,0:T(8,128)} %bitcast.2), calls=%async_computation.2 | async-start | bytes 1572864 | tf_op jit(solution)/shard_map/cond/branch_1_fun/all_to_all | solution.py:390
  42.2 12.9 %copy-start.15 = (s32[512,128]{1,0:T(8,128)S(1)}, s32[512,128]{1,0:T(8,128)}, u32[]{:S(2)}) copy-start(s32[512,128]{1,0:T(8,128)} %get-tuple-element.47.slot.slot_hbm) | copy-start | bytes 786436 | tf_op jit(solution)/shard_map/cond
  46.5 1.2 %copy-start.10 = (f32[512,768]{1,0:T(8,128)}, f32[512,768]{1,0:T(8,128)S(1)}, u32[]{:S(2)}) copy-start(f32[512,768]{1,0:T(8,128)S(1)} %get-tuple-element.58.rest_hbm) | copy-start | bytes 4718596 | tf_op jit(solution)/shard_map/cond
  47.7 15.1 %copy-start.4 = (f32[512,256]{1,0:T(8,128)}, f32[512,256]{1,0:T(8,128)S(1)}, u32[]{:S(2)}) copy-start(f32[512,256]{1,0:T(8,128)S(1)} %get-tuple-element.54.r_own.first_hbm) | copy-start | bytes 1572868 | tf_op jit(solution)/shard_map/cond
  47.7 15.1 %collective-permute-start.7 = (f32[512,256]{1,0:T(8,128)S(1)}, f32[512,256]{1,0:T(8,128)S(1)}, u32[]{:S(2)}, u32[]{:S(2)}) collective-permute-start(f32[512,256]{1,0:T(8,128)S(1)} %get-tuple-element.54.r_own.first_hbm), channel_id=1, source_target_pairs={{0,1},{1,0},{2,3},{3,2},{4,5},{5,4},{6,7},{7,6},{8,9},{9,8},{10,11... | collective-permute-start | bytes 1572872 | tf_op jit(solution)/shard_map/cond/branch_1_fun/ppermute | solution.py:329
  55.8 7.1 %copy-start.3 = (f32[512,256]{1,0:T(8,128)}, f32[512,256]{1,0:T(8,128)S(1)}, u32[]{:S(2)}) copy-start(f32[512,256]{1,0:T(8,128)S(1)} %branch_1_fun.6.w_own.w_first_hbm) | copy-start | bytes 1572868 | tf_op jit(solution)/shard_map/cond
  55.8 7.1 %collective-permute-start.6 = (f32[512,256]{1,0:T(8,128)S(1)}, f32[512,256]{1,0:T(8,128)S(1)}, u32[]{:S(2)}, u32[]{:S(2)}) collective-permute-start(f32[512,256]{1,0:T(8,128)S(1)} %branch_1_fun.6.w_own.w_first_hbm), channel_id=1, source_target_pairs={{0,1},{1,0},{2,3},{3,2},{4,5},{5,4},{6,7},{7,6},{8,9},{9,8},{10,11... | collective-permute-start | bytes 1572872 | tf_op jit(solution)/shard_map/cond/branch_1_fun/ppermute | solution.py:329
  58.3 4.6 %copy-start.19 = (f32[2,512,128]{2,1,0:T(8,128)S(1)}, f32[2,512,128]{2,1,0:T(8,128)}, u32[]{:S(2)}) copy-start(f32[2,512,128]{2,1,0:T(8,128)} %get-tuple-element.55.active) | copy-start | bytes 1572868 | tf_op jit(solution)/shard_map/cond
  58.3 42.3 %all-to-all-start.3 = ((f32[16,48,768]{2,1,0:T(8,128)}), f32[16,48,768]{2,1,0:T(8,128)}, u32[]{:S(2)}, u32[]{:S(2)}) async-start(f32[16,48,768]{2,1,0:T(8,128)} %bitcast.4), calls=%async_computation.3 | async-start | bytes 4718592 | tf_op jit(solution)/shard_map/cond/branch_1_fun/all_to_all | solution.py:391
  66.8 0.8 copy-start.11
  67.6 8.2 %collective-permute-start.8 = (f32[512,256]{1,0:T(8,128)S(1)}, f32[512,256]{1,0:T(8,128)S(1)}, u32[]{:S(2)}, u32[]{:S(2)}) collective-permute-start(f32[512,256]{1,0:T(8,128)S(1)} %get-tuple-element.56), channel_id=1, source_target_pairs={{0,2},{1,7},{8,10},{9,15},{16,18},{17,23},{24,26},{25,31},{32,34},... | collective-permute-start | bytes 1572872 | tf_op jit(solution)/shard_map/cond/branch_1_fun/ppermute | solution.py:402
  75.9 26.3 %copy-start.14 = (f32[512,256]{1,0:T(8,128)}, f32[512,256]{1,0:T(8,128)S(1)}, u32[]{:S(2)}) copy-start(f32[512,256]{1,0:T(8,128)S(1)} %broadcast_select_fusion.n_early) | copy-start | bytes 1572868 | tf_op jit(solution)/shard_map/cond
  75.9 7.4 %collective-permute-start.9 = (f32[512,256]{1,0:T(8,128)S(1)}, f32[512,256]{1,0:T(8,128)S(1)}, u32[]{:S(2)}, u32[]{:S(2)}) collective-permute-start(f32[512,256]{1,0:T(8,128)S(1)} %broadcast_select_fusion.n_early), channel_id=1, source_target_pairs={{1,3},{0,6},{2,4},{7,5},{9,11},{8,14},{10,12},{15,13},{17,19},{16,... | collective-permute-start | bytes 1572872 | tf_op jit(solution)/shard_map/cond/branch_1_fun/ppermute | solution.py:404
  77.3 23.4 %collective-permute-start.10 = (f32[512,256]{1,0:T(8,128)S(1)}, f32[512,256]{1,0:T(8,128)S(1)}, u32[]{:S(2)}, u32[]{:S(2)}) collective-permute-start(f32[512,256]{1,0:T(8,128)S(1)} %broadcast_select_fusion.n_early), channel_id=1, source_target_pairs={{0,1},{1,0},{2,3},{7,6},{8,9},{9,8},{10,11},{15,14},{16,17},{17,16... | collective-permute-start | bytes 1572872 | tf_op jit(solution)/shard_map/cond/branch_1_fun/ppermute | solution.py:405
  83.3 17.3 %copy-start.16 = (f32[512,256]{1,0:T(8,128)}, f32[512,256]{1,0:T(8,128)S(1)}, u32[]{:S(2)}) copy-start(f32[512,256]{1,0:T(8,128)S(1)} %collective-permute-done.9.n_late) | copy-start | bytes 1572868 | tf_op jit(solution)/shard_map/cond
  83.3 17.3 %collective-permute-start.11 = (f32[512,256]{1,0:T(8,128)S(1)}, f32[512,256]{1,0:T(8,128)S(1)}, u32[]{:S(2)}, u32[]{:S(2)}) collective-permute-start(f32[512,256]{1,0:T(8,128)S(1)} %collective-permute-done.9.n_late), channel_id=1, source_target_pairs={{3,2},{6,7},{4,5},{5,4},{11,10},{14,15},{12,13},{13,12},{19,18},{2... | collective-permute-start | bytes 1572872 | tf_op jit(solution)/shard_map/cond/branch_1_fun/ppermute | solution.py:406
  100.6 0.8 copy-start.17
  101.4 0.8 copy-start.18

commit v6 on v5

--- a/solution.py
+++ b/solution.py
@@ -55,7 +55,12 @@
     return jnp.sum(jnp.where(iota((rows, n), 0) == d, values, 0), axis=0, keepdims=True)
 
 
-def index_kernel(place, local_picks, level_picks, order, own_out, active_out, give_out, slot_out, fits_out):
+def turn(apart):
+    apart = apart & 3
+    return jnp.where(apart == 0, 0, jnp.where(apart == 1, 2, jnp.where(apart == 2, 3, 1)))
+
+
+def index_kernel(place, local_picks, level_picks, order, own_out, active_out, give_out, slot_out, xy_out, yx_out, fits_out):
     rows = active_out.shape[1]
     keep = give_out.shape[0]
     p = place[0]
@@ -85,6 +90,10 @@
     rank = jnp.sum(before.astype(jnp.int32), axis=0, keepdims=True)
     fits_out[0] = (jnp.max(rank) < keep).astype(jnp.int32)
     slot_out[...] = jnp.broadcast_to(d * keep + rank, (128, n)).T
+    across = turn(d - p)
+    down = turn((d >> 2) - (p >> 2))
+    xy_out[...] = jnp.broadcast_to((down * 4 + across) * keep + rank, (128, n)).T
+    yx_out[...] = jnp.broadcast_to((across * 4 + down) * keep + rank, (128, n)).T
     mine = (iota((keep, n), 0) == rank) & (d == p)
     give = jnp.sum(jnp.where(mine, r + 2, 0), axis=1, keepdims=True) - 2
     give_out[...] = jnp.broadcast_to(give, (keep, 128))
@@ -161,7 +170,7 @@
         out[u * keep : (u + 1) * keep, :] = pick(hot, front[:, u * B : (u + 1) * B])
 
 
-def lead_kernel(payload, front_rows, give, send_first, send_rest):
+def lead_kernel(payload, front_rows, give, send_first, send_xy, send_yx):
     (high, low), code = unpack(payload)
     keep = give.shape[0]
     chosen = give[:, 0:1] * 4
@@ -169,9 +178,10 @@
     sums = front_rows[...] + (dot(hot, high) + dot(hot, low))
     for i in range(send_first.shape[0] // keep):
         send_first[i * keep : (i + 1) * keep, :] = sums[:keep]
-    for i in range(send_rest.shape[0] // keep):
-        for u in range(1, 4):
-            send_rest[i * keep : (i + 1) * keep, (u - 1) * B : u * B] = sums[u * keep : (u + 1) * keep]
+    send_xy[:, :B] = sums[keep : 2 * keep]
+    send_xy[:, B:] = sums[2 * keep : 3 * keep, : B // 2]
+    send_yx[:, : B // 2] = sums[2 * keep : 3 * keep, B // 2 :]
+    send_yx[:, B // 2 :] = sums[3 * keep :]
 
 
 def tiles_kernel(payload, front, first_out, rest_out):
@@ -185,7 +195,15 @@
             rest_out[:, (u - 1) * B : u * B] = tile
 
 
-def sort_kernel(slot, gathered, out):
+def join_kernel(a0, a1, a2, a3, b0, b1, b2, b3, a_out, b_out, joined_out):
+    size = a0.shape[0]
+    for i, (a, b) in enumerate(((a0, b0), (a1, b1), (a2, b2), (a3, b3))):
+        a_out[i * size : (i + 1) * size, :] = a[...]
+        b_out[i * size : (i + 1) * size, :] = b[...]
+    joined_out[...] = jnp.zeros_like(joined_out)
+
+
+def sort_kernel(slot, gathered, joined, out):
     out[...] = pick(rows_hot(slot, gathered.shape[0]), gathered[...])
 
 
@@ -198,6 +216,16 @@
     x = by_row * (two - diag * by_col)
     xs = halves(x)
     return dot3(xs, halves(two - dot3(halves(diag), xs)))
+
+
+def sort_rest_kernel(xy, yx, a0, a1, a2, a3, b0, b1, b2, b3, high_out, low_out):
+    width = a0.shape[1]
+    for slot, parts, at in ((xy, (a0, a1, a2, a3), 0), (yx, (b0, b1, b2, b3), width)):
+        size = a0.shape[0]
+        hot = rows_hot(slot, 4 * size)
+        high, low = halves(jnp.concatenate([part[...] for part in parts], axis=0))
+        high_out[:, at : at + width] = dot(hot, high).astype(BF16)
+        low_out[:, at : at + width] = dot(hot, low).astype(BF16)
 
 
 def panel_kernel(place, w_own, w_other, r_own, r_other, active, half_out, tile_out):
@@ -238,8 +266,8 @@
 
 
 def finish_kernel(
-    place, slot_hbm, n_early, n_late, o_early, o_late, first_hbm, w_first_hbm, tile_hbm, rest_hbm, w_rest_hbm, out_hbm,
-    slot, n_own, n_other, first, w_first, tile, rest, w_rest, out, sems
+    place, n_early, n_late, o_early, o_late, first_hbm, w_first_hbm, tile_hbm, rest_hbm, high_hbm, low_hbm, out_hbm,
+    n_own, n_other, first, w_first, tile, rest, high, low, out, sems
 ):
     q = place[1]
     even = q % 2 == 0
@@ -264,12 +292,12 @@
         copy(o_late, n_other, sems.at[1]).start()
 
     moves = [
-        copy(slot_hbm, slot, sems.at[2]),
+        copy(w_first_hbm, w_first, sems.at[2]),
         copy(first_hbm, first, sems.at[3]),
-        copy(w_first_hbm, w_first, sems.at[4]),
-        copy(tile_hbm, tile, sems.at[5]),
-        copy(rest_hbm, rest, sems.at[6]),
-        copy(w_rest_hbm, w_rest, sems.at[7]),
+        copy(tile_hbm, tile, sems.at[4]),
+        copy(high_hbm, high, sems.at[5]),
+        copy(low_hbm, low, sems.at[6]),
+        copy(rest_hbm, rest, sems.at[7]),
     ]
     for move in moves:
         move.start()
@@ -277,29 +305,26 @@
     copy(o_early, n_other, sems.at[1]).wait()
     h0, l0 = halves(jnp.where(even, n_own[...], n_other[...]))
     h1, l1 = halves(jnp.where(even, n_other[...], n_own[...]))
-    for move in moves[1:4]:
-        move.wait()
     rows = first.shape[0]
     half = out.shape[1]
-    new = first[...] - (dot3((h0, l0), halves(w_first[:B])) + dot3((h1, l1), halves(w_first[B:])))
+    block = half // 2
+    for move in moves[:3]:
+        move.wait()
+    n_high = jnp.concatenate([h0, h1], axis=1)
+    n_low = jnp.concatenate([l0, l1], axis=1)
+    new = first[...] - dot3((n_high, n_low), halves(w_first[...]))
     new = jnp.where(q < 2, tile[...], new)
     for t in range(rows // half):
         out[t, :, 0, :] = new[t * half : (t + 1) * half]
-    moves[0].wait()
-    hot = rows_hot(slot, w_rest.shape[0])
-    high = (dot(h0, hot[:B]) + dot(h1, hot[B:])).astype(BF16)
-    low = (dot(l0, hot[:B]) + dot(l1, hot[B:])).astype(BF16)
-    for move in moves[4:]:
+    for move in moves[3:]:
         move.wait()
-    w = [halves(w_rest[:, u * B : (u + 1) * B]) for u in range(3)]
-    block = half // 2
     sent = []
     for i in range(rows // block):
         t, at = i * block // half, i * block % half
         span = slice(i * block, (i + 1) * block)
-        n = (high[span], low[span])
         for u in range(1, 4):
-            out[t, at : at + block, u, :] = rest[span, (u - 1) * B : u * B] - dot3(n, w[u - 1])
+            cols = slice((u - 1) * B, u * B)
+            out[t, at : at + block, u, :] = rest[span, cols] - dot3((n_high[span], n_low[span]), (high[:, cols], low[:, cols]))
         done = copy(out.at[t, at : at + block], out_hbm.at[t, at : at + block], sems.at[8 + i])
         done.start()
         sent.append(done)
@@ -327,6 +352,18 @@
 
 def core_swap(x):
     return lax.ppermute(x, "pcol", [(i, i ^ 1) for i in range(lax.axis_size("pcol"))])
+
+
+def shift_x(step):
+    return [(p, p // 4 * 4 + (p + step) % 4) for p in range(16)]
+
+
+def shift_y(step):
+    return [(p, (p + 4 * step) % 16) for p in range(16)]
+
+
+def ring(x, shift):
+    return [x] + [lax.ppermute(x, "prow", shift(step)) for step in (1, -1, 2)]
 
 
 def spread_z(x, z):
@@ -362,13 +399,16 @@
     )(place, partials[0], targets[0].T, counts).reshape(sources * 17, 1, 128)
     payload = lax.all_to_all(payload, ("prow", "pcol"), 0, 0, tiled=True).reshape(sources * 17, 128)
 
-    own, active, give, slot, fits = call(
+    lists = shaped(2 * B, 128, dtype=jnp.int32)
+    own, active, give, slot, xy, yx, fits = call(
         index_kernel,
         (
-            shaped(2 * B, 128, dtype=jnp.int32),
+            lists,
             shaped(2, rows, 128),
             shaped(KEEP, 128, dtype=jnp.int32),
-            shaped(2 * B, 128, dtype=jnp.int32),
+            lists,
+            lists,
+            lists,
             shaped(1, dtype=jnp.int32),
         ),
         4,
@@ -383,17 +423,35 @@
 
     front_rows = call(front_kernel, shaped(4 * KEEP, B), 2, scalars=0, flops=10**8, moved=3 * 10**6)(flat, give)
 
-    def gather(payload, flat, own, active, give, slot, place, front_rows):
-        send_first, send_rest = call(
-            lead_kernel, (shaped(copies, B), shaped(copies, cols - B)), 3, scalars=0, flops=10**8, moved=2 * 10**6
+    def gather(payload, flat, own, active, give, slot, xy, yx, place, front_rows):
+        wide = (cols - B) // 2
+        send_first, send_xy, send_yx = call(
+            lead_kernel,
+            (shaped(copies, B), shaped(KEEP, wide), shaped(KEEP, wide)),
+            3,
+            scalars=0,
+            flops=10**8,
+            moved=2 * 10**6,
         )(payload, front_rows, give)
         w_first = lax.all_to_all(send_first, "prow", 0, 0, tiled=True)
-        w_rest = lax.all_to_all(send_rest, "prow", 0, 0, tiled=True)
+        send_xy, send_yx, joined = call(
+            join_kernel, (shaped(4 * KEEP, wide), shaped(4 * KEEP, wide), shaped(8, 128)), 8, scalars=0, moved=2 * 10**6
+        )(*ring(send_xy, shift_x), *ring(send_yx, shift_y))
+        all_xy = ring(send_xy, shift_y)
+        all_yx = ring(send_yx, shift_x)
         first, rest = call(
             tiles_kernel, (shaped(rows, B), shaped(rows, cols - B)), 2, scalars=0, flops=4 * 10**9, moved=6 * 10**6
         )(payload, flat)
         r_other = core_swap(first)
-        w_first = call(sort_kernel, shaped(2 * B, B), 2, scalars=0, flops=10**8, moved=10**6)(slot, w_first)
+        w_first = call(sort_kernel, shaped(2 * B, B), 3, scalars=0, flops=10**8, moved=10**6)(slot, w_first, joined)
+        w_high, w_low = call(
+            sort_rest_kernel,
+            (shaped(2 * B, cols - B, dtype=BF16), shaped(2 * B, cols - B, dtype=BF16)),
+            10,
+            scalars=0,
+            flops=10**9,
+            moved=4 * 10**6,
+        )(xy, yx, *all_xy, *all_yx)
         w_other = core_swap(w_first)
         half, tile = call(
             panel_kernel, (shaped(rows, B), shaped(rows, B)), 6, flops=2 * 10**9, moved=4 * 10**6
@@ -410,22 +468,22 @@
             in_specs=[SM] + [HBM] * 10,
             out_specs=HBM,
             scratch_shapes=[
-                pltpu.VMEM((2 * B, 128), jnp.int32),
                 pltpu.VMEM((rows, B), F32),
                 pltpu.VMEM((rows, B), F32),
                 pltpu.VMEM((rows, B), F32),
                 pltpu.VMEM((2 * B, B), F32),
                 pltpu.VMEM((rows, B), F32),
                 pltpu.VMEM((rows, cols - B), F32),
-                pltpu.VMEM((copies, cols - B), F32),
+                pltpu.VMEM((2 * B, cols - B), BF16),
+                pltpu.VMEM((2 * B, cols - B), BF16),
                 pltpu.VMEM(front.shape, F32),
                 pltpu.SemaphoreType.DMA((12,)),
             ],
             cost_estimate=pl.CostEstimate(flops=4 * 10**9, bytes_accessed=8 * 10**6, transcendentals=0),
             **ALONE,
-        )(place, slot, n_early, n_late, o_early, o_late, first, w_first, tile, rest, w_rest)
-
-    def add_up(payload, flat, own, active, give, slot, place, front_rows):
+        )(place, n_early, n_late, o_early, o_late, first, w_first, tile, rest, w_high, w_low)
+
+    def add_up(payload, flat, own, active, give, slot, xy, yx, place, front_rows):
         matrix, pivots = call(
             assemble_kernel, (shaped(rows, cols), shaped(2 * B, cols)), 3, scalars=0, flops=4 * 10**9, moved=8 * 10**6
         )(payload, flat, own)
@@ -445,7 +503,7 @@
         )
         return out.reshape(front.shape)
 
-    return lax.cond(fits[0] == 1, gather, add_up, payload, flat, own, active, give, slot, place, front_rows)
+    return lax.cond(fits[0] == 1, gather, add_up, payload, flat, own, active, give, slot, xy, yx, place, front_rows)
 
 
 def solution(mesh):

time: 111 us -> 121 us (1.090)
  the two profiles are of different devices: /device:TPU:1 before, /device:TPU:65 now
where the time goes in v6:
time: 121 us
  waiting for transfers between devices  46.2 us (38%)
  starting transfers between devices  38.8 us (32%)
  Pallas kernels  26.1 us (22%)
  local copies, waits for them, and re-layouts  7.95 us (7%)
    ppermute x12, waiting for transfers between devices, ring(): return [x] + [lax.ppermute(x, 'prow', shift(step)) for step in (1, -1, 2)]  18.9 us
    ppermute x12, starting transfers between devices, ring(): return [x] + [lax.ppermute(x, 'prow', shift(step)) for step in (1, -1, 2)]  15.5 us
    ppermute x1, waiting for transfers between devices, gather(): n_late = lax.ppermute(n_early, 'pcol', [(1, 3), (0, 6), (2, 4), (7, 5)])  13.6 us
    all_to_all x1, waiting for transfers between devices, body(): lax.all_to_all(payload, ('prow', 'pcol'), 0, 0, tiled=True)  11.7 us
    all_to_all x1, starting transfers between devices, body(): lax.all_to_all(payload, ('prow', 'pcol'), 0, 0, tiled=True)  10.8 us
    cond x34, local copies, waits for them, and re-layouts  7.46 us
    pallas_call x1, Pallas kernels, gather(): pl.pallas_call(finish_kernel, out_shape=shaped(*front.shape), in_specs=[S...  6.09 us
    pallas_call x1, Pallas kernels, gather(): call(tiles_kernel, (shaped(rows, B), shaped(rows, cols - B)), 2, scalars=...  4.36 us
  transfers between devices with their start and end apart: 20, of which 7 were waited for; matrix products, arithmetic and copies ran while one was open for 0% of the time, Pallas kernels for 9%

profile of v6, /device:TPU:65, one launch (start us, length us, event | category | flops | bytes accessed | tf_op | source)
XLA Modules:
  0.0 120.6 jit_solution(1788261067925784680)
XLA Ops:
  0.0 0.1 pad_add_fusion.place
  0.1 2.8 %shard_map.76 = f32[2176,128]{1,0:T(8,128)} custom-call(s32[3]{0:T(128)S(1)} %pad_add_fusion.place, f32[128,8,256]{2,1,0:T(8,128)} %bitcast.28, s32[8,128]{1,0:T(8,128)} %bitcast.29, s32[1,128]{1,0:T(1,128)} %counts_hbm.1), custom_call_target="tpu_custom_call" | custom-call | flops 1000000 | bytes 2000000 | tf_op jit(solution)/shard_map/pallas_call | solution.py:386
  2.9 10.8 %all-to-all-start.3 = ((f32[2176,1,128]{2,1,0:T(1,128)}), f32[2176,1,128]{2,1,0:T(1,128)}, u32[]{:S(2)}, u32[]{:S(2)}) async-start(f32[2176,1,128]{2,1,0:T(1,128)} %bitcast.26), calls=%async_computation.3 | async-start | bytes 2228224 | tf_op jit(solution)/shard_map/all_to_all | solution.py:400
  13.7 0.0 copy-start.17
  13.7 3.2 %shard_map.75 = (s32[512,128]{1,0:T(8,128)S(1)}, f32[2,512,128]{2,1,0:T(8,128)}, s32[48,128]{1,0:T(8,128)S(1)}, s32[512,128]{1,0:T(8,128)}, s32[512,128]{1,0:T(8,128)}, /*index=5*/s32[512,128]{1,0:T(8,128)}, s32[1]{0:T(128)}) custom-call(s32[3]{0:T(128)S(1)} %pad_add_fusion.place, s32[2,16,256]{2,1,0:T(8,128)S(1)} %copy-done.10, ...), custom_call_target="tpu_custom_call" | custom-call | flops 1000000000 | bytes 1000000 | tf_op jit(solution)/shard_map/pallas_call | solution.py:403
  17.6 0.5 copy.11
  18.1 0.5 shard_map.77
  18.7 11.7 %all-to-all-done.3 = f32[2176,1,128]{2,1,0:T(1,128)} async-done(((f32[2176,1,128]{2,1,0:T(1,128)}), f32[2176,1,128]{2,1,0:T(1,128)}, u32[]{:S(2)}, u32[]{:S(2)}) %all-to-all-start.3) | async-done | bytes 1114144 | tf_op jit(solution)/shard_map/all_to_all | solution.py:400
  30.3 90.1 %conditional.1 = (f32[2,256,4,256]{3,2,1,0:T(4,128)}) conditional(s32[]{:T(128)} %bitcast.7, (f32[2176,128]{1,0:T(8,128)}, f32[512,1024]{1,0:T(8,128)S(1)}, s32[512,128]{1,0:T(8,128)S(1)}, s32[]{:T(128)}, s32[3]{0:T(128)S(1)}, /*index=5*/f32[2,512,128]{2,1,0:T(8,128)}) %tuple.19, (s32[]{:T(128)}, f32[2176,128]{1,0:T(8,128)}, ...), branch_computations={%region_0.2_spmd, %region_2.3_spmd} | conditional | flops 11200131072 | bytes 95617456 | solution.py:506
  30.3 1.3 %copy-done.16 = f32[512,1024]{1,0:T(8,128)} copy-done((f32[512,1024]{1,0:T(8,128)}, f32[512,1024]{1,0:T(8,128)S(1)}, u32[]{:S(2)}) %copy-start.16) | copy-done | bytes 2097176 | tf_op jit(solution)/shard_map/cond
  31.7 2.6 %branch_1_fun.7 = (f32[768,256]{1,0:T(8,128)}, f32[48,384]{1,0:T(8,128)S(1)}, f32[48,384]{1,0:T(8,128)S(1)}) custom-call(f32[2176,128]{1,0:T(8,128)} %get-tuple-element.53.payload, f32[192,256]{1,0:T(8,128)S(1)} %get-tuple-element.54.front_rows, s32[48,128]{1,0:T(8,128)S(1)} %get-tuple-element.55.give), custom_call_target="tpu_custom_call" | custom-call | flops 100000000 | bytes 2000000 | tf_op jit(solution)/shard_map/cond/branch_1_fun/pallas_call | solution.py:428
  34.2 3.7 %all-to-all-start.2 = ((f32[16,48,256]{2,1,0:T(8,128)}), f32[16,48,256]{2,1,0:T(8,128)S(1)}, u32[]{:S(2)}, u32[]{:S(2)}) async-start(f32[16,48,256]{2,1,0:T(8,128)} %bitcast.2), calls=%async_computation.2 | async-start | bytes 1572864 | tf_op jit(solution)/shard_map/cond/branch_1_fun/all_to_all | solution.py:436
  38.0 2.9 %collective-permute-start.8 = (f32[48,384]{1,0:T(8,128)S(1)}, f32[48,384]{1,0:T(8,128)S(1)}, u32[]{:S(2)}, u32[]{:S(2)}) collective-permute-start(f32[48,384]{1,0:T(8,128)S(1)} %get-tuple-element.57.a0), channel_id=1, source_target_pairs={{0,16},{8,24},{16,0},{24,8},{32,48},{40,56},{48,32},{56,40},{64,80... | collective-permute-start | bytes 221192 | tf_op jit(solution)/shard_map/cond/branch_1_fun/ppermute | solution.py:366
  40.9 0.9 collective-permute-start.7
  41.8 0.6 collective-permute-start.6
  42.3 2.7 %collective-permute-start.11 = (f32[48,384]{1,0:T(8,128)S(1)}, f32[48,384]{1,0:T(8,128)S(1)}, u32[]{:S(2)}, u32[]{:S(2)}) collective-permute-start(f32[48,384]{1,0:T(8,128)S(1)} %get-tuple-element.58.b0), channel_id=1, source_target_pairs={{0,64},{8,72},{16,80},{24,88},{32,96},{40,104},{48,112},{56,120},{... | collective-permute-start | bytes 221192 | tf_op jit(solution)/shard_map/cond/branch_1_fun/ppermute | solution.py:366
  45.0 0.9 collective-permute-start.10
  45.9 4.9 %collective-permute-done.8.a3 = f32[48,384]{1,0:T(8,128)S(1)} collective-permute-done((f32[48,384]{1,0:T(8,128)S(1)}, f32[48,384]{1,0:T(8,128)S(1)}, u32[]{:S(2)}, u32[]{:S(2)}) %collective-permute-start.8) | collective-permute-done | bytes 73760 | tf_op jit(solution)/shard_map/cond/branch_1_fun/ppermute | solution.py:366
  50.8 0.9 collective-permute-start.9
  51.7 4.4 %branch_1_fun.10 = (f32[512,256]{1,0:T(8,128)S(1)}, f32[512,768]{1,0:T(8,128)S(1)}) custom-call(f32[2176,128]{1,0:T(8,128)} %get-tuple-element.53.payload, f32[512,1024]{1,0:T(8,128)} %copy-done.16), custom_call_target="tpu_custom_call" | custom-call | flops 4000000000 | bytes 6000000 | tf_op jit(solution)/shard_map/cond/branch_1_fun/pallas_call | solution.py:442
  56.1 1.2 copy-done.14
  57.2 3.4 %collective-permute-start.13 = (f32[512,256]{1,0:T(8,128)S(1)}, f32[512,256]{1,0:T(8,128)S(1)}, u32[]{:S(2)}, u32[]{:S(2)}) collective-permute-start(f32[512,256]{1,0:T(8,128)S(1)} %get-tuple-element.61.r_own.first_hbm), channel_id=1, source_target_pairs={{0,1},{1,0},{2,3},{3,2},{4,5},{5,4},{6,7},{7,6},{8,9},{9,8},{10,11... | collective-permute-start | bytes 1572872 | tf_op jit(solution)/shard_map/cond/branch_1_fun/ppermute | solution.py:354
  60.8 0.7 copy-done.7
  61.5 0.7 branch_1_fun.9.w_own.w_first_hbm
  62.2 0.1 collective-permute-start.12
  62.3 1.9 %collective-permute-done.12.w_other = f32[512,256]{1,0:T(8,128)S(1)} collective-permute-done((f32[512,256]{1,0:T(8,128)S(1)}, f32[512,256]{1,0:T(8,128)S(1)}, u32[]{:S(2)}, u32[]{:S(2)}) %collective-permute-start.12) | collective-permute-done | bytes 524320 | tf_op jit(solution)/shard_map/cond/branch_1_fun/ppermute | solution.py:354
  64.2 3.9 %branch_1_fun.11 = (f32[512,256]{1,0:T(8,128)S(1)}, f32[512,256]{1,0:T(8,128)S(1)}) custom-call(s32[3]{0:T(128)S(1)} %get-tuple-element.50.place, f32[512,256]{1,0:T(8,128)S(1)} %branch_1_fun.9.w_own.w_first_hbm, f32[512,256]{1,0:T(8,128)S(1)} %collective-permute-done.12.w_other, f32[512,256]{1,0:T(8,128)S(1)} %get-tuple-element.61.r_own.first_hbm, ...), custom_call_target="tpu_custom_call" | custom-call | flops 2000000000 | bytes 4000000 | tf_op jit(solution)/shard_map/cond/branch_1_fun/pallas_call | solution.py:456
  68.2 0.8 copy-done.15
  69.0 0.7 collective-permute-start.14
  69.7 0.1 broadcast_select_fusion.n_early
  69.8 1.3 %collective-permute-start.15 = (f32[512,256]{1,0:T(8,128)S(1)}, f32[512,256]{1,0:T(8,128)S(1)}, u32[]{:S(2)}, u32[]{:S(2)}) collective-permute-start(f32[512,256]{1,0:T(8,128)S(1)} %broadcast_select_fusion.n_early), channel_id=1, source_target_pairs={{1,3},{0,6},{2,4},{7,5},{9,11},{8,14},{10,12},{15,13},{17,19},{16,... | collective-permute-start | bytes 1572872 | tf_op jit(solution)/shard_map/cond/branch_1_fun/ppermute | solution.py:462
  71.1 2.5 %collective-permute-start.20 = (f32[192,384]{1,0:T(8,128)S(1)}, f32[192,384]{1,0:T(8,128)S(1)}, u32[]{:S(2)}, u32[]{:S(2)}) collective-permute-start(f32[192,384]{1,0:T(8,128)S(1)} %get-tuple-element.68.a0), channel_id=1, source_target_pairs={{0,64},{8,72},{16,80},{24,88},{32,96},{40,104},{48,112},{56,120},{... | collective-permute-start | bytes 884744 | tf_op jit(solution)/shard_map/cond/branch_1_fun/ppermute | solution.py:366
  73.6 1.2 collective-permute-start.19
  74.7 0.3 collective-permute-start.18
  75.0 0.7 collective-permute-start.16
  75.7 13.6 %collective-permute-done.15.n_late = f32[512,256]{1,0:T(8,128)S(1)} collective-permute-done((f32[512,256]{1,0:T(8,128)S(1)}, f32[512,256]{1,0:T(8,128)S(1)}, u32[]{:S(2)}, u32[]{:S(2)}) %collective-permute-start.15) | collective-permute-done | bytes 524320 | tf_op jit(solution)/shard_map/cond/branch_1_fun/ppermute | solution.py:462
  89.4 2.6 %collective-permute-start.17 = (f32[512,256]{1,0:T(8,128)S(1)}, f32[512,256]{1,0:T(8,128)S(1)}, u32[]{:S(2)}, u32[]{:S(2)}) collective-permute-start(f32[512,256]{1,0:T(8,128)S(1)} %collective-permute-done.15.n_late), channel_id=1, source_target_pairs={{3,2},{6,7},{4,5},{5,4},{11,10},{14,15},{12,13},{13,12},{19,18},{2... | collective-permute-start | bytes 1572872 | tf_op jit(solution)/shard_map/cond/branch_1_fun/ppermute | solution.py:464
  92.0 0.3 collective-permute-start.23
  92.3 2.4 %collective-permute-start.22 = (f32[192,384]{1,0:T(8,128)S(1)}, f32[192,384]{1,0:T(8,128)S(1)}, u32[]{:S(2)}, u32[]{:S(2)}) collective-permute-start(f32[192,384]{1,0:T(8,128)S(1)} %copy-done.8), channel_id=1, source_target_pairs={{0,24},{8,0},{16,8},{24,16},{32,56},{40,32},{48,40},{56,48},{64,88... | collective-permute-start | bytes 884744 | tf_op jit(solution)/shard_map/cond/branch_1_fun/ppermute | solution.py:366
  94.7 7.5 %collective-permute-done.23.b3 = f32[192,384]{1,0:T(8,128)S(1)} collective-permute-done((f32[192,384]{1,0:T(8,128)S(1)}, f32[192,384]{1,0:T(8,128)S(1)}, u32[]{:S(2)}, u32[]{:S(2)}) %collective-permute-start.23) | collective-permute-done | bytes 294944 | tf_op jit(solution)/shard_map/cond/branch_1_fun/ppermute | solution.py:366
  102.2 4.7 %collective-permute-done.22.b2 = f32[192,384]{1,0:T(8,128)S(1)} collective-permute-done((f32[192,384]{1,0:T(8,128)S(1)}, f32[192,384]{1,0:T(8,128)S(1)}, u32[]{:S(2)}, u32[]{:S(2)}) %collective-permute-start.22) | collective-permute-done | bytes 294944 | tf_op jit(solution)/shard_map/cond/branch_1_fun/ppermute | solution.py:366
  106.9 1.9 %collective-permute-done.21.b1 = f32[192,384]{1,0:T(8,128)S(1)} collective-permute-done((f32[192,384]{1,0:T(8,128)S(1)}, f32[192,384]{1,0:T(8,128)S(1)}, u32[]{:S(2)}, u32[]{:S(2)}) %collective-permute-start.21) | collective-permute-done | bytes 294944 | tf_op jit(solution)/shard_map/cond/branch_1_fun/ppermute | solution.py:366
  108.8 1.8 %branch_1_fun.12 = (bf16[512,768]{1,0:T(8,128)(2,1)S(1)}, bf16[512,768]{1,0:T(8,128)(2,1)S(1)}) custom-call(s32[512,128]{1,0:T(8,128)S(1)} %copy-done.23, s32[512,128]{1,0:T(8,128)S(1)} %copy-done.24, f32[192,384]{1,0:T(8,128)S(1)} %get-tuple-element.68.a0, f32[192,384]{1,0:T(8,128)S(1)} %collective-permute-done.18.a1, ...), custom_call_target="tpu_custom_call" | custom-call | flops 1000000000 | bytes 4000000 | tf_op jit(solution)/shard_map/cond/branch_1_fun/pallas_call | solution.py:447
  110.7 0.9 copy-done.12
  111.5 0.9 copy-done.13
  112.5 0.8 copy-done.21
  113.2 0.8 copy-done.22
  114.1 6.1 %branch_1_fun.13 = f32[2,256,4,256]{3,2,1,0:T(4,128)} custom-call(s32[3]{0:T(128)S(1)} %get-tuple-element.50.place, f32[512,256]{1,0:T(8,128)} %copy-done.18, f32[512,256]{1,0:T(8,128)} %copy-done.20, f32[512,256]{1,0:T(8,128)} %copy-done.21, f32[512,256]{1,0:T(8,128)} %copy-done.22, f32[512,256]{1,0:T(8,128)} %copy-done.4, f32[512,256]{1,0:T(8,128)} %copy-done.3, ...), custom_call_target="tpu_custom_call" | custom-call | flops 4000000000 | bytes 8000000 | tf_op jit(solution)/shard_map/cond/branch_1_fun/pallas_call | solution.py:465
  (48 shorter events, 0.1 us)
Async XLA Ops:
  0.1 13.6 %copy-start.9 = (s32[2,4,16,256]{3,2,1,0:T(8,128)S(1)}, s32[2,4,16,256]{3,2,1,0:T(8,128)}, u32[]{:S(2)}) copy-start(s32[2,4,16,256]{3,2,1,0:T(8,128)} %level_picks.1) | copy-start | bytes 393220
  0.1 13.6 %copy-start.10 = (s32[2,16,256]{2,1,0:T(8,128)S(1)}, s32[2,16,256]{2,1,0:T(8,128)}, u32[]{:S(2)}) copy-start(s32[2,16,256]{2,1,0:T(8,128)} %local_picks.1) | copy-start | bytes 98308
  0.1 13.6 %copy-start.11 = (s32[2,256]{1,0:T(2,128)S(1)}, s32[2,256]{1,0:T(2,128)}, u32[]{:S(2)}) copy-start(s32[2,256]{1,0:T(2,128)} %order.1) | copy-start | bytes 6148
  2.9 27.4 %all-to-all-start.3 = ((f32[2176,1,128]{2,1,0:T(1,128)}), f32[2176,1,128]{2,1,0:T(1,128)}, u32[]{:S(2)}, u32[]{:S(2)}) async-start(f32[2176,1,128]{2,1,0:T(1,128)} %bitcast.26), calls=%async_computation.3 | async-start | bytes 2228224 | tf_op jit(solution)/shard_map/all_to_all | solution.py:400
  13.7 3.9 %copy-start.17 = (f32[2,256,4,256]{3,2,1,0:T(4,128)S(1)}, f32[2,256,4,256]{3,2,1,0:T(4,128)}, u32[]{:S(2)}) copy-start(f32[2,256,4,256]{3,2,1,0:T(4,128)} %param.9) | copy-start | bytes 6291460
  30.3 1.3 %copy-start.16 = (f32[512,1024]{1,0:T(8,128)}, f32[512,1024]{1,0:T(8,128)S(1)}, u32[]{:S(2)}) copy-start(f32[512,1024]{1,0:T(8,128)S(1)} %get-tuple-element.60.front) | copy-start | bytes 6291460 | tf_op jit(solution)/shard_map/cond
  34.2 27.2 %all-to-all-start.2 = ((f32[16,48,256]{2,1,0:T(8,128)}), f32[16,48,256]{2,1,0:T(8,128)S(1)}, u32[]{:S(2)}, u32[]{:S(2)}) async-start(f32[16,48,256]{2,1,0:T(8,128)} %bitcast.2), calls=%async_computation.2 | async-start | bytes 1572864 | tf_op jit(solution)/shard_map/cond/branch_1_fun/all_to_all | solution.py:436
  38.0 12.8 %collective-permute-start.8 = (f32[48,384]{1,0:T(8,128)S(1)}, f32[48,384]{1,0:T(8,128)S(1)}, u32[]{:S(2)}, u32[]{:S(2)}) collective-permute-start(f32[48,384]{1,0:T(8,128)S(1)} %get-tuple-element.57.a0), channel_id=1, source_target_pairs={{0,16},{8,24},{16,0},{24,8},{32,48},{40,56},{48,32},{56,40},{64,80... | collective-permute-start | bytes 221192 | tf_op jit(solution)/shard_map/cond/branch_1_fun/ppermute | solution.py:366
  40.9 16.4 %collective-permute-start.7 = (f32[48,384]{1,0:T(8,128)S(1)}, f32[48,384]{1,0:T(8,128)S(1)}, u32[]{:S(2)}, u32[]{:S(2)}) collective-permute-start(f32[48,384]{1,0:T(8,128)S(1)} %get-tuple-element.57.a0), channel_id=1, source_target_pairs={{0,24},{8,0},{16,8},{24,16},{32,56},{40,32},{48,40},{56,48},{64,88... | collective-permute-start | bytes 221192 | tf_op jit(solution)/shard_map/cond/branch_1_fun/ppermute | solution.py:366
  41.8 18.9 %collective-permute-start.6 = (f32[48,384]{1,0:T(8,128)S(1)}, f32[48,384]{1,0:T(8,128)S(1)}, u32[]{:S(2)}, u32[]{:S(2)}) collective-permute-start(f32[48,384]{1,0:T(8,128)S(1)} %get-tuple-element.57.a0), channel_id=1, source_target_pairs={{0,8},{8,16},{16,24},{24,0},{32,40},{40,48},{48,56},{56,32},{64,72... | collective-permute-start | bytes 221192 | tf_op jit(solution)/shard_map/cond/branch_1_fun/ppermute | solution.py:366
  42.3 18.4 %collective-permute-start.11 = (f32[48,384]{1,0:T(8,128)S(1)}, f32[48,384]{1,0:T(8,128)S(1)}, u32[]{:S(2)}, u32[]{:S(2)}) collective-permute-start(f32[48,384]{1,0:T(8,128)S(1)} %get-tuple-element.58.b0), channel_id=1, source_target_pairs={{0,64},{8,72},{16,80},{24,88},{32,96},{40,104},{48,112},{56,120},{... | collective-permute-start | bytes 221192 | tf_op jit(solution)/shard_map/cond/branch_1_fun/ppermute | solution.py:366
  45.0 15.7 %collective-permute-start.10 = (f32[48,384]{1,0:T(8,128)S(1)}, f32[48,384]{1,0:T(8,128)S(1)}, u32[]{:S(2)}, u32[]{:S(2)}) collective-permute-start(f32[48,384]{1,0:T(8,128)S(1)} %get-tuple-element.58.b0), channel_id=1, source_target_pairs={{0,96},{8,104},{16,112},{24,120},{32,0},{40,8},{48,16},{56,24},{64... | collective-permute-start | bytes 221192 | tf_op jit(solution)/shard_map/cond/branch_1_fun/ppermute | solution.py:366
  50.8 9.9 %collective-permute-start.9 = (f32[48,384]{1,0:T(8,128)S(1)}, f32[48,384]{1,0:T(8,128)S(1)}, u32[]{:S(2)}, u32[]{:S(2)}) collective-permute-start(f32[48,384]{1,0:T(8,128)S(1)} %get-tuple-element.58.b0), channel_id=1, source_target_pairs={{0,32},{8,40},{16,48},{24,56},{32,64},{40,72},{48,80},{56,88},{64,... | collective-permute-start | bytes 221192 | tf_op jit(solution)/shard_map/cond/branch_1_fun/ppermute | solution.py:366
  51.7 9.8 %copy-start.19 = (s32[512,128]{1,0:T(8,128)S(1)}, s32[512,128]{1,0:T(8,128)}, u32[]{:S(2)}) copy-start(s32[512,128]{1,0:T(8,128)} %get-tuple-element.52.slot) | copy-start | bytes 786436 | tf_op jit(solution)/shard_map/cond
  56.0 1.2 copy-start.14
  57.2 10.9 %copy-start.4 = (f32[512,256]{1,0:T(8,128)}, f32[512,256]{1,0:T(8,128)S(1)}, u32[]{:S(2)}) copy-start(f32[512,256]{1,0:T(8,128)S(1)} %get-tuple-element.61.r_own.first_hbm) | copy-start | bytes 1572868 | tf_op jit(solution)/shard_map/cond
  57.2 7.0 %copy-start.25 = (f32[2,512,128]{2,1,0:T(8,128)S(1)}, f32[2,512,128]{2,1,0:T(8,128)}, u32[]{:S(2)}) copy-start(f32[2,512,128]{2,1,0:T(8,128)} %get-tuple-element.62.active) | copy-start | bytes 1572868 | tf_op jit(solution)/shard_map/cond
  57.2 5.1 %collective-permute-start.13 = (f32[512,256]{1,0:T(8,128)S(1)}, f32[512,256]{1,0:T(8,128)S(1)}, u32[]{:S(2)}, u32[]{:S(2)}) collective-permute-start(f32[512,256]{1,0:T(8,128)S(1)} %get-tuple-element.61.r_own.first_hbm), channel_id=1, source_target_pairs={{0,1},{1,0},{2,3},{3,2},{4,5},{5,4},{6,7},{7,6},{8,9},{9,8},{10,11... | collective-permute-start | bytes 1572872 | tf_op jit(solution)/shard_map/cond/branch_1_fun/ppermute | solution.py:354
  60.8 0.7 copy-start.7
  62.2 5.9 %copy-start.3 = (f32[512,256]{1,0:T(8,128)}, f32[512,256]{1,0:T(8,128)S(1)}, u32[]{:S(2)}) copy-start(f32[512,256]{1,0:T(8,128)S(1)} %branch_1_fun.9.w_own.w_first_hbm) | copy-start | bytes 1572868 | tf_op jit(solution)/shard_map/cond
  62.2 2.0 %collective-permute-start.12 = (f32[512,256]{1,0:T(8,128)S(1)}, f32[512,256]{1,0:T(8,128)S(1)}, u32[]{:S(2)}, u32[]{:S(2)}) collective-permute-start(f32[512,256]{1,0:T(8,128)S(1)} %branch_1_fun.9.w_own.w_first_hbm), channel_id=1, source_target_pairs={{0,1},{1,0},{2,3},{3,2},{4,5},{5,4},{6,7},{7,6},{8,9},{9,8},{10,11... | collective-permute-start | bytes 1572872 | tf_op jit(solution)/shard_map/cond/branch_1_fun/ppermute | solution.py:354
  64.2 27.7 %copy-start.8 = (f32[192,384]{1,0:T(8,128)S(1)}, f32[192,384]{1,0:T(8,128)}, u32[]{:S(2)}) copy-start(f32[192,384]{1,0:T(8,128)} %copy-done.7) | copy-start | bytes 884740 | tf_op jit(solution)/shard_map/cond
  64.2 44.6 %copy-start.23 = (s32[512,128]{1,0:T(8,128)S(1)}, s32[512,128]{1,0:T(8,128)}, u32[]{:S(2)}) copy-start(s32[512,128]{1,0:T(8,128)} %get-tuple-element.66.xy) | copy-start | bytes 786436 | tf_op jit(solution)/shard_map/cond
  64.2 44.6 %copy-start.24 = (s32[512,128]{1,0:T(8,128)S(1)}, s32[512,128]{1,0:T(8,128)}, u32[]{:S(2)}) copy-start(s32[512,128]{1,0:T(8,128)} %get-tuple-element.67.yx) | copy-start | bytes 786436 | tf_op jit(solution)/shard_map/cond
  68.2 0.8 copy-start.15
  69.0 0.7 collective-permute-start.14
  69.8 44.3 %copy-start.18 = (f32[512,256]{1,0:T(8,128)}, f32[512,256]{1,0:T(8,128)S(1)}, u32[]{:S(2)}) copy-start(f32[512,256]{1,0:T(8,128)S(1)} %broadcast_select_fusion.n_early) | copy-start | bytes 1572868 | tf_op jit(solution)/shard_map/cond
  69.8 19.6 %collective-permute-start.15 = (f32[512,256]{1,0:T(8,128)S(1)}, f32[512,256]{1,0:T(8,128)S(1)}, u32[]{:S(2)}, u32[]{:S(2)}) collective-permute-start(f32[512,256]{1,0:T(8,128)S(1)} %broadcast_select_fusion.n_early), channel_id=1, source_target_pairs={{1,3},{0,6},{2,4},{7,5},{9,11},{8,14},{10,12},{15,13},{17,19},{16,... | collective-permute-start | bytes 1572872 | tf_op jit(solution)/shard_map/cond/branch_1_fun/ppermute | solution.py:462
  71.1 20.9 %collective-permute-start.20 = (f32[192,384]{1,0:T(8,128)S(1)}, f32[192,384]{1,0:T(8,128)S(1)}, u32[]{:S(2)}, u32[]{:S(2)}) collective-permute-start(f32[192,384]{1,0:T(8,128)S(1)} %get-tuple-element.68.a0), channel_id=1, source_target_pairs={{0,64},{8,72},{16,80},{24,88},{32,96},{40,104},{48,112},{56,120},{... | collective-permute-start | bytes 884744 | tf_op jit(solution)/shard_map/cond/branch_1_fun/ppermute | solution.py:366
  73.6 18.7 %collective-permute-start.19 = (f32[192,384]{1,0:T(8,128)S(1)}, f32[192,384]{1,0:T(8,128)S(1)}, u32[]{:S(2)}, u32[]{:S(2)}) collective-permute-start(f32[192,384]{1,0:T(8,128)S(1)} %get-tuple-element.68.a0), channel_id=1, source_target_pairs={{0,96},{8,104},{16,112},{24,120},{32,0},{40,8},{48,16},{56,24},{64... | collective-permute-start | bytes 884744 | tf_op jit(solution)/shard_map/cond/branch_1_fun/ppermute | solution.py:366
  74.7 20.0 %collective-permute-start.18 = (f32[192,384]{1,0:T(8,128)S(1)}, f32[192,384]{1,0:T(8,128)S(1)}, u32[]{:S(2)}, u32[]{:S(2)}) collective-permute-start(f32[192,384]{1,0:T(8,128)S(1)} %get-tuple-element.68.a0), channel_id=1, source_target_pairs={{0,32},{8,40},{16,48},{24,56},{32,64},{40,72},{48,80},{56,88},{64,... | collective-permute-start | bytes 884744 | tf_op jit(solution)/shard_map/cond/branch_1_fun/ppermute | solution.py:366
  75.0 37.4 %collective-permute-start.16 = (f32[512,256]{1,0:T(8,128)S(1)}, f32[512,256]{1,0:T(8,128)S(1)}, u32[]{:S(2)}, u32[]{:S(2)}) collective-permute-start(f32[512,256]{1,0:T(8,128)S(1)} %broadcast_select_fusion.n_early), channel_id=1, source_target_pairs={{0,1},{1,0},{2,3},{7,6},{8,9},{9,8},{10,11},{15,14},{16,17},{17,16... | collective-permute-start | bytes 1572872 | tf_op jit(solution)/shard_map/cond/branch_1_fun/ppermute | solution.py:463
  89.4 23.1 %copy-start.20 = (f32[512,256]{1,0:T(8,128)}, f32[512,256]{1,0:T(8,128)S(1)}, u32[]{:S(2)}) copy-start(f32[512,256]{1,0:T(8,128)S(1)} %collective-permute-done.15.n_late) | copy-start | bytes 1572868 | tf_op jit(solution)/shard_map/cond
  89.4 23.1 %collective-permute-start.17 = (f32[512,256]{1,0:T(8,128)S(1)}, f32[512,256]{1,0:T(8,128)S(1)}, u32[]{:S(2)}, u32[]{:S(2)}) collective-permute-start(f32[512,256]{1,0:T(8,128)S(1)} %collective-permute-done.15.n_late), channel_id=1, source_target_pairs={{3,2},{6,7},{4,5},{5,4},{11,10},{14,15},{12,13},{13,12},{19,18},{2... | collective-permute-start | bytes 1572872 | tf_op jit(solution)/shard_map/cond/branch_1_fun/ppermute | solution.py:464
  92.0 10.3 %collective-permute-start.23 = (f32[192,384]{1,0:T(8,128)S(1)}, f32[192,384]{1,0:T(8,128)S(1)}, u32[]{:S(2)}, u32[]{:S(2)}) collective-permute-start(f32[192,384]{1,0:T(8,128)S(1)} %copy-done.8), channel_id=1, source_target_pairs={{0,16},{8,24},{16,0},{24,8},{32,48},{40,56},{48,32},{56,40},{64,80... | collective-permute-start | bytes 884744 | tf_op jit(solution)/shard_map/cond/branch_1_fun/ppermute | solution.py:366
  92.3 14.6 %collective-permute-start.22 = (f32[192,384]{1,0:T(8,128)S(1)}, f32[192,384]{1,0:T(8,128)S(1)}, u32[]{:S(2)}, u32[]{:S(2)}) collective-permute-start(f32[192,384]{1,0:T(8,128)S(1)} %copy-done.8), channel_id=1, source_target_pairs={{0,24},{8,0},{16,8},{24,16},{32,56},{40,32},{48,40},{56,48},{64,88... | collective-permute-start | bytes 884744 | tf_op jit(solution)/shard_map/cond/branch_1_fun/ppermute | solution.py:366
  94.7 14.1 %collective-permute-start.21 = (f32[192,384]{1,0:T(8,128)S(1)}, f32[192,384]{1,0:T(8,128)S(1)}, u32[]{:S(2)}, u32[]{:S(2)}) collective-permute-start(f32[192,384]{1,0:T(8,128)S(1)} %copy-done.8), channel_id=1, source_target_pairs={{0,8},{8,16},{16,24},{24,0},{32,40},{40,48},{48,56},{56,32},{64,72... | collective-permute-start | bytes 884744 | tf_op jit(solution)/shard_map/cond/branch_1_fun/ppermute | solution.py:366
  110.7 0.9 copy-start.12
  111.5 0.9 copy-start.13
  112.5 0.8 copy-start.21
  113.2 0.8 copy-start.22

commit v7 on v6

--- a/solution.py
+++ b/solution.py
@@ -170,18 +170,16 @@
         out[u * keep : (u + 1) * keep, :] = pick(hot, front[:, u * B : (u + 1) * B])
 
 
-def lead_kernel(payload, front_rows, give, send_first, send_xy, send_yx):
+def lead_kernel(payload, front_rows, give, send_first, send_rest):
     (high, low), code = unpack(payload)
     keep = give.shape[0]
     chosen = give[:, 0:1] * 4
     hot = jnp.concatenate([(chosen + u == code).astype(F32) for u in range(4)], axis=0).astype(BF16)
     sums = front_rows[...] + (dot(hot, high) + dot(hot, low))
-    for i in range(send_first.shape[0] // keep):
-        send_first[i * keep : (i + 1) * keep, :] = sums[:keep]
-    send_xy[:, :B] = sums[keep : 2 * keep]
-    send_xy[:, B:] = sums[2 * keep : 3 * keep, : B // 2]
-    send_yx[:, : B // 2] = sums[2 * keep : 3 * keep, B // 2 :]
-    send_yx[:, B // 2 :] = sums[3 * keep :]
+    send_first[...] = sums[:keep]
+    for i in range(send_rest.shape[0] // keep):
+        for u in range(1, 4):
+            send_rest[i * keep : (i + 1) * keep, (u - 1) * B : u * B] = sums[u * keep : (u + 1) * keep]
 
 
 def tiles_kernel(payload, front, first_out, rest_out):
@@ -195,16 +193,22 @@
             rest_out[:, (u - 1) * B : u * B] = tile
 
 
-def join_kernel(a0, a1, a2, a3, b0, b1, b2, b3, a_out, b_out, joined_out):
+def join_kernel(a0, a1, a2, a3, out):
     size = a0.shape[0]
-    for i, (a, b) in enumerate(((a0, b0), (a1, b1), (a2, b2), (a3, b3))):
-        a_out[i * size : (i + 1) * size, :] = a[...]
-        b_out[i * size : (i + 1) * size, :] = b[...]
-    joined_out[...] = jnp.zeros_like(joined_out)
-
-
-def sort_kernel(slot, gathered, joined, out):
-    out[...] = pick(rows_hot(slot, gathered.shape[0]), gathered[...])
+    for i, a in enumerate((a0, a1, a2, a3)):
+        out[i * size : (i + 1) * size, :] = a[...]
+
+
+def sort_first_kernel(slot, a0, a1, a2, a3, out):
+    hot = rows_hot(slot, 4 * a0.shape[0])
+    out[...] = pick(hot, jnp.concatenate([part[...] for part in (a0, a1, a2, a3)], axis=0))
+
+
+def sort_rest_kernel(slot, gathered, high_out, low_out):
+    hot = rows_hot(slot, gathered.shape[0])
+    high, low = halves(gathered[...])
+    high_out[...] = dot(hot, high).astype(BF16)
+    low_out[...] = dot(hot, low).astype(BF16)
 
 
 def inverse_of(diag):
@@ -216,16 +220,6 @@
     x = by_row * (two - diag * by_col)
     xs = halves(x)
     return dot3(xs, halves(two - dot3(halves(diag), xs)))
-
-
-def sort_rest_kernel(xy, yx, a0, a1, a2, a3, b0, b1, b2, b3, high_out, low_out):
-    width = a0.shape[1]
-    for slot, parts, at in ((xy, (a0, a1, a2, a3), 0), (yx, (b0, b1, b2, b3), width)):
-        size = a0.shape[0]
-        hot = rows_hot(slot, 4 * size)
-        high, low = halves(jnp.concatenate([part[...] for part in parts], axis=0))
-        high_out[:, at : at + width] = dot(hot, high).astype(BF16)
-        low_out[:, at : at + width] = dot(hot, low).astype(BF16)
 
 
 def panel_kernel(place, w_own, w_other, r_own, r_other, active, half_out, tile_out):
@@ -423,35 +417,19 @@
 
     front_rows = call(front_kernel, shaped(4 * KEEP, B), 2, scalars=0, flops=10**8, moved=3 * 10**6)(flat, give)
 
-    def gather(payload, flat, own, active, give, slot, xy, yx, place, front_rows):
-        wide = (cols - B) // 2
-        send_first, send_xy, send_yx = call(
-            lead_kernel,
-            (shaped(copies, B), shaped(KEEP, wide), shaped(KEEP, wide)),
-            3,
-            scalars=0,
-            flops=10**8,
-            moved=2 * 10**6,
-        )(payload, front_rows, give)
-        w_first = lax.all_to_all(send_first, "prow", 0, 0, tiled=True)
-        send_xy, send_yx, joined = call(
-            join_kernel, (shaped(4 * KEEP, wide), shaped(4 * KEEP, wide), shaped(8, 128)), 8, scalars=0, moved=2 * 10**6
-        )(*ring(send_xy, shift_x), *ring(send_yx, shift_y))
-        all_xy = ring(send_xy, shift_y)
-        all_yx = ring(send_yx, shift_x)
+    send_first, send_rest = call(
+        lead_kernel, (shaped(KEEP, B), shaped(copies, cols - B)), 3, scalars=0, flops=10**8, moved=2 * 10**6
+    )(payload, front_rows, give)
+    w_rest = lax.all_to_all(send_rest, "prow", 0, 0, tiled=True)
+
+    def panels(payload, flat, send_first, xy, active, place):
+        joined = call(join_kernel, shaped(4 * KEEP, B), 4, scalars=0, moved=10**6)(*ring(send_first, shift_x))
+        w_parts = ring(joined, shift_y)
         first, rest = call(
             tiles_kernel, (shaped(rows, B), shaped(rows, cols - B)), 2, scalars=0, flops=4 * 10**9, moved=6 * 10**6
         )(payload, flat)
         r_other = core_swap(first)
-        w_first = call(sort_kernel, shaped(2 * B, B), 3, scalars=0, flops=10**8, moved=10**6)(slot, w_first, joined)
-        w_high, w_low = call(
-            sort_rest_kernel,
-            (shaped(2 * B, cols - B, dtype=BF16), shaped(2 * B, cols - B, dtype=BF16)),
-            10,
-            scalars=0,
-            flops=10**9,
-            moved=4 * 10**6,
-        )(xy, yx, *all_xy, *all_yx)
+        w_first = call(sort_first_kernel, shaped(2 * B, B), 5, scalars=0, flops=10**8, moved=10**6)(xy, *w_parts)
         w_other = core_swap(w_first)
         half, tile = call(
             panel_kernel, (shaped(rows, B), shaped(rows, B)), 6, flops=2 * 10**9, moved=4 * 10**6
@@ -459,9 +437,28 @@
         q = place[1]
         step = lax.ppermute(half, "pcol", [(0, 2), (1, 7)])
         n_early = jnp.where((q == 2) | (q == 7), step, half)
-        n_late = lax.ppermute(n_early, "pcol", [(1, 3), (0, 6), (2, 4), (7, 5)])
-        o_early = lax.ppermute(n_early, "pcol", [(0, 1), (1, 0), (2, 3), (7, 6)])
-        o_late = lax.ppermute(n_late, "pcol", [(3, 2), (6, 7), (4, 5), (5, 4)])
+        return n_early, first, w_first, tile, rest
+
+    def nothing(payload, flat, send_first, xy, active, place):
+        square = jnp.zeros((rows, B), F32)
+        return square, square, jnp.zeros((2 * B, B), F32), square, jnp.zeros((rows, cols - B), F32)
+
+    n_early, first, w_first, tile, rest = lax.cond(
+        fits[0] == 1, panels, nothing, payload, flat, send_first, xy, active, place
+    )
+    n_late = lax.ppermute(n_early, "pcol", [(1, 3), (0, 6), (2, 4), (7, 5)])
+    o_early = lax.ppermute(n_early, "pcol", [(0, 1), (1, 0), (2, 3), (7, 6)])
+    o_late = lax.ppermute(n_late, "pcol", [(3, 2), (6, 7), (4, 5), (5, 4)])
+    w_high, w_low = call(
+        sort_rest_kernel,
+        (shaped(2 * B, cols - B, dtype=BF16), shaped(2 * B, cols - B, dtype=BF16)),
+        2,
+        scalars=0,
+        flops=10**9,
+        moved=4 * 10**6,
+    )(slot, w_rest)
+
+    def finish(payload, flat, own, active, place, *arrays):
         return pl.pallas_call(
             finish_kernel,
             out_shape=shaped(*front.shape),
@@ -481,9 +478,9 @@
             ],
             cost_estimate=pl.CostEstimate(flops=4 * 10**9, bytes_accessed=8 * 10**6, transcendentals=0),
             **ALONE,
-        )(place, n_early, n_late, o_early, o_late, first, w_first, tile, rest, w_high, w_low)
-
-    def add_up(payload, flat, own, active, give, slot, xy, yx, place, front_rows):
+        )(place, *arrays)
+
+    def add_up(payload, flat, own, active, place, *arrays):
         matrix, pivots = call(
             assemble_kernel, (shaped(rows, cols), shaped(2 * B, cols)), 3, scalars=0, flops=4 * 10**9, moved=8 * 10**6
         )(payload, flat, own)
@@ -503,7 +500,26 @@
         )
         return out.reshape(front.shape)
 
-    return lax.cond(fits[0] == 1, gather, add_up, payload, flat, own, active, give, slot, xy, yx, place, front_rows)
+    return lax.cond(
+        fits[0] == 1,
+        finish,
+        add_up,
+        payload,
+        flat,
+        own,
+        active,
+        place,
+        n_early,
+        n_late,
+        o_early,
+        o_late,
+        first,
+        w_first,
+        tile,
+        rest,
+        w_high,
+        w_low,
+    )
 
 
 def solution(mesh):

time: 121 us -> 126 us (1.041)
  waiting for transfers between devices: 46.2 us -> 59 us
  starting transfers between devices: 38.8 us -> 33.3 us
  local copies, waits for them, and re-layouts: 7.95 us -> 3.24 us
  Pallas kernels: 26.1 us -> 27.6 us
    ppermute x12 -> x6, waiting for transfers between devices: 18.9 us -> 28.8 us  [ring(): return [x] + [lax.ppermute(x, 'prow', shift(step)) for step in (1, -1, 2)]]
    cond x34 -> x2, local copies, waits for them, and re-layouts: 7.46 us -> 0.01 us
    ppermute x12 -> x6, starting transfers between devices: 15.5 us -> 8.73 us  [ring(): return [x] + [lax.ppermute(x, 'prow', shift(step)) for step in (1, -1, 2)]]
    ppermute x4, waiting for transfers between devices: 13.7 us -> 17.1 us  [the longest x1 17.1 us: body(): n_late = lax.ppermute(n_early, 'pcol', [(1, 3), (0, 6), (2, 4), (7, 5)])]
    unnamed x9 -> x21, local copies, waits for them, and re-layouts: 0.49 us -> 3.23 us
    pallas_call x7, Pallas kernels: 19.6 us -> 21 us  [the longest x1 5.98 us: finish(): pl.pallas_call(finish_kernel, out_shape=shaped(*front.shape), in_specs=[S...]
    ppermute x4, starting transfers between devices: 5.23 us -> 6.66 us  [the longest x1 2.05 us: body(): o_late = lax.ppermute(n_late, 'pcol', [(3, 2), (6, 7), (4, 5), (5, 4)])]
  transfers between devices with their start and end apart: 20 -> 14, of which waited for: 7 -> 4; matrix products, arithmetic and copies ran while one was open for 0% -> 1% of each run, Pallas kernels for 9% -> 14%
where the time goes in v7:
time: 126 us; the launch traced here: 125 us
  waiting for transfers between devices  59 us (47%)
  starting transfers between devices  33.3 us (26%)
  Pallas kernels  27.6 us (22%)
  local copies, waits for them, and re-layouts  3.24 us (3%)
    ppermute x6, waiting for transfers between devices, ring(): return [x] + [lax.ppermute(x, 'prow', shift(step)) for step in (1, -1, 2)]  28.8 us
    ppermute x1, waiting for transfers between devices, body(): n_late = lax.ppermute(n_early, 'pcol', [(1, 3), (0, 6), (2, 4), (7, 5)])  17.1 us
    all_to_all x1, waiting for transfers between devices, body(): lax.all_to_all(payload, ('prow', 'pcol'), 0, 0, tiled=True)  11.4 us
    all_to_all x1, starting transfers between devices, body(): lax.all_to_all(payload, ('prow', 'pcol'), 0, 0, tiled=True)  10.4 us
    ppermute x6, starting transfers between devices, ring(): return [x] + [lax.ppermute(x, 'prow', shift(step)) for step in (1, -1, 2)]  8.73 us
    pallas_call x1, Pallas kernels, finish(): pl.pallas_call(finish_kernel, out_shape=shaped(*front.shape), in_specs=[S...  5.98 us
    pallas_call x1, Pallas kernels, panels(): call(tiles_kernel, (shaped(rows, B), shaped(rows, cols - B)), 2, scalars=...  5.52 us
    pallas_call x1, Pallas kernels, panels(): call(panel_kernel, (shaped(rows, B), shaped(rows, B)), 6, flops=2 * 10 **...  5.01 us
  transfers between devices with their start and end apart: 14, of which 4 were waited for; matrix products, arithmetic and copies ran while one was open for 1% of the time, Pallas kernels for 14%

profile of v7, /device:TPU:65, one launch (start us, length us, event | category | flops | bytes accessed | tf_op | source)
XLA Modules:
  0.0 125.1 jit_solution(7968060412219059415)
XLA Ops:
  0.0 0.1 pad_add_fusion.place
  0.1 2.9 %shard_map.76 = f32[2176,128]{1,0:T(8,128)} custom-call(s32[3]{0:T(128)S(1)} %pad_add_fusion.place, f32[128,8,256]{2,1,0:T(8,128)} %bitcast.32, s32[8,128]{1,0:T(8,128)} %bitcast.33, s32[1,128]{1,0:T(1,128)} %counts_hbm.1), custom_call_target="tpu_custom_call" | custom-call | flops 1000000 | bytes 2000000 | tf_op jit(solution)/shard_map/pallas_call | solution.py:380
  2.9 10.4 %all-to-all-start.2 = ((f32[2176,1,128]{2,1,0:T(1,128)}), f32[2176,1,128]{2,1,0:T(1,128)S(1)}, u32[]{:S(2)}, u32[]{:S(2)}) async-start(f32[2176,1,128]{2,1,0:T(1,128)} %bitcast.30), calls=%async_computation.2 | async-start | bytes 2228224 | tf_op jit(solution)/shard_map/all_to_all | solution.py:394
  13.3 0.0 copy-start.13
  13.3 3.1 %shard_map.75 = (s32[512,128]{1,0:T(8,128)}, f32[2,512,128]{2,1,0:T(8,128)}, s32[48,128]{1,0:T(8,128)S(1)}, s32[512,128]{1,0:T(8,128)S(1)}, s32[512,128]{1,0:T(8...) custom-call(s32[3]{0:T(128)S(1)} %pad_add_fusion.place, s32[2,16,256]{2,1,0:T(8,128)S(1)} %copy-done.7, ...), custom_call_target="tpu_custom_call" | custom-call | flops 1000000000 | bytes 1000000 | tf_op jit(solution)/shard_map/pallas_call | solution.py:397
  16.5 0.5 copy.11
  17.0 0.0 copy-start.9
  17.0 1.3 %copy-done.9 = f32[64,8,4,256]{3,1,2,0:T(8,128)} copy-done((f32[64,8,4,256]{3,1,2,0:T(8,128)}, f32[64,8,4,256]{3,1,2,0:T(8,128)S(1)}, u32[]{:S(2)}) %copy-start.9) | copy-done | bytes 2097176
  18.3 0.6 shard_map.77.front_rows
  18.9 11.4 %all-to-all-done.2 = f32[2176,1,128]{2,1,0:T(1,128)S(1)} async-done(((f32[2176,1,128]{2,1,0:T(1,128)}), f32[2176,1,128]{2,1,0:T(1,128)S(1)}, u32[]{:S(2)}, u32[]{:S(2)}) %all-to-all-start.2) | async-done | bytes 1114144 | tf_op jit(solution)/shard_map/all_to_all | solution.py:394
  30.3 0.6 shard_map.78
  30.9 1.4 %copy-done.3 = f32[768,768]{1,0:T(8,128)} copy-done((f32[768,768]{1,0:T(8,128)}, f32[768,768]{1,0:T(8,128)S(1)}, u32[]{:S(2)}) %copy-start.3) | copy-done | bytes 2359320
  32.3 0.0 copy-done.11
  32.3 3.7 %all-to-all-start.3 = ((f32[16,48,768]{2,1,0:T(8,128)}), f32[16,48,768]{2,1,0:T(8,128)S(1)}, u32[]{:S(2)}, u32[]{:S(2)}) async-start(f32[16,48,768]{2,1,0:T(8,128)} %bitcast.22), calls=%async_computation.3 | async-start | bytes 4718592 | tf_op jit(solution)/shard_map/all_to_all | solution.py:423
  36.7 57.5 %conditional.2 = (f32[512,256]{1,0:T(8,128)}, f32[512,256]{1,0:T(8,128)}, f32[512,256]{1,0:T(8,128)}, f32[512,256]{1,0:T(8,128)}, f32[512,768]{1,0:T(8,128)}) conditional(s32[]{:T(128)} %bitcast.5, () %tuple.22, (s32[]{:T(128)}, f32[48,256]{1,0:T(8,128)S(1)}, s32[512,128]{1,0:T(8,128)S(1)}, f32[2176,128]{1,0:T(8,128)}, f32[512,1024]{1,0:T(8,128)}, ...), branch_computations={%region_0.0_spmd, %region_1.2_spmd} | conditional | flops 6100130816 | bytes 24911040 | solution.py:446
  36.8 3.0 %collective-permute-start.2 = (f32[48,256]{1,0:T(8,128)S(1)}, f32[48,256]{1,0:T(8,128)S(1)}, u32[]{:S(2)}, u32[]{:S(2)}) collective-permute-start(f32[48,256]{1,0:T(8,128)S(1)} %get-tuple-element.59.a0), channel_id=1, source_target_pairs={{0,16},{8,24},{16,0},{24,8},{32,48},{40,56},{48,32},{56,40},{64,80... | collective-permute-start | bytes 147464 | tf_op jit(solution)/shard_map/cond/branch_1_fun/ppermute | solution.py:360
  39.7 0.9 collective-permute-start.1
  40.6 0.6 collective-permute-start
  41.2 28.8 %collective-permute-done.2.a3 = f32[48,256]{1,0:T(8,128)S(1)} collective-permute-done((f32[48,256]{1,0:T(8,128)S(1)}, f32[48,256]{1,0:T(8,128)S(1)}, u32[]{:S(2)}, u32[]{:S(2)}) %collective-permute-start.2) | collective-permute-done | bytes 49184 | tf_op jit(solution)/shard_map/cond/branch_1_fun/ppermute | solution.py:360
  70.0 0.0 collective-permute-done.1.a2
  70.0 0.0 collective-permute-done.a1
  70.0 2.8 %collective-permute-start.5 = (f32[192,256]{1,0:T(8,128)S(1)}, f32[192,256]{1,0:T(8,128)S(1)}, u32[]{:S(2)}, u32[]{:S(2)}) collective-permute-start(f32[192,256]{1,0:T(8,128)S(1)} %branch_1_fun.5.a0), channel_id=1, source_target_pairs={{0,64},{8,72},{16,80},{24,88},{32,96},{40,104},{48,112},{56,120},{... | collective-permute-start | bytes 589832 | tf_op jit(solution)/shard_map/cond/branch_1_fun/ppermute | solution.py:360
  72.9 0.1 collective-permute-start.4
  73.0 1.3 %collective-permute-start.3 = (f32[192,256]{1,0:T(8,128)S(1)}, f32[192,256]{1,0:T(8,128)S(1)}, u32[]{:S(2)}, u32[]{:S(2)}) collective-permute-start(f32[192,256]{1,0:T(8,128)S(1)} %branch_1_fun.5.a0), channel_id=1, source_target_pairs={{0,32},{8,40},{16,48},{24,56},{32,64},{40,72},{48,80},{56,88},{64,... | collective-permute-start | bytes 589832 | tf_op jit(solution)/shard_map/cond/branch_1_fun/ppermute | solution.py:360
  74.3 5.5 %branch_1_fun.7 = (f32[512,256]{1,0:T(8,128)}, f32[512,768]{1,0:T(8,128)}) custom-call(f32[2176,128]{1,0:T(8,128)} %get-tuple-element.60.payload, f32[512,1024]{1,0:T(8,128)} %get-tuple-element.61.front), custom_call_target="tpu_custom_call" | custom-call | flops 4000000000 | bytes 6000000 | tf_op jit(solution)/shard_map/cond/branch_1_fun/pallas_call | solution.py:428
  79.9 3.3 %collective-permute-start.7 = (f32[512,256]{1,0:T(8,128)}, f32[512,256]{1,0:T(8,128)S(1)}, u32[]{:S(2)}, u32[]{:S(2)}) collective-permute-start(f32[512,256]{1,0:T(8,128)} %get-tuple-element.129.r_own), channel_id=1, source_target_pairs={{0,1},{1,0},{2,3},{3,2},{4,5},{5,4},{6,7},{7,6},{8,9},{9,8},{10,11... | collective-permute-start | bytes 1572872 | tf_op jit(solution)/shard_map/cond/branch_1_fun/ppermute | solution.py:348
  83.2 0.0 collective-permute-done.5.a3
  83.2 0.0 collective-permute-done.4.a2
  83.2 0.0 collective-permute-done.3.a1
  83.2 1.5 %branch_1_fun.6.w_own = f32[512,256]{1,0:T(8,128)} custom-call(s32[512,128]{1,0:T(8,128)S(1)} %get-tuple-element.58.slot, f32[192,256]{1,0:T(8,128)S(1)} %branch_1_fun.5.a0, f32[192,256]{1,0:T(8,128)S(1)} %collective-permute-done.3.a1, f32[192,256]{1,0:T(8,128)S(1)} %collective-permute-done.4.a2, f32[192,256]{1,0:T(8,128)S(1)} %collective-permute-done.5.a3), custom_call_target="tpu_custom_call" | custom-call | flops 100000000 | bytes 1000000 | tf_op jit(solution)/shard_map/cond/branch_1_fun/pallas_call | solution.py:432
  84.7 0.4 collective-permute-start.6
  85.1 0.0 collective-permute-done.7.r_other
  85.1 1.7 %collective-permute-done.6.w_other = f32[512,256]{1,0:T(8,128)S(1)} collective-permute-done((f32[512,256]{1,0:T(8,128)}, f32[512,256]{1,0:T(8,128)S(1)}, u32[]{:S(2)}, u32[]{:S(2)}) %collective-permute-start.6) | collective-permute-done | bytes 524320 | tf_op jit(solution)/shard_map/cond/branch_1_fun/ppermute | solution.py:348
  86.9 5.0 %branch_1_fun.8 = (f32[512,256]{1,0:T(8,128)S(1)}, f32[512,256]{1,0:T(8,128)}) custom-call(s32[3]{0:T(128)S(1)} %get-tuple-element.57.place, f32[512,256]{1,0:T(8,128)} %branch_1_fun.6.w_own, f32[512,256]{1,0:T(8,128)S(1)} %collective-permute-done.6.w_other, f32[512,256]{1,0:T(8,128)} %get-tuple-element.129.r_own, ...), custom_call_target="tpu_custom_call" | custom-call | flops 2000000000 | bytes 4000000 | tf_op jit(solution)/shard_map/cond/branch_1_fun/pallas_call | solution.py:434
  91.9 1.5 %collective-permute-start.8 = (f32[512,256]{1,0:T(8,128)S(1)}, f32[512,256]{1,0:T(8,128)}, u32[]{:S(2)}, u32[]{:S(2)}) collective-permute-start(f32[512,256]{1,0:T(8,128)S(1)} %get-tuple-element.64), channel_id=1, source_target_pairs={{0,2},{1,7},{8,10},{9,15},{16,18},{17,23},{24,26},{25,31},{32,34},... | collective-permute-start | bytes 1572872 | tf_op jit(solution)/shard_map/cond/branch_1_fun/ppermute | solution.py:438
  93.4 0.0 collective-permute-done.8
  93.4 0.9 broadcast_select_fusion
  94.3 1.4 %collective-permute-start.15 = (f32[512,256]{1,0:T(8,128)}, f32[512,256]{1,0:T(8,128)S(1)}, u32[]{:S(2)}, u32[]{:S(2)}) collective-permute-start(f32[512,256]{1,0:T(8,128)} %get-tuple-element.113), channel_id=1, source_target_pairs={{1,3},{0,6},{2,4},{7,5},{9,11},{8,14},{10,12},{15,13},{17,19},{16,... | collective-permute-start | bytes 1572872 | tf_op jit(solution)/shard_map/ppermute | solution.py:449
  95.7 1.7 %collective-permute-start.16 = (f32[512,256]{1,0:T(8,128)}, f32[512,256]{1,0:T(8,128)}, u32[]{:S(2)}, u32[]{:S(2)}) collective-permute-start(f32[512,256]{1,0:T(8,128)} %get-tuple-element.113), channel_id=1, source_target_pairs={{0,1},{1,0},{2,3},{7,6},{8,9},{9,8},{10,11},{15,14},{16,17},{17,16... | collective-permute-start | bytes 1572872 | tf_op jit(solution)/shard_map/ppermute | solution.py:450
  97.4 17.1 %collective-permute-done.15 = f32[512,256]{1,0:T(8,128)S(1)} collective-permute-done((f32[512,256]{1,0:T(8,128)}, f32[512,256]{1,0:T(8,128)S(1)}, u32[]{:S(2)}, u32[]{:S(2)}) %collective-permute-start.15) | collective-permute-done | bytes 524320 | tf_op jit(solution)/shard_map/ppermute | solution.py:449
  114.4 2.1 %collective-permute-start.17 = (f32[512,256]{1,0:T(8,128)S(1)}, f32[512,256]{1,0:T(8,128)}, u32[]{:S(2)}, u32[]{:S(2)}) collective-permute-start(f32[512,256]{1,0:T(8,128)S(1)} %collective-permute-done.15), channel_id=1, source_target_pairs={{3,2},{6,7},{4,5},{5,4},{11,10},{14,15},{12,13},{13,12},{19,18},{2... | collective-permute-start | bytes 1572872 | tf_op jit(solution)/shard_map/ppermute | solution.py:451
  116.5 0.0 all-to-all-done.3
  116.5 0.0 copy-start.10
  116.5 2.4 %shard_map.79 = (bf16[512,768]{1,0:T(8,128)(2,1)}, bf16[512,768]{1,0:T(8,128)(2,1)}) custom-call(s32[512,128]{1,0:T(8,128)S(1)} %get-tuple-element.118.slot, f32[768,768]{1,0:T(8,128)S(1)} %bitcast.21), custom_call_target="tpu_custom_call" | custom-call | flops 1000000000 | bytes 4000000 | tf_op jit(solution)/shard_map/pallas_call | solution.py:452
  118.9 0.0 collective-permute-done.16
  118.9 0.0 collective-permute-done.17
  119.0 6.0 %conditional.3 = (f32[2,256,4,256]{3,2,1,0:T(4,128)}) conditional(s32[]{:T(128)} %bitcast.5, (f32[2176,128]{1,0:T(8,128)S(1)}, f32[512,1024]{1,0:T(8,128)S(1)}, s32[512,128]{1,0:T(8,128)S(1)}, s32[]{:T(128)}, s32[3]{0:T(128)S(1)}, /*index=5*/f32[2,512,128]{2,1,0:T(8,128)}) %tuple.35, (s32[3]{0:T(128)S(1)}, f32[512,256]{1,0:T(8,128)}, ...), branch_computations={%region_2.4_spmd, %region_4.5_spmd} | conditional | flops 8000884736 | bytes 85798736 | solution.py:503
  119.0 6.0 %branch_1_fun.9 = f32[2,256,4,256]{3,2,1,0:T(4,128)} custom-call(s32[3]{0:T(128)S(1)} %get-tuple-element.77.place, f32[512,256]{1,0:T(8,128)} %get-tuple-element.78.n_early, f32[512,256]{1,0:T(8,128)S(1)} %get-tuple-element.79.n_late, f32[512,256]{1,0:T(8,128)} %get-tuple-element.80.o_early, f32[512,256]{1,0:T(8,128)} %get-tuple-element.81.o_late, ...), custom_call_target="tpu_custom_call" | custom-call | flops 4000000000 | bytes 8000000 | tf_op jit(solution)/shard_map/cond/branch_1_fun/pallas_call | solution.py:462
  (17 shorter events, 0.0 us)
Async XLA Ops:
  0.1 13.2 %copy-start.6 = (s32[2,4,16,256]{3,2,1,0:T(8,128)S(1)}, s32[2,4,16,256]{3,2,1,0:T(8,128)}, u32[]{:S(2)}) copy-start(s32[2,4,16,256]{3,2,1,0:T(8,128)} %level_picks.1) | copy-start | bytes 393220
  0.1 13.2 %copy-start.7 = (s32[2,16,256]{2,1,0:T(8,128)S(1)}, s32[2,16,256]{2,1,0:T(8,128)}, u32[]{:S(2)}) copy-start(s32[2,16,256]{2,1,0:T(8,128)} %local_picks.1) | copy-start | bytes 98308
  0.1 13.2 %copy-start.8 = (s32[2,256]{1,0:T(2,128)S(1)}, s32[2,256]{1,0:T(2,128)}, u32[]{:S(2)}) copy-start(s32[2,256]{1,0:T(2,128)} %order.1) | copy-start | bytes 6148
  2.9 27.3 %all-to-all-start.2 = ((f32[2176,1,128]{2,1,0:T(1,128)}), f32[2176,1,128]{2,1,0:T(1,128)S(1)}, u32[]{:S(2)}, u32[]{:S(2)}) async-start(f32[2176,1,128]{2,1,0:T(1,128)} %bitcast.30), calls=%async_computation.2 | async-start | bytes 2228224 | tf_op jit(solution)/shard_map/all_to_all | solution.py:394
  13.3 3.2 %copy-start.13 = (f32[2,256,4,256]{3,2,1,0:T(4,128)S(1)}, f32[2,256,4,256]{3,2,1,0:T(4,128)}, u32[]{:S(2)}) copy-start(f32[2,256,4,256]{3,2,1,0:T(4,128)} %param.11) | copy-start | bytes 6291460
  17.0 1.3 %copy-start.9 = (f32[64,8,4,256]{3,1,2,0:T(8,128)}, f32[64,8,4,256]{3,1,2,0:T(8,128)S(1)}, u32[]{:S(2)}) copy-start(f32[64,8,4,256]{3,1,2,0:T(8,128)S(1)} %copy.11) | copy-start | bytes 6291460
  30.2 2.1 %copy-start.11 = (f32[2176,1,128]{2,1,0:T(1,128)}, f32[2176,1,128]{2,1,0:T(1,128)S(1)}, u32[]{:S(2)}) copy-start(f32[2176,1,128]{2,1,0:T(1,128)S(1)} %all-to-all-done.2) | copy-start | bytes 3342340
  30.9 1.4 %copy-start.3 = (f32[768,768]{1,0:T(8,128)}, f32[768,768]{1,0:T(8,128)S(1)}, u32[]{:S(2)}) copy-start(f32[768,768]{1,0:T(8,128)S(1)} %get-tuple-element.119) | copy-start | bytes 7077892
  32.3 84.2 %all-to-all-start.3 = ((f32[16,48,768]{2,1,0:T(8,128)}), f32[16,48,768]{2,1,0:T(8,128)S(1)}, u32[]{:S(2)}, u32[]{:S(2)}) async-start(f32[16,48,768]{2,1,0:T(8,128)} %bitcast.22), calls=%async_computation.3 | async-start | bytes 4718592 | tf_op jit(solution)/shard_map/all_to_all | solution.py:423
  36.8 33.2 %collective-permute-start.2 = (f32[48,256]{1,0:T(8,128)S(1)}, f32[48,256]{1,0:T(8,128)S(1)}, u32[]{:S(2)}, u32[]{:S(2)}) collective-permute-start(f32[48,256]{1,0:T(8,128)S(1)} %get-tuple-element.59.a0), channel_id=1, source_target_pairs={{0,16},{8,24},{16,0},{24,8},{32,48},{40,56},{48,32},{56,40},{64,80... | collective-permute-start | bytes 147464 | tf_op jit(solution)/shard_map/cond/branch_1_fun/ppermute | solution.py:360
  39.7 30.3 %collective-permute-start.1 = (f32[48,256]{1,0:T(8,128)S(1)}, f32[48,256]{1,0:T(8,128)S(1)}, u32[]{:S(2)}, u32[]{:S(2)}) collective-permute-start(f32[48,256]{1,0:T(8,128)S(1)} %get-tuple-element.59.a0), channel_id=1, source_target_pairs={{0,24},{8,0},{16,8},{24,16},{32,56},{40,32},{48,40},{56,48},{64,88... | collective-permute-start | bytes 147464 | tf_op jit(solution)/shard_map/cond/branch_1_fun/ppermute | solution.py:360
  40.6 29.4 %collective-permute-start = (f32[48,256]{1,0:T(8,128)S(1)}, f32[48,256]{1,0:T(8,128)S(1)}, u32[]{:S(2)}, u32[]{:S(2)}) collective-permute-start(f32[48,256]{1,0:T(8,128)S(1)} %get-tuple-element.59.a0), channel_id=1, source_target_pairs={{0,8},{8,16},{16,24},{24,0},{32,40},{40,48},{48,56},{56,32},{64,72... | collective-permute-start | bytes 147464 | tf_op jit(solution)/shard_map/cond/branch_1_fun/ppermute | solution.py:360
  70.0 13.2 %collective-permute-start.5 = (f32[192,256]{1,0:T(8,128)S(1)}, f32[192,256]{1,0:T(8,128)S(1)}, u32[]{:S(2)}, u32[]{:S(2)}) collective-permute-start(f32[192,256]{1,0:T(8,128)S(1)} %branch_1_fun.5.a0), channel_id=1, source_target_pairs={{0,64},{8,72},{16,80},{24,88},{32,96},{40,104},{48,112},{56,120},{... | collective-permute-start | bytes 589832 | tf_op jit(solution)/shard_map/cond/branch_1_fun/ppermute | solution.py:360
  72.9 10.3 %collective-permute-start.4 = (f32[192,256]{1,0:T(8,128)S(1)}, f32[192,256]{1,0:T(8,128)S(1)}, u32[]{:S(2)}, u32[]{:S(2)}) collective-permute-start(f32[192,256]{1,0:T(8,128)S(1)} %branch_1_fun.5.a0), channel_id=1, source_target_pairs={{0,96},{8,104},{16,112},{24,120},{32,0},{40,8},{48,16},{56,24},{64... | collective-permute-start | bytes 589832 | tf_op jit(solution)/shard_map/cond/branch_1_fun/ppermute | solution.py:360
  73.0 10.2 %collective-permute-start.3 = (f32[192,256]{1,0:T(8,128)S(1)}, f32[192,256]{1,0:T(8,128)S(1)}, u32[]{:S(2)}, u32[]{:S(2)}) collective-permute-start(f32[192,256]{1,0:T(8,128)S(1)} %branch_1_fun.5.a0), channel_id=1, source_target_pairs={{0,32},{8,40},{16,48},{24,56},{32,64},{40,72},{48,80},{56,88},{64,... | collective-permute-start | bytes 589832 | tf_op jit(solution)/shard_map/cond/branch_1_fun/ppermute | solution.py:360
  74.3 12.5 %copy-start.14 = (f32[2,512,128]{2,1,0:T(8,128)S(1)}, f32[2,512,128]{2,1,0:T(8,128)}, u32[]{:S(2)}) copy-start(f32[2,512,128]{2,1,0:T(8,128)} %get-tuple-element.63.active) | copy-start | bytes 1572868 | tf_op jit(solution)/shard_map/cond
  79.9 5.3 %collective-permute-start.7 = (f32[512,256]{1,0:T(8,128)}, f32[512,256]{1,0:T(8,128)S(1)}, u32[]{:S(2)}, u32[]{:S(2)}) collective-permute-start(f32[512,256]{1,0:T(8,128)} %get-tuple-element.129.r_own), channel_id=1, source_target_pairs={{0,1},{1,0},{2,3},{3,2},{4,5},{5,4},{6,7},{7,6},{8,9},{9,8},{10,11... | collective-permute-start | bytes 1572872 | tf_op jit(solution)/shard_map/cond/branch_1_fun/ppermute | solution.py:348
  84.7 2.2 %collective-permute-start.6 = (f32[512,256]{1,0:T(8,128)}, f32[512,256]{1,0:T(8,128)S(1)}, u32[]{:S(2)}, u32[]{:S(2)}) collective-permute-start(f32[512,256]{1,0:T(8,128)} %branch_1_fun.6.w_own), channel_id=1, source_target_pairs={{0,1},{1,0},{2,3},{3,2},{4,5},{5,4},{6,7},{7,6},{8,9},{9,8},{10,11... | collective-permute-start | bytes 1572872 | tf_op jit(solution)/shard_map/cond/branch_1_fun/ppermute | solution.py:348
  91.9 1.5 %collective-permute-start.8 = (f32[512,256]{1,0:T(8,128)S(1)}, f32[512,256]{1,0:T(8,128)}, u32[]{:S(2)}, u32[]{:S(2)}) collective-permute-start(f32[512,256]{1,0:T(8,128)S(1)} %get-tuple-element.64), channel_id=1, source_target_pairs={{0,2},{1,7},{8,10},{9,15},{16,18},{17,23},{24,26},{25,31},{32,34},... | collective-permute-start | bytes 1572872 | tf_op jit(solution)/shard_map/cond/branch_1_fun/ppermute | solution.py:438
  94.3 24.7 %copy-start.15 = (s32[512,128]{1,0:T(8,128)S(1)}, s32[512,128]{1,0:T(8,128)}, u32[]{:S(2)}) copy-start(s32[512,128]{1,0:T(8,128)} %get-tuple-element.108) | copy-start | bytes 786436
  94.3 20.2 %collective-permute-start.15 = (f32[512,256]{1,0:T(8,128)}, f32[512,256]{1,0:T(8,128)S(1)}, u32[]{:S(2)}, u32[]{:S(2)}) collective-permute-start(f32[512,256]{1,0:T(8,128)} %get-tuple-element.113), channel_id=1, source_target_pairs={{1,3},{0,6},{2,4},{7,5},{9,11},{8,14},{10,12},{15,13},{17,19},{16,... | collective-permute-start | bytes 1572872 | tf_op jit(solution)/shard_map/ppermute | solution.py:449
  95.7 23.2 %collective-permute-start.16 = (f32[512,256]{1,0:T(8,128)}, f32[512,256]{1,0:T(8,128)}, u32[]{:S(2)}, u32[]{:S(2)}) collective-permute-start(f32[512,256]{1,0:T(8,128)} %get-tuple-element.113), channel_id=1, source_target_pairs={{0,1},{1,0},{2,3},{7,6},{8,9},{9,8},{10,11},{15,14},{16,17},{17,16... | collective-permute-start | bytes 1572872 | tf_op jit(solution)/shard_map/ppermute | solution.py:450
  114.4 4.5 %collective-permute-start.17 = (f32[512,256]{1,0:T(8,128)S(1)}, f32[512,256]{1,0:T(8,128)}, u32[]{:S(2)}, u32[]{:S(2)}) collective-permute-start(f32[512,256]{1,0:T(8,128)S(1)} %collective-permute-done.15), channel_id=1, source_target_pairs={{3,2},{6,7},{4,5},{5,4},{11,10},{14,15},{12,13},{13,12},{19,18},{2... | collective-permute-start | bytes 1572872 | tf_op jit(solution)/shard_map/ppermute | solution.py:451
  116.5 2.4 %copy-start.10 = (f32[64,8,4,256]{3,1,2,0:T(8,128)S(1)}, f32[64,8,4,256]{3,1,2,0:T(8,128)}, u32[]{:S(2)}) copy-start(f32[64,8,4,256]{3,1,2,0:T(8,128)} %copy-done.9) | copy-start | bytes 6291460
  116.5 2.4 %copy-start.12 = (f32[2176,1,128]{2,1,0:T(1,128)S(1)}, f32[2176,1,128]{2,1,0:T(1,128)}, u32[]{:S(2)}) copy-start(f32[2176,1,128]{2,1,0:T(1,128)} %copy-done.11) | copy-start | bytes 3342340

commit v8 on v7

--- a/solution.py
+++ b/solution.py
@@ -60,7 +60,7 @@
     return jnp.where(apart == 0, 0, jnp.where(apart == 1, 2, jnp.where(apart == 2, 3, 1)))
 
 
-def index_kernel(place, local_picks, level_picks, order, own_out, active_out, give_out, slot_out, xy_out, yx_out, fits_out):
+def index_kernel(place, local_picks, level_picks, order, own_out, active_out, give_out, slot_out, xy_out, fits_out):
     rows = active_out.shape[1]
     keep = give_out.shape[0]
     p = place[0]
@@ -93,7 +93,6 @@
     across = turn(d - p)
     down = turn((d >> 2) - (p >> 2))
     xy_out[...] = jnp.broadcast_to((down * 4 + across) * keep + rank, (128, n)).T
-    yx_out[...] = jnp.broadcast_to((across * 4 + down) * keep + rank, (128, n)).T
     mine = (iota((keep, n), 0) == rank) & (d == p)
     give = jnp.sum(jnp.where(mine, r + 2, 0), axis=1, keepdims=True) - 2
     give_out[...] = jnp.broadcast_to(give, (keep, 128))
@@ -176,10 +175,10 @@
     chosen = give[:, 0:1] * 4
     hot = jnp.concatenate([(chosen + u == code).astype(F32) for u in range(4)], axis=0).astype(BF16)
     sums = front_rows[...] + (dot(hot, high) + dot(hot, low))
-    send_first[...] = sums[:keep]
-    for i in range(send_rest.shape[0] // keep):
-        for u in range(1, 4):
-            send_rest[i * keep : (i + 1) * keep, (u - 1) * B : u * B] = sums[u * keep : (u + 1) * keep]
+    for i in range(send_first.shape[0] // keep):
+        send_first[i * keep : (i + 1) * keep, :] = sums[:keep]
+    for u in range(1, 4):
+        send_rest[:, (u - 1) * B : u * B] = sums[u * keep : (u + 1) * keep]
 
 
 def tiles_kernel(payload, front, first_out, rest_out):
@@ -199,16 +198,8 @@
         out[i * size : (i + 1) * size, :] = a[...]
 
 
-def sort_first_kernel(slot, a0, a1, a2, a3, out):
-    hot = rows_hot(slot, 4 * a0.shape[0])
-    out[...] = pick(hot, jnp.concatenate([part[...] for part in (a0, a1, a2, a3)], axis=0))
-
-
-def sort_rest_kernel(slot, gathered, high_out, low_out):
-    hot = rows_hot(slot, gathered.shape[0])
-    high, low = halves(gathered[...])
-    high_out[...] = dot(hot, high).astype(BF16)
-    low_out[...] = dot(hot, low).astype(BF16)
+def sort_first_kernel(slot, gathered, out):
+    out[...] = pick(rows_hot(slot, gathered.shape[0]), gathered[...])
 
 
 def inverse_of(diag):
@@ -260,8 +251,8 @@
 
 
 def finish_kernel(
-    place, n_early, n_late, o_early, o_late, first_hbm, w_first_hbm, tile_hbm, rest_hbm, high_hbm, low_hbm, out_hbm,
-    n_own, n_other, first, w_first, tile, rest, high, low, out, sems
+    place, n_early, n_late, o_early, o_late, first_hbm, w_first_hbm, tile_hbm, rest_hbm, xy_hbm, a0, a1, a2, a3, out_hbm,
+    n_own, n_other, first, w_first, tile, rest, xy, w_rest, out, sems
 ):
     q = place[1]
     even = q % 2 == 0
@@ -285,13 +276,17 @@
     def _():
         copy(o_late, n_other, sems.at[1]).start()
 
+    size = a0.shape[0]
     moves = [
-        copy(w_first_hbm, w_first, sems.at[2]),
-        copy(first_hbm, first, sems.at[3]),
-        copy(tile_hbm, tile, sems.at[4]),
-        copy(high_hbm, high, sems.at[5]),
-        copy(low_hbm, low, sems.at[6]),
-        copy(rest_hbm, rest, sems.at[7]),
+        copy(xy_hbm, xy, sems.at[2]),
+        copy(w_first_hbm, w_first, sems.at[3]),
+        copy(first_hbm, first, sems.at[4]),
+        copy(tile_hbm, tile, sems.at[5]),
+        copy(a0, w_rest.at[:size], sems.at[6]),
+        copy(a1, w_rest.at[size : 2 * size], sems.at[7]),
+        copy(a2, w_rest.at[2 * size : 3 * size], sems.at[8]),
+        copy(a3, w_rest.at[3 * size :], sems.at[9]),
+        copy(rest_hbm, rest, sems.at[10]),
     ]
     for move in moves:
         move.start()
@@ -302,24 +297,29 @@
     rows = first.shape[0]
     half = out.shape[1]
     block = half // 2
-    for move in moves[:3]:
-        move.wait()
+    moves[0].wait()
     n_high = jnp.concatenate([h0, h1], axis=1)
     n_low = jnp.concatenate([l0, l1], axis=1)
+    hot = rows_hot(xy, w_rest.shape[0])
+    high = dot(n_high, hot).astype(BF16)
+    low = dot(n_low, hot).astype(BF16)
+    for move in moves[1:4]:
+        move.wait()
     new = first[...] - dot3((n_high, n_low), halves(w_first[...]))
     new = jnp.where(q < 2, tile[...], new)
     for t in range(rows // half):
         out[t, :, 0, :] = new[t * half : (t + 1) * half]
-    for move in moves[3:]:
+    for move in moves[4:]:
         move.wait()
+    w = [halves(w_rest[:, u * B : (u + 1) * B]) for u in range(3)]
     sent = []
     for i in range(rows // block):
         t, at = i * block // half, i * block % half
         span = slice(i * block, (i + 1) * block)
         for u in range(1, 4):
             cols = slice((u - 1) * B, u * B)
-            out[t, at : at + block, u, :] = rest[span, cols] - dot3((n_high[span], n_low[span]), (high[:, cols], low[:, cols]))
-        done = copy(out.at[t, at : at + block], out_hbm.at[t, at : at + block], sems.at[8 + i])
+            out[t, at : at + block, u, :] = rest[span, cols] - dot3((high[span], low[span]), w[u - 1])
+        done = copy(out.at[t, at : at + block], out_hbm.at[t, at : at + block], sems.at[11 + i])
         done.start()
         sent.append(done)
     for done in sent:
@@ -394,13 +394,12 @@
     payload = lax.all_to_all(payload, ("prow", "pcol"), 0, 0, tiled=True).reshape(sources * 17, 128)
 
     lists = shaped(2 * B, 128, dtype=jnp.int32)
-    own, active, give, slot, xy, yx, fits = call(
+    own, active, give, slot, xy, fits = call(
         index_kernel,
         (
             lists,
             shaped(2, rows, 128),
             shaped(KEEP, 128, dtype=jnp.int32),
-            lists,
             lists,
             lists,
             shaped(1, dtype=jnp.int32),
@@ -418,18 +417,18 @@
     front_rows = call(front_kernel, shaped(4 * KEEP, B), 2, scalars=0, flops=10**8, moved=3 * 10**6)(flat, give)
 
     send_first, send_rest = call(
-        lead_kernel, (shaped(KEEP, B), shaped(copies, cols - B)), 3, scalars=0, flops=10**8, moved=2 * 10**6
+        lead_kernel, (shaped(copies, B), shaped(KEEP, cols - B)), 3, scalars=0, flops=10**8, moved=2 * 10**6
     )(payload, front_rows, give)
-    w_rest = lax.all_to_all(send_rest, "prow", 0, 0, tiled=True)
-
-    def panels(payload, flat, send_first, xy, active, place):
-        joined = call(join_kernel, shaped(4 * KEEP, B), 4, scalars=0, moved=10**6)(*ring(send_first, shift_x))
-        w_parts = ring(joined, shift_y)
-        first, rest = call(
-            tiles_kernel, (shaped(rows, B), shaped(rows, cols - B)), 2, scalars=0, flops=4 * 10**9, moved=6 * 10**6
-        )(payload, flat)
+    w_first = lax.all_to_all(send_first, "prow", 0, 0, tiled=True)
+    joined = call(join_kernel, shaped(4 * KEEP, cols - B), 4, scalars=0, moved=10**6)(*ring(send_rest, shift_x))
+    w_parts = ring(joined, shift_y)
+    first, rest = call(
+        tiles_kernel, (shaped(rows, B), shaped(rows, cols - B)), 2, scalars=0, flops=4 * 10**9, moved=6 * 10**6
+    )(payload, flat)
+
+    def panels(w_first, first, slot, active, place, joined):
         r_other = core_swap(first)
-        w_first = call(sort_first_kernel, shaped(2 * B, B), 5, scalars=0, flops=10**8, moved=10**6)(xy, *w_parts)
+        w_first = call(sort_first_kernel, shaped(2 * B, B), 2, scalars=0, flops=10**8, moved=10**6)(slot, w_first)
         w_other = core_swap(w_first)
         half, tile = call(
             panel_kernel, (shaped(rows, B), shaped(rows, B)), 6, flops=2 * 10**9, moved=4 * 10**6
@@ -437,32 +436,24 @@
         q = place[1]
         step = lax.ppermute(half, "pcol", [(0, 2), (1, 7)])
         n_early = jnp.where((q == 2) | (q == 7), step, half)
-        return n_early, first, w_first, tile, rest
-
-    def nothing(payload, flat, send_first, xy, active, place):
+        n_late = lax.ppermute(n_early, "pcol", [(1, 3), (0, 6), (2, 4), (7, 5)])
+        o_early = lax.ppermute(n_early, "pcol", [(0, 1), (1, 0), (2, 3), (7, 6)])
+        o_late = lax.ppermute(n_late, "pcol", [(3, 2), (6, 7), (4, 5), (5, 4)])
+        return n_early, n_late, o_early, o_late, w_first, tile
+
+    def nothing(w_first, first, slot, active, place, joined):
         square = jnp.zeros((rows, B), F32)
-        return square, square, jnp.zeros((2 * B, B), F32), square, jnp.zeros((rows, cols - B), F32)
-
-    n_early, first, w_first, tile, rest = lax.cond(
-        fits[0] == 1, panels, nothing, payload, flat, send_first, xy, active, place
+        return square, square, square, square, jnp.zeros((2 * B, B), F32), square
+
+    n_early, n_late, o_early, o_late, w_first, tile = lax.cond(
+        fits[0] == 1, panels, nothing, w_first, first, slot, active, place, joined
     )
-    n_late = lax.ppermute(n_early, "pcol", [(1, 3), (0, 6), (2, 4), (7, 5)])
-    o_early = lax.ppermute(n_early, "pcol", [(0, 1), (1, 0), (2, 3), (7, 6)])
-    o_late = lax.ppermute(n_late, "pcol", [(3, 2), (6, 7), (4, 5), (5, 4)])
-    w_high, w_low = call(
-        sort_rest_kernel,
-        (shaped(2 * B, cols - B, dtype=BF16), shaped(2 * B, cols - B, dtype=BF16)),
-        2,
-        scalars=0,
-        flops=10**9,
-        moved=4 * 10**6,
-    )(slot, w_rest)
 
     def finish(payload, flat, own, active, place, *arrays):
         return pl.pallas_call(
             finish_kernel,
             out_shape=shaped(*front.shape),
-            in_specs=[SM] + [HBM] * 10,
+            in_specs=[SM] + [HBM] * 13,
             out_specs=HBM,
             scratch_shapes=[
                 pltpu.VMEM((rows, B), F32),
@@ -471,10 +462,10 @@
                 pltpu.VMEM((2 * B, B), F32),
                 pltpu.VMEM((rows, B), F32),
                 pltpu.VMEM((rows, cols - B), F32),
-                pltpu.VMEM((2 * B, cols - B), BF16),
-                pltpu.VMEM((2 * B, cols - B), BF16),
+                pltpu.VMEM((2 * B, 128), jnp.int32),
+                pltpu.VMEM((copies, cols - B), F32),
                 pltpu.VMEM(front.shape, F32),
-                pltpu.SemaphoreType.DMA((12,)),
+                pltpu.SemaphoreType.DMA((15,)),
             ],
             cost_estimate=pl.CostEstimate(flops=4 * 10**9, bytes_accessed=8 * 10**6, transcendentals=0),
             **ALONE,
@@ -517,8 +508,8 @@
         w_first,
         tile,
         rest,
-        w_high,
-        w_low,
+        xy,
+        *w_parts,
     )
 
 

time: 126 us -> 111 us (0.88)
  waiting for transfers between devices: 59 us -> 47.5 us
  local copies, waits for them, and re-layouts: 3.24 us -> 0.49 us
  starting transfers between devices: 33.3 us -> 31.2 us
  Pallas kernels: 27.6 us -> 29.3 us
    ppermute x6, waiting for transfers between devices: 28.8 us -> 14 us  [ring(): return [x] + [lax.ppermute(x, 'prow', shift(step)) for step in (1, -1, 2)]]
    unnamed x21 -> x11, local copies, waits for them, and re-layouts: 3.23 us -> 0.49 us
    ppermute x2, starting transfers between devices: 3.76 us -> 1.69 us  [core_swap(): lax.ppermute(x, 'pcol', [(i, i ^ 1) for i in range(lax.axis_size('pcol'))])]
    pallas_call x1, Pallas kernels: 5.98 us -> 7.73 us  [finish(): pl.pallas_call(finish_kernel, out_shape=shaped(*front.shape), in_specs=[S...]
    ppermute x3, waiting for transfers between devices: 17.1 us -> 18.7 us  [the longest x1 16.9 us: panels(): n_late = lax.ppermute(n_early, 'pcol', [(1, 3), (0, 6), (2, 4), (7, 5)])]
    pallas_call x5 -> x4, Pallas kernels: 10 us -> 9.84 us  [the longest x1 4.85 us: body(): call(tiles_kernel, (shaped(rows, B), shaped(rows, cols - B)), 2, scalars=...]
  transfers between devices with their start and end apart: 14 -> 14, of which waited for: 4 -> 8; matrix products, arithmetic and copies ran while one was open for 1% -> 1% of each run, Pallas kernels for 14% -> 15%
where the time goes in v8:
time: 111 us
  waiting for transfers between devices  47.5 us (43%)
  starting transfers between devices  31.2 us (28%)
  Pallas kernels  29.3 us (26%)
    ppermute x1, waiting for transfers between devices, panels(): n_late = lax.ppermute(n_early, 'pcol', [(1, 3), (0, 6), (2, 4), (7, 5)])  16.9 us
    ppermute x6, waiting for transfers between devices, ring(): return [x] + [lax.ppermute(x, 'prow', shift(step)) for step in (1, -1, 2)]  14 us
    all_to_all x1, waiting for transfers between devices, body(): lax.all_to_all(payload, ('prow', 'pcol'), 0, 0, tiled=True)  12.3 us
    all_to_all x1, starting transfers between devices, body(): lax.all_to_all(payload, ('prow', 'pcol'), 0, 0, tiled=True)  10.8 us
    ppermute x6, starting transfers between devices, ring(): return [x] + [lax.ppermute(x, 'prow', shift(step)) for step in (1, -1, 2)]  8.49 us
    pallas_call x1, Pallas kernels, finish(): pl.pallas_call(finish_kernel, out_shape=shaped(*front.shape), in_specs=[S...  7.73 us
    pallas_call x1, Pallas kernels, panels(): call(panel_kernel, (shaped(rows, B), shaped(rows, B)), 6, flops=2 * 10 **...  5.15 us
    pallas_call x1, Pallas kernels, body(): call(tiles_kernel, (shaped(rows, B), shaped(rows, cols - B)), 2, scalars=...  4.85 us
  transfers between devices with their start and end apart: 14, of which 8 were waited for; matrix products, arithmetic and copies ran while one was open for 1% of the time, Pallas kernels for 15%

profile of v8, /device:TPU:65, one launch (start us, length us, event | category | flops | bytes accessed | tf_op | source)
XLA Modules:
  0.0 110.8 jit_solution(15137630208754123701)
XLA Ops:
  0.0 0.1 pad_add_fusion.place
  0.1 2.8 %shard_map.76 = f32[2176,128]{1,0:T(8,128)} custom-call(s32[3]{0:T(128)S(1)} %pad_add_fusion.place, f32[128,8,256]{2,1,0:T(8,128)} %bitcast.28, s32[8,128]{1,0:T(8,128)} %bitcast.29, s32[1,128]{1,0:T(1,128)} %counts_hbm.1), custom_call_target="tpu_custom_call" | custom-call | flops 1000000 | bytes 2000000 | tf_op jit(solution)/shard_map/pallas_call | solution.py:380
  2.9 10.8 %all-to-all-start.2 = ((f32[2176,1,128]{2,1,0:T(1,128)}), f32[2176,1,128]{2,1,0:T(1,128)}, u32[]{:S(2)}, u32[]{:S(2)}) async-start(f32[2176,1,128]{2,1,0:T(1,128)} %bitcast.25), calls=%async_computation.2 | async-start | bytes 2228224 | tf_op jit(solution)/shard_map/all_to_all | solution.py:394
  13.7 0.0 copy-done.5
  13.7 0.0 copy-done.6
  13.7 0.0 copy-done.7
  13.7 0.0 copy-start.8
  13.7 3.2 %shard_map.75 = (s32[512,128]{1,0:T(8,128)}, f32[2,512,128]{2,1,0:T(8,128)}, s32[48,128]{1,0:T(8,128)S(1)}, s32[512,128]{1,0:T(8,128)}, s32[512,128]{1,0:T(8,128)}, /*index=5*/s32[1]{0:T(128)}) custom-call(s32[3]{0:T(128)S(1)} %pad_add_fusion.place, s32[2,16,256]{2,1,0:T(8,128)S(1)} %copy-done.6, s32[2,4,16,256]{3,2,1,0:T(8,128)S(1)} %copy-done.5, ...), custom_call_target="tpu_custom_call" | custom-call | flops 1000000000 | bytes 1000000 | tf_op jit(solution)/shard_map/pallas_call | solution.py:397
  17.0 0.0 copy-done.8
  17.0 0.5 copy.11
  17.4 0.5 shard_map.77.front_rows
  18.0 12.3 %all-to-all-done.2 = f32[2176,1,128]{2,1,0:T(1,128)} async-done(((f32[2176,1,128]{2,1,0:T(1,128)}), f32[2176,1,128]{2,1,0:T(1,128)}, u32[]{:S(2)}, u32[]{:S(2)}) %all-to-all-start.2) | async-done | bytes 1114144 | tf_op jit(solution)/shard_map/all_to_all | solution.py:394
  30.3 2.6 %shard_map.78 = (f32[768,256]{1,0:T(8,128)}, f32[48,768]{1,0:T(8,128)S(1)}) custom-call(f32[2176,128]{1,0:T(8,128)} %bitcast.12.payload, f32[192,256]{1,0:T(8,128)S(1)} %shard_map.77.front_rows, s32[48,128]{1,0:T(8,128)S(1)} %get-tuple-element.116.give), custom_call_target="tpu_custom_call" | custom-call | flops 100000000 | bytes 2000000 | tf_op jit(solution)/shard_map/pallas_call | solution.py:419
  32.9 3.7 %all-to-all-start.3 = ((f32[16,48,256]{2,1,0:T(8,128)}), f32[16,48,256]{2,1,0:T(8,128)S(1)}, u32[]{:S(2)}, u32[]{:S(2)}) async-start(f32[16,48,256]{2,1,0:T(8,128)} %bitcast.13), calls=%async_computation.3 | async-start | bytes 1572864 | tf_op jit(solution)/shard_map/all_to_all | solution.py:422
  36.7 2.9 %collective-permute-start.14 = (f32[48,768]{1,0:T(8,128)S(1)}, f32[48,768]{1,0:T(8,128)S(1)}, u32[]{:S(2)}, u32[]{:S(2)}) collective-permute-start(f32[48,768]{1,0:T(8,128)S(1)} %get-tuple-element.128.a0), channel_id=1, source_target_pairs={{0,16},{8,24},{16,0},{24,8},{32,48},{40,56},{48,32},{56,40},{64,80... | collective-permute-start | bytes 442376 | tf_op jit(solution)/shard_map/ppermute | solution.py:360
  39.5 0.9 collective-permute-start.13
  40.4 0.6 collective-permute-start.12
  41.0 9.8 %collective-permute-done.14.a3 = f32[48,768]{1,0:T(8,128)S(1)} collective-permute-done((f32[48,768]{1,0:T(8,128)S(1)}, f32[48,768]{1,0:T(8,128)S(1)}, u32[]{:S(2)}, u32[]{:S(2)}) %collective-permute-start.14) | collective-permute-done | bytes 147488 | tf_op jit(solution)/shard_map/ppermute | solution.py:360
  50.8 1.9 %collective-permute-done.13.a2 = f32[48,768]{1,0:T(8,128)S(1)} collective-permute-done((f32[48,768]{1,0:T(8,128)S(1)}, f32[48,768]{1,0:T(8,128)S(1)}, u32[]{:S(2)}, u32[]{:S(2)}) %collective-permute-start.13) | collective-permute-done | bytes 147488 | tf_op jit(solution)/shard_map/ppermute | solution.py:360
  52.7 2.2 %collective-permute-done.12.a1 = f32[48,768]{1,0:T(8,128)S(1)} collective-permute-done((f32[48,768]{1,0:T(8,128)S(1)}, f32[48,768]{1,0:T(8,128)S(1)}, u32[]{:S(2)}, u32[]{:S(2)}) %collective-permute-start.12) | collective-permute-done | bytes 147488 | tf_op jit(solution)/shard_map/ppermute | solution.py:360
  55.0 0.9 shard_map.80
  55.9 2.7 %collective-permute-start.17 = (f32[192,768]{1,0:T(8,128)}, f32[192,768]{1,0:T(8,128)}, u32[]{:S(2)}, u32[]{:S(2)}) collective-permute-start(f32[192,768]{1,0:T(8,128)} %shard_map.80), channel_id=1, source_target_pairs={{0,64},{8,72},{16,80},{24,88},{32,96},{40,104},{48,112},{56,120},{... | collective-permute-start | bytes 1769480 | tf_op jit(solution)/shard_map/ppermute | solution.py:360
  58.6 0.9 collective-permute-start.16
  59.4 0.6 collective-permute-start.15
  60.7 0.0 copy-start.9
  60.7 4.9 %shard_map.79 = (f32[512,256]{1,0:T(8,128)}, f32[512,768]{1,0:T(8,128)}) custom-call(f32[2176,128]{1,0:T(8,128)} %bitcast.12.payload, f32[512,1024]{1,0:T(8,128)S(1)} %bitcast.23), custom_call_target="tpu_custom_call" | custom-call | flops 4000000000 | bytes 6000000 | tf_op jit(solution)/shard_map/pallas_call | solution.py:425
  65.5 0.0 all-to-all-done.3
  65.5 37.1 %conditional.2 = (f32[512,256]{1,0:T(8,128)}, f32[512,256]{1,0:T(8,128)}, f32[512,256]{1,0:T(8,128)}, f32[512,256]{1,0:T(8,128)}, f32[512,256]{1,0:T(8,128)}, /*index=5*/f32[512,256]{1,0:T(8,128)}) conditional(s32[]{:T(128)} %bitcast.6, () %tuple.22, (s32[]{:T(128)}, f32[16,48,256]{2,1,0:T(8,128)S(1)}, s32[512,128]{1,0:T(8,128)S(1)}, ...), branch_computations={%region_0.0_spmd, %region_1.2_spmd} | conditional | flops 2100131072 | bytes 19156086 | solution.py:448
  65.5 1.5 %branch_1_fun.3.w_own = f32[512,256]{1,0:T(8,128)} custom-call(s32[512,128]{1,0:T(8,128)S(1)} %get-tuple-element.63.slot, f32[768,256]{1,0:T(8,128)S(1)} %bitcast.26), custom_call_target="tpu_custom_call" | custom-call | flops 100000000 | bytes 1000000 | tf_op jit(solution)/shard_map/cond/branch_1_fun/pallas_call | solution.py:431
  67.1 1.7 %collective-permute-start = (f32[512,256]{1,0:T(8,128)}, f32[512,256]{1,0:T(8,128)S(1)}, u32[]{:S(2)}, u32[]{:S(2)}) collective-permute-start(f32[512,256]{1,0:T(8,128)} %branch_1_fun.3.w_own), channel_id=1, source_target_pairs={{0,1},{1,0},{2,3},{3,2},{4,5},{5,4},{6,7},{7,6},{8,9},{9,8},{10,11... | collective-permute-start | bytes 1572872 | tf_op jit(solution)/shard_map/cond/branch_1_fun/ppermute | solution.py:348
  68.7 0.0 collective-permute-start.1
  68.7 1.7 %collective-permute-done.w_other = f32[512,256]{1,0:T(8,128)S(1)} collective-permute-done((f32[512,256]{1,0:T(8,128)}, f32[512,256]{1,0:T(8,128)S(1)}, u32[]{:S(2)}, u32[]{:S(2)}) %collective-permute-start) | collective-permute-done | bytes 524320 | tf_op jit(solution)/shard_map/cond/branch_1_fun/ppermute | solution.py:348
  70.5 0.7 collective-permute-done.1.r_other
  71.2 5.1 %branch_1_fun.4 = (f32[512,256]{1,0:T(8,128)S(1)}, f32[512,256]{1,0:T(8,128)}) custom-call(s32[3]{0:T(128)S(1)} %get-tuple-element.62.place, f32[512,256]{1,0:T(8,128)} %branch_1_fun.3.w_own, f32[512,256]{1,0:T(8,128)S(1)} %collective-permute-done.w_other, f32[512,256]{1,0:T(8,128)} %get-tuple-element.65.r_own, ...), custom_call_target="tpu_custom_call" | custom-call | flops 2000000000 | bytes 4000000 | tf_op jit(solution)/shard_map/cond/branch_1_fun/pallas_call | solution.py:433
  76.4 0.7 collective-permute-start.2
  77.1 0.0 collective-permute-done.2
  77.1 1.0 broadcast_select_fusion
  78.0 1.3 %collective-permute-start.3 = (f32[512,256]{1,0:T(8,128)}, f32[512,256]{1,0:T(8,128)}, u32[]{:S(2)}, u32[]{:S(2)}) collective-permute-start(f32[512,256]{1,0:T(8,128)} %broadcast_select_fusion), channel_id=1, source_target_pairs={{1,3},{0,6},{2,4},{7,5},{9,11},{8,14},{10,12},{15,13},{17,19},{16,... | collective-permute-start | bytes 1572872 | tf_op jit(solution)/shard_map/cond/branch_1_fun/ppermute | solution.py:439
  79.3 1.5 %collective-permute-start.4 = (f32[512,256]{1,0:T(8,128)}, f32[512,256]{1,0:T(8,128)}, u32[]{:S(2)}, u32[]{:S(2)}) collective-permute-start(f32[512,256]{1,0:T(8,128)} %broadcast_select_fusion), channel_id=1, source_target_pairs={{0,1},{1,0},{2,3},{7,6},{8,9},{9,8},{10,11},{15,14},{16,17},{17,16... | collective-permute-start | bytes 1572872 | tf_op jit(solution)/shard_map/cond/branch_1_fun/ppermute | solution.py:440
  80.8 16.9 %collective-permute-done.3 = f32[512,256]{1,0:T(8,128)} collective-permute-done((f32[512,256]{1,0:T(8,128)}, f32[512,256]{1,0:T(8,128)}, u32[]{:S(2)}, u32[]{:S(2)}) %collective-permute-start.3) | collective-permute-done | bytes 524320 | tf_op jit(solution)/shard_map/cond/branch_1_fun/ppermute | solution.py:439
  97.7 3.1 %collective-permute-start.5 = (f32[512,256]{1,0:T(8,128)}, f32[512,256]{1,0:T(8,128)}, u32[]{:S(2)}, u32[]{:S(2)}) collective-permute-start(f32[512,256]{1,0:T(8,128)} %collective-permute-done.3), channel_id=1, source_target_pairs={{3,2},{6,7},{4,5},{5,4},{11,10},{14,15},{12,13},{13,12},{19,18},{2... | collective-permute-start | bytes 1572872 | tf_op jit(solution)/shard_map/cond/branch_1_fun/ppermute | solution.py:441
  100.8 0.0 collective-permute-done.4
  100.8 1.8 %collective-permute-done.5 = f32[512,256]{1,0:T(8,128)} collective-permute-done((f32[512,256]{1,0:T(8,128)}, f32[512,256]{1,0:T(8,128)}, u32[]{:S(2)}, u32[]{:S(2)}) %collective-permute-start.5) | collective-permute-done | bytes 524320 | tf_op jit(solution)/shard_map/cond/branch_1_fun/ppermute | solution.py:441
  102.7 0.0 collective-permute-done.17
  102.7 0.0 collective-permute-done.16
  102.7 0.0 collective-permute-done.15
  102.7 8.0 %conditional.3 = (f32[2,256,4,256]{3,2,1,0:T(4,128)}) conditional(s32[]{:T(128)} %bitcast.6, (f32[2176,128]{1,0:T(8,128)}, f32[512,1024]{1,0:T(8,128)S(1)}, s32[512,128]{1,0:T(8,128)}, s32[]{:T(128)}, s32[3]{0:T(128)S(1)}, /*index=5*/f32[2,512,128]{2,1,0:T(8,128)}) %tuple.31, (s32[3]{0:T(128)S(1)}, f32[512,256]{1,0:T(8,128)}, f32[512,256]{1,0:T(8,128)}, ...), branch_computations={%region_2.4_spmd, %region_4.5_spmd} | conditional | flops 8000884736 | bytes 85798736 | solution.py:494
  102.9 7.7 %branch_1_fun.5 = f32[2,256,4,256]{3,2,1,0:T(4,128)} custom-call(s32[3]{0:T(128)S(1)} %get-tuple-element.79.place, f32[512,256]{1,0:T(8,128)} %get-tuple-element.80.n_early, f32[512,256]{1,0:T(8,128)} %get-tuple-element.81.n_late, f32[512,256]{1,0:T(8,128)} %get-tuple-element.82.o_early, f32[512,256]{1,0:T(8,128)} %get-tuple-element.83.o_late, ...), custom_call_target="tpu_custom_call" | custom-call | flops 4000000000 | bytes 8000000 | tf_op jit(solution)/shard_map/cond/branch_1_fun/pallas_call | solution.py:453
  (4 shorter events, 0.0 us)
Async XLA Ops:
  0.1 13.6 %copy-start.5 = (s32[2,4,16,256]{3,2,1,0:T(8,128)S(1)}, s32[2,4,16,256]{3,2,1,0:T(8,128)}, u32[]{:S(2)}) copy-start(s32[2,4,16,256]{3,2,1,0:T(8,128)} %level_picks.1) | copy-start | bytes 393220
  0.1 13.6 %copy-start.6 = (s32[2,16,256]{2,1,0:T(8,128)S(1)}, s32[2,16,256]{2,1,0:T(8,128)}, u32[]{:S(2)}) copy-start(s32[2,16,256]{2,1,0:T(8,128)} %local_picks.1) | copy-start | bytes 98308
  0.1 13.6 %copy-start.7 = (s32[2,256]{1,0:T(2,128)S(1)}, s32[2,256]{1,0:T(2,128)}, u32[]{:S(2)}) copy-start(s32[2,256]{1,0:T(2,128)} %order.1) | copy-start | bytes 6148
  2.9 27.4 %all-to-all-start.2 = ((f32[2176,1,128]{2,1,0:T(1,128)}), f32[2176,1,128]{2,1,0:T(1,128)}, u32[]{:S(2)}, u32[]{:S(2)}) async-start(f32[2176,1,128]{2,1,0:T(1,128)} %bitcast.25), calls=%async_computation.2 | async-start | bytes 2228224 | tf_op jit(solution)/shard_map/all_to_all | solution.py:394
  13.7 3.2 %copy-start.8 = (f32[2,256,4,256]{3,2,1,0:T(4,128)S(1)}, f32[2,256,4,256]{3,2,1,0:T(4,128)}, u32[]{:S(2)}) copy-start(f32[2,256,4,256]{3,2,1,0:T(4,128)} %param.11) | copy-start | bytes 6291460
  32.9 32.6 %all-to-all-start.3 = ((f32[16,48,256]{2,1,0:T(8,128)}), f32[16,48,256]{2,1,0:T(8,128)S(1)}, u32[]{:S(2)}, u32[]{:S(2)}) async-start(f32[16,48,256]{2,1,0:T(8,128)} %bitcast.13), calls=%async_computation.3 | async-start | bytes 1572864 | tf_op jit(solution)/shard_map/all_to_all | solution.py:422
  36.7 14.2 %collective-permute-start.14 = (f32[48,768]{1,0:T(8,128)S(1)}, f32[48,768]{1,0:T(8,128)S(1)}, u32[]{:S(2)}, u32[]{:S(2)}) collective-permute-start(f32[48,768]{1,0:T(8,128)S(1)} %get-tuple-element.128.a0), channel_id=1, source_target_pairs={{0,16},{8,24},{16,0},{24,8},{32,48},{40,56},{48,32},{56,40},{64,80... | collective-permute-start | bytes 442376 | tf_op jit(solution)/shard_map/ppermute | solution.py:360
  39.5 13.2 %collective-permute-start.13 = (f32[48,768]{1,0:T(8,128)S(1)}, f32[48,768]{1,0:T(8,128)S(1)}, u32[]{:S(2)}, u32[]{:S(2)}) collective-permute-start(f32[48,768]{1,0:T(8,128)S(1)} %get-tuple-element.128.a0), channel_id=1, source_target_pairs={{0,24},{8,0},{16,8},{24,16},{32,56},{40,32},{48,40},{56,48},{64,88... | collective-permute-start | bytes 442376 | tf_op jit(solution)/shard_map/ppermute | solution.py:360
  40.4 14.6 %collective-permute-start.12 = (f32[48,768]{1,0:T(8,128)S(1)}, f32[48,768]{1,0:T(8,128)S(1)}, u32[]{:S(2)}, u32[]{:S(2)}) collective-permute-start(f32[48,768]{1,0:T(8,128)S(1)} %get-tuple-element.128.a0), channel_id=1, source_target_pairs={{0,8},{8,16},{16,24},{24,0},{32,40},{40,48},{48,56},{56,32},{64,72... | collective-permute-start | bytes 442376 | tf_op jit(solution)/shard_map/ppermute | solution.py:360
  55.9 46.8 %collective-permute-start.17 = (f32[192,768]{1,0:T(8,128)}, f32[192,768]{1,0:T(8,128)}, u32[]{:S(2)}, u32[]{:S(2)}) collective-permute-start(f32[192,768]{1,0:T(8,128)} %shard_map.80), channel_id=1, source_target_pairs={{0,64},{8,72},{16,80},{24,88},{32,96},{40,104},{48,112},{56,120},{... | collective-permute-start | bytes 1769480 | tf_op jit(solution)/shard_map/ppermute | solution.py:360
  58.6 44.1 %collective-permute-start.16 = (f32[192,768]{1,0:T(8,128)}, f32[192,768]{1,0:T(8,128)}, u32[]{:S(2)}, u32[]{:S(2)}) collective-permute-start(f32[192,768]{1,0:T(8,128)} %shard_map.80), channel_id=1, source_target_pairs={{0,96},{8,104},{16,112},{24,120},{32,0},{40,8},{48,16},{56,24},{64... | collective-permute-start | bytes 1769480 | tf_op jit(solution)/shard_map/ppermute | solution.py:360
  59.4 43.2 %collective-permute-start.15 = (f32[192,768]{1,0:T(8,128)}, f32[192,768]{1,0:T(8,128)}, u32[]{:S(2)}, u32[]{:S(2)}) collective-permute-start(f32[192,768]{1,0:T(8,128)} %shard_map.80), channel_id=1, source_target_pairs={{0,32},{8,40},{16,48},{24,56},{32,64},{40,72},{48,80},{56,88},{64,... | collective-permute-start | bytes 1769480 | tf_op jit(solution)/shard_map/ppermute | solution.py:360
  60.7 4.9 %copy-start.9 = (s32[512,128]{1,0:T(8,128)S(1)}, s32[512,128]{1,0:T(8,128)}, u32[]{:S(2)}) copy-start(s32[512,128]{1,0:T(8,128)} %get-tuple-element.118) | copy-start | bytes 786436
  67.1 3.4 %collective-permute-start = (f32[512,256]{1,0:T(8,128)}, f32[512,256]{1,0:T(8,128)S(1)}, u32[]{:S(2)}, u32[]{:S(2)}) collective-permute-start(f32[512,256]{1,0:T(8,128)} %branch_1_fun.3.w_own), channel_id=1, source_target_pairs={{0,1},{1,0},{2,3},{3,2},{4,5},{5,4},{6,7},{7,6},{8,9},{9,8},{10,11... | collective-permute-start | bytes 1572872 | tf_op jit(solution)/shard_map/cond/branch_1_fun/ppermute | solution.py:348
  68.7 2.5 %collective-permute-start.1 = (f32[512,256]{1,0:T(8,128)}, f32[512,256]{1,0:T(8,128)S(1)}, u32[]{:S(2)}, u32[]{:S(2)}) collective-permute-start(f32[512,256]{1,0:T(8,128)} %get-tuple-element.65.r_own), channel_id=1, source_target_pairs={{0,1},{1,0},{2,3},{3,2},{4,5},{5,4},{6,7},{7,6},{8,9},{9,8},{10,11... | collective-permute-start | bytes 1572872 | tf_op jit(solution)/shard_map/cond/branch_1_fun/ppermute | solution.py:348
  76.4 0.7 collective-permute-start.2
  78.0 19.6 %collective-permute-start.3 = (f32[512,256]{1,0:T(8,128)}, f32[512,256]{1,0:T(8,128)}, u32[]{:S(2)}, u32[]{:S(2)}) collective-permute-start(f32[512,256]{1,0:T(8,128)} %broadcast_select_fusion), channel_id=1, source_target_pairs={{1,3},{0,6},{2,4},{7,5},{9,11},{8,14},{10,12},{15,13},{17,19},{16,... | collective-permute-start | bytes 1572872 | tf_op jit(solution)/shard_map/cond/branch_1_fun/ppermute | solution.py:439
  79.3 21.5 %collective-permute-start.4 = (f32[512,256]{1,0:T(8,128)}, f32[512,256]{1,0:T(8,128)}, u32[]{:S(2)}, u32[]{:S(2)}) collective-permute-start(f32[512,256]{1,0:T(8,128)} %broadcast_select_fusion), channel_id=1, source_target_pairs={{0,1},{1,0},{2,3},{7,6},{8,9},{9,8},{10,11},{15,14},{16,17},{17,16... | collective-permute-start | bytes 1572872 | tf_op jit(solution)/shard_map/cond/branch_1_fun/ppermute | solution.py:440
  97.7 5.0 %collective-permute-start.5 = (f32[512,256]{1,0:T(8,128)}, f32[512,256]{1,0:T(8,128)}, u32[]{:S(2)}, u32[]{:S(2)}) collective-permute-start(f32[512,256]{1,0:T(8,128)} %collective-permute-done.3), channel_id=1, source_target_pairs={{3,2},{6,7},{4,5},{5,4},{11,10},{14,15},{12,13},{13,12},{19,18},{2... | collective-permute-start | bytes 1572872 | tf_op jit(solution)/shard_map/cond/branch_1_fun/ppermute | solution.py:441

commit v9 on v8

--- a/solution.py
+++ b/solution.py
@@ -89,10 +89,10 @@
     before = (d_col == d) & (iota((n, n), 0) < iota((n, n), 1))
     rank = jnp.sum(before.astype(jnp.int32), axis=0, keepdims=True)
     fits_out[0] = (jnp.max(rank) < keep).astype(jnp.int32)
-    slot_out[...] = jnp.broadcast_to(d * keep + rank, (128, n)).T
+    slot_out[...] = rows_hot(jnp.broadcast_to(d * keep + rank, (128, n)).T, slot_out.shape[1])
     across = turn(d - p)
     down = turn((d >> 2) - (p >> 2))
-    xy_out[...] = jnp.broadcast_to((down * 4 + across) * keep + rank, (128, n)).T
+    xy_out[...] = rows_hot(jnp.broadcast_to((down * 4 + across) * keep + rank, (128, n)).T, xy_out.shape[1])
     mine = (iota((keep, n), 0) == rank) & (d == p)
     give = jnp.sum(jnp.where(mine, r + 2, 0), axis=1, keepdims=True) - 2
     give_out[...] = jnp.broadcast_to(give, (keep, 128))
@@ -181,7 +181,8 @@
         send_rest[:, (u - 1) * B : u * B] = sums[u * keep : (u + 1) * keep]
 
 
-def tiles_kernel(payload, front, first_out, rest_out):
+def tiles_kernel(payload, front, first_out, rest_out, done_out):
+    done_out[...] = jnp.zeros_like(done_out)
     (high, low), code = unpack(payload)
     for u in range(4):
         hot = hot_of(code, front.shape[0], u)
@@ -192,14 +193,14 @@
             rest_out[:, (u - 1) * B : u * B] = tile
 
 
-def join_kernel(a0, a1, a2, a3, out):
+def join_kernel(done, a0, a1, a2, a3, out):
     size = a0.shape[0]
     for i, a in enumerate((a0, a1, a2, a3)):
         out[i * size : (i + 1) * size, :] = a[...]
 
 
 def sort_first_kernel(slot, gathered, out):
-    out[...] = pick(rows_hot(slot, gathered.shape[0]), gathered[...])
+    out[...] = pick(slot[...], gathered[...])
 
 
 def inverse_of(diag):
@@ -251,30 +252,23 @@
 
 
 def finish_kernel(
-    place, n_early, n_late, o_early, o_late, first_hbm, w_first_hbm, tile_hbm, rest_hbm, xy_hbm, a0, a1, a2, a3, out_hbm,
-    n_own, n_other, first, w_first, tile, rest, xy, w_rest, out, sems
+    place, n_early, n_last, o_early, o_last, tile_hbm, first_hbm, w_first_hbm, rest_hbm, xy_hbm,
+    a0, a1, a2, a3, out_hbm, n_own, n_other, first, w_first, tile, rest, xy, w_rest, out, sems
 ):
     q = place[1]
     even = q % 2 == 0
-    own_early = (q < 3) | (q == 7)
-    other_early = (q < 2) | (q == 3) | (q == 6)
+    far = (q == 4) | (q == 5)
     copy = pltpu.make_async_copy
 
-    @pl.when(own_early)
+    @pl.when(far)
+    def _():
+        copy(n_last, n_own, sems.at[0]).start()
+        copy(o_last, n_other, sems.at[1]).start()
+
+    @pl.when(jnp.logical_not(far))
     def _():
         copy(n_early, n_own, sems.at[0]).start()
-
-    @pl.when(jnp.logical_not(own_early))
-    def _():
-        copy(n_late, n_own, sems.at[0]).start()
-
-    @pl.when(other_early)
-    def _():
         copy(o_early, n_other, sems.at[1]).start()
-
-    @pl.when(jnp.logical_not(other_early))
-    def _():
-        copy(o_late, n_other, sems.at[1]).start()
 
     size = a0.shape[0]
     moves = [
@@ -300,7 +294,7 @@
     moves[0].wait()
     n_high = jnp.concatenate([h0, h1], axis=1)
     n_low = jnp.concatenate([l0, l1], axis=1)
-    hot = rows_hot(xy, w_rest.shape[0])
+    hot = xy[...]
     high = dot(n_high, hot).astype(BF16)
     low = dot(n_low, hot).astype(BF16)
     for move in moves[1:4]:
@@ -393,15 +387,16 @@
     )(place, partials[0], targets[0].T, counts).reshape(sources * 17, 1, 128)
     payload = lax.all_to_all(payload, ("prow", "pcol"), 0, 0, tiled=True).reshape(sources * 17, 128)
 
-    lists = shaped(2 * B, 128, dtype=jnp.int32)
+    copies = lax.axis_size("prow") * KEEP
+    hots = shaped(2 * B, copies, dtype=BF16)
     own, active, give, slot, xy, fits = call(
         index_kernel,
         (
-            lists,
+            shaped(2 * B, 128, dtype=jnp.int32),
             shaped(2, rows, 128),
             shaped(KEEP, 128, dtype=jnp.int32),
-            lists,
-            lists,
+            hots,
+            hots,
             shaped(1, dtype=jnp.int32),
         ),
         4,
@@ -411,7 +406,6 @@
     )(place, local_picks, level_picks, order)
     front, own = lax.optimization_barrier((front, own))
     flat = front.reshape(rows, cols)
-    copies = lax.axis_size("prow") * KEEP
     share_rows = 2 * B // lax.axis_size("prow")
 
     front_rows = call(front_kernel, shaped(4 * KEEP, B), 2, scalars=0, flops=10**8, moved=3 * 10**6)(flat, give)
@@ -420,34 +414,39 @@
         lead_kernel, (shaped(copies, B), shaped(KEEP, cols - B)), 3, scalars=0, flops=10**8, moved=2 * 10**6
     )(payload, front_rows, give)
     w_first = lax.all_to_all(send_first, "prow", 0, 0, tiled=True)
-    joined = call(join_kernel, shaped(4 * KEEP, cols - B), 4, scalars=0, moved=10**6)(*ring(send_rest, shift_x))
+    first, rest, done = call(
+        tiles_kernel,
+        (shaped(rows, B), shaped(rows, cols - B), shaped(8, 128)),
+        2,
+        scalars=0,
+        flops=4 * 10**9,
+        moved=6 * 10**6,
+    )(payload, flat)
+    joined = call(join_kernel, shaped(4 * KEEP, cols - B), 5, scalars=0, moved=10**6)(done, *ring(send_rest, shift_x))
     w_parts = ring(joined, shift_y)
-    first, rest = call(
-        tiles_kernel, (shaped(rows, B), shaped(rows, cols - B)), 2, scalars=0, flops=4 * 10**9, moved=6 * 10**6
-    )(payload, flat)
-
-    def panels(w_first, first, slot, active, place, joined):
+    w_first = call(sort_first_kernel, shaped(2 * B, B), 2, scalars=0, flops=10**8, moved=10**6)(slot, w_first)
+
+    def panels(w_first, first, active, place, joined):
         r_other = core_swap(first)
-        w_first = call(sort_first_kernel, shaped(2 * B, B), 2, scalars=0, flops=10**8, moved=10**6)(slot, w_first)
         w_other = core_swap(w_first)
         half, tile = call(
             panel_kernel, (shaped(rows, B), shaped(rows, B)), 6, flops=2 * 10**9, moved=4 * 10**6
         )(place, w_first, w_other, first, r_other, active)
         q = place[1]
+        near = (q == 2) | (q == 7)
+        side = (q == 3) | (q == 6)
         step = lax.ppermute(half, "pcol", [(0, 2), (1, 7)])
-        n_early = jnp.where((q == 2) | (q == 7), step, half)
-        n_late = lax.ppermute(n_early, "pcol", [(1, 3), (0, 6), (2, 4), (7, 5)])
-        o_early = lax.ppermute(n_early, "pcol", [(0, 1), (1, 0), (2, 3), (7, 6)])
-        o_late = lax.ppermute(n_late, "pcol", [(3, 2), (6, 7), (4, 5), (5, 4)])
-        return n_early, n_late, o_early, o_late, w_first, tile
-
-    def nothing(w_first, first, slot, active, place, joined):
-        square = jnp.zeros((rows, B), F32)
-        return square, square, square, square, jnp.zeros((2 * B, B), F32), square
-
-    n_early, n_late, o_early, o_late, w_first, tile = lax.cond(
-        fits[0] == 1, panels, nothing, w_first, first, slot, active, place, joined
-    )
+        late = lax.ppermute(half, "pcol", [(1, 3), (0, 6)])
+        last = lax.ppermute(step, "pcol", [(2, 4), (7, 5)])
+        early = jnp.where(side, late, jnp.where(near, step, half))
+        o_early = lax.ppermute(early, "pcol", [(0, 1), (1, 0), (2, 3), (3, 2), (6, 7), (7, 6)])
+        o_last = lax.ppermute(last, "pcol", [(4, 5), (5, 4)])
+        return early, last, o_early, o_last, tile
+
+    def nothing(w_first, first, active, place, joined):
+        return (jnp.zeros((rows, B), F32),) * 5
+
+    parts = lax.cond(fits[0] == 1, panels, nothing, w_first, first, active, place, joined)
 
     def finish(payload, flat, own, active, place, *arrays):
         return pl.pallas_call(
@@ -462,7 +461,7 @@
                 pltpu.VMEM((2 * B, B), F32),
                 pltpu.VMEM((rows, B), F32),
                 pltpu.VMEM((rows, cols - B), F32),
-                pltpu.VMEM((2 * B, 128), jnp.int32),
+                pltpu.VMEM((2 * B, copies), BF16),
                 pltpu.VMEM((copies, cols - B), F32),
                 pltpu.VMEM(front.shape, F32),
                 pltpu.SemaphoreType.DMA((15,)),
@@ -500,13 +499,9 @@
         own,
         active,
         place,
-        n_early,
-        n_late,
-        o_early,
-        o_late,
+        *parts,
         first,
         w_first,
-        tile,
         rest,
         xy,
         *w_parts,

time: 111 us -> 112 us (level)
  the two profiles are of different devices: /device:TPU:65 before, /device:TPU:75 now
where the time goes in v9:
time: 112 us
  waiting for transfers between devices  43.2 us (39%)
  starting transfers between devices  35 us (31%)
  Pallas kernels  28.8 us (26%)
  local copies, waits for them, and re-layouts  2.81 us (3%)
    ppermute x1, waiting for transfers between devices, panels(): last = lax.ppermute(step, 'pcol', [(2, 4), (7, 5)])  28.8 us
    all_to_all x1, starting transfers between devices, body(): lax.all_to_all(payload, ('prow', 'pcol'), 0, 0, tiled=True)  10.3 us
    all_to_all x1, waiting for transfers between devices, body(): lax.all_to_all(payload, ('prow', 'pcol'), 0, 0, tiled=True)  9.63 us
    pallas_call x1, Pallas kernels, finish(): pl.pallas_call(finish_kernel, out_shape=shaped(*front.shape), in_specs=[S...  7.58 us
    all_to_all x1, starting transfers between devices, body(): w_first = lax.all_to_all(send_first, 'prow', 0, 0, tiled=True)  6.72 us
    ppermute x6, starting transfers between devices, ring(): return [x] + [lax.ppermute(x, 'prow', shift(step)) for step in (1, -1, 2)]  6.63 us
    pallas_call x1, Pallas kernels, body(): call(tiles_kernel, (shaped(rows, B), shaped(rows, cols - B), shaped(8, 12...  5.16 us
    pallas_call x1, Pallas kernels, panels(): call(panel_kernel, (shaped(rows, B), shaped(rows, B)), 6, flops=2 * 10 **...  5.16 us
  transfers between devices with their start and end apart: 15, of which 6 were waited for; matrix products, arithmetic and copies ran while one was open for 1% of the time, Pallas kernels for 14%

profile of v9, /device:TPU:75, one launch (start us, length us, event | category | flops | bytes accessed | tf_op | source)
XLA Modules:
  0.0 111.9 jit_solution(14874333142746819077)
XLA Ops:
  0.0 0.1 pad_add_fusion.place
  0.1 2.9 %shard_map.76 = f32[2176,128]{1,0:T(8,128)} custom-call(s32[3]{0:T(128)S(1)} %pad_add_fusion.place, f32[128,8,256]{2,1,0:T(8,128)} %bitcast.31, s32[8,128]{1,0:T(8,128)} %bitcast.32, s32[1,128]{1,0:T(1,128)} %counts_hbm.1), custom_call_target="tpu_custom_call" | custom-call | flops 1000000 | bytes 2000000 | tf_op jit(solution)/shard_map/pallas_call | solution.py:374
  2.9 10.3 %all-to-all-start.2 = ((f32[2176,1,128]{2,1,0:T(1,128)}), f32[2176,1,128]{2,1,0:T(1,128)S(1)}, u32[]{:S(2)}, u32[]{:S(2)}) async-start(f32[2176,1,128]{2,1,0:T(1,128)} %bitcast.29), calls=%async_computation.2 | async-start | bytes 2228224 | tf_op jit(solution)/shard_map/all_to_all | solution.py:388
  13.3 0.0 copy-done.5
  13.3 0.0 copy-start.12
  13.3 3.4 %shard_map.75 = (s32[512,128]{1,0:T(8,128)S(1)}, f32[2,512,128]{2,1,0:T(8,128)}, s32[48,128]{1,0:T(8,128)S(1)}, bf16[512,768]{1,0:T(8,128)(2,1)S(1)}, bf16[512,768]{1,0:T(8,128)(2,1)}, /*index=5*/s32[1]{0:T(128)}) custom-call(s32[3]{0:T(128)S(1)} %pad_add_fusion.place, s32[2,16,256]{2,1,0:T(8,128)S(1)} %copy-done.6, s32[2,4,16,256]{3,2,1,0:T(8,128)S(1)} %copy-done.5, ...), custom_call_target="tpu_custom_call" | custom-call | flops 1000000000 | bytes 1000000 | tf_op jit(solution)/shard_map/pallas_call | solution.py:392
  16.7 0.5 copy.11
  17.2 0.0 copy-start.8
  17.2 1.3 %copy-done.8 = f32[64,8,4,256]{3,1,2,0:T(8,128)} copy-done((f32[64,8,4,256]{3,1,2,0:T(8,128)}, f32[64,8,4,256]{3,1,2,0:T(8,128)S(1)}, u32[]{:S(2)}) %copy-start.8) | copy-done | bytes 2097176
  18.5 0.6 shard_map.77.front_rows
  19.0 9.6 %all-to-all-done.2 = f32[2176,1,128]{2,1,0:T(1,128)S(1)} async-done(((f32[2176,1,128]{2,1,0:T(1,128)}), f32[2176,1,128]{2,1,0:T(1,128)S(1)}, u32[]{:S(2)}, u32[]{:S(2)}) %all-to-all-start.2) | async-done | bytes 1114144 | tf_op jit(solution)/shard_map/all_to_all | solution.py:388
  28.7 1.0 copy-done.10
  29.7 2.7 %shard_map.78 = (f32[768,256]{1,0:T(8,128)}, f32[48,768]{1,0:T(8,128)S(1)}) custom-call(f32[2176,128]{1,0:T(8,128)} %bitcast.26, f32[192,256]{1,0:T(8,128)S(1)} %shard_map.77.front_rows, s32[48,128]{1,0:T(8,128)S(1)} %get-tuple-element.113.give), custom_call_target="tpu_custom_call" | custom-call | flops 100000000 | bytes 2000000 | tf_op jit(solution)/shard_map/pallas_call | solution.py:413
  32.4 1.8 %collective-permute-start.15 = (f32[48,768]{1,0:T(8,128)S(1)}, f32[48,768]{1,0:T(8,128)S(1)}, u32[]{:S(2)}, u32[]{:S(2)}) collective-permute-start(f32[48,768]{1,0:T(8,128)S(1)} %get-tuple-element.124.a0), channel_id=1, source_target_pairs={{0,16},{8,24},{16,0},{24,8},{32,48},{40,56},{48,32},{56,40},{64,80... | collective-permute-start | bytes 442376 | tf_op jit(solution)/shard_map/ppermute | solution.py:354
  34.2 0.1 collective-permute-start.14
  34.3 1.4 %collective-permute-start.13 = (f32[48,768]{1,0:T(8,128)S(1)}, f32[48,768]{1,0:T(8,128)S(1)}, u32[]{:S(2)}, u32[]{:S(2)}) collective-permute-start(f32[48,768]{1,0:T(8,128)S(1)} %get-tuple-element.124.a0), channel_id=1, source_target_pairs={{0,8},{8,16},{16,24},{24,0},{32,40},{40,48},{48,56},{56,32},{64,72... | collective-permute-start | bytes 442376 | tf_op jit(solution)/shard_map/ppermute | solution.py:354
  35.7 6.7 %all-to-all-start.3 = ((f32[16,48,256]{2,1,0:T(8,128)}), f32[16,48,256]{2,1,0:T(8,128)S(1)}, u32[]{:S(2)}, u32[]{:S(2)}) async-start(f32[16,48,256]{2,1,0:T(8,128)} %bitcast.12), calls=%async_computation.3 | async-start | bytes 1572864 | tf_op jit(solution)/shard_map/all_to_all | solution.py:416
  42.4 5.2 %shard_map.80 = (f32[512,256]{1,0:T(8,128)}, f32[512,768]{1,0:T(8,128)}, f32[8,128]{1,0:T(8,128)S(1)}) custom-call(f32[2176,128]{1,0:T(8,128)S(1)} %bitcast.28, f32[512,1024]{1,0:T(8,128)} %bitcast.24), custom_call_target="tpu_custom_call" | custom-call | flops 4000000000 | bytes 6000000 | tf_op jit(solution)/shard_map/pallas_call | solution.py:417
  47.5 0.0 collective-permute-done.15.a3
  47.5 0.0 collective-permute-done.14.a2
  47.6 0.0 collective-permute-done.13.a1
  47.6 1.9 %collective-permute-start.18 = (f32[192,768]{1,0:T(8,128)S(1)}, f32[192,768]{1,0:T(8,128)}, u32[]{:S(2)}, u32[]{:S(2)}) collective-permute-start(f32[192,768]{1,0:T(8,128)S(1)} %shard_map.81), channel_id=1, source_target_pairs={{0,64},{8,72},{16,80},{24,88},{32,96},{40,104},{48,112},{56,120},{... | collective-permute-start | bytes 1769480 | tf_op jit(solution)/shard_map/ppermute | solution.py:354
  49.5 1.2 %collective-permute-start.17 = (f32[192,768]{1,0:T(8,128)S(1)}, f32[192,768]{1,0:T(8,128)}, u32[]{:S(2)}, u32[]{:S(2)}) collective-permute-start(f32[192,768]{1,0:T(8,128)S(1)} %shard_map.81), channel_id=1, source_target_pairs={{0,96},{8,104},{16,112},{24,120},{32,0},{40,8},{48,16},{56,24},{64... | collective-permute-start | bytes 1769480 | tf_op jit(solution)/shard_map/ppermute | solution.py:354
  50.7 0.3 collective-permute-start.16
  51.5 0.7 all-to-all-done.3
  52.2 1.4 %shard_map.79 = f32[512,256]{1,0:T(8,128)} custom-call(bf16[512,768]{1,0:T(8,128)(2,1)S(1)} %get-tuple-element.112.slot, f32[768,256]{1,0:T(8,128)S(1)} %bitcast.21), custom_call_target="tpu_custom_call" | custom-call | flops 100000000 | bytes 1000000 | tf_op jit(solution)/shard_map/pallas_call | solution.py:427
  53.6 50.3 %conditional.2 = (f32[512,256]{1,0:T(8,128)}, f32[512,256]{1,0:T(8,128)}, f32[512,256]{1,0:T(8,128)}, f32[512,256]{1,0:T(8,128)}, f32[512,256]{1,0:T(8,128)}) conditional(s32[]{:T(128)} %bitcast.5, () %tuple.22, (s32[]{:T(128)}, f32[512,256]{1,0:T(8,128)}, f32[512,256]{1,0:T(8,128)S(1)}, s32[3]{0:T(128)S(1)}, f32[2,512,128]{2,1,0:T(8,128)}) %tuple.33), branch_computations={%region_0.0_spmd, %region_1.2_spmd} | conditional | flops 2000262144 | bytes 22874760 | solution.py:449
  53.6 3.3 %collective-permute-start = (f32[512,256]{1,0:T(8,128)}, f32[512,256]{1,0:T(8,128)S(1)}, u32[]{:S(2)}, u32[]{:S(2)}) collective-permute-start(f32[512,256]{1,0:T(8,128)} %get-tuple-element.60.w_own), channel_id=1, source_target_pairs={{0,1},{1,0},{2,3},{3,2},{4,5},{5,4},{6,7},{7,6},{8,9},{9,8},{10,11... | collective-permute-start | bytes 1572872 | tf_op jit(solution)/shard_map/cond/branch_1_fun/ppermute | solution.py:342
  56.9 0.1 collective-permute-start.1
  57.0 1.7 %collective-permute-done.w_other = f32[512,256]{1,0:T(8,128)S(1)} collective-permute-done((f32[512,256]{1,0:T(8,128)}, f32[512,256]{1,0:T(8,128)S(1)}, u32[]{:S(2)}, u32[]{:S(2)}) %collective-permute-start) | collective-permute-done | bytes 524320 | tf_op jit(solution)/shard_map/cond/branch_1_fun/ppermute | solution.py:342
  58.6 0.5 collective-permute-done.1.r_other
  59.2 5.2 %branch_1_fun.2 = (f32[512,256]{1,0:T(8,128)S(1)}, f32[512,256]{1,0:T(8,128)}) custom-call(s32[3]{0:T(128)S(1)} %get-tuple-element.59.place, f32[512,256]{1,0:T(8,128)} %get-tuple-element.60.w_own, f32[512,256]{1,0:T(8,128)S(1)} %collective-permute-done.w_other, f32[512,256]{1,0:T(8,128)} %copy-done.14, f32[512,256]{1,0:T(8,128)S(1)} %collective-permute-done.1.r_other, ...), custom_call_target="tpu_custom_call" | custom-call | flops 2000000000 | bytes 4000000 | tf_op jit(solution)/shard_map/cond/branch_1_fun/pallas_call | solution.py:432
  64.3 1.5 %collective-permute-start.3 = (f32[512,256]{1,0:T(8,128)S(1)}, f32[512,256]{1,0:T(8,128)}, u32[]{:S(2)}, u32[]{:S(2)}) collective-permute-start(f32[512,256]{1,0:T(8,128)S(1)} %get-tuple-element.63), channel_id=1, source_target_pairs={{0,2},{1,7},{8,10},{9,15},{16,18},{17,23},{24,26},{25,31},{32,34},... | collective-permute-start | bytes 1572872 | tf_op jit(solution)/shard_map/cond/branch_1_fun/ppermute | solution.py:438
  65.8 1.5 %collective-permute-start.2 = (f32[512,256]{1,0:T(8,128)S(1)}, f32[512,256]{1,0:T(8,128)}, u32[]{:S(2)}, u32[]{:S(2)}) collective-permute-start(f32[512,256]{1,0:T(8,128)S(1)} %get-tuple-element.63), channel_id=1, source_target_pairs={{1,3},{0,6},{9,11},{8,14},{17,19},{16,22},{25,27},{24,30},{33,35},... | collective-permute-start | bytes 1572872 | tf_op jit(solution)/shard_map/cond/branch_1_fun/ppermute | solution.py:439
  67.2 0.0 collective-permute-done.3
  67.2 1.3 %collective-permute-start.4 = (f32[512,256]{1,0:T(8,128)}, f32[512,256]{1,0:T(8,128)}, u32[]{:S(2)}, u32[]{:S(2)}) collective-permute-start(f32[512,256]{1,0:T(8,128)} %collective-permute-done.3), channel_id=1, source_target_pairs={{2,4},{7,5},{10,12},{15,13},{18,20},{23,21},{26,28},{31,29},{34,36... | collective-permute-start | bytes 1572872 | tf_op jit(solution)/shard_map/cond/branch_1_fun/ppermute | solution.py:440
  68.5 0.0 collective-permute-done.2
  68.6 0.9 select_select_fusion
  69.5 1.5 %collective-permute-start.5 = (f32[512,256]{1,0:T(8,128)}, f32[512,256]{1,0:T(8,128)}, u32[]{:S(2)}, u32[]{:S(2)}) collective-permute-start(f32[512,256]{1,0:T(8,128)} %select_select_fusion), channel_id=1, source_target_pairs={{0,1},{1,0},{2,3},{3,2},{6,7},{7,6},{8,9},{9,8},{10,11},{11,10},{1... | collective-permute-start | bytes 1572872 | tf_op jit(solution)/shard_map/cond/branch_1_fun/ppermute | solution.py:442
  70.9 28.8 %collective-permute-done.4 = f32[512,256]{1,0:T(8,128)} collective-permute-done((f32[512,256]{1,0:T(8,128)}, f32[512,256]{1,0:T(8,128)}, u32[]{:S(2)}, u32[]{:S(2)}) %collective-permute-start.4) | collective-permute-done | bytes 524320 | tf_op jit(solution)/shard_map/cond/branch_1_fun/ppermute | solution.py:440
  99.7 2.3 %collective-permute-start.6 = (f32[512,256]{1,0:T(8,128)}, f32[512,256]{1,0:T(8,128)}, u32[]{:S(2)}, u32[]{:S(2)}) collective-permute-start(f32[512,256]{1,0:T(8,128)} %collective-permute-done.4), channel_id=1, source_target_pairs={{4,5},{5,4},{12,13},{13,12},{20,21},{21,20},{28,29},{29,28},{36,37... | collective-permute-start | bytes 1572872 | tf_op jit(solution)/shard_map/cond/branch_1_fun/ppermute | solution.py:443
  102.1 0.0 collective-permute-done.5
  102.1 1.8 %collective-permute-done.6 = f32[512,256]{1,0:T(8,128)} collective-permute-done((f32[512,256]{1,0:T(8,128)}, f32[512,256]{1,0:T(8,128)}, u32[]{:S(2)}, u32[]{:S(2)}) %collective-permute-start.6) | collective-permute-done | bytes 524320 | tf_op jit(solution)/shard_map/cond/branch_1_fun/ppermute | solution.py:443
  103.9 0.0 collective-permute-done.18
  103.9 0.0 collective-permute-done.17
  103.9 0.0 collective-permute-done.16
  103.9 7.8 %conditional.3 = (f32[2,256,4,256]{3,2,1,0:T(4,128)}) conditional(s32[]{:T(128)} %bitcast.5, (f32[2176,128]{1,0:T(8,128)}, f32[512,1024]{1,0:T(8,128)S(1)}, s32[512,128]{1,0:T(8,128)S(1)}, s32[]{:T(128)}, s32[3]{0:T(128)S(1)}, /*index=5*/f32[2,512,128]{2,1,0:T(8,128)}) %tuple.32, (s32[3]{0:T(128)S(1)}, f32[512,256]{1,0:T(8,128)}, ...), branch_computations={%region_2.4_spmd, %region_4.5_spmd} | conditional | flops 8000884736 | bytes 85798736 | solution.py:493
  104.2 7.6 %branch_1_fun.3 = f32[2,256,4,256]{3,2,1,0:T(4,128)} custom-call(s32[3]{0:T(128)S(1)} %get-tuple-element.75.place, f32[512,256]{1,0:T(8,128)} %get-tuple-element.76.n_early, f32[512,256]{1,0:T(8,128)} %get-tuple-element.77.n_last, f32[512,256]{1,0:T(8,128)} %get-tuple-element.78.o_early, f32[512,256]{1,0:T(8,128)} %get-tuple-element.79.o_last, ...), custom_call_target="tpu_custom_call" | custom-call | flops 4000000000 | bytes 8000000 | tf_op jit(solution)/shard_map/cond/branch_1_fun/pallas_call | solution.py:452
  (16 shorter events, 0.1 us)
Async XLA Ops:
  0.1 13.2 %copy-start.5 = (s32[2,4,16,256]{3,2,1,0:T(8,128)S(1)}, s32[2,4,16,256]{3,2,1,0:T(8,128)}, u32[]{:S(2)}) copy-start(s32[2,4,16,256]{3,2,1,0:T(8,128)} %level_picks.1) | copy-start | bytes 393220
  0.1 13.2 %copy-start.6 = (s32[2,16,256]{2,1,0:T(8,128)S(1)}, s32[2,16,256]{2,1,0:T(8,128)}, u32[]{:S(2)}) copy-start(s32[2,16,256]{2,1,0:T(8,128)} %local_picks.1) | copy-start | bytes 98308
  0.1 13.2 %copy-start.7 = (s32[2,256]{1,0:T(2,128)S(1)}, s32[2,256]{1,0:T(2,128)}, u32[]{:S(2)}) copy-start(s32[2,256]{1,0:T(2,128)} %order.1) | copy-start | bytes 6148
  2.9 25.7 %all-to-all-start.2 = ((f32[2176,1,128]{2,1,0:T(1,128)}), f32[2176,1,128]{2,1,0:T(1,128)S(1)}, u32[]{:S(2)}, u32[]{:S(2)}) async-start(f32[2176,1,128]{2,1,0:T(1,128)} %bitcast.29), calls=%async_computation.2 | async-start | bytes 2228224 | tf_op jit(solution)/shard_map/all_to_all | solution.py:388
  13.3 3.4 %copy-start.12 = (f32[2,256,4,256]{3,2,1,0:T(4,128)S(1)}, f32[2,256,4,256]{3,2,1,0:T(4,128)}, u32[]{:S(2)}) copy-start(f32[2,256,4,256]{3,2,1,0:T(4,128)} %param.11) | copy-start | bytes 6291460
  17.2 1.3 %copy-start.8 = (f32[64,8,4,256]{3,1,2,0:T(8,128)}, f32[64,8,4,256]{3,1,2,0:T(8,128)S(1)}, u32[]{:S(2)}) copy-start(f32[64,8,4,256]{3,1,2,0:T(8,128)S(1)} %copy.11) | copy-start | bytes 6291460
  28.7 1.0 copy-start.10
  29.7 12.7 %copy-start.11 = (f32[2176,1,128]{2,1,0:T(1,128)S(1)}, f32[2176,1,128]{2,1,0:T(1,128)}, u32[]{:S(2)}) copy-start(f32[2176,1,128]{2,1,0:T(1,128)} %copy-done.10) | copy-start | bytes 3342340
  32.4 15.2 %collective-permute-start.15 = (f32[48,768]{1,0:T(8,128)S(1)}, f32[48,768]{1,0:T(8,128)S(1)}, u32[]{:S(2)}, u32[]{:S(2)}) collective-permute-start(f32[48,768]{1,0:T(8,128)S(1)} %get-tuple-element.124.a0), channel_id=1, source_target_pairs={{0,16},{8,24},{16,0},{24,8},{32,48},{40,56},{48,32},{56,40},{64,80... | collective-permute-start | bytes 442376 | tf_op jit(solution)/shard_map/ppermute | solution.py:354
  34.2 13.4 %collective-permute-start.14 = (f32[48,768]{1,0:T(8,128)S(1)}, f32[48,768]{1,0:T(8,128)S(1)}, u32[]{:S(2)}, u32[]{:S(2)}) collective-permute-start(f32[48,768]{1,0:T(8,128)S(1)} %get-tuple-element.124.a0), channel_id=1, source_target_pairs={{0,24},{8,0},{16,8},{24,16},{32,56},{40,32},{48,40},{56,48},{64,88... | collective-permute-start | bytes 442376 | tf_op jit(solution)/shard_map/ppermute | solution.py:354
  34.3 13.3 %collective-permute-start.13 = (f32[48,768]{1,0:T(8,128)S(1)}, f32[48,768]{1,0:T(8,128)S(1)}, u32[]{:S(2)}, u32[]{:S(2)}) collective-permute-start(f32[48,768]{1,0:T(8,128)S(1)} %get-tuple-element.124.a0), channel_id=1, source_target_pairs={{0,8},{8,16},{16,24},{24,0},{32,40},{40,48},{48,56},{56,32},{64,72... | collective-permute-start | bytes 442376 | tf_op jit(solution)/shard_map/ppermute | solution.py:354
  35.7 16.6 %all-to-all-start.3 = ((f32[16,48,256]{2,1,0:T(8,128)}), f32[16,48,256]{2,1,0:T(8,128)S(1)}, u32[]{:S(2)}, u32[]{:S(2)}) async-start(f32[16,48,256]{2,1,0:T(8,128)} %bitcast.12), calls=%async_computation.3 | async-start | bytes 1572864 | tf_op jit(solution)/shard_map/all_to_all | solution.py:416
  47.6 6.0 %copy-start.13 = (f32[512,256]{1,0:T(8,128)S(1)}, f32[512,256]{1,0:T(8,128)}, u32[]{:S(2)}) copy-start(f32[512,256]{1,0:T(8,128)} %get-tuple-element.115) | copy-start | bytes 1572868
  47.6 56.3 %collective-permute-start.18 = (f32[192,768]{1,0:T(8,128)S(1)}, f32[192,768]{1,0:T(8,128)}, u32[]{:S(2)}, u32[]{:S(2)}) collective-permute-start(f32[192,768]{1,0:T(8,128)S(1)} %shard_map.81), channel_id=1, source_target_pairs={{0,64},{8,72},{16,80},{24,88},{32,96},{40,104},{48,112},{56,120},{... | collective-permute-start | bytes 1769480 | tf_op jit(solution)/shard_map/ppermute | solution.py:354
  49.5 54.4 %collective-permute-start.17 = (f32[192,768]{1,0:T(8,128)S(1)}, f32[192,768]{1,0:T(8,128)}, u32[]{:S(2)}, u32[]{:S(2)}) collective-permute-start(f32[192,768]{1,0:T(8,128)S(1)} %shard_map.81), channel_id=1, source_target_pairs={{0,96},{8,104},{16,112},{24,120},{32,0},{40,8},{48,16},{56,24},{64... | collective-permute-start | bytes 1769480 | tf_op jit(solution)/shard_map/ppermute | solution.py:354
  50.7 53.3 %collective-permute-start.16 = (f32[192,768]{1,0:T(8,128)S(1)}, f32[192,768]{1,0:T(8,128)}, u32[]{:S(2)}, u32[]{:S(2)}) collective-permute-start(f32[192,768]{1,0:T(8,128)S(1)} %shard_map.81), channel_id=1, source_target_pairs={{0,32},{8,40},{16,48},{24,56},{32,64},{40,72},{48,80},{56,88},{64,... | collective-permute-start | bytes 1769480 | tf_op jit(solution)/shard_map/ppermute | solution.py:354
  53.6 50.3 %copy-start.9 = (f32[64,8,4,256]{3,1,2,0:T(8,128)S(1)}, f32[64,8,4,256]{3,1,2,0:T(8,128)}, u32[]{:S(2)}) copy-start(f32[64,8,4,256]{3,1,2,0:T(8,128)} %copy-done.8) | copy-start | bytes 6291460
  53.6 5.6 %copy-start.14 = (f32[512,256]{1,0:T(8,128)}, f32[512,256]{1,0:T(8,128)S(1)}, u32[]{:S(2)}) copy-start(f32[512,256]{1,0:T(8,128)S(1)} %get-tuple-element.61.r_own) | copy-start | bytes 1572868 | tf_op jit(solution)/shard_map/cond
  53.6 5.0 %collective-permute-start = (f32[512,256]{1,0:T(8,128)}, f32[512,256]{1,0:T(8,128)S(1)}, u32[]{:S(2)}, u32[]{:S(2)}) collective-permute-start(f32[512,256]{1,0:T(8,128)} %get-tuple-element.60.w_own), channel_id=1, source_target_pairs={{0,1},{1,0},{2,3},{3,2},{4,5},{5,4},{6,7},{7,6},{8,9},{9,8},{10,11... | collective-permute-start | bytes 1572872 | tf_op jit(solution)/shard_map/cond/branch_1_fun/ppermute | solution.py:342
  56.9 2.3 %collective-permute-start.1 = (f32[512,256]{1,0:T(8,128)S(1)}, f32[512,256]{1,0:T(8,128)S(1)}, u32[]{:S(2)}, u32[]{:S(2)}) collective-permute-start(f32[512,256]{1,0:T(8,128)S(1)} %get-tuple-element.61.r_own), channel_id=1, source_target_pairs={{0,1},{1,0},{2,3},{3,2},{4,5},{5,4},{6,7},{7,6},{8,9},{9,8},{10,11... | collective-permute-start | bytes 1572872 | tf_op jit(solution)/shard_map/cond/branch_1_fun/ppermute | solution.py:342
  64.3 2.9 %collective-permute-start.3 = (f32[512,256]{1,0:T(8,128)S(1)}, f32[512,256]{1,0:T(8,128)}, u32[]{:S(2)}, u32[]{:S(2)}) collective-permute-start(f32[512,256]{1,0:T(8,128)S(1)} %get-tuple-element.63), channel_id=1, source_target_pairs={{0,2},{1,7},{8,10},{9,15},{16,18},{17,23},{24,26},{25,31},{32,34},... | collective-permute-start | bytes 1572872 | tf_op jit(solution)/shard_map/cond/branch_1_fun/ppermute | solution.py:438
  65.8 2.8 %collective-permute-start.2 = (f32[512,256]{1,0:T(8,128)S(1)}, f32[512,256]{1,0:T(8,128)}, u32[]{:S(2)}, u32[]{:S(2)}) collective-permute-start(f32[512,256]{1,0:T(8,128)S(1)} %get-tuple-element.63), channel_id=1, source_target_pairs={{1,3},{0,6},{9,11},{8,14},{17,19},{16,22},{25,27},{24,30},{33,35},... | collective-permute-start | bytes 1572872 | tf_op jit(solution)/shard_map/cond/branch_1_fun/ppermute | solution.py:439
  67.2 32.5 %collective-permute-start.4 = (f32[512,256]{1,0:T(8,128)}, f32[512,256]{1,0:T(8,128)}, u32[]{:S(2)}, u32[]{:S(2)}) collective-permute-start(f32[512,256]{1,0:T(8,128)} %collective-permute-done.3), channel_id=1, source_target_pairs={{2,4},{7,5},{10,12},{15,13},{18,20},{23,21},{26,28},{31,29},{34,36... | collective-permute-start | bytes 1572872 | tf_op jit(solution)/shard_map/cond/branch_1_fun/ppermute | solution.py:440
  69.5 32.6 %collective-permute-start.5 = (f32[512,256]{1,0:T(8,128)}, f32[512,256]{1,0:T(8,128)}, u32[]{:S(2)}, u32[]{:S(2)}) collective-permute-start(f32[512,256]{1,0:T(8,128)} %select_select_fusion), channel_id=1, source_target_pairs={{0,1},{1,0},{2,3},{3,2},{6,7},{7,6},{8,9},{9,8},{10,11},{11,10},{1... | collective-permute-start | bytes 1572872 | tf_op jit(solution)/shard_map/cond/branch_1_fun/ppermute | solution.py:442
  99.7 4.2 %collective-permute-start.6 = (f32[512,256]{1,0:T(8,128)}, f32[512,256]{1,0:T(8,128)}, u32[]{:S(2)}, u32[]{:S(2)}) collective-permute-start(f32[512,256]{1,0:T(8,128)} %collective-permute-done.4), channel_id=1, source_target_pairs={{4,5},{5,4},{12,13},{13,12},{20,21},{21,20},{28,29},{29,28},{36,37... | collective-permute-start | bytes 1572872 | tf_op jit(solution)/shard_map/cond/branch_1_fun/ppermute | solution.py:443

commit v10 on v9

--- a/solution.py
+++ b/solution.py
@@ -193,13 +193,14 @@
             rest_out[:, (u - 1) * B : u * B] = tile
 
 
-def join_kernel(done, a0, a1, a2, a3, out):
+def join_kernel(tiles_done, sort_done, a0, a1, a2, a3, out):
     size = a0.shape[0]
     for i, a in enumerate((a0, a1, a2, a3)):
         out[i * size : (i + 1) * size, :] = a[...]
 
 
-def sort_first_kernel(slot, gathered, out):
+def sort_first_kernel(slot, gathered, out, done_out):
+    done_out[...] = jnp.zeros_like(done_out)
     out[...] = pick(slot[...], gathered[...])
 
 
@@ -422,9 +423,13 @@
         flops=4 * 10**9,
         moved=6 * 10**6,
     )(payload, flat)
-    joined = call(join_kernel, shaped(4 * KEEP, cols - B), 5, scalars=0, moved=10**6)(done, *ring(send_rest, shift_x))
+    w_first, sorted_ = call(
+        sort_first_kernel, (shaped(2 * B, B), shaped(8, 128)), 2, scalars=0, flops=10**8, moved=10**6
+    )(slot, w_first)
+    joined = call(join_kernel, shaped(4 * KEEP, cols - B), 6, scalars=0, moved=10**6)(
+        done, sorted_, *ring(send_rest, shift_x)
+    )
     w_parts = ring(joined, shift_y)
-    w_first = call(sort_first_kernel, shaped(2 * B, B), 2, scalars=0, flops=10**8, moved=10**6)(slot, w_first)
 
     def panels(w_first, first, active, place, joined):
         r_other = core_swap(first)

time: 112 us -> 105 us (0.938)
  the two profiles are of different devices: /device:TPU:75 before, /device:TPU:65 now
where the time goes in v10:
time: 105 us
  waiting for transfers between devices  39.3 us (37%)
  starting transfers between devices  34.1 us (32%)
  Pallas kernels  27.5 us (26%)
  local copies, waits for them, and re-layouts  1.82 us (2%)
    ppermute x1, waiting for transfers between devices, panels(): last = lax.ppermute(step, 'pcol', [(2, 4), (7, 5)])  17 us
    all_to_all x1, waiting for transfers between devices, body(): lax.all_to_all(payload, ('prow', 'pcol'), 0, 0, tiled=True)  11.2 us
    all_to_all x1, starting transfers between devices, body(): lax.all_to_all(payload, ('prow', 'pcol'), 0, 0, tiled=True)  10.4 us
    ppermute x6, starting transfers between devices, ring(): return [x] + [lax.ppermute(x, 'prow', shift(step)) for step in (1, -1, 2)]  8.57 us
    pallas_call x1, Pallas kernels, finish(): pl.pallas_call(finish_kernel, out_shape=shaped(*front.shape), in_specs=[S...  7.58 us
    pallas_call x1, Pallas kernels, body(): call(tiles_kernel, (shaped(rows, B), shaped(rows, cols - B), shaped(8, 12...  5.5 us
    pallas_call x1, Pallas kernels, panels(): call(panel_kernel, (shaped(rows, B), shaped(rows, B)), 6, flops=2 * 10 **...  4.84 us
    ppermute x1, starting transfers between devices, panels(): o_last = lax.ppermute(last, 'pcol', [(4, 5), (5, 4)])  3.89 us
  transfers between devices with their start and end apart: 15, of which 8 were waited for; matrix products, arithmetic and copies ran while one was open for 1% of the time, Pallas kernels for 15%

profile of v10, /device:TPU:65, one launch (start us, length us, event | category | flops | bytes accessed | tf_op | source)
XLA Modules:
  0.0 104.9 jit_solution(4634431465800112595)
XLA Ops:
  0.0 0.1 pad_add_fusion.place
  0.1 2.9 %shard_map.76 = f32[2176,128]{1,0:T(8,128)} custom-call(s32[3]{0:T(128)S(1)} %pad_add_fusion.place, f32[128,8,256]{2,1,0:T(8,128)} %bitcast.31, s32[8,128]{1,0:T(8,128)} %bitcast.32, s32[1,128]{1,0:T(1,128)} %counts_hbm.1), custom_call_target="tpu_custom_call" | custom-call | flops 1000000 | bytes 2000000 | tf_op jit(solution)/shard_map/pallas_call | solution.py:375
  2.9 10.4 %all-to-all-start.2 = ((f32[2176,1,128]{2,1,0:T(1,128)}), f32[2176,1,128]{2,1,0:T(1,128)S(1)}, u32[]{:S(2)}, u32[]{:S(2)}) async-start(f32[2176,1,128]{2,1,0:T(1,128)} %bitcast.29), calls=%async_computation.2 | async-start | bytes 2228224 | tf_op jit(solution)/shard_map/all_to_all | solution.py:389
  13.3 0.0 copy-done.5
  13.3 0.0 copy-start.11
  13.4 3.4 %shard_map.75 = (s32[512,128]{1,0:T(8,128)S(1)}, f32[2,512,128]{2,1,0:T(8,128)}, s32[48,128]{1,0:T(8,128)S(1)}, bf16[512,768]{1,0:T(8,128)(2,1)S(1)}, bf16[512,768]{1,0:T(8,128)(2,1)}, /*index=5*/s32[1]{0:T(128)}) custom-call(s32[3]{0:T(128)S(1)} %pad_add_fusion.place, s32[2,16,256]{2,1,0:T(8,128)S(1)} %copy-done.6, s32[2,4,16,256]{3,2,1,0:T(8,128)S(1)} %copy-done.5, ...), custom_call_target="tpu_custom_call" | custom-call | flops 1000000000 | bytes 1000000 | tf_op jit(solution)/shard_map/pallas_call | solution.py:393
  16.7 0.5 copy.11
  17.2 0.0 copy-start.8
  17.2 1.3 %copy-done.8 = f32[64,8,4,256]{3,1,2,0:T(8,128)} copy-done((f32[64,8,4,256]{3,1,2,0:T(8,128)}, f32[64,8,4,256]{3,1,2,0:T(8,128)S(1)}, u32[]{:S(2)}) %copy-start.8) | copy-done | bytes 2097176
  18.5 0.6 shard_map.77.front_rows
  19.1 11.2 %all-to-all-done.2 = f32[2176,1,128]{2,1,0:T(1,128)S(1)} async-done(((f32[2176,1,128]{2,1,0:T(1,128)}), f32[2176,1,128]{2,1,0:T(1,128)S(1)}, u32[]{:S(2)}, u32[]{:S(2)}) %all-to-all-start.2) | async-done | bytes 1114144 | tf_op jit(solution)/shard_map/all_to_all | solution.py:389
  30.3 1.4 %shard_map.78 = (f32[768,256]{1,0:T(8,128)}, f32[48,768]{1,0:T(8,128)S(1)}) custom-call(f32[2176,128]{1,0:T(8,128)S(1)} %bitcast.26, f32[192,256]{1,0:T(8,128)S(1)} %shard_map.77.front_rows, s32[48,128]{1,0:T(8,128)S(1)} %get-tuple-element.115.give), custom_call_target="tpu_custom_call" | custom-call | flops 100000000 | bytes 2000000 | tf_op jit(solution)/shard_map/pallas_call | solution.py:414
  31.6 3.8 %all-to-all-start.3 = ((f32[16,48,256]{2,1,0:T(8,128)}), f32[16,48,256]{2,1,0:T(8,128)S(1)}, u32[]{:S(2)}, u32[]{:S(2)}) async-start(f32[16,48,256]{2,1,0:T(8,128)} %bitcast.12), calls=%async_computation.3 | async-start | bytes 1572864 | tf_op jit(solution)/shard_map/all_to_all | solution.py:417
  35.4 2.9 %collective-permute-start.15 = (f32[48,768]{1,0:T(8,128)S(1)}, f32[48,768]{1,0:T(8,128)S(1)}, u32[]{:S(2)}, u32[]{:S(2)}) collective-permute-start(f32[48,768]{1,0:T(8,128)S(1)} %get-tuple-element.128.a0), channel_id=1, source_target_pairs={{0,16},{8,24},{16,0},{24,8},{32,48},{40,56},{48,32},{56,40},{64,80... | collective-permute-start | bytes 442376 | tf_op jit(solution)/shard_map/ppermute | solution.py:355
  38.3 0.9 collective-permute-start.14
  39.1 0.6 collective-permute-start.13
  39.7 5.5 %shard_map.80 = (f32[512,256]{1,0:T(8,128)}, f32[512,768]{1,0:T(8,128)}, f32[8,128]{1,0:T(8,128)S(1)}) custom-call(f32[2176,128]{1,0:T(8,128)} %bitcast.27, f32[512,1024]{1,0:T(8,128)} %bitcast.24), custom_call_target="tpu_custom_call" | custom-call | flops 4000000000 | bytes 6000000 | tf_op jit(solution)/shard_map/pallas_call | solution.py:418
  45.2 3.2 %all-to-all-done.3 = f32[16,48,256]{2,1,0:T(8,128)S(1)} async-done(((f32[16,48,256]{2,1,0:T(8,128)}), f32[16,48,256]{2,1,0:T(8,128)S(1)}, u32[]{:S(2)}, u32[]{:S(2)}) %all-to-all-start.3) | async-done | bytes 786464 | tf_op jit(solution)/shard_map/all_to_all | solution.py:417
  48.4 1.4 %shard_map.79 = (f32[512,256]{1,0:T(8,128)}, f32[8,128]{1,0:T(8,128)S(1)}) custom-call(bf16[512,768]{1,0:T(8,128)(2,1)S(1)} %get-tuple-element.114.slot, f32[768,256]{1,0:T(8,128)S(1)} %bitcast.21), custom_call_target="tpu_custom_call" | custom-call | flops 100000000 | bytes 1000000 | tf_op jit(solution)/shard_map/pallas_call | solution.py:426
  49.8 0.0 collective-permute-done.15.a3
  49.8 1.6 %collective-permute-done.14.a2 = f32[48,768]{1,0:T(8,128)S(1)} collective-permute-done((f32[48,768]{1,0:T(8,128)S(1)}, f32[48,768]{1,0:T(8,128)S(1)}, u32[]{:S(2)}, u32[]{:S(2)}) %collective-permute-start.14) | collective-permute-done | bytes 147488 | tf_op jit(solution)/shard_map/ppermute | solution.py:355
  51.4 2.2 %collective-permute-done.13.a1 = f32[48,768]{1,0:T(8,128)S(1)} collective-permute-done((f32[48,768]{1,0:T(8,128)S(1)}, f32[48,768]{1,0:T(8,128)S(1)}, u32[]{:S(2)}, u32[]{:S(2)}) %collective-permute-start.13) | collective-permute-done | bytes 147488 | tf_op jit(solution)/shard_map/ppermute | solution.py:355
  53.7 2.8 %collective-permute-start.18 = (f32[192,768]{1,0:T(8,128)S(1)}, f32[192,768]{1,0:T(8,128)}, u32[]{:S(2)}, u32[]{:S(2)}) collective-permute-start(f32[192,768]{1,0:T(8,128)S(1)} %shard_map.81), channel_id=1, source_target_pairs={{0,64},{8,72},{16,80},{24,88},{32,96},{40,104},{48,112},{56,120},{... | collective-permute-start | bytes 1769480 | tf_op jit(solution)/shard_map/ppermute | solution.py:355
  56.5 0.9 collective-permute-start.17
  57.4 0.6 collective-permute-start.16
  58.5 0.0 copy-start.9
  58.6 38.3 %conditional.2 = (f32[512,256]{1,0:T(8,128)}, f32[512,256]{1,0:T(8,128)}, f32[512,256]{1,0:T(8,128)}, f32[512,256]{1,0:T(8,128)}, f32[512,256]{1,0:T(8,128)}) conditional(s32[]{:T(128)} %bitcast.5, () %tuple.22, (s32[]{:T(128)}, f32[512,256]{1,0:T(8,128)}, f32[512,256]{1,0:T(8,128)S(1)}, s32[3]{0:T(128)S(1)}, f32[2,512,128]{2,1,0:T(8,128)S(1)}) %tuple.34), branch_computations={%region_0.0_spmd, %region_1.2_spmd} | conditional | flops 2000262144 | bytes 20777580 | solution.py:454
  58.6 1.8 %collective-permute-start = (f32[512,256]{1,0:T(8,128)}, f32[512,256]{1,0:T(8,128)S(1)}, u32[]{:S(2)}, u32[]{:S(2)}) collective-permute-start(f32[512,256]{1,0:T(8,128)} %get-tuple-element.60.w_own), channel_id=1, source_target_pairs={{0,1},{1,0},{2,3},{3,2},{4,5},{5,4},{6,7},{7,6},{8,9},{9,8},{10,11... | collective-permute-start | bytes 1572872 | tf_op jit(solution)/shard_map/cond/branch_1_fun/ppermute | solution.py:343
  60.4 0.1 collective-permute-start.1
  60.4 1.7 %collective-permute-done.w_other = f32[512,256]{1,0:T(8,128)S(1)} collective-permute-done((f32[512,256]{1,0:T(8,128)}, f32[512,256]{1,0:T(8,128)S(1)}, u32[]{:S(2)}, u32[]{:S(2)}) %collective-permute-start) | collective-permute-done | bytes 524320 | tf_op jit(solution)/shard_map/cond/branch_1_fun/ppermute | solution.py:343
  62.1 0.5 collective-permute-done.1.r_other
  62.6 4.8 %branch_1_fun.2 = (f32[512,256]{1,0:T(8,128)S(1)}, f32[512,256]{1,0:T(8,128)}) custom-call(s32[3]{0:T(128)S(1)} %get-tuple-element.59.place, f32[512,256]{1,0:T(8,128)} %get-tuple-element.60.w_own, f32[512,256]{1,0:T(8,128)S(1)} %collective-permute-done.w_other, f32[512,256]{1,0:T(8,128)S(1)} %get-tuple-element.61.r_own, ...), custom_call_target="tpu_custom_call" | custom-call | flops 2000000000 | bytes 4000000 | tf_op jit(solution)/shard_map/cond/branch_1_fun/pallas_call | solution.py:437
  67.5 1.5 %collective-permute-start.3 = (f32[512,256]{1,0:T(8,128)S(1)}, f32[512,256]{1,0:T(8,128)}, u32[]{:S(2)}, u32[]{:S(2)}) collective-permute-start(f32[512,256]{1,0:T(8,128)S(1)} %get-tuple-element.63), channel_id=1, source_target_pairs={{0,2},{1,7},{8,10},{9,15},{16,18},{17,23},{24,26},{25,31},{32,34},... | collective-permute-start | bytes 1572872 | tf_op jit(solution)/shard_map/cond/branch_1_fun/ppermute | solution.py:443
  68.9 1.5 %collective-permute-start.2 = (f32[512,256]{1,0:T(8,128)S(1)}, f32[512,256]{1,0:T(8,128)}, u32[]{:S(2)}, u32[]{:S(2)}) collective-permute-start(f32[512,256]{1,0:T(8,128)S(1)} %get-tuple-element.63), channel_id=1, source_target_pairs={{1,3},{0,6},{9,11},{8,14},{17,19},{16,22},{25,27},{24,30},{33,35},... | collective-permute-start | bytes 1572872 | tf_op jit(solution)/shard_map/cond/branch_1_fun/ppermute | solution.py:444
  70.4 0.0 collective-permute-done.3
  70.4 1.3 %collective-permute-start.4 = (f32[512,256]{1,0:T(8,128)}, f32[512,256]{1,0:T(8,128)}, u32[]{:S(2)}, u32[]{:S(2)}) collective-permute-start(f32[512,256]{1,0:T(8,128)} %collective-permute-done.3), channel_id=1, source_target_pairs={{2,4},{7,5},{10,12},{15,13},{18,20},{23,21},{26,28},{31,29},{34,36... | collective-permute-start | bytes 1572872 | tf_op jit(solution)/shard_map/cond/branch_1_fun/ppermute | solution.py:445
  71.7 0.0 collective-permute-done.2
  71.7 0.9 select_select_fusion
  72.6 1.5 %collective-permute-start.5 = (f32[512,256]{1,0:T(8,128)}, f32[512,256]{1,0:T(8,128)}, u32[]{:S(2)}, u32[]{:S(2)}) collective-permute-start(f32[512,256]{1,0:T(8,128)} %select_select_fusion), channel_id=1, source_target_pairs={{0,1},{1,0},{2,3},{3,2},{6,7},{7,6},{8,9},{9,8},{10,11},{11,10},{1... | collective-permute-start | bytes 1572872 | tf_op jit(solution)/shard_map/cond/branch_1_fun/ppermute | solution.py:447
  74.1 17.0 %collective-permute-done.4 = f32[512,256]{1,0:T(8,128)} collective-permute-done((f32[512,256]{1,0:T(8,128)}, f32[512,256]{1,0:T(8,128)}, u32[]{:S(2)}, u32[]{:S(2)}) %collective-permute-start.4) | collective-permute-done | bytes 524320 | tf_op jit(solution)/shard_map/cond/branch_1_fun/ppermute | solution.py:445
  91.1 3.9 %collective-permute-start.6 = (f32[512,256]{1,0:T(8,128)}, f32[512,256]{1,0:T(8,128)}, u32[]{:S(2)}, u32[]{:S(2)}) collective-permute-start(f32[512,256]{1,0:T(8,128)} %collective-permute-done.4), channel_id=1, source_target_pairs={{4,5},{5,4},{12,13},{13,12},{20,21},{21,20},{28,29},{29,28},{36,37... | collective-permute-start | bytes 1572872 | tf_op jit(solution)/shard_map/cond/branch_1_fun/ppermute | solution.py:448
  95.0 0.0 collective-permute-done.5
  95.0 1.8 %collective-permute-done.6 = f32[512,256]{1,0:T(8,128)} collective-permute-done((f32[512,256]{1,0:T(8,128)}, f32[512,256]{1,0:T(8,128)}, u32[]{:S(2)}, u32[]{:S(2)}) %collective-permute-start.6) | collective-permute-done | bytes 524320 | tf_op jit(solution)/shard_map/cond/branch_1_fun/ppermute | solution.py:448
  96.9 0.0 collective-permute-done.18
  96.9 0.0 collective-permute-done.17
  96.9 0.0 collective-permute-done.16
  96.9 7.8 %conditional.3 = (f32[2,256,4,256]{3,2,1,0:T(4,128)}) conditional(s32[]{:T(128)} %bitcast.5, (f32[2176,128]{1,0:T(8,128)}, f32[512,1024]{1,0:T(8,128)S(1)}, s32[512,128]{1,0:T(8,128)S(1)}, s32[]{:T(128)}, s32[3]{0:T(128)S(1)}, /*index=5*/f32[2,512,128]{2,1,0:T(8,128)}) %tuple.32, (s32[3]{0:T(128)S(1)}, f32[512,256]{1,0:T(8,128)}, ...), branch_computations={%region_2.4_spmd, %region_4.5_spmd} | conditional | flops 8000884736 | bytes 85798736 | solution.py:498
  97.2 7.6 %branch_1_fun.3 = f32[2,256,4,256]{3,2,1,0:T(4,128)} custom-call(s32[3]{0:T(128)S(1)} %get-tuple-element.75.place, f32[512,256]{1,0:T(8,128)} %get-tuple-element.76.n_early, f32[512,256]{1,0:T(8,128)} %get-tuple-element.77.n_last, f32[512,256]{1,0:T(8,128)} %get-tuple-element.78.o_early, f32[512,256]{1,0:T(8,128)} %get-tuple-element.79.o_last, ...), custom_call_target="tpu_custom_call" | custom-call | flops 4000000000 | bytes 8000000 | tf_op jit(solution)/shard_map/cond/branch_1_fun/pallas_call | solution.py:457
  (14 shorter events, 0.1 us)
Async XLA Ops:
  0.1 13.2 %copy-start.5 = (s32[2,4,16,256]{3,2,1,0:T(8,128)S(1)}, s32[2,4,16,256]{3,2,1,0:T(8,128)}, u32[]{:S(2)}) copy-start(s32[2,4,16,256]{3,2,1,0:T(8,128)} %level_picks.1) | copy-start | bytes 393220
  0.1 13.2 %copy-start.6 = (s32[2,16,256]{2,1,0:T(8,128)S(1)}, s32[2,16,256]{2,1,0:T(8,128)}, u32[]{:S(2)}) copy-start(s32[2,16,256]{2,1,0:T(8,128)} %local_picks.1) | copy-start | bytes 98308
  0.1 13.3 %copy-start.7 = (s32[2,256]{1,0:T(2,128)S(1)}, s32[2,256]{1,0:T(2,128)}, u32[]{:S(2)}) copy-start(s32[2,256]{1,0:T(2,128)} %order.1) | copy-start | bytes 6148
  2.9 27.3 %all-to-all-start.2 = ((f32[2176,1,128]{2,1,0:T(1,128)}), f32[2176,1,128]{2,1,0:T(1,128)S(1)}, u32[]{:S(2)}, u32[]{:S(2)}) async-start(f32[2176,1,128]{2,1,0:T(1,128)} %bitcast.29), calls=%async_computation.2 | async-start | bytes 2228224 | tf_op jit(solution)/shard_map/all_to_all | solution.py:389
  13.3 3.4 %copy-start.11 = (f32[2,256,4,256]{3,2,1,0:T(4,128)S(1)}, f32[2,256,4,256]{3,2,1,0:T(4,128)}, u32[]{:S(2)}) copy-start(f32[2,256,4,256]{3,2,1,0:T(4,128)} %param.11) | copy-start | bytes 6291460
  17.2 1.3 %copy-start.8 = (f32[64,8,4,256]{3,1,2,0:T(8,128)}, f32[64,8,4,256]{3,1,2,0:T(8,128)S(1)}, u32[]{:S(2)}) copy-start(f32[64,8,4,256]{3,1,2,0:T(8,128)S(1)} %copy.11) | copy-start | bytes 6291460
  30.3 1.4 %copy-start.10 = (f32[2176,1,128]{2,1,0:T(1,128)}, f32[2176,1,128]{2,1,0:T(1,128)S(1)}, u32[]{:S(2)}) copy-start(f32[2176,1,128]{2,1,0:T(1,128)S(1)} %all-to-all-done.2) | copy-start | bytes 3342340
  31.6 16.8 %all-to-all-start.3 = ((f32[16,48,256]{2,1,0:T(8,128)}), f32[16,48,256]{2,1,0:T(8,128)S(1)}, u32[]{:S(2)}, u32[]{:S(2)}) async-start(f32[16,48,256]{2,1,0:T(8,128)} %bitcast.12), calls=%async_computation.3 | async-start | bytes 1572864 | tf_op jit(solution)/shard_map/all_to_all | solution.py:417
  35.4 14.4 %collective-permute-start.15 = (f32[48,768]{1,0:T(8,128)S(1)}, f32[48,768]{1,0:T(8,128)S(1)}, u32[]{:S(2)}, u32[]{:S(2)}) collective-permute-start(f32[48,768]{1,0:T(8,128)S(1)} %get-tuple-element.128.a0), channel_id=1, source_target_pairs={{0,16},{8,24},{16,0},{24,8},{32,48},{40,56},{48,32},{56,40},{64,80... | collective-permute-start | bytes 442376 | tf_op jit(solution)/shard_map/ppermute | solution.py:355
  38.3 13.2 %collective-permute-start.14 = (f32[48,768]{1,0:T(8,128)S(1)}, f32[48,768]{1,0:T(8,128)S(1)}, u32[]{:S(2)}, u32[]{:S(2)}) collective-permute-start(f32[48,768]{1,0:T(8,128)S(1)} %get-tuple-element.128.a0), channel_id=1, source_target_pairs={{0,24},{8,0},{16,8},{24,16},{32,56},{40,32},{48,40},{56,48},{64,88... | collective-permute-start | bytes 442376 | tf_op jit(solution)/shard_map/ppermute | solution.py:355
  39.1 14.6 %collective-permute-start.13 = (f32[48,768]{1,0:T(8,128)S(1)}, f32[48,768]{1,0:T(8,128)S(1)}, u32[]{:S(2)}, u32[]{:S(2)}) collective-permute-start(f32[48,768]{1,0:T(8,128)S(1)} %get-tuple-element.128.a0), channel_id=1, source_target_pairs={{0,8},{8,16},{16,24},{24,0},{32,40},{40,48},{48,56},{56,32},{64,72... | collective-permute-start | bytes 442376 | tf_op jit(solution)/shard_map/ppermute | solution.py:355
  48.4 10.1 %copy-start.12 = (f32[512,256]{1,0:T(8,128)S(1)}, f32[512,256]{1,0:T(8,128)}, u32[]{:S(2)}) copy-start(f32[512,256]{1,0:T(8,128)} %get-tuple-element.118) | copy-start | bytes 1572868
  48.4 10.1 %copy-start.13 = (f32[2,512,128]{2,1,0:T(8,128)S(1)}, f32[2,512,128]{2,1,0:T(8,128)}, u32[]{:S(2)}) copy-start(f32[2,512,128]{2,1,0:T(8,128)} %get-tuple-element.113) | copy-start | bytes 1572868
  53.7 43.2 %collective-permute-start.18 = (f32[192,768]{1,0:T(8,128)S(1)}, f32[192,768]{1,0:T(8,128)}, u32[]{:S(2)}, u32[]{:S(2)}) collective-permute-start(f32[192,768]{1,0:T(8,128)S(1)} %shard_map.81), channel_id=1, source_target_pairs={{0,64},{8,72},{16,80},{24,88},{32,96},{40,104},{48,112},{56,120},{... | collective-permute-start | bytes 1769480 | tf_op jit(solution)/shard_map/ppermute | solution.py:355
  56.5 40.4 %collective-permute-start.17 = (f32[192,768]{1,0:T(8,128)S(1)}, f32[192,768]{1,0:T(8,128)}, u32[]{:S(2)}, u32[]{:S(2)}) collective-permute-start(f32[192,768]{1,0:T(8,128)S(1)} %shard_map.81), channel_id=1, source_target_pairs={{0,96},{8,104},{16,112},{24,120},{32,0},{40,8},{48,16},{56,24},{64... | collective-permute-start | bytes 1769480 | tf_op jit(solution)/shard_map/ppermute | solution.py:355
  57.4 39.5 %collective-permute-start.16 = (f32[192,768]{1,0:T(8,128)S(1)}, f32[192,768]{1,0:T(8,128)}, u32[]{:S(2)}, u32[]{:S(2)}) collective-permute-start(f32[192,768]{1,0:T(8,128)S(1)} %shard_map.81), channel_id=1, source_target_pairs={{0,32},{8,40},{16,48},{24,56},{32,64},{40,72},{48,80},{56,88},{64,... | collective-permute-start | bytes 1769480 | tf_op jit(solution)/shard_map/ppermute | solution.py:355
  58.5 38.4 %copy-start.9 = (f32[64,8,4,256]{3,1,2,0:T(8,128)S(1)}, f32[64,8,4,256]{3,1,2,0:T(8,128)}, u32[]{:S(2)}) copy-start(f32[64,8,4,256]{3,1,2,0:T(8,128)} %copy-done.8) | copy-start | bytes 6291460
  58.6 3.5 %collective-permute-start = (f32[512,256]{1,0:T(8,128)}, f32[512,256]{1,0:T(8,128)S(1)}, u32[]{:S(2)}, u32[]{:S(2)}) collective-permute-start(f32[512,256]{1,0:T(8,128)} %get-tuple-element.60.w_own), channel_id=1, source_target_pairs={{0,1},{1,0},{2,3},{3,2},{4,5},{5,4},{6,7},{7,6},{8,9},{9,8},{10,11... | collective-permute-start | bytes 1572872 | tf_op jit(solution)/shard_map/cond/branch_1_fun/ppermute | solution.py:343
  60.4 2.3 %collective-permute-start.1 = (f32[512,256]{1,0:T(8,128)S(1)}, f32[512,256]{1,0:T(8,128)S(1)}, u32[]{:S(2)}, u32[]{:S(2)}) collective-permute-start(f32[512,256]{1,0:T(8,128)S(1)} %get-tuple-element.61.r_own), channel_id=1, source_target_pairs={{0,1},{1,0},{2,3},{3,2},{4,5},{5,4},{6,7},{7,6},{8,9},{9,8},{10,11... | collective-permute-start | bytes 1572872 | tf_op jit(solution)/shard_map/cond/branch_1_fun/ppermute | solution.py:343
  67.5 2.9 %collective-permute-start.3 = (f32[512,256]{1,0:T(8,128)S(1)}, f32[512,256]{1,0:T(8,128)}, u32[]{:S(2)}, u32[]{:S(2)}) collective-permute-start(f32[512,256]{1,0:T(8,128)S(1)} %get-tuple-element.63), channel_id=1, source_target_pairs={{0,2},{1,7},{8,10},{9,15},{16,18},{17,23},{24,26},{25,31},{32,34},... | collective-permute-start | bytes 1572872 | tf_op jit(solution)/shard_map/cond/branch_1_fun/ppermute | solution.py:443
  68.9 2.8 %collective-permute-start.2 = (f32[512,256]{1,0:T(8,128)S(1)}, f32[512,256]{1,0:T(8,128)}, u32[]{:S(2)}, u32[]{:S(2)}) collective-permute-start(f32[512,256]{1,0:T(8,128)S(1)} %get-tuple-element.63), channel_id=1, source_target_pairs={{1,3},{0,6},{9,11},{8,14},{17,19},{16,22},{25,27},{24,30},{33,35},... | collective-permute-start | bytes 1572872 | tf_op jit(solution)/shard_map/cond/branch_1_fun/ppermute | solution.py:444
  70.4 20.7 %collective-permute-start.4 = (f32[512,256]{1,0:T(8,128)}, f32[512,256]{1,0:T(8,128)}, u32[]{:S(2)}, u32[]{:S(2)}) collective-permute-start(f32[512,256]{1,0:T(8,128)} %collective-permute-done.3), channel_id=1, source_target_pairs={{2,4},{7,5},{10,12},{15,13},{18,20},{23,21},{26,28},{31,29},{34,36... | collective-permute-start | bytes 1572872 | tf_op jit(solution)/shard_map/cond/branch_1_fun/ppermute | solution.py:445
  72.6 22.4 %collective-permute-start.5 = (f32[512,256]{1,0:T(8,128)}, f32[512,256]{1,0:T(8,128)}, u32[]{:S(2)}, u32[]{:S(2)}) collective-permute-start(f32[512,256]{1,0:T(8,128)} %select_select_fusion), channel_id=1, source_target_pairs={{0,1},{1,0},{2,3},{3,2},{6,7},{7,6},{8,9},{9,8},{10,11},{11,10},{1... | collective-permute-start | bytes 1572872 | tf_op jit(solution)/shard_map/cond/branch_1_fun/ppermute | solution.py:447
  91.1 5.8 %collective-permute-start.6 = (f32[512,256]{1,0:T(8,128)}, f32[512,256]{1,0:T(8,128)}, u32[]{:S(2)}, u32[]{:S(2)}) collective-permute-start(f32[512,256]{1,0:T(8,128)} %collective-permute-done.4), channel_id=1, source_target_pairs={{4,5},{5,4},{12,13},{13,12},{20,21},{21,20},{28,29},{29,28},{36,37... | collective-permute-start | bytes 1572872 | tf_op jit(solution)/shard_map/cond/branch_1_fun/ppermute | solution.py:448

commit v11 on v9

--- a/solution.py
+++ b/solution.py
@@ -98,7 +98,7 @@
     give_out[...] = jnp.broadcast_to(give, (keep, 128))
 
 
-def pack_kernel(place, partials_hbm, targets_hbm, counts_hbm, out, partials, targets, counts, sems):
+def pack_kernel(place, partials_hbm, targets_hbm, counts_hbm, out_hbm, partials, targets, counts, out, sems, out_sems):
     slots, sources = targets.shape
     parts = sems.shape[0] - 2
     step = sources // parts
@@ -120,12 +120,18 @@
     codes = jnp.concatenate([codes] * (128 // slots), axis=0)
     codes = jnp.where(iota(codes.shape, 0) // slots == place[2] % (128 // slots), codes, 0)
     row = codes.astype(F32).T
+    sent = []
     for i in range(parts):
         large[i].wait()
         for s in range(i * step, (i + 1) * step):
             out[17 * s : 17 * s + 8, :] = partials[s, :, :128]
             out[17 * s + 8 : 17 * s + 16, :] = partials[s, :, 128:]
             out[17 * s + 16 : 17 * s + 17, :] = row[s : s + 1, :]
+        span = slice(17 * step * i, 17 * step * (i + 1))
+        sent.append(pltpu.make_async_copy(out.at[span], out_hbm.at[span], out_sems.at[i]))
+        sent[-1].start()
+    for copy in sent:
+        copy.wait()
 
 
 def unpack(payload):
@@ -181,8 +187,7 @@
         send_rest[:, (u - 1) * B : u * B] = sums[u * keep : (u + 1) * keep]
 
 
-def tiles_kernel(payload, front, first_out, rest_out, done_out):
-    done_out[...] = jnp.zeros_like(done_out)
+def tiles_kernel(payload, front, first_out, rest_out):
     (high, low), code = unpack(payload)
     for u in range(4):
         hot = hot_of(code, front.shape[0], u)
@@ -193,14 +198,11 @@
             rest_out[:, (u - 1) * B : u * B] = tile
 
 
-def join_kernel(done, a0, a1, a2, a3, out):
+def first_kernel(r_done, slot, gathered, a0, a1, a2, a3, first_out, joined_out):
     size = a0.shape[0]
-    for i, a in enumerate((a0, a1, a2, a3)):
-        out[i * size : (i + 1) * size, :] = a[...]
-
-
-def sort_first_kernel(slot, gathered, out):
-    out[...] = pick(slot[...], gathered[...])
+    for i, part in enumerate((a0, a1, a2, a3)):
+        joined_out[i * size : (i + 1) * size, :] = part[...]
+    first_out[...] = pick(slot[...], gathered[...])
 
 
 def inverse_of(diag):
@@ -375,12 +377,14 @@
         pack_kernel,
         out_shape=shaped(sources * 17, 128),
         in_specs=[SM, HBM, HBM, HBM],
-        out_specs=VM,
+        out_specs=HBM,
         scratch_shapes=[
             pltpu.VMEM((sources, slots, B), F32),
             pltpu.VMEM((slots, sources), jnp.int32),
             pltpu.VMEM((1, sources), jnp.int32),
+            pltpu.VMEM((sources * 17, 128), F32),
             pltpu.SemaphoreType.DMA((6,)),
+            pltpu.SemaphoreType.DMA((4,)),
         ],
         cost_estimate=pl.CostEstimate(flops=10**6, bytes_accessed=2 * 10**6, transcendentals=0),
         **ALONE,
@@ -414,21 +418,30 @@
         lead_kernel, (shaped(copies, B), shaped(KEEP, cols - B)), 3, scalars=0, flops=10**8, moved=2 * 10**6
     )(payload, front_rows, give)
     w_first = lax.all_to_all(send_first, "prow", 0, 0, tiled=True)
-    first, rest, done = call(
+    first, rest = call(
         tiles_kernel,
-        (shaped(rows, B), shaped(rows, cols - B), shaped(8, 128)),
+        (shaped(rows, B), shaped(rows, cols - B)),
         2,
         scalars=0,
         flops=4 * 10**9,
         moved=6 * 10**6,
     )(payload, flat)
-    joined = call(join_kernel, shaped(4 * KEEP, cols - B), 5, scalars=0, moved=10**6)(done, *ring(send_rest, shift_x))
+    r_other = core_swap(first)
+    whole = lambda *shape: pl.BlockSpec(shape, lambda i: (0, 0))
+    w_first, joined = pl.pallas_call(
+        first_kernel,
+        out_shape=(shaped(2 * B, B), shaped(4 * KEEP, cols - B)),
+        grid=(1,),
+        in_specs=[whole(8, 128), whole(2 * B, copies), whole(copies, B)] + [whole(KEEP, cols - B)] * 4,
+        out_specs=(whole(2 * B, B), whole(4 * KEEP, cols - B)),
+        cost_estimate=pl.CostEstimate(flops=10**8, bytes_accessed=2 * 10**6, transcendentals=0),
+        **PARAMS,
+    )(r_other, slot, w_first, *ring(send_rest, shift_x))
+    w_other = core_swap(w_first)
     w_parts = ring(joined, shift_y)
-    w_first = call(sort_first_kernel, shaped(2 * B, B), 2, scalars=0, flops=10**8, moved=10**6)(slot, w_first)
-
-    def panels(w_first, first, active, place, joined):
-        r_other = core_swap(first)
-        w_other = core_swap(w_first)
+
+
+    def panels(w_first, w_other, first, r_other, active, place, joined):
         half, tile = call(
             panel_kernel, (shaped(rows, B), shaped(rows, B)), 6, flops=2 * 10**9, moved=4 * 10**6
         )(place, w_first, w_other, first, r_other, active)
@@ -443,10 +456,10 @@
         o_last = lax.ppermute(last, "pcol", [(4, 5), (5, 4)])
         return early, last, o_early, o_last, tile
 
-    def nothing(w_first, first, active, place, joined):
+    def nothing(w_first, w_other, first, r_other, active, place, joined):
         return (jnp.zeros((rows, B), F32),) * 5
 
-    parts = lax.cond(fits[0] == 1, panels, nothing, w_first, first, active, place, joined)
+    parts = lax.cond(fits[0] == 1, panels, nothing, w_first, w_other, first, r_other, active, place, joined)
 
     def finish(payload, flat, own, active, place, *arrays):
         return pl.pallas_call(

time: 112 us -> 106 us (0.946)
  the two profiles are of different devices: /device:TPU:75 before, /device:TPU:65 now
where the time goes in v11:
time: 106 us
  waiting for transfers between devices  38.6 us (36%)
  starting transfers between devices  35.3 us (33%)
  Pallas kernels  27.3 us (26%)
  local copies, waits for them, and re-layouts  2.62 us (2%)
    ppermute x1, waiting for transfers between devices, panels(): last = lax.ppermute(step, 'pcol', [(2, 4), (7, 5)])  17 us
    all_to_all x1, waiting for transfers between devices, body(): lax.all_to_all(payload, ('prow', 'pcol'), 0, 0, tiled=True)  11.2 us
    all_to_all x1, starting transfers between devices, body(): lax.all_to_all(payload, ('prow', 'pcol'), 0, 0, tiled=True)  10.4 us
    ppermute x6, starting transfers between devices, ring(): return [x] + [lax.ppermute(x, 'prow', shift(step)) for step in (1, -1, 2)]  8.71 us
    pallas_call x1, Pallas kernels, finish(): pl.pallas_call(finish_kernel, out_shape=shaped(*front.shape), in_specs=[S...  7.59 us
    ppermute x6, waiting for transfers between devices, ring(): return [x] + [lax.ppermute(x, 'prow', shift(step)) for step in (1, -1, 2)]  7.47 us
    pallas_call x1, Pallas kernels, body(): call(tiles_kernel, (shaped(rows, B), shaped(rows, cols - B)), 2, scalars=...  5.5 us
    pallas_call x1, Pallas kernels, panels(): call(panel_kernel, (shaped(rows, B), shaped(rows, B)), 6, flops=2 * 10 **...  4.76 us
  transfers between devices with their start and end apart: 15, of which 7 were waited for; matrix products, arithmetic and copies ran while one was open for 1% of the time, Pallas kernels for 13%

profile of v11, /device:TPU:65, one launch (start us, length us, event | category | flops | bytes accessed | tf_op | source)
XLA Modules:
  0.0 106.1 jit_solution(12584897318237531761)
XLA Ops:
  0.0 0.1 pad_add_fusion.place
  0.1 2.7 %shard_map.76 = f32[2176,128]{1,0:T(8,128)} custom-call(s32[3]{0:T(128)S(1)} %pad_add_fusion.place, f32[128,8,256]{2,1,0:T(8,128)} %bitcast.31, s32[8,128]{1,0:T(8,128)} %bitcast.32, s32[1,128]{1,0:T(1,128)} %counts_hbm.1), custom_call_target="tpu_custom_call" | custom-call | flops 1000000 | bytes 2000000 | tf_op jit(solution)/shard_map/pallas_call | solution.py:376
  2.7 10.4 %all-to-all-start.2 = ((f32[2176,1,128]{2,1,0:T(1,128)}), f32[2176,1,128]{2,1,0:T(1,128)S(1)}, u32[]{:S(2)}, u32[]{:S(2)}) async-start(f32[2176,1,128]{2,1,0:T(1,128)} %bitcast.29), calls=%async_computation.2 | async-start | bytes 2228224 | tf_op jit(solution)/shard_map/all_to_all | solution.py:392
  13.1 0.0 copy-done.5
  13.1 0.0 copy-start.11
  13.1 3.4 %shard_map.75 = (s32[512,128]{1,0:T(8,128)S(1)}, f32[2,512,128]{2,1,0:T(8,128)}, s32[48,128]{1,0:T(8,128)S(1)}, bf16[512,768]{1,0:T(8,128)(2,1)S(1)}, bf16[512,768]{1,0:T(8,128)(2,1)}, /*index=5*/s32[1]{0:T(128)}) custom-call(s32[3]{0:T(128)S(1)} %pad_add_fusion.place, s32[2,16,256]{2,1,0:T(8,128)S(1)} %copy-done.6, s32[2,4,16,256]{3,2,1,0:T(8,128)S(1)} %copy-done.5, ...), custom_call_target="tpu_custom_call" | custom-call | flops 1000000000 | bytes 1000000 | tf_op jit(solution)/shard_map/pallas_call | solution.py:396
  16.5 0.5 copy.11
  17.0 0.0 copy-start.8
  17.0 1.3 %copy-done.8 = f32[64,8,4,256]{3,1,2,0:T(8,128)} copy-done((f32[64,8,4,256]{3,1,2,0:T(8,128)}, f32[64,8,4,256]{3,1,2,0:T(8,128)S(1)}, u32[]{:S(2)}) %copy-start.8) | copy-done | bytes 2097176
  18.3 0.6 shard_map.78.front_rows
  18.9 11.2 %all-to-all-done.2 = f32[2176,1,128]{2,1,0:T(1,128)S(1)} async-done(((f32[2176,1,128]{2,1,0:T(1,128)}), f32[2176,1,128]{2,1,0:T(1,128)S(1)}, u32[]{:S(2)}, u32[]{:S(2)}) %all-to-all-start.2) | async-done | bytes 1114144 | tf_op jit(solution)/shard_map/all_to_all | solution.py:392
  30.1 1.4 %shard_map.79 = (f32[768,256]{1,0:T(8,128)}, f32[48,768]{1,0:T(8,128)S(1)}) custom-call(f32[2176,128]{1,0:T(8,128)S(1)} %bitcast.26, f32[192,256]{1,0:T(8,128)S(1)} %shard_map.78.front_rows, s32[48,128]{1,0:T(8,128)S(1)} %get-tuple-element.121.give), custom_call_target="tpu_custom_call" | custom-call | flops 100000000 | bytes 2000000 | tf_op jit(solution)/shard_map/pallas_call | solution.py:417
  31.4 3.7 %all-to-all-start.3 = ((f32[16,48,256]{2,1,0:T(8,128)}), f32[16,48,256]{2,1,0:T(8,128)S(1)}, u32[]{:S(2)}, u32[]{:S(2)}) async-start(f32[16,48,256]{2,1,0:T(8,128)} %bitcast.12), calls=%async_computation.3 | async-start | bytes 1572864 | tf_op jit(solution)/shard_map/all_to_all | solution.py:420
  35.2 5.5 %shard_map.77 = (f32[512,256]{1,0:T(8,128)S(1)}, f32[512,768]{1,0:T(8,128)}) custom-call(f32[2176,128]{1,0:T(8,128)} %bitcast.27, f32[512,1024]{1,0:T(8,128)} %bitcast.24), custom_call_target="tpu_custom_call" | custom-call | flops 4000000000 | bytes 6000000 | tf_op jit(solution)/shard_map/pallas_call | solution.py:421
  40.7 1.1 %collective-permute-start.11 = (f32[512,256]{1,0:T(8,128)S(1)}, f32[512,256]{1,0:T(8,128)S(1)}, u32[]{:S(2)}, u32[]{:S(2)}) collective-permute-start(f32[512,256]{1,0:T(8,128)S(1)} %get-tuple-element.119), channel_id=1, source_target_pairs={{0,1},{1,0},{2,3},{3,2},{4,5},{5,4},{6,7},{7,6},{8,9},{9,8},{10,11... | collective-permute-start | bytes 1572872 | tf_op jit(solution)/shard_map/ppermute | solution.py:344
  41.8 3.2 %collective-permute-start.14 = (f32[48,768]{1,0:T(8,128)S(1)}, f32[48,768]{1,0:T(8,128)S(1)}, u32[]{:S(2)}, u32[]{:S(2)}) collective-permute-start(f32[48,768]{1,0:T(8,128)S(1)} %get-tuple-element.123.a0), channel_id=1, source_target_pairs={{0,16},{8,24},{16,0},{24,8},{32,48},{40,56},{48,32},{56,40},{64,80... | collective-permute-start | bytes 442376 | tf_op jit(solution)/shard_map/ppermute | solution.py:356
  44.9 0.9 collective-permute-start.13
  45.8 0.6 collective-permute-start.12
  46.4 2.9 %collective-permute-done.14.a3 = f32[48,768]{1,0:T(8,128)S(1)} collective-permute-done((f32[48,768]{1,0:T(8,128)S(1)}, f32[48,768]{1,0:T(8,128)S(1)}, u32[]{:S(2)}, u32[]{:S(2)}) %collective-permute-start.14) | collective-permute-done | bytes 147488 | tf_op jit(solution)/shard_map/ppermute | solution.py:356
  49.2 3.2 %collective-permute-done.13.a2 = f32[48,768]{1,0:T(8,128)S(1)} collective-permute-done((f32[48,768]{1,0:T(8,128)S(1)}, f32[48,768]{1,0:T(8,128)S(1)}, u32[]{:S(2)}, u32[]{:S(2)}) %collective-permute-start.13) | collective-permute-done | bytes 147488 | tf_op jit(solution)/shard_map/ppermute | solution.py:356
  52.4 1.4 %collective-permute-done.12.a1 = f32[48,768]{1,0:T(8,128)S(1)} collective-permute-done((f32[48,768]{1,0:T(8,128)S(1)}, f32[48,768]{1,0:T(8,128)S(1)}, u32[]{:S(2)}, u32[]{:S(2)}) %collective-permute-start.12) | collective-permute-done | bytes 147488 | tf_op jit(solution)/shard_map/ppermute | solution.py:356
  53.8 0.0 collective-permute-done.11.r_done
  53.8 0.0 all-to-all-done.3
  53.9 1.6 %shard_map.80 = (f32[512,256]{1,0:T(8,128)}, f32[192,768]{1,0:T(8,128)}) custom-call(f32[512,256]{1,0:T(8,128)S(1)} %collective-permute-done.11.r_done, bf16[512,768]{1,0:T(8,128)(2,1)S(1)} %get-tuple-element.120.slot, f32[768,256]{1,0:T(8,128)S(1)} %bitcast.21, f32[48,768]{1,0:T(8,128)S(1)} %get-tuple-element.123.a0, ...), custom_call_target="tpu_custom_call" | custom-call | flops 100000000 | bytes 2000000 | tf_op jit(solution)/shard_map/pallas_call | solution.py:431
  55.4 2.6 %collective-permute-start.18 = (f32[192,768]{1,0:T(8,128)}, f32[192,768]{1,0:T(8,128)}, u32[]{:S(2)}, u32[]{:S(2)}) collective-permute-start(f32[192,768]{1,0:T(8,128)} %get-tuple-element.132), channel_id=1, source_target_pairs={{0,64},{8,72},{16,80},{24,88},{32,96},{40,104},{48,112},{56,120},{... | collective-permute-start | bytes 1769480 | tf_op jit(solution)/shard_map/ppermute | solution.py:356
  58.1 0.9 collective-permute-start.17
  58.9 0.6 collective-permute-start.16
  59.5 1.7 %collective-permute-start.15 = (f32[512,256]{1,0:T(8,128)}, f32[512,256]{1,0:T(8,128)S(1)}, u32[]{:S(2)}, u32[]{:S(2)}) collective-permute-start(f32[512,256]{1,0:T(8,128)} %get-tuple-element.124), channel_id=1, source_target_pairs={{0,1},{1,0},{2,3},{3,2},{4,5},{5,4},{6,7},{7,6},{8,9},{9,8},{10,11... | collective-permute-start | bytes 1572872 | tf_op jit(solution)/shard_map/ppermute | solution.py:344
  61.9 1.1 %collective-permute-done.15 = f32[512,256]{1,0:T(8,128)S(1)} collective-permute-done((f32[512,256]{1,0:T(8,128)}, f32[512,256]{1,0:T(8,128)S(1)}, u32[]{:S(2)}, u32[]{:S(2)}) %collective-permute-start.15) | collective-permute-done | bytes 524320 | tf_op jit(solution)/shard_map/ppermute | solution.py:344
  63.0 35.0 %conditional.2 = (f32[512,256]{1,0:T(8,128)}, f32[512,256]{1,0:T(8,128)}, f32[512,256]{1,0:T(8,128)}, f32[512,256]{1,0:T(8,128)}, f32[512,256]{1,0:T(8,128)S(1)}) conditional(s32[]{:T(128)} %bitcast.5, () %tuple.22, (s32[]{:T(128)}, s32[3]{0:T(128)S(1)}, f32[512,256]{1,0:T(8,128)}, f32[512,256]{1,0:T(8,128)S(1)}, f32[512,256]{1,0:T(8,128)S(1)}, ...), branch_computations={%region_0.0_spmd, %region_1.2_spmd} | conditional | flops 2000262144 | bytes 18680376 | solution.py:462
  63.0 0.8 copy-done.12
  63.8 4.8 %branch_1_fun.2 = (f32[512,256]{1,0:T(8,128)S(1)}, f32[512,256]{1,0:T(8,128)S(1)}) custom-call(s32[3]{0:T(128)S(1)} %get-tuple-element.63.place, f32[512,256]{1,0:T(8,128)} %get-tuple-element.64.w_own, f32[512,256]{1,0:T(8,128)S(1)} %get-tuple-element.65.w_other, f32[512,256]{1,0:T(8,128)S(1)} %get-tuple-element.66.r_own, f32[512,256]{1,0:T(8,128)} %copy-done.12, ...), custom_call_target="tpu_custom_call" | custom-call | flops 2000000000 | bytes 4000000 | tf_op jit(solution)/shard_map/cond/branch_1_fun/pallas_call | solution.py:445
  68.6 1.5 %collective-permute-start.1 = (f32[512,256]{1,0:T(8,128)S(1)}, f32[512,256]{1,0:T(8,128)}, u32[]{:S(2)}, u32[]{:S(2)}) collective-permute-start(f32[512,256]{1,0:T(8,128)S(1)} %get-tuple-element.69), channel_id=1, source_target_pairs={{0,2},{1,7},{8,10},{9,15},{16,18},{17,23},{24,26},{25,31},{32,34},... | collective-permute-start | bytes 1572872 | tf_op jit(solution)/shard_map/cond/branch_1_fun/ppermute | solution.py:451
  70.1 1.5 %collective-permute-start = (f32[512,256]{1,0:T(8,128)S(1)}, f32[512,256]{1,0:T(8,128)}, u32[]{:S(2)}, u32[]{:S(2)}) collective-permute-start(f32[512,256]{1,0:T(8,128)S(1)} %get-tuple-element.69), channel_id=1, source_target_pairs={{1,3},{0,6},{9,11},{8,14},{17,19},{16,22},{25,27},{24,30},{33,35},... | collective-permute-start | bytes 1572872 | tf_op jit(solution)/shard_map/cond/branch_1_fun/ppermute | solution.py:452
  71.6 0.0 collective-permute-done.1
  71.6 1.3 %collective-permute-start.2 = (f32[512,256]{1,0:T(8,128)}, f32[512,256]{1,0:T(8,128)}, u32[]{:S(2)}, u32[]{:S(2)}) collective-permute-start(f32[512,256]{1,0:T(8,128)} %collective-permute-done.1), channel_id=1, source_target_pairs={{2,4},{7,5},{10,12},{15,13},{18,20},{23,21},{26,28},{31,29},{34,36... | collective-permute-start | bytes 1572872 | tf_op jit(solution)/shard_map/cond/branch_1_fun/ppermute | solution.py:453
  72.9 0.0 collective-permute-done
  72.9 0.9 select_select_fusion
  73.8 1.4 %collective-permute-start.3 = (f32[512,256]{1,0:T(8,128)}, f32[512,256]{1,0:T(8,128)}, u32[]{:S(2)}, u32[]{:S(2)}) collective-permute-start(f32[512,256]{1,0:T(8,128)} %select_select_fusion), channel_id=1, source_target_pairs={{0,1},{1,0},{2,3},{3,2},{6,7},{7,6},{8,9},{9,8},{10,11},{11,10},{1... | collective-permute-start | bytes 1572872 | tf_op jit(solution)/shard_map/cond/branch_1_fun/ppermute | solution.py:455
  75.3 17.0 %collective-permute-done.2 = f32[512,256]{1,0:T(8,128)} collective-permute-done((f32[512,256]{1,0:T(8,128)}, f32[512,256]{1,0:T(8,128)}, u32[]{:S(2)}, u32[]{:S(2)}) %collective-permute-start.2) | collective-permute-done | bytes 524320 | tf_op jit(solution)/shard_map/cond/branch_1_fun/ppermute | solution.py:453
  92.2 4.0 %collective-permute-start.4 = (f32[512,256]{1,0:T(8,128)}, f32[512,256]{1,0:T(8,128)}, u32[]{:S(2)}, u32[]{:S(2)}) collective-permute-start(f32[512,256]{1,0:T(8,128)} %collective-permute-done.2), channel_id=1, source_target_pairs={{4,5},{5,4},{12,13},{13,12},{20,21},{21,20},{28,29},{29,28},{36,37... | collective-permute-start | bytes 1572872 | tf_op jit(solution)/shard_map/cond/branch_1_fun/ppermute | solution.py:456
  96.2 0.0 collective-permute-done.3
  96.2 1.8 %collective-permute-done.4 = f32[512,256]{1,0:T(8,128)} collective-permute-done((f32[512,256]{1,0:T(8,128)}, f32[512,256]{1,0:T(8,128)}, u32[]{:S(2)}, u32[]{:S(2)}) %collective-permute-start.4) | collective-permute-done | bytes 524320 | tf_op jit(solution)/shard_map/cond/branch_1_fun/ppermute | solution.py:456
  98.1 0.0 collective-permute-done.18
  98.1 0.0 collective-permute-done.17
  98.1 0.0 collective-permute-done.16
  98.1 7.8 %conditional.3 = (f32[2,256,4,256]{3,2,1,0:T(4,128)}) conditional(s32[]{:T(128)} %bitcast.5, (f32[2176,128]{1,0:T(8,128)}, f32[512,1024]{1,0:T(8,128)S(1)}, s32[512,128]{1,0:T(8,128)S(1)}, s32[]{:T(128)}, s32[3]{0:T(128)S(1)}, /*index=5*/f32[2,512,128]{2,1,0:T(8,128)}) %tuple.32, (s32[3]{0:T(128)S(1)}, f32[512,256]{1,0:T(8,128)}, ...), branch_computations={%region_2.4_spmd, %region_4.5_spmd} | conditional | flops 8000884736 | bytes 85798736 | solution.py:506
  98.3 7.6 %branch_1_fun.3 = f32[2,256,4,256]{3,2,1,0:T(4,128)} custom-call(s32[3]{0:T(128)S(1)} %get-tuple-element.81.place, f32[512,256]{1,0:T(8,128)} %get-tuple-element.82.n_early, f32[512,256]{1,0:T(8,128)} %get-tuple-element.83.n_last, f32[512,256]{1,0:T(8,128)} %get-tuple-element.84.o_early, f32[512,256]{1,0:T(8,128)} %get-tuple-element.85.o_last, ...), custom_call_target="tpu_custom_call" | custom-call | flops 4000000000 | bytes 8000000 | tf_op jit(solution)/shard_map/cond/branch_1_fun/pallas_call | solution.py:465
  (15 shorter events, 0.0 us)
Async XLA Ops:
  0.1 13.0 %copy-start.5 = (s32[2,4,16,256]{3,2,1,0:T(8,128)S(1)}, s32[2,4,16,256]{3,2,1,0:T(8,128)}, u32[]{:S(2)}) copy-start(s32[2,4,16,256]{3,2,1,0:T(8,128)} %level_picks.1) | copy-start | bytes 393220
  0.1 13.0 %copy-start.6 = (s32[2,16,256]{2,1,0:T(8,128)S(1)}, s32[2,16,256]{2,1,0:T(8,128)}, u32[]{:S(2)}) copy-start(s32[2,16,256]{2,1,0:T(8,128)} %local_picks.1) | copy-start | bytes 98308
  0.1 13.0 %copy-start.7 = (s32[2,256]{1,0:T(2,128)S(1)}, s32[2,256]{1,0:T(2,128)}, u32[]{:S(2)}) copy-start(s32[2,256]{1,0:T(2,128)} %order.1) | copy-start | bytes 6148
  2.7 27.3 %all-to-all-start.2 = ((f32[2176,1,128]{2,1,0:T(1,128)}), f32[2176,1,128]{2,1,0:T(1,128)S(1)}, u32[]{:S(2)}, u32[]{:S(2)}) async-start(f32[2176,1,128]{2,1,0:T(1,128)} %bitcast.29), calls=%async_computation.2 | async-start | bytes 2228224 | tf_op jit(solution)/shard_map/all_to_all | solution.py:392
  13.1 3.4 %copy-start.11 = (f32[2,256,4,256]{3,2,1,0:T(4,128)S(1)}, f32[2,256,4,256]{3,2,1,0:T(4,128)}, u32[]{:S(2)}) copy-start(f32[2,256,4,256]{3,2,1,0:T(4,128)} %param.11) | copy-start | bytes 6291460
  17.0 1.3 %copy-start.8 = (f32[64,8,4,256]{3,1,2,0:T(8,128)}, f32[64,8,4,256]{3,1,2,0:T(8,128)S(1)}, u32[]{:S(2)}) copy-start(f32[64,8,4,256]{3,1,2,0:T(8,128)S(1)} %copy.11) | copy-start | bytes 6291460
  30.0 1.4 %copy-start.10 = (f32[2176,1,128]{2,1,0:T(1,128)}, f32[2176,1,128]{2,1,0:T(1,128)S(1)}, u32[]{:S(2)}) copy-start(f32[2176,1,128]{2,1,0:T(1,128)S(1)} %all-to-all-done.2) | copy-start | bytes 3342340
  31.4 22.4 %all-to-all-start.3 = ((f32[16,48,256]{2,1,0:T(8,128)}), f32[16,48,256]{2,1,0:T(8,128)S(1)}, u32[]{:S(2)}, u32[]{:S(2)}) async-start(f32[16,48,256]{2,1,0:T(8,128)} %bitcast.12), calls=%async_computation.3 | async-start | bytes 1572864 | tf_op jit(solution)/shard_map/all_to_all | solution.py:420
  40.7 13.2 %copy-start.13 = (f32[512,256]{1,0:T(8,128)}, f32[512,256]{1,0:T(8,128)S(1)}, u32[]{:S(2)}) copy-start(f32[512,256]{1,0:T(8,128)S(1)} %get-tuple-element.119) | copy-start | bytes 1572868
  40.7 13.2 %collective-permute-start.11 = (f32[512,256]{1,0:T(8,128)S(1)}, f32[512,256]{1,0:T(8,128)S(1)}, u32[]{:S(2)}, u32[]{:S(2)}) collective-permute-start(f32[512,256]{1,0:T(8,128)S(1)} %get-tuple-element.119), channel_id=1, source_target_pairs={{0,1},{1,0},{2,3},{3,2},{4,5},{5,4},{6,7},{7,6},{8,9},{9,8},{10,11... | collective-permute-start | bytes 1572872 | tf_op jit(solution)/shard_map/ppermute | solution.py:344
  41.8 7.5 %collective-permute-start.14 = (f32[48,768]{1,0:T(8,128)S(1)}, f32[48,768]{1,0:T(8,128)S(1)}, u32[]{:S(2)}, u32[]{:S(2)}) collective-permute-start(f32[48,768]{1,0:T(8,128)S(1)} %get-tuple-element.123.a0), channel_id=1, source_target_pairs={{0,16},{8,24},{16,0},{24,8},{32,48},{40,56},{48,32},{56,40},{64,80... | collective-permute-start | bytes 442376 | tf_op jit(solution)/shard_map/ppermute | solution.py:356
  44.9 7.5 %collective-permute-start.13 = (f32[48,768]{1,0:T(8,128)S(1)}, f32[48,768]{1,0:T(8,128)S(1)}, u32[]{:S(2)}, u32[]{:S(2)}) collective-permute-start(f32[48,768]{1,0:T(8,128)S(1)} %get-tuple-element.123.a0), channel_id=1, source_target_pairs={{0,24},{8,0},{16,8},{24,16},{32,56},{40,32},{48,40},{56,48},{64,88... | collective-permute-start | bytes 442376 | tf_op jit(solution)/shard_map/ppermute | solution.py:356
  45.8 8.0 %collective-permute-start.12 = (f32[48,768]{1,0:T(8,128)S(1)}, f32[48,768]{1,0:T(8,128)S(1)}, u32[]{:S(2)}, u32[]{:S(2)}) collective-permute-start(f32[48,768]{1,0:T(8,128)S(1)} %get-tuple-element.123.a0), channel_id=1, source_target_pairs={{0,8},{8,16},{16,24},{24,0},{32,40},{40,48},{48,56},{56,32},{64,72... | collective-permute-start | bytes 442376 | tf_op jit(solution)/shard_map/ppermute | solution.py:356
  53.9 9.2 %copy-start.14 = (f32[512,256]{1,0:T(8,128)S(1)}, f32[512,256]{1,0:T(8,128)}, u32[]{:S(2)}) copy-start(f32[512,256]{1,0:T(8,128)} %copy-done.13) | copy-start | bytes 1572868
  55.4 42.6 %collective-permute-start.18 = (f32[192,768]{1,0:T(8,128)}, f32[192,768]{1,0:T(8,128)}, u32[]{:S(2)}, u32[]{:S(2)}) collective-permute-start(f32[192,768]{1,0:T(8,128)} %get-tuple-element.132), channel_id=1, source_target_pairs={{0,64},{8,72},{16,80},{24,88},{32,96},{40,104},{48,112},{56,120},{... | collective-permute-start | bytes 1769480 | tf_op jit(solution)/shard_map/ppermute | solution.py:356
  58.1 40.0 %collective-permute-start.17 = (f32[192,768]{1,0:T(8,128)}, f32[192,768]{1,0:T(8,128)}, u32[]{:S(2)}, u32[]{:S(2)}) collective-permute-start(f32[192,768]{1,0:T(8,128)} %get-tuple-element.132), channel_id=1, source_target_pairs={{0,96},{8,104},{16,112},{24,120},{32,0},{40,8},{48,16},{56,24},{64... | collective-permute-start | bytes 1769480 | tf_op jit(solution)/shard_map/ppermute | solution.py:356
  58.9 39.1 %collective-permute-start.16 = (f32[192,768]{1,0:T(8,128)}, f32[192,768]{1,0:T(8,128)}, u32[]{:S(2)}, u32[]{:S(2)}) collective-permute-start(f32[192,768]{1,0:T(8,128)} %get-tuple-element.132), channel_id=1, source_target_pairs={{0,32},{8,40},{16,48},{24,56},{32,64},{40,72},{48,80},{56,88},{64,... | collective-permute-start | bytes 1769480 | tf_op jit(solution)/shard_map/ppermute | solution.py:356
  59.5 3.5 %collective-permute-start.15 = (f32[512,256]{1,0:T(8,128)}, f32[512,256]{1,0:T(8,128)S(1)}, u32[]{:S(2)}, u32[]{:S(2)}) collective-permute-start(f32[512,256]{1,0:T(8,128)} %get-tuple-element.124), channel_id=1, source_target_pairs={{0,1},{1,0},{2,3},{3,2},{4,5},{5,4},{6,7},{7,6},{8,9},{9,8},{10,11... | collective-permute-start | bytes 1572872 | tf_op jit(solution)/shard_map/ppermute | solution.py:344
  63.0 35.1 %copy-start.9 = (f32[64,8,4,256]{3,1,2,0:T(8,128)S(1)}, f32[64,8,4,256]{3,1,2,0:T(8,128)}, u32[]{:S(2)}) copy-start(f32[64,8,4,256]{3,1,2,0:T(8,128)} %copy-done.8) | copy-start | bytes 6291460
  63.0 0.8 copy-start.12
  68.6 3.0 %collective-permute-start.1 = (f32[512,256]{1,0:T(8,128)S(1)}, f32[512,256]{1,0:T(8,128)}, u32[]{:S(2)}, u32[]{:S(2)}) collective-permute-start(f32[512,256]{1,0:T(8,128)S(1)} %get-tuple-element.69), channel_id=1, source_target_pairs={{0,2},{1,7},{8,10},{9,15},{16,18},{17,23},{24,26},{25,31},{32,34},... | collective-permute-start | bytes 1572872 | tf_op jit(solution)/shard_map/cond/branch_1_fun/ppermute | solution.py:451
  70.1 2.8 %collective-permute-start = (f32[512,256]{1,0:T(8,128)S(1)}, f32[512,256]{1,0:T(8,128)}, u32[]{:S(2)}, u32[]{:S(2)}) collective-permute-start(f32[512,256]{1,0:T(8,128)S(1)} %get-tuple-element.69), channel_id=1, source_target_pairs={{1,3},{0,6},{9,11},{8,14},{17,19},{16,22},{25,27},{24,30},{33,35},... | collective-permute-start | bytes 1572872 | tf_op jit(solution)/shard_map/cond/branch_1_fun/ppermute | solution.py:452
  71.6 20.7 %collective-permute-start.2 = (f32[512,256]{1,0:T(8,128)}, f32[512,256]{1,0:T(8,128)}, u32[]{:S(2)}, u32[]{:S(2)}) collective-permute-start(f32[512,256]{1,0:T(8,128)} %collective-permute-done.1), channel_id=1, source_target_pairs={{2,4},{7,5},{10,12},{15,13},{18,20},{23,21},{26,28},{31,29},{34,36... | collective-permute-start | bytes 1572872 | tf_op jit(solution)/shard_map/cond/branch_1_fun/ppermute | solution.py:453
  73.8 22.4 %collective-permute-start.3 = (f32[512,256]{1,0:T(8,128)}, f32[512,256]{1,0:T(8,128)}, u32[]{:S(2)}, u32[]{:S(2)}) collective-permute-start(f32[512,256]{1,0:T(8,128)} %select_select_fusion), channel_id=1, source_target_pairs={{0,1},{1,0},{2,3},{3,2},{6,7},{7,6},{8,9},{9,8},{10,11},{11,10},{1... | collective-permute-start | bytes 1572872 | tf_op jit(solution)/shard_map/cond/branch_1_fun/ppermute | solution.py:455
  92.2 5.8 %collective-permute-start.4 = (f32[512,256]{1,0:T(8,128)}, f32[512,256]{1,0:T(8,128)}, u32[]{:S(2)}, u32[]{:S(2)}) collective-permute-start(f32[512,256]{1,0:T(8,128)} %collective-permute-done.2), channel_id=1, source_target_pairs={{4,5},{5,4},{12,13},{13,12},{20,21},{21,20},{28,29},{29,28},{36,37... | collective-permute-start | bytes 1572872 | tf_op jit(solution)/shard_map/cond/branch_1_fun/ppermute | solution.py:456

commit v12 on v10

--- a/solution.py
+++ b/solution.py
@@ -98,7 +98,7 @@
     give_out[...] = jnp.broadcast_to(give, (keep, 128))
 
 
-def pack_kernel(place, partials_hbm, targets_hbm, counts_hbm, out, partials, targets, counts, sems):
+def pack_kernel(place, partials_hbm, targets_hbm, counts_hbm, out_hbm, partials, targets, counts, out, sems, out_sems):
     slots, sources = targets.shape
     parts = sems.shape[0] - 2
     step = sources // parts
@@ -120,12 +120,18 @@
     codes = jnp.concatenate([codes] * (128 // slots), axis=0)
     codes = jnp.where(iota(codes.shape, 0) // slots == place[2] % (128 // slots), codes, 0)
     row = codes.astype(F32).T
+    sent = []
     for i in range(parts):
         large[i].wait()
         for s in range(i * step, (i + 1) * step):
             out[17 * s : 17 * s + 8, :] = partials[s, :, :128]
             out[17 * s + 8 : 17 * s + 16, :] = partials[s, :, 128:]
             out[17 * s + 16 : 17 * s + 17, :] = row[s : s + 1, :]
+        span = slice(17 * step * i, 17 * step * (i + 1))
+        sent.append(pltpu.make_async_copy(out.at[span], out_hbm.at[span], out_sems.at[i]))
+        sent[-1].start()
+    for copy in sent:
+        copy.wait()
 
 
 def unpack(payload):
@@ -253,23 +259,24 @@
 
 
 def finish_kernel(
-    place, n_early, n_last, o_early, o_last, tile_hbm, first_hbm, w_first_hbm, rest_hbm, xy_hbm,
+    place, n_early, n_late, o_early, o_late, tile_hbm, first_hbm, w_first_hbm, rest_hbm, xy_hbm,
     a0, a1, a2, a3, out_hbm, n_own, n_other, first, w_first, tile, rest, xy, w_rest, out, sems
 ):
     q = place[1]
     even = q % 2 == 0
-    far = (q == 4) | (q == 5)
     copy = pltpu.make_async_copy
-
-    @pl.when(far)
-    def _():
-        copy(n_last, n_own, sems.at[0]).start()
-        copy(o_last, n_other, sems.at[1]).start()
-
-    @pl.when(jnp.logical_not(far))
-    def _():
-        copy(n_early, n_own, sems.at[0]).start()
-        copy(o_early, n_other, sems.at[1]).start()
+    for early, first_of, second_of, target, at in (
+        ((q < 3) | (q == 7), n_early, n_late, n_own, 0),
+        ((q < 2) | (q == 3) | (q == 6), o_early, o_late, n_other, 1),
+    ):
+
+        @pl.when(early)
+        def _():
+            copy(first_of, target, sems.at[at]).start()
+
+        @pl.when(jnp.logical_not(early))
+        def _():
+            copy(second_of, target, sems.at[at]).start()
 
     size = a0.shape[0]
     moves = [
@@ -376,12 +383,14 @@
         pack_kernel,
         out_shape=shaped(sources * 17, 128),
         in_specs=[SM, HBM, HBM, HBM],
-        out_specs=VM,
+        out_specs=HBM,
         scratch_shapes=[
             pltpu.VMEM((sources, slots, B), F32),
             pltpu.VMEM((slots, sources), jnp.int32),
             pltpu.VMEM((1, sources), jnp.int32),
+            pltpu.VMEM((sources * 17, 128), F32),
             pltpu.SemaphoreType.DMA((6,)),
+            pltpu.SemaphoreType.DMA((4,)),
         ],
         cost_estimate=pl.CostEstimate(flops=10**6, bytes_accessed=2 * 10**6, transcendentals=0),
         **ALONE,
@@ -438,15 +447,12 @@
             panel_kernel, (shaped(rows, B), shaped(rows, B)), 6, flops=2 * 10**9, moved=4 * 10**6
         )(place, w_first, w_other, first, r_other, active)
         q = place[1]
-        near = (q == 2) | (q == 7)
-        side = (q == 3) | (q == 6)
         step = lax.ppermute(half, "pcol", [(0, 2), (1, 7)])
-        late = lax.ppermute(half, "pcol", [(1, 3), (0, 6)])
-        last = lax.ppermute(step, "pcol", [(2, 4), (7, 5)])
-        early = jnp.where(side, late, jnp.where(near, step, half))
-        o_early = lax.ppermute(early, "pcol", [(0, 1), (1, 0), (2, 3), (3, 2), (6, 7), (7, 6)])
-        o_last = lax.ppermute(last, "pcol", [(4, 5), (5, 4)])
-        return early, last, o_early, o_last, tile
+        n_early = jnp.where((q == 2) | (q == 7), step, half)
+        n_late = lax.ppermute(n_early, "pcol", [(1, 3), (0, 6), (2, 4), (7, 5)])
+        o_early = lax.ppermute(n_early, "pcol", [(0, 1), (1, 0), (2, 3), (7, 6)])
+        o_late = lax.ppermute(n_late, "pcol", [(3, 2), (6, 7), (4, 5), (5, 4)])
+        return n_early, n_late, o_early, o_late, tile
 
     def nothing(w_first, first, active, place, joined):
         return (jnp.zeros((rows, B), F32),) * 5

time: 105 us -> 103 us (0.981)
  starting transfers between devices: 34.1 us -> 31.6 us
    ppermute x4 -> x3, starting transfers between devices: 8.08 us -> 5.57 us  [the longest x1 2.83 us: panels(): o_late = lax.ppermute(n_late, 'pcol', [(3, 2), (6, 7), (4, 5), (5, 4)])]
    ppermute x4 -> x3, waiting for transfers between devices: 18.9 us -> 19.4 us  [the longest x1 17.5 us: panels(): n_late = lax.ppermute(n_early, 'pcol', [(1, 3), (0, 6), (2, 4), (7, 5)])]
  transfers between devices with their start and end apart: 15 -> 14, of which waited for: 8 -> 8; matrix products, arithmetic and copies ran while one was open for 1% -> 1% of each run, Pallas kernels for 15% -> 15%
where the time goes in v12:
time: 103 us
  waiting for transfers between devices  39.9 us (39%)
  starting transfers between devices  31.6 us (31%)
  Pallas kernels  27.3 us (27%)
  local copies, waits for them, and re-layouts  1.82 us (2%)
    ppermute x1, waiting for transfers between devices, panels(): n_late = lax.ppermute(n_early, 'pcol', [(1, 3), (0, 6), (2, 4), (7, 5)])  17.5 us
    all_to_all x1, waiting for transfers between devices, body(): lax.all_to_all(payload, ('prow', 'pcol'), 0, 0, tiled=True)  11.2 us
    all_to_all x1, starting transfers between devices, body(): lax.all_to_all(payload, ('prow', 'pcol'), 0, 0, tiled=True)  10.4 us
    ppermute x6, starting transfers between devices, ring(): return [x] + [lax.ppermute(x, 'prow', shift(step)) for step in (1, -1, 2)]  8.57 us
    pallas_call x1, Pallas kernels, finish(): pl.pallas_call(finish_kernel, out_shape=shaped(*front.shape), in_specs=[S...  7.59 us
    pallas_call x1, Pallas kernels, body(): call(tiles_kernel, (shaped(rows, B), shaped(rows, cols - B), shaped(8, 12...  5.49 us
    pallas_call x1, Pallas kernels, panels(): call(panel_kernel, (shaped(rows, B), shaped(rows, B)), 6, flops=2 * 10 **...  4.83 us
    ppermute x6, waiting for transfers between devices, ring(): return [x] + [lax.ppermute(x, 'prow', shift(step)) for step in (1, -1, 2)]  3.89 us
  transfers between devices with their start and end apart: 14, of which 8 were waited for; matrix products, arithmetic and copies ran while one was open for 1% of the time, Pallas kernels for 15%

profile of v12, /device:TPU:65, one launch (start us, length us, event | category | flops | bytes accessed | tf_op | source)
XLA Modules:
  0.0 102.8 jit_solution(14526297747989953392)
XLA Ops:
  0.0 0.1 pad_add_fusion.place
  0.1 2.6 %shard_map.76 = f32[2176,128]{1,0:T(8,128)} custom-call(s32[3]{0:T(128)S(1)} %pad_add_fusion.place, f32[128,8,256]{2,1,0:T(8,128)} %bitcast.31, s32[8,128]{1,0:T(8,128)} %bitcast.32, s32[1,128]{1,0:T(1,128)} %counts_hbm.1), custom_call_target="tpu_custom_call" | custom-call | flops 1000000 | bytes 2000000 | tf_op jit(solution)/shard_map/pallas_call | solution.py:382
  2.7 10.4 %all-to-all-start.2 = ((f32[2176,1,128]{2,1,0:T(1,128)}), f32[2176,1,128]{2,1,0:T(1,128)S(1)}, u32[]{:S(2)}, u32[]{:S(2)}) async-start(f32[2176,1,128]{2,1,0:T(1,128)} %bitcast.29), calls=%async_computation.2 | async-start | bytes 2228224 | tf_op jit(solution)/shard_map/all_to_all | solution.py:398
  13.1 0.0 copy-done.5
  13.1 0.0 copy-start.11
  13.1 3.4 %shard_map.75 = (s32[512,128]{1,0:T(8,128)S(1)}, f32[2,512,128]{2,1,0:T(8,128)}, s32[48,128]{1,0:T(8,128)S(1)}, bf16[512,768]{1,0:T(8,128)(2,1)S(1)}, bf16[512,768]{1,0:T(8,128)(2,1)}, /*index=5*/s32[1]{0:T(128)}) custom-call(s32[3]{0:T(128)S(1)} %pad_add_fusion.place, s32[2,16,256]{2,1,0:T(8,128)S(1)} %copy-done.6, s32[2,4,16,256]{3,2,1,0:T(8,128)S(1)} %copy-done.5, ...), custom_call_target="tpu_custom_call" | custom-call | flops 1000000000 | bytes 1000000 | tf_op jit(solution)/shard_map/pallas_call | solution.py:402
  16.5 0.0 copy-done.11
  16.5 0.5 copy.11
  17.0 0.0 copy-start.8
  17.0 1.3 %copy-done.8 = f32[64,8,4,256]{3,1,2,0:T(8,128)} copy-done((f32[64,8,4,256]{3,1,2,0:T(8,128)}, f32[64,8,4,256]{3,1,2,0:T(8,128)S(1)}, u32[]{:S(2)}) %copy-start.8) | copy-done | bytes 2097176
  18.3 0.6 shard_map.77.front_rows
  18.9 11.2 %all-to-all-done.2 = f32[2176,1,128]{2,1,0:T(1,128)S(1)} async-done(((f32[2176,1,128]{2,1,0:T(1,128)}), f32[2176,1,128]{2,1,0:T(1,128)S(1)}, u32[]{:S(2)}, u32[]{:S(2)}) %all-to-all-start.2) | async-done | bytes 1114144 | tf_op jit(solution)/shard_map/all_to_all | solution.py:398
  30.0 1.4 %shard_map.78 = (f32[768,256]{1,0:T(8,128)}, f32[48,768]{1,0:T(8,128)S(1)}) custom-call(f32[2176,128]{1,0:T(8,128)S(1)} %bitcast.26, f32[192,256]{1,0:T(8,128)S(1)} %shard_map.77.front_rows, s32[48,128]{1,0:T(8,128)S(1)} %get-tuple-element.115.give), custom_call_target="tpu_custom_call" | custom-call | flops 100000000 | bytes 2000000 | tf_op jit(solution)/shard_map/pallas_call | solution.py:423
  31.4 0.0 copy-done.10
  31.4 3.7 %all-to-all-start.3 = ((f32[16,48,256]{2,1,0:T(8,128)}), f32[16,48,256]{2,1,0:T(8,128)S(1)}, u32[]{:S(2)}, u32[]{:S(2)}) async-start(f32[16,48,256]{2,1,0:T(8,128)} %bitcast.12), calls=%async_computation.3 | async-start | bytes 1572864 | tf_op jit(solution)/shard_map/all_to_all | solution.py:426
  35.2 2.9 %collective-permute-start.14 = (f32[48,768]{1,0:T(8,128)S(1)}, f32[48,768]{1,0:T(8,128)S(1)}, u32[]{:S(2)}, u32[]{:S(2)}) collective-permute-start(f32[48,768]{1,0:T(8,128)S(1)} %get-tuple-element.128.a0), channel_id=1, source_target_pairs={{0,16},{8,24},{16,0},{24,8},{32,48},{40,56},{48,32},{56,40},{64,80... | collective-permute-start | bytes 442376 | tf_op jit(solution)/shard_map/ppermute | solution.py:362
  38.0 0.9 collective-permute-start.13
  38.9 0.6 collective-permute-start.12
  39.5 5.5 %shard_map.80 = (f32[512,256]{1,0:T(8,128)}, f32[512,768]{1,0:T(8,128)}, f32[8,128]{1,0:T(8,128)S(1)}) custom-call(f32[2176,128]{1,0:T(8,128)} %bitcast.27, f32[512,1024]{1,0:T(8,128)} %bitcast.24), custom_call_target="tpu_custom_call" | custom-call | flops 4000000000 | bytes 6000000 | tf_op jit(solution)/shard_map/pallas_call | solution.py:427
  45.0 3.2 %all-to-all-done.3 = f32[16,48,256]{2,1,0:T(8,128)S(1)} async-done(((f32[16,48,256]{2,1,0:T(8,128)}), f32[16,48,256]{2,1,0:T(8,128)S(1)}, u32[]{:S(2)}, u32[]{:S(2)}) %all-to-all-start.3) | async-done | bytes 786464 | tf_op jit(solution)/shard_map/all_to_all | solution.py:426
  48.2 1.4 %shard_map.79 = (f32[512,256]{1,0:T(8,128)}, f32[8,128]{1,0:T(8,128)S(1)}) custom-call(bf16[512,768]{1,0:T(8,128)(2,1)S(1)} %get-tuple-element.114.slot, f32[768,256]{1,0:T(8,128)S(1)} %bitcast.21), custom_call_target="tpu_custom_call" | custom-call | flops 100000000 | bytes 1000000 | tf_op jit(solution)/shard_map/pallas_call | solution.py:435
  49.6 0.0 collective-permute-done.14.a3
  49.6 1.6 %collective-permute-done.13.a2 = f32[48,768]{1,0:T(8,128)S(1)} collective-permute-done((f32[48,768]{1,0:T(8,128)S(1)}, f32[48,768]{1,0:T(8,128)S(1)}, u32[]{:S(2)}, u32[]{:S(2)}) %collective-permute-start.13) | collective-permute-done | bytes 147488 | tf_op jit(solution)/shard_map/ppermute | solution.py:362
  51.2 2.2 %collective-permute-done.12.a1 = f32[48,768]{1,0:T(8,128)S(1)} collective-permute-done((f32[48,768]{1,0:T(8,128)S(1)}, f32[48,768]{1,0:T(8,128)S(1)}, u32[]{:S(2)}, u32[]{:S(2)}) %collective-permute-start.12) | collective-permute-done | bytes 147488 | tf_op jit(solution)/shard_map/ppermute | solution.py:362
  53.5 2.8 %collective-permute-start.17 = (f32[192,768]{1,0:T(8,128)S(1)}, f32[192,768]{1,0:T(8,128)}, u32[]{:S(2)}, u32[]{:S(2)}) collective-permute-start(f32[192,768]{1,0:T(8,128)S(1)} %shard_map.81), channel_id=1, source_target_pairs={{0,64},{8,72},{16,80},{24,88},{32,96},{40,104},{48,112},{56,120},{... | collective-permute-start | bytes 1769480 | tf_op jit(solution)/shard_map/ppermute | solution.py:362
  56.3 0.9 collective-permute-start.16
  57.2 0.6 collective-permute-start.15
  58.5 0.0 copy-start.9
  58.5 36.2 %conditional.2 = (f32[512,256]{1,0:T(8,128)}, f32[512,256]{1,0:T(8,128)}, f32[512,256]{1,0:T(8,128)}, f32[512,256]{1,0:T(8,128)}, f32[512,256]{1,0:T(8,128)}) conditional(s32[]{:T(128)} %bitcast.5, () %tuple.22, (s32[]{:T(128)}, f32[512,256]{1,0:T(8,128)}, f32[512,256]{1,0:T(8,128)S(1)}, s32[3]{0:T(128)S(1)}, f32[2,512,128]{2,1,0:T(8,128)S(1)}) %tuple.34), branch_computations={%region_0.0_spmd, %region_1.2_spmd} | conditional | flops 2000131072 | bytes 18156078 | solution.py:460
  58.5 1.8 %collective-permute-start = (f32[512,256]{1,0:T(8,128)}, f32[512,256]{1,0:T(8,128)S(1)}, u32[]{:S(2)}, u32[]{:S(2)}) collective-permute-start(f32[512,256]{1,0:T(8,128)} %get-tuple-element.60.w_own), channel_id=1, source_target_pairs={{0,1},{1,0},{2,3},{3,2},{4,5},{5,4},{6,7},{7,6},{8,9},{9,8},{10,11... | collective-permute-start | bytes 1572872 | tf_op jit(solution)/shard_map/cond/branch_1_fun/ppermute | solution.py:350
  60.3 0.1 collective-permute-start.1
  60.4 1.7 %collective-permute-done.w_other = f32[512,256]{1,0:T(8,128)S(1)} collective-permute-done((f32[512,256]{1,0:T(8,128)}, f32[512,256]{1,0:T(8,128)S(1)}, u32[]{:S(2)}, u32[]{:S(2)}) %collective-permute-start) | collective-permute-done | bytes 524320 | tf_op jit(solution)/shard_map/cond/branch_1_fun/ppermute | solution.py:350
  62.0 0.5 collective-permute-done.1.r_other
  62.6 4.8 %branch_1_fun.2 = (f32[512,256]{1,0:T(8,128)S(1)}, f32[512,256]{1,0:T(8,128)}) custom-call(s32[3]{0:T(128)S(1)} %get-tuple-element.59.place, f32[512,256]{1,0:T(8,128)} %get-tuple-element.60.w_own, f32[512,256]{1,0:T(8,128)S(1)} %collective-permute-done.w_other, f32[512,256]{1,0:T(8,128)S(1)} %get-tuple-element.61.r_own, ...), custom_call_target="tpu_custom_call" | custom-call | flops 2000000000 | bytes 4000000 | tf_op jit(solution)/shard_map/cond/branch_1_fun/pallas_call | solution.py:446
  67.4 1.5 %collective-permute-start.2 = (f32[512,256]{1,0:T(8,128)S(1)}, f32[512,256]{1,0:T(8,128)}, u32[]{:S(2)}, u32[]{:S(2)}) collective-permute-start(f32[512,256]{1,0:T(8,128)S(1)} %get-tuple-element.63), channel_id=1, source_target_pairs={{0,2},{1,7},{8,10},{9,15},{16,18},{17,23},{24,26},{25,31},{32,34},... | collective-permute-start | bytes 1572872 | tf_op jit(solution)/shard_map/cond/branch_1_fun/ppermute | solution.py:450
  68.9 0.0 collective-permute-done.2
  68.9 0.9 broadcast_select_fusion
  69.7 1.3 %collective-permute-start.3 = (f32[512,256]{1,0:T(8,128)}, f32[512,256]{1,0:T(8,128)}, u32[]{:S(2)}, u32[]{:S(2)}) collective-permute-start(f32[512,256]{1,0:T(8,128)} %broadcast_select_fusion), channel_id=1, source_target_pairs={{1,3},{0,6},{2,4},{7,5},{9,11},{8,14},{10,12},{15,13},{17,19},{16,... | collective-permute-start | bytes 1572872 | tf_op jit(solution)/shard_map/cond/branch_1_fun/ppermute | solution.py:452
  71.0 1.5 %collective-permute-start.4 = (f32[512,256]{1,0:T(8,128)}, f32[512,256]{1,0:T(8,128)}, u32[]{:S(2)}, u32[]{:S(2)}) collective-permute-start(f32[512,256]{1,0:T(8,128)} %broadcast_select_fusion), channel_id=1, source_target_pairs={{0,1},{1,0},{2,3},{7,6},{8,9},{9,8},{10,11},{15,14},{16,17},{17,16... | collective-permute-start | bytes 1572872 | tf_op jit(solution)/shard_map/cond/branch_1_fun/ppermute | solution.py:453
  72.5 17.5 %collective-permute-done.3 = f32[512,256]{1,0:T(8,128)} collective-permute-done((f32[512,256]{1,0:T(8,128)}, f32[512,256]{1,0:T(8,128)}, u32[]{:S(2)}, u32[]{:S(2)}) %collective-permute-start.3) | collective-permute-done | bytes 524320 | tf_op jit(solution)/shard_map/cond/branch_1_fun/ppermute | solution.py:452
  90.0 2.8 %collective-permute-start.5 = (f32[512,256]{1,0:T(8,128)}, f32[512,256]{1,0:T(8,128)}, u32[]{:S(2)}, u32[]{:S(2)}) collective-permute-start(f32[512,256]{1,0:T(8,128)} %collective-permute-done.3), channel_id=1, source_target_pairs={{3,2},{6,7},{4,5},{5,4},{11,10},{14,15},{12,13},{13,12},{19,18},{2... | collective-permute-start | bytes 1572872 | tf_op jit(solution)/shard_map/cond/branch_1_fun/ppermute | solution.py:454
  92.9 0.0 collective-permute-done.4
  92.9 1.8 %collective-permute-done.5 = f32[512,256]{1,0:T(8,128)} collective-permute-done((f32[512,256]{1,0:T(8,128)}, f32[512,256]{1,0:T(8,128)}, u32[]{:S(2)}, u32[]{:S(2)}) %collective-permute-start.5) | collective-permute-done | bytes 524320 | tf_op jit(solution)/shard_map/cond/branch_1_fun/ppermute | solution.py:454
  94.7 0.0 collective-permute-done.17
  94.7 0.0 collective-permute-done.16
  94.7 0.0 collective-permute-done.15
  94.7 7.8 %conditional.3 = (f32[2,256,4,256]{3,2,1,0:T(4,128)}) conditional(s32[]{:T(128)} %bitcast.5, (f32[2176,128]{1,0:T(8,128)}, f32[512,1024]{1,0:T(8,128)S(1)}, s32[512,128]{1,0:T(8,128)S(1)}, s32[]{:T(128)}, s32[3]{0:T(128)S(1)}, /*index=5*/f32[2,512,128]{2,1,0:T(8,128)}) %tuple.32, (s32[3]{0:T(128)S(1)}, f32[512,256]{1,0:T(8,128)}, ...), branch_computations={%region_2.4_spmd, %region_4.5_spmd} | conditional | flops 8000884736 | bytes 85798736 | solution.py:504
  95.0 7.6 %branch_1_fun.3 = f32[2,256,4,256]{3,2,1,0:T(4,128)} custom-call(s32[3]{0:T(128)S(1)} %get-tuple-element.75.place, f32[512,256]{1,0:T(8,128)} %get-tuple-element.76.n_early, f32[512,256]{1,0:T(8,128)} %get-tuple-element.77.n_late, f32[512,256]{1,0:T(8,128)} %get-tuple-element.78.o_early, f32[512,256]{1,0:T(8,128)} %get-tuple-element.79.o_late, ...), custom_call_target="tpu_custom_call" | custom-call | flops 4000000000 | bytes 8000000 | tf_op jit(solution)/shard_map/cond/branch_1_fun/pallas_call | solution.py:463
  (12 shorter events, 0.1 us)
Async XLA Ops:
  0.1 13.0 %copy-start.5 = (s32[2,4,16,256]{3,2,1,0:T(8,128)S(1)}, s32[2,4,16,256]{3,2,1,0:T(8,128)}, u32[]{:S(2)}) copy-start(s32[2,4,16,256]{3,2,1,0:T(8,128)} %level_picks.1) | copy-start | bytes 393220
  0.1 13.0 %copy-start.6 = (s32[2,16,256]{2,1,0:T(8,128)S(1)}, s32[2,16,256]{2,1,0:T(8,128)}, u32[]{:S(2)}) copy-start(s32[2,16,256]{2,1,0:T(8,128)} %local_picks.1) | copy-start | bytes 98308
  0.1 13.0 %copy-start.7 = (s32[2,256]{1,0:T(2,128)S(1)}, s32[2,256]{1,0:T(2,128)}, u32[]{:S(2)}) copy-start(s32[2,256]{1,0:T(2,128)} %order.1) | copy-start | bytes 6148
  2.7 27.3 %all-to-all-start.2 = ((f32[2176,1,128]{2,1,0:T(1,128)}), f32[2176,1,128]{2,1,0:T(1,128)S(1)}, u32[]{:S(2)}, u32[]{:S(2)}) async-start(f32[2176,1,128]{2,1,0:T(1,128)} %bitcast.29), calls=%async_computation.2 | async-start | bytes 2228224 | tf_op jit(solution)/shard_map/all_to_all | solution.py:398
  13.1 3.4 %copy-start.11 = (f32[2,256,4,256]{3,2,1,0:T(4,128)S(1)}, f32[2,256,4,256]{3,2,1,0:T(4,128)}, u32[]{:S(2)}) copy-start(f32[2,256,4,256]{3,2,1,0:T(4,128)} %param.11) | copy-start | bytes 6291460
  17.0 1.3 %copy-start.8 = (f32[64,8,4,256]{3,1,2,0:T(8,128)}, f32[64,8,4,256]{3,1,2,0:T(8,128)S(1)}, u32[]{:S(2)}) copy-start(f32[64,8,4,256]{3,1,2,0:T(8,128)S(1)} %copy.11) | copy-start | bytes 6291460
  30.0 1.4 %copy-start.10 = (f32[2176,1,128]{2,1,0:T(1,128)}, f32[2176,1,128]{2,1,0:T(1,128)S(1)}, u32[]{:S(2)}) copy-start(f32[2176,1,128]{2,1,0:T(1,128)S(1)} %all-to-all-done.2) | copy-start | bytes 3342340
  31.4 16.8 %all-to-all-start.3 = ((f32[16,48,256]{2,1,0:T(8,128)}), f32[16,48,256]{2,1,0:T(8,128)S(1)}, u32[]{:S(2)}, u32[]{:S(2)}) async-start(f32[16,48,256]{2,1,0:T(8,128)} %bitcast.12), calls=%async_computation.3 | async-start | bytes 1572864 | tf_op jit(solution)/shard_map/all_to_all | solution.py:426
  35.2 14.4 %collective-permute-start.14 = (f32[48,768]{1,0:T(8,128)S(1)}, f32[48,768]{1,0:T(8,128)S(1)}, u32[]{:S(2)}, u32[]{:S(2)}) collective-permute-start(f32[48,768]{1,0:T(8,128)S(1)} %get-tuple-element.128.a0), channel_id=1, source_target_pairs={{0,16},{8,24},{16,0},{24,8},{32,48},{40,56},{48,32},{56,40},{64,80... | collective-permute-start | bytes 442376 | tf_op jit(solution)/shard_map/ppermute | solution.py:362
  38.0 13.2 %collective-permute-start.13 = (f32[48,768]{1,0:T(8,128)S(1)}, f32[48,768]{1,0:T(8,128)S(1)}, u32[]{:S(2)}, u32[]{:S(2)}) collective-permute-start(f32[48,768]{1,0:T(8,128)S(1)} %get-tuple-element.128.a0), channel_id=1, source_target_pairs={{0,24},{8,0},{16,8},{24,16},{32,56},{40,32},{48,40},{56,48},{64,88... | collective-permute-start | bytes 442376 | tf_op jit(solution)/shard_map/ppermute | solution.py:362
  38.9 14.6 %collective-permute-start.12 = (f32[48,768]{1,0:T(8,128)S(1)}, f32[48,768]{1,0:T(8,128)S(1)}, u32[]{:S(2)}, u32[]{:S(2)}) collective-permute-start(f32[48,768]{1,0:T(8,128)S(1)} %get-tuple-element.128.a0), channel_id=1, source_target_pairs={{0,8},{8,16},{16,24},{24,0},{32,40},{40,48},{48,56},{56,32},{64,72... | collective-permute-start | bytes 442376 | tf_op jit(solution)/shard_map/ppermute | solution.py:362
  48.2 10.3 %copy-start.12 = (f32[512,256]{1,0:T(8,128)S(1)}, f32[512,256]{1,0:T(8,128)}, u32[]{:S(2)}) copy-start(f32[512,256]{1,0:T(8,128)} %get-tuple-element.118) | copy-start | bytes 1572868
  48.2 10.3 %copy-start.13 = (f32[2,512,128]{2,1,0:T(8,128)S(1)}, f32[2,512,128]{2,1,0:T(8,128)}, u32[]{:S(2)}) copy-start(f32[2,512,128]{2,1,0:T(8,128)} %get-tuple-element.113) | copy-start | bytes 1572868
  53.5 41.2 %collective-permute-start.17 = (f32[192,768]{1,0:T(8,128)S(1)}, f32[192,768]{1,0:T(8,128)}, u32[]{:S(2)}, u32[]{:S(2)}) collective-permute-start(f32[192,768]{1,0:T(8,128)S(1)} %shard_map.81), channel_id=1, source_target_pairs={{0,64},{8,72},{16,80},{24,88},{32,96},{40,104},{48,112},{56,120},{... | collective-permute-start | bytes 1769480 | tf_op jit(solution)/shard_map/ppermute | solution.py:362
  56.3 38.4 %collective-permute-start.16 = (f32[192,768]{1,0:T(8,128)S(1)}, f32[192,768]{1,0:T(8,128)}, u32[]{:S(2)}, u32[]{:S(2)}) collective-permute-start(f32[192,768]{1,0:T(8,128)S(1)} %shard_map.81), channel_id=1, source_target_pairs={{0,96},{8,104},{16,112},{24,120},{32,0},{40,8},{48,16},{56,24},{64... | collective-permute-start | bytes 1769480 | tf_op jit(solution)/shard_map/ppermute | solution.py:362
  57.2 37.6 %collective-permute-start.15 = (f32[192,768]{1,0:T(8,128)S(1)}, f32[192,768]{1,0:T(8,128)}, u32[]{:S(2)}, u32[]{:S(2)}) collective-permute-start(f32[192,768]{1,0:T(8,128)S(1)} %shard_map.81), channel_id=1, source_target_pairs={{0,32},{8,40},{16,48},{24,56},{32,64},{40,72},{48,80},{56,88},{64,... | collective-permute-start | bytes 1769480 | tf_op jit(solution)/shard_map/ppermute | solution.py:362
  58.5 36.3 %copy-start.9 = (f32[64,8,4,256]{3,1,2,0:T(8,128)S(1)}, f32[64,8,4,256]{3,1,2,0:T(8,128)}, u32[]{:S(2)}) copy-start(f32[64,8,4,256]{3,1,2,0:T(8,128)} %copy-done.8) | copy-start | bytes 6291460
  58.5 3.5 %collective-permute-start = (f32[512,256]{1,0:T(8,128)}, f32[512,256]{1,0:T(8,128)S(1)}, u32[]{:S(2)}, u32[]{:S(2)}) collective-permute-start(f32[512,256]{1,0:T(8,128)} %get-tuple-element.60.w_own), channel_id=1, source_target_pairs={{0,1},{1,0},{2,3},{3,2},{4,5},{5,4},{6,7},{7,6},{8,9},{9,8},{10,11... | collective-permute-start | bytes 1572872 | tf_op jit(solution)/shard_map/cond/branch_1_fun/ppermute | solution.py:350
  60.3 2.3 %collective-permute-start.1 = (f32[512,256]{1,0:T(8,128)S(1)}, f32[512,256]{1,0:T(8,128)S(1)}, u32[]{:S(2)}, u32[]{:S(2)}) collective-permute-start(f32[512,256]{1,0:T(8,128)S(1)} %get-tuple-element.61.r_own), channel_id=1, source_target_pairs={{0,1},{1,0},{2,3},{3,2},{4,5},{5,4},{6,7},{7,6},{8,9},{9,8},{10,11... | collective-permute-start | bytes 1572872 | tf_op jit(solution)/shard_map/cond/branch_1_fun/ppermute | solution.py:350
  67.4 1.5 %collective-permute-start.2 = (f32[512,256]{1,0:T(8,128)S(1)}, f32[512,256]{1,0:T(8,128)}, u32[]{:S(2)}, u32[]{:S(2)}) collective-permute-start(f32[512,256]{1,0:T(8,128)S(1)} %get-tuple-element.63), channel_id=1, source_target_pairs={{0,2},{1,7},{8,10},{9,15},{16,18},{17,23},{24,26},{25,31},{32,34},... | collective-permute-start | bytes 1572872 | tf_op jit(solution)/shard_map/cond/branch_1_fun/ppermute | solution.py:450
  69.7 20.3 %collective-permute-start.3 = (f32[512,256]{1,0:T(8,128)}, f32[512,256]{1,0:T(8,128)}, u32[]{:S(2)}, u32[]{:S(2)}) collective-permute-start(f32[512,256]{1,0:T(8,128)} %broadcast_select_fusion), channel_id=1, source_target_pairs={{1,3},{0,6},{2,4},{7,5},{9,11},{8,14},{10,12},{15,13},{17,19},{16,... | collective-permute-start | bytes 1572872 | tf_op jit(solution)/shard_map/cond/branch_1_fun/ppermute | solution.py:452
  71.0 21.8 %collective-permute-start.4 = (f32[512,256]{1,0:T(8,128)}, f32[512,256]{1,0:T(8,128)}, u32[]{:S(2)}, u32[]{:S(2)}) collective-permute-start(f32[512,256]{1,0:T(8,128)} %broadcast_select_fusion), channel_id=1, source_target_pairs={{0,1},{1,0},{2,3},{7,6},{8,9},{9,8},{10,11},{15,14},{16,17},{17,16... | collective-permute-start | bytes 1572872 | tf_op jit(solution)/shard_map/cond/branch_1_fun/ppermute | solution.py:453
  90.0 4.7 %collective-permute-start.5 = (f32[512,256]{1,0:T(8,128)}, f32[512,256]{1,0:T(8,128)}, u32[]{:S(2)}, u32[]{:S(2)}) collective-permute-start(f32[512,256]{1,0:T(8,128)} %collective-permute-done.3), channel_id=1, source_target_pairs={{3,2},{6,7},{4,5},{5,4},{11,10},{14,15},{12,13},{13,12},{19,18},{2... | collective-permute-start | bytes 1572872 | tf_op jit(solution)/shard_map/cond/branch_1_fun/ppermute | solution.py:454

commit v13 on v12

--- a/solution.py
+++ b/solution.py
@@ -187,19 +187,22 @@
         send_rest[:, (u - 1) * B : u * B] = sums[u * keep : (u + 1) * keep]
 
 
-def tiles_kernel(payload, front, first_out, rest_out, done_out):
+def tile_kernel(payload, front, first_out):
+    (high, low), code = unpack(payload)
+    hot = hot_of(code, front.shape[0], 0)
+    first_out[...] = front[...] + (dot(hot, high) + dot(hot, low))
+
+
+def tiles_kernel(payload, front, rest_out, done_out):
     done_out[...] = jnp.zeros_like(done_out)
     (high, low), code = unpack(payload)
-    for u in range(4):
+    for u in range(1, 4):
+        cols = slice(u * B, (u + 1) * B)
         hot = hot_of(code, front.shape[0], u)
-        tile = front[:, u * B : (u + 1) * B] + (dot(hot, high) + dot(hot, low))
-        if u == 0:
-            first_out[...] = tile
-        else:
-            rest_out[:, (u - 1) * B : u * B] = tile
-
-
-def join_kernel(tiles_done, sort_done, a0, a1, a2, a3, out):
+        rest_out[:, cols.start - B : cols.stop - B] = front[:, cols] + (dot(hot, high) + dot(hot, low))
+
+
+def join_kernel(r_done, tiles_done, sort_done, a0, a1, a2, a3, out):
     size = a0.shape[0]
     for i, a in enumerate((a0, a1, a2, a3)):
         out[i * size : (i + 1) * size, :] = a[...]
@@ -389,8 +392,8 @@
             pltpu.VMEM((slots, sources), jnp.int32),
             pltpu.VMEM((1, sources), jnp.int32),
             pltpu.VMEM((sources * 17, 128), F32),
-            pltpu.SemaphoreType.DMA((6,)),
-            pltpu.SemaphoreType.DMA((4,)),
+            pltpu.SemaphoreType.DMA((10,)),
+            pltpu.SemaphoreType.DMA((8,)),
         ],
         cost_estimate=pl.CostEstimate(flops=10**6, bytes_accessed=2 * 10**6, transcendentals=0),
         **ALONE,
@@ -424,24 +427,40 @@
         lead_kernel, (shaped(copies, B), shaped(KEEP, cols - B)), 3, scalars=0, flops=10**8, moved=2 * 10**6
     )(payload, front_rows, give)
     w_first = lax.all_to_all(send_first, "prow", 0, 0, tiled=True)
-    first, rest, done = call(
+    whole = lambda *shape: pl.BlockSpec(shape, lambda i: (0, 0))
+    first = pl.pallas_call(
+        tile_kernel,
+        out_shape=shaped(rows, B),
+        grid=(1,),
+        in_specs=[whole(*payload.shape), whole(rows, B)],
+        out_specs=whole(rows, B),
+        cost_estimate=pl.CostEstimate(flops=10**9, bytes_accessed=2 * 10**6, transcendentals=0),
+        **PARAMS,
+    )(payload, flat)
+    rest, done = call(
         tiles_kernel,
-        (shaped(rows, B), shaped(rows, cols - B), shaped(8, 128)),
+        (shaped(rows, cols - B), shaped(8, 128)),
         2,
         scalars=0,
         flops=4 * 10**9,
         moved=6 * 10**6,
     )(payload, flat)
+    r_other = core_swap(first)
     w_first, sorted_ = call(
         sort_first_kernel, (shaped(2 * B, B), shaped(8, 128)), 2, scalars=0, flops=10**8, moved=10**6
     )(slot, w_first)
-    joined = call(join_kernel, shaped(4 * KEEP, cols - B), 6, scalars=0, moved=10**6)(
-        done, sorted_, *ring(send_rest, shift_x)
-    )
+    joined = pl.pallas_call(
+        join_kernel,
+        out_shape=shaped(4 * KEEP, cols - B),
+        grid=(1,),
+        in_specs=[whole(8, 128)] * 3 + [whole(KEEP, cols - B)] * 4,
+        out_specs=whole(4 * KEEP, cols - B),
+        cost_estimate=pl.CostEstimate(flops=0, bytes_accessed=10**6, transcendentals=0),
+        **PARAMS,
+    )(r_other, done, sorted_, *ring(send_rest, shift_x))
     w_parts = ring(joined, shift_y)
 
-    def panels(w_first, first, active, place, joined):
-        r_other = core_swap(first)
+    def panels(w_first, first, r_other, active, place, joined):
         w_other = core_swap(w_first)
         half, tile = call(
             panel_kernel, (shaped(rows, B), shaped(rows, B)), 6, flops=2 * 10**9, moved=4 * 10**6
@@ -454,10 +473,10 @@
         o_late = lax.ppermute(n_late, "pcol", [(3, 2), (6, 7), (4, 5), (5, 4)])
         return n_early, n_late, o_early, o_late, tile
 
-    def nothing(w_first, first, active, place, joined):
+    def nothing(w_first, first, r_other, active, place, joined):
         return (jnp.zeros((rows, B), F32),) * 5
 
-    parts = lax.cond(fits[0] == 1, panels, nothing, w_first, first, active, place, joined)
+    parts = lax.cond(fits[0] == 1, panels, nothing, w_first, first, r_other, active, place, joined)
 
     def finish(payload, flat, own, active, place, *arrays):
         return pl.pallas_call(

time: 103 us -> 104 us (level)
  waiting for transfers between devices: 39.9 us -> 38.1 us
  starting transfers between devices: 31.6 us -> 32.9 us
    all_to_all x1, waiting for transfers between devices: 3.2 us -> 1.93 us  [body(): w_first = lax.all_to_all(send_first, 'prow', 0, 0, tiled=True)]
    ppermute x2, starting transfers between devices: 1.86 us -> 2.95 us  [core_swap(): lax.ppermute(x, 'pcol', [(i, i ^ 1) for i in range(lax.axis_size('pcol'))])]
    unnamed x19 -> x27, local copies, waits for them, and re-layouts: 1.82 us -> 2.63 us
    pallas_call x2 -> x3, Pallas kernels: 5.52 us -> 5.96 us  [the longest x1 3 us: body(): call(tiles_kernel, (shaped(rows, cols - B), shaped(8, 128)), 2, scalars=0...]
  transfers between devices with their start and end apart: 14 -> 14, of which waited for: 8 -> 7; matrix products, arithmetic and copies ran while one was open for 1% -> 1% of each run, Pallas kernels for 15% -> 15%
where the time goes in v13:
time: 104 us
  waiting for transfers between devices  38.1 us (37%)
  starting transfers between devices  32.9 us (32%)
  Pallas kernels  27.9 us (27%)
  local copies, waits for them, and re-layouts  2.63 us (3%)
    ppermute x1, waiting for transfers between devices, panels(): n_late = lax.ppermute(n_early, 'pcol', [(1, 3), (0, 6), (2, 4), (7, 5)])  17.5 us
    all_to_all x1, waiting for transfers between devices, body(): lax.all_to_all(payload, ('prow', 'pcol'), 0, 0, tiled=True)  11.2 us
    all_to_all x1, starting transfers between devices, body(): lax.all_to_all(payload, ('prow', 'pcol'), 0, 0, tiled=True)  10.4 us
    ppermute x6, starting transfers between devices, ring(): return [x] + [lax.ppermute(x, 'prow', shift(step)) for step in (1, -1, 2)]  8.86 us
    pallas_call x1, Pallas kernels, finish(): pl.pallas_call(finish_kernel, out_shape=shaped(*front.shape), in_specs=[S...  7.58 us
    pallas_call x1, Pallas kernels, panels(): call(panel_kernel, (shaped(rows, B), shaped(rows, B)), 6, flops=2 * 10 **...  4.99 us
    ppermute x6, waiting for transfers between devices, ring(): return [x] + [lax.ppermute(x, 'prow', shift(step)) for step in (1, -1, 2)]  3.89 us
    all_to_all x1, starting transfers between devices, body(): w_first = lax.all_to_all(send_first, 'prow', 0, 0, tiled=True)  3.73 us
  transfers between devices with their start and end apart: 14, of which 7 were waited for; matrix products, arithmetic and copies ran while one was open for 1% of the time, Pallas kernels for 15%

profile of v13, /device:TPU:65, one launch (start us, length us, event | category | flops | bytes accessed | tf_op | source)
XLA Modules:
  0.0 103.9 jit_solution(7573261495862079960)
XLA Ops:
  0.0 0.1 pad_add_fusion.place
  0.1 2.7 %shard_map.76 = f32[2176,128]{1,0:T(8,128)} custom-call(s32[3]{0:T(128)S(1)} %pad_add_fusion.place, f32[128,8,256]{2,1,0:T(8,128)} %bitcast.33, s32[8,128]{1,0:T(8,128)} %bitcast.34, s32[1,128]{1,0:T(1,128)} %counts_hbm.1), custom_call_target="tpu_custom_call" | custom-call | flops 1000000 | bytes 2000000 | tf_op jit(solution)/shard_map/pallas_call | solution.py:385
  2.8 10.4 %all-to-all-start.2 = ((f32[2176,1,128]{2,1,0:T(1,128)}), f32[2176,1,128]{2,1,0:T(1,128)S(1)}, u32[]{:S(2)}, u32[]{:S(2)}) async-start(f32[2176,1,128]{2,1,0:T(1,128)} %bitcast.31), calls=%async_computation.2 | async-start | bytes 2228224 | tf_op jit(solution)/shard_map/all_to_all | solution.py:401
  13.2 0.0 copy-start.13
  13.2 3.4 %shard_map.75 = (s32[512,128]{1,0:T(8,128)S(1)}, f32[2,512,128]{2,1,0:T(8,128)}, s32[48,128]{1,0:T(8,128)S(1)}, bf16[512,768]{1,0:T(8,128)(2,1)S(1)}, bf16[512,768]{1,0:T(8,128)(2,1)}, /*index=5*/s32[1]{0:T(128)}) custom-call(s32[3]{0:T(128)S(1)} %pad_add_fusion.place, s32[2,16,256]{2,1,0:T(8,128)S(1)} %copy-done.6, s32[2,4,16,256]{3,2,1,0:T(8,128)S(1)} %copy-done.5, ...), custom_call_target="tpu_custom_call" | custom-call | flops 1000000000 | bytes 1000000 | tf_op jit(solution)/shard_map/pallas_call | solution.py:405
  16.6 0.5 copy.11
  17.1 0.0 copy-start.8
  17.1 1.3 %copy-done.8 = f32[64,8,4,256]{3,1,2,0:T(8,128)} copy-done((f32[64,8,4,256]{3,1,2,0:T(8,128)}, f32[64,8,4,256]{3,1,2,0:T(8,128)S(1)}, u32[]{:S(2)}) %copy-start.8) | copy-done | bytes 2097176
  18.4 0.6 shard_map.77.front_rows
  18.9 11.2 %all-to-all-done.2 = f32[2176,1,128]{2,1,0:T(1,128)S(1)} async-done(((f32[2176,1,128]{2,1,0:T(1,128)}), f32[2176,1,128]{2,1,0:T(1,128)S(1)}, u32[]{:S(2)}, u32[]{:S(2)}) %all-to-all-start.2) | async-done | bytes 1114144 | tf_op jit(solution)/shard_map/all_to_all | solution.py:401
  30.1 1.4 %shard_map.78 = (f32[768,256]{1,0:T(8,128)}, f32[48,768]{1,0:T(8,128)S(1)}) custom-call(f32[2176,128]{1,0:T(8,128)S(1)} %bitcast.27, f32[192,256]{1,0:T(8,128)S(1)} %shard_map.77.front_rows, s32[48,128]{1,0:T(8,128)S(1)} %get-tuple-element.117.give), custom_call_target="tpu_custom_call" | custom-call | flops 100000000 | bytes 2000000 | tf_op jit(solution)/shard_map/pallas_call | solution.py:426
  31.5 3.7 %all-to-all-start.3 = ((f32[16,48,256]{2,1,0:T(8,128)}), f32[16,48,256]{2,1,0:T(8,128)S(1)}, u32[]{:S(2)}, u32[]{:S(2)}) async-start(f32[16,48,256]{2,1,0:T(8,128)} %bitcast.12), calls=%async_computation.3 | async-start | bytes 1572864 | tf_op jit(solution)/shard_map/all_to_all | solution.py:429
  35.2 0.0 copy-start.9
  35.2 2.2 %shard_map.80 = f32[512,256]{1,0:T(8,128)S(1)} custom-call(f32[2176,128]{1,0:T(8,128)} %bitcast.28, f32[512,1024]{1,0:T(8,128)} %bitcast.24), custom_call_target="tpu_custom_call" | custom-call | flops 1000000000 | bytes 2000000 | tf_op jit(solution)/shard_map/pallas_call | solution.py:431
  37.5 1.2 %collective-permute-start.11 = (f32[512,256]{1,0:T(8,128)S(1)}, f32[512,256]{1,0:T(8,128)S(1)}, u32[]{:S(2)}, u32[]{:S(2)}) collective-permute-start(f32[512,256]{1,0:T(8,128)S(1)} %shard_map.80), channel_id=1, source_target_pairs={{0,1},{1,0},{2,3},{3,2},{4,5},{5,4},{6,7},{7,6},{8,9},{9,8},{10,11... | collective-permute-start | bytes 1572872 | tf_op jit(solution)/shard_map/ppermute | solution.py:353
  38.7 3.2 %collective-permute-start.14 = (f32[48,768]{1,0:T(8,128)S(1)}, f32[48,768]{1,0:T(8,128)S(1)}, u32[]{:S(2)}, u32[]{:S(2)}) collective-permute-start(f32[48,768]{1,0:T(8,128)S(1)} %get-tuple-element.129.a0), channel_id=1, source_target_pairs={{0,16},{8,24},{16,0},{24,8},{32,48},{40,56},{48,32},{56,40},{64,80... | collective-permute-start | bytes 442376 | tf_op jit(solution)/shard_map/ppermute | solution.py:365
  41.8 0.9 collective-permute-start.13
  42.7 0.6 collective-permute-start.12
  43.3 3.0 %shard_map.81 = (f32[512,768]{1,0:T(8,128)}, f32[8,128]{1,0:T(8,128)S(1)}) custom-call(f32[2176,128]{1,0:T(8,128)S(1)} %bitcast.30, f32[512,1024]{1,0:T(8,128)S(1)} %bitcast.25), custom_call_target="tpu_custom_call" | custom-call | flops 4000000000 | bytes 6000000 | tf_op jit(solution)/shard_map/pallas_call | solution.py:440
  46.3 1.9 %all-to-all-done.3 = f32[16,48,256]{2,1,0:T(8,128)S(1)} async-done(((f32[16,48,256]{2,1,0:T(8,128)}), f32[16,48,256]{2,1,0:T(8,128)S(1)}, u32[]{:S(2)}, u32[]{:S(2)}) %all-to-all-start.3) | async-done | bytes 786464 | tf_op jit(solution)/shard_map/all_to_all | solution.py:429
  48.3 1.4 %shard_map.79 = (f32[512,256]{1,0:T(8,128)}, f32[8,128]{1,0:T(8,128)S(1)}) custom-call(bf16[512,768]{1,0:T(8,128)(2,1)S(1)} %get-tuple-element.116.slot, f32[768,256]{1,0:T(8,128)S(1)} %bitcast.21), custom_call_target="tpu_custom_call" | custom-call | flops 100000000 | bytes 1000000 | tf_op jit(solution)/shard_map/pallas_call | solution.py:449
  49.7 0.0 collective-permute-done.14.a3
  49.7 1.6 %collective-permute-done.13.a2 = f32[48,768]{1,0:T(8,128)S(1)} collective-permute-done((f32[48,768]{1,0:T(8,128)S(1)}, f32[48,768]{1,0:T(8,128)S(1)}, u32[]{:S(2)}, u32[]{:S(2)}) %collective-permute-start.13) | collective-permute-done | bytes 147488 | tf_op jit(solution)/shard_map/ppermute | solution.py:365
  51.3 2.2 %collective-permute-done.12.a1 = f32[48,768]{1,0:T(8,128)S(1)} collective-permute-done((f32[48,768]{1,0:T(8,128)S(1)}, f32[48,768]{1,0:T(8,128)S(1)}, u32[]{:S(2)}, u32[]{:S(2)}) %collective-permute-start.12) | collective-permute-done | bytes 147488 | tf_op jit(solution)/shard_map/ppermute | solution.py:365
  53.5 0.0 collective-permute-done.11.r_done
  53.5 0.8 copy-done.16
  54.3 0.7 shard_map.82
  55.1 2.8 %collective-permute-start.17 = (f32[192,768]{1,0:T(8,128)S(1)}, f32[192,768]{1,0:T(8,128)}, u32[]{:S(2)}, u32[]{:S(2)}) collective-permute-start(f32[192,768]{1,0:T(8,128)S(1)} %shard_map.82), channel_id=1, source_target_pairs={{0,64},{8,72},{16,80},{24,88},{32,96},{40,104},{48,112},{56,120},{... | collective-permute-start | bytes 1769480 | tf_op jit(solution)/shard_map/ppermute | solution.py:365
  57.8 0.9 collective-permute-start.16
  58.7 0.6 collective-permute-start.15
  60.0 0.0 copy-start.10
  60.0 35.9 %conditional.2 = (f32[512,256]{1,0:T(8,128)}, f32[512,256]{1,0:T(8,128)}, f32[512,256]{1,0:T(8,128)}, f32[512,256]{1,0:T(8,128)}, f32[512,256]{1,0:T(8,128)}) conditional(s32[]{:T(128)} %bitcast.5, () %tuple.22, (s32[]{:T(128)}, f32[512,256]{1,0:T(8,128)}, s32[3]{0:T(128)S(1)}, f32[512,256]{1,0:T(8,128)S(1)}, f32[512,256]{1,0:T(8,128)}, ...), branch_computations={%region_0.0_spmd, %region_1.2_spmd} | conditional | flops 2000131072 | bytes 16058886 | solution.py:479
  60.0 1.8 %collective-permute-start = (f32[512,256]{1,0:T(8,128)}, f32[512,256]{1,0:T(8,128)S(1)}, u32[]{:S(2)}, u32[]{:S(2)}) collective-permute-start(f32[512,256]{1,0:T(8,128)} %get-tuple-element.62.w_own), channel_id=1, source_target_pairs={{0,1},{1,0},{2,3},{3,2},{4,5},{5,4},{6,7},{7,6},{8,9},{9,8},{10,11... | collective-permute-start | bytes 1572872 | tf_op jit(solution)/shard_map/cond/branch_1_fun/ppermute | solution.py:353
  61.8 1.7 %collective-permute-done.w_other = f32[512,256]{1,0:T(8,128)S(1)} collective-permute-done((f32[512,256]{1,0:T(8,128)}, f32[512,256]{1,0:T(8,128)S(1)}, u32[]{:S(2)}, u32[]{:S(2)}) %collective-permute-start) | collective-permute-done | bytes 524320 | tf_op jit(solution)/shard_map/cond/branch_1_fun/ppermute | solution.py:353
  63.5 5.0 %branch_1_fun.2 = (f32[512,256]{1,0:T(8,128)S(1)}, f32[512,256]{1,0:T(8,128)}) custom-call(s32[3]{0:T(128)S(1)} %get-tuple-element.61.place, f32[512,256]{1,0:T(8,128)} %get-tuple-element.62.w_own, f32[512,256]{1,0:T(8,128)S(1)} %collective-permute-done.w_other, f32[512,256]{1,0:T(8,128)S(1)} %get-tuple-element.63.r_own, ...), custom_call_target="tpu_custom_call" | custom-call | flops 2000000000 | bytes 4000000 | tf_op jit(solution)/shard_map/cond/branch_1_fun/pallas_call | solution.py:465
  68.5 1.5 %collective-permute-start.1 = (f32[512,256]{1,0:T(8,128)S(1)}, f32[512,256]{1,0:T(8,128)}, u32[]{:S(2)}, u32[]{:S(2)}) collective-permute-start(f32[512,256]{1,0:T(8,128)S(1)} %get-tuple-element.66), channel_id=1, source_target_pairs={{0,2},{1,7},{8,10},{9,15},{16,18},{17,23},{24,26},{25,31},{32,34},... | collective-permute-start | bytes 1572872 | tf_op jit(solution)/shard_map/cond/branch_1_fun/ppermute | solution.py:469
  70.0 0.9 broadcast_select_fusion
  70.8 1.3 %collective-permute-start.2 = (f32[512,256]{1,0:T(8,128)}, f32[512,256]{1,0:T(8,128)}, u32[]{:S(2)}, u32[]{:S(2)}) collective-permute-start(f32[512,256]{1,0:T(8,128)} %broadcast_select_fusion), channel_id=1, source_target_pairs={{1,3},{0,6},{2,4},{7,5},{9,11},{8,14},{10,12},{15,13},{17,19},{16,... | collective-permute-start | bytes 1572872 | tf_op jit(solution)/shard_map/cond/branch_1_fun/ppermute | solution.py:471
  72.1 1.5 %collective-permute-start.3 = (f32[512,256]{1,0:T(8,128)}, f32[512,256]{1,0:T(8,128)}, u32[]{:S(2)}, u32[]{:S(2)}) collective-permute-start(f32[512,256]{1,0:T(8,128)} %broadcast_select_fusion), channel_id=1, source_target_pairs={{0,1},{1,0},{2,3},{7,6},{8,9},{9,8},{10,11},{15,14},{16,17},{17,16... | collective-permute-start | bytes 1572872 | tf_op jit(solution)/shard_map/cond/branch_1_fun/ppermute | solution.py:472
  73.6 17.5 %collective-permute-done.2 = f32[512,256]{1,0:T(8,128)} collective-permute-done((f32[512,256]{1,0:T(8,128)}, f32[512,256]{1,0:T(8,128)}, u32[]{:S(2)}, u32[]{:S(2)}) %collective-permute-start.2) | collective-permute-done | bytes 524320 | tf_op jit(solution)/shard_map/cond/branch_1_fun/ppermute | solution.py:471
  91.1 2.8 %collective-permute-start.4 = (f32[512,256]{1,0:T(8,128)}, f32[512,256]{1,0:T(8,128)}, u32[]{:S(2)}, u32[]{:S(2)}) collective-permute-start(f32[512,256]{1,0:T(8,128)} %collective-permute-done.2), channel_id=1, source_target_pairs={{3,2},{6,7},{4,5},{5,4},{11,10},{14,15},{12,13},{13,12},{19,18},{2... | collective-permute-start | bytes 1572872 | tf_op jit(solution)/shard_map/cond/branch_1_fun/ppermute | solution.py:473
  94.0 0.0 collective-permute-done.3
  94.0 1.8 %collective-permute-done.4 = f32[512,256]{1,0:T(8,128)} collective-permute-done((f32[512,256]{1,0:T(8,128)}, f32[512,256]{1,0:T(8,128)}, u32[]{:S(2)}, u32[]{:S(2)}) %collective-permute-start.4) | collective-permute-done | bytes 524320 | tf_op jit(solution)/shard_map/cond/branch_1_fun/ppermute | solution.py:473
  95.8 0.0 collective-permute-done.17
  95.8 0.0 collective-permute-done.16
  95.8 0.0 collective-permute-done.15
  95.8 7.8 %conditional.3 = (f32[2,256,4,256]{3,2,1,0:T(4,128)}) conditional(s32[]{:T(128)} %bitcast.5, (f32[2176,128]{1,0:T(8,128)}, f32[512,1024]{1,0:T(8,128)S(1)}, s32[512,128]{1,0:T(8,128)S(1)}, s32[]{:T(128)}, s32[3]{0:T(128)S(1)}, /*index=5*/f32[2,512,128]{2,1,0:T(8,128)}) %tuple.32, (s32[3]{0:T(128)S(1)}, f32[512,256]{1,0:T(8,128)}, ...), branch_computations={%region_2.4_spmd, %region_4.5_spmd} | conditional | flops 8000884736 | bytes 85798736 | solution.py:523
  96.1 7.6 %branch_1_fun.3 = f32[2,256,4,256]{3,2,1,0:T(4,128)} custom-call(s32[3]{0:T(128)S(1)} %get-tuple-element.78.place, f32[512,256]{1,0:T(8,128)} %get-tuple-element.79.n_early, f32[512,256]{1,0:T(8,128)} %get-tuple-element.80.n_late, f32[512,256]{1,0:T(8,128)} %get-tuple-element.81.o_early, f32[512,256]{1,0:T(8,128)} %get-tuple-element.82.o_late, ...), custom_call_target="tpu_custom_call" | custom-call | flops 4000000000 | bytes 8000000 | tf_op jit(solution)/shard_map/cond/branch_1_fun/pallas_call | solution.py:482
  (21 shorter events, 0.0 us)
Async XLA Ops:
  0.1 13.1 %copy-start.5 = (s32[2,4,16,256]{3,2,1,0:T(8,128)S(1)}, s32[2,4,16,256]{3,2,1,0:T(8,128)}, u32[]{:S(2)}) copy-start(s32[2,4,16,256]{3,2,1,0:T(8,128)} %level_picks.1) | copy-start | bytes 393220
  0.1 13.1 %copy-start.6 = (s32[2,16,256]{2,1,0:T(8,128)S(1)}, s32[2,16,256]{2,1,0:T(8,128)}, u32[]{:S(2)}) copy-start(s32[2,16,256]{2,1,0:T(8,128)} %local_picks.1) | copy-start | bytes 98308
  0.1 13.1 %copy-start.7 = (s32[2,256]{1,0:T(2,128)S(1)}, s32[2,256]{1,0:T(2,128)}, u32[]{:S(2)}) copy-start(s32[2,256]{1,0:T(2,128)} %order.1) | copy-start | bytes 6148
  2.8 27.3 %all-to-all-start.2 = ((f32[2176,1,128]{2,1,0:T(1,128)}), f32[2176,1,128]{2,1,0:T(1,128)S(1)}, u32[]{:S(2)}, u32[]{:S(2)}) async-start(f32[2176,1,128]{2,1,0:T(1,128)} %bitcast.31), calls=%async_computation.2 | async-start | bytes 2228224 | tf_op jit(solution)/shard_map/all_to_all | solution.py:401
  13.2 3.4 %copy-start.13 = (f32[2,256,4,256]{3,2,1,0:T(4,128)S(1)}, f32[2,256,4,256]{3,2,1,0:T(4,128)}, u32[]{:S(2)}) copy-start(f32[2,256,4,256]{3,2,1,0:T(4,128)} %param.11) | copy-start | bytes 6291460
  17.1 1.3 %copy-start.8 = (f32[64,8,4,256]{3,1,2,0:T(8,128)}, f32[64,8,4,256]{3,1,2,0:T(8,128)S(1)}, u32[]{:S(2)}) copy-start(f32[64,8,4,256]{3,1,2,0:T(8,128)S(1)} %copy.11) | copy-start | bytes 6291460
  30.1 1.4 %copy-start.11 = (f32[2176,1,128]{2,1,0:T(1,128)}, f32[2176,1,128]{2,1,0:T(1,128)S(1)}, u32[]{:S(2)}) copy-start(f32[2176,1,128]{2,1,0:T(1,128)S(1)} %all-to-all-done.2) | copy-start | bytes 3342340
  31.5 16.8 %all-to-all-start.3 = ((f32[16,48,256]{2,1,0:T(8,128)}), f32[16,48,256]{2,1,0:T(8,128)S(1)}, u32[]{:S(2)}, u32[]{:S(2)}) async-start(f32[16,48,256]{2,1,0:T(8,128)} %bitcast.12), calls=%async_computation.3 | async-start | bytes 1572864 | tf_op jit(solution)/shard_map/all_to_all | solution.py:429
  35.2 8.1 %copy-start.9 = (f32[64,8,4,256]{3,1,2,0:T(8,128)S(1)}, f32[64,8,4,256]{3,1,2,0:T(8,128)}, u32[]{:S(2)}) copy-start(f32[64,8,4,256]{3,1,2,0:T(8,128)} %copy-done.8) | copy-start | bytes 6291460
  35.2 8.1 %copy-start.12 = (f32[2176,1,128]{2,1,0:T(1,128)S(1)}, f32[2176,1,128]{2,1,0:T(1,128)}, u32[]{:S(2)}) copy-start(f32[2176,1,128]{2,1,0:T(1,128)} %copy-done.11) | copy-start | bytes 3342340
  37.5 8.8 %copy-start.14 = (f32[512,256]{1,0:T(8,128)}, f32[512,256]{1,0:T(8,128)S(1)}, u32[]{:S(2)}) copy-start(f32[512,256]{1,0:T(8,128)S(1)} %shard_map.80) | copy-start | bytes 1572868
  37.5 16.0 %collective-permute-start.11 = (f32[512,256]{1,0:T(8,128)S(1)}, f32[512,256]{1,0:T(8,128)S(1)}, u32[]{:S(2)}, u32[]{:S(2)}) collective-permute-start(f32[512,256]{1,0:T(8,128)S(1)} %shard_map.80), channel_id=1, source_target_pairs={{0,1},{1,0},{2,3},{3,2},{4,5},{5,4},{6,7},{7,6},{8,9},{9,8},{10,11... | collective-permute-start | bytes 1572872 | tf_op jit(solution)/shard_map/ppermute | solution.py:353
  38.7 11.0 %collective-permute-start.14 = (f32[48,768]{1,0:T(8,128)S(1)}, f32[48,768]{1,0:T(8,128)S(1)}, u32[]{:S(2)}, u32[]{:S(2)}) collective-permute-start(f32[48,768]{1,0:T(8,128)S(1)} %get-tuple-element.129.a0), channel_id=1, source_target_pairs={{0,16},{8,24},{16,0},{24,8},{32,48},{40,56},{48,32},{56,40},{64,80... | collective-permute-start | bytes 442376 | tf_op jit(solution)/shard_map/ppermute | solution.py:365
  41.8 9.4 %collective-permute-start.13 = (f32[48,768]{1,0:T(8,128)S(1)}, f32[48,768]{1,0:T(8,128)S(1)}, u32[]{:S(2)}, u32[]{:S(2)}) collective-permute-start(f32[48,768]{1,0:T(8,128)S(1)} %get-tuple-element.129.a0), channel_id=1, source_target_pairs={{0,24},{8,0},{16,8},{24,16},{32,56},{40,32},{48,40},{56,48},{64,88... | collective-permute-start | bytes 442376 | tf_op jit(solution)/shard_map/ppermute | solution.py:365
  42.7 10.8 %collective-permute-start.12 = (f32[48,768]{1,0:T(8,128)S(1)}, f32[48,768]{1,0:T(8,128)S(1)}, u32[]{:S(2)}, u32[]{:S(2)}) collective-permute-start(f32[48,768]{1,0:T(8,128)S(1)} %get-tuple-element.129.a0), channel_id=1, source_target_pairs={{0,8},{8,16},{16,24},{24,0},{32,40},{40,48},{48,56},{56,32},{64,72... | collective-permute-start | bytes 442376 | tf_op jit(solution)/shard_map/ppermute | solution.py:365
  48.2 11.7 %copy-start.15 = (f32[512,256]{1,0:T(8,128)S(1)}, f32[512,256]{1,0:T(8,128)}, u32[]{:S(2)}) copy-start(f32[512,256]{1,0:T(8,128)} %copy-done.14) | copy-start | bytes 1572868
  48.2 11.7 %copy-start.17 = (f32[2,512,128]{2,1,0:T(8,128)S(1)}, f32[2,512,128]{2,1,0:T(8,128)}, u32[]{:S(2)}) copy-start(f32[2,512,128]{2,1,0:T(8,128)} %get-tuple-element.115) | copy-start | bytes 1572868
  53.5 0.8 copy-start.16
  55.1 40.8 %collective-permute-start.17 = (f32[192,768]{1,0:T(8,128)S(1)}, f32[192,768]{1,0:T(8,128)}, u32[]{:S(2)}, u32[]{:S(2)}) collective-permute-start(f32[192,768]{1,0:T(8,128)S(1)} %shard_map.82), channel_id=1, source_target_pairs={{0,64},{8,72},{16,80},{24,88},{32,96},{40,104},{48,112},{56,120},{... | collective-permute-start | bytes 1769480 | tf_op jit(solution)/shard_map/ppermute | solution.py:365
  57.8 38.0 %collective-permute-start.16 = (f32[192,768]{1,0:T(8,128)S(1)}, f32[192,768]{1,0:T(8,128)}, u32[]{:S(2)}, u32[]{:S(2)}) collective-permute-start(f32[192,768]{1,0:T(8,128)S(1)} %shard_map.82), channel_id=1, source_target_pairs={{0,96},{8,104},{16,112},{24,120},{32,0},{40,8},{48,16},{56,24},{64... | collective-permute-start | bytes 1769480 | tf_op jit(solution)/shard_map/ppermute | solution.py:365
  58.7 37.1 %collective-permute-start.15 = (f32[192,768]{1,0:T(8,128)S(1)}, f32[192,768]{1,0:T(8,128)}, u32[]{:S(2)}, u32[]{:S(2)}) collective-permute-start(f32[192,768]{1,0:T(8,128)S(1)} %shard_map.82), channel_id=1, source_target_pairs={{0,32},{8,40},{16,48},{24,56},{32,64},{40,72},{48,80},{56,88},{64,... | collective-permute-start | bytes 1769480 | tf_op jit(solution)/shard_map/ppermute | solution.py:365
  60.0 35.9 %copy-start.10 = (f32[64,8,4,256]{3,1,2,0:T(8,128)S(1)}, f32[64,8,4,256]{3,1,2,0:T(8,128)}, u32[]{:S(2)}) copy-start(f32[64,8,4,256]{3,1,2,0:T(8,128)} %copy-done.8) | copy-start | bytes 6291460
  60.0 3.5 %collective-permute-start = (f32[512,256]{1,0:T(8,128)}, f32[512,256]{1,0:T(8,128)S(1)}, u32[]{:S(2)}, u32[]{:S(2)}) collective-permute-start(f32[512,256]{1,0:T(8,128)} %get-tuple-element.62.w_own), channel_id=1, source_target_pairs={{0,1},{1,0},{2,3},{3,2},{4,5},{5,4},{6,7},{7,6},{8,9},{9,8},{10,11... | collective-permute-start | bytes 1572872 | tf_op jit(solution)/shard_map/cond/branch_1_fun/ppermute | solution.py:353
  68.5 1.5 %collective-permute-start.1 = (f32[512,256]{1,0:T(8,128)S(1)}, f32[512,256]{1,0:T(8,128)}, u32[]{:S(2)}, u32[]{:S(2)}) collective-permute-start(f32[512,256]{1,0:T(8,128)S(1)} %get-tuple-element.66), channel_id=1, source_target_pairs={{0,2},{1,7},{8,10},{9,15},{16,18},{17,23},{24,26},{25,31},{32,34},... | collective-permute-start | bytes 1572872 | tf_op jit(solution)/shard_map/cond/branch_1_fun/ppermute | solution.py:469
  70.8 20.3 %collective-permute-start.2 = (f32[512,256]{1,0:T(8,128)}, f32[512,256]{1,0:T(8,128)}, u32[]{:S(2)}, u32[]{:S(2)}) collective-permute-start(f32[512,256]{1,0:T(8,128)} %broadcast_select_fusion), channel_id=1, source_target_pairs={{1,3},{0,6},{2,4},{7,5},{9,11},{8,14},{10,12},{15,13},{17,19},{16,... | collective-permute-start | bytes 1572872 | tf_op jit(solution)/shard_map/cond/branch_1_fun/ppermute | solution.py:471
  72.1 21.8 %collective-permute-start.3 = (f32[512,256]{1,0:T(8,128)}, f32[512,256]{1,0:T(8,128)}, u32[]{:S(2)}, u32[]{:S(2)}) collective-permute-start(f32[512,256]{1,0:T(8,128)} %broadcast_select_fusion), channel_id=1, source_target_pairs={{0,1},{1,0},{2,3},{7,6},{8,9},{9,8},{10,11},{15,14},{16,17},{17,16... | collective-permute-start | bytes 1572872 | tf_op jit(solution)/shard_map/cond/branch_1_fun/ppermute | solution.py:472
  91.1 4.7 %collective-permute-start.4 = (f32[512,256]{1,0:T(8,128)}, f32[512,256]{1,0:T(8,128)}, u32[]{:S(2)}, u32[]{:S(2)}) collective-permute-start(f32[512,256]{1,0:T(8,128)} %collective-permute-done.2), channel_id=1, source_target_pairs={{3,2},{6,7},{4,5},{5,4},{11,10},{14,15},{12,13},{13,12},{19,18},{2... | collective-permute-start | bytes 1572872 | tf_op jit(solution)/shard_map/cond/branch_1_fun/ppermute | solution.py:473

commit v14 on v13

--- a/solution.py
+++ b/solution.py
@@ -202,13 +202,13 @@
         rest_out[:, cols.start - B : cols.stop - B] = front[:, cols] + (dot(hot, high) + dot(hot, low))
 
 
-def join_kernel(r_done, tiles_done, sort_done, a0, a1, a2, a3, out):
+def join_kernel(tiles_done, sort_done, a0, a1, a2, a3, out):
     size = a0.shape[0]
     for i, a in enumerate((a0, a1, a2, a3)):
         out[i * size : (i + 1) * size, :] = a[...]
 
 
-def sort_first_kernel(slot, gathered, out, done_out):
+def sort_first_kernel(r_done, slot, gathered, out, done_out):
     done_out[...] = jnp.zeros_like(done_out)
     out[...] = pick(slot[...], gathered[...])
 
@@ -437,6 +437,7 @@
         cost_estimate=pl.CostEstimate(flops=10**9, bytes_accessed=2 * 10**6, transcendentals=0),
         **PARAMS,
     )(payload, flat)
+    r_other = core_swap(first)
     rest, done = call(
         tiles_kernel,
         (shaped(rows, cols - B), shaped(8, 128)),
@@ -445,19 +446,12 @@
         flops=4 * 10**9,
         moved=6 * 10**6,
     )(payload, flat)
-    r_other = core_swap(first)
     w_first, sorted_ = call(
-        sort_first_kernel, (shaped(2 * B, B), shaped(8, 128)), 2, scalars=0, flops=10**8, moved=10**6
-    )(slot, w_first)
-    joined = pl.pallas_call(
-        join_kernel,
-        out_shape=shaped(4 * KEEP, cols - B),
-        grid=(1,),
-        in_specs=[whole(8, 128)] * 3 + [whole(KEEP, cols - B)] * 4,
-        out_specs=whole(4 * KEEP, cols - B),
-        cost_estimate=pl.CostEstimate(flops=0, bytes_accessed=10**6, transcendentals=0),
-        **PARAMS,
-    )(r_other, done, sorted_, *ring(send_rest, shift_x))
+        sort_first_kernel, (shaped(2 * B, B), shaped(8, 128)), 3, scalars=0, flops=10**8, moved=10**6
+    )(r_other, slot, w_first)
+    joined = call(join_kernel, shaped(4 * KEEP, cols - B), 6, scalars=0, moved=10**6)(
+        done, sorted_, *ring(send_rest, shift_x)
+    )
     w_parts = ring(joined, shift_y)
 
     def panels(w_first, first, r_other, active, place, joined):

time: 104 us -> 103 us (level)
    unnamed x27 -> x25, local copies, waits for them, and re-layouts: 2.63 us -> 1.83 us
where the time goes in v14:
time: 103 us; the launch traced here: 102 us
  waiting for transfers between devices  38.1 us (37%)
  starting transfers between devices  32.9 us (32%)
  Pallas kernels  27.4 us (27%)
  local copies, waits for them, and re-layouts  1.83 us (2%)
    ppermute x1, waiting for transfers between devices, panels(): n_late = lax.ppermute(n_early, 'pcol', [(1, 3), (0, 6), (2, 4), (7, 5)])  17.6 us
    all_to_all x1, waiting for transfers between devices, body(): lax.all_to_all(payload, ('prow', 'pcol'), 0, 0, tiled=True)  11.2 us
    all_to_all x1, starting transfers between devices, body(): lax.all_to_all(payload, ('prow', 'pcol'), 0, 0, tiled=True)  10.4 us
    ppermute x6, starting transfers between devices, ring(): return [x] + [lax.ppermute(x, 'prow', shift(step)) for step in (1, -1, 2)]  8.87 us
    pallas_call x1, Pallas kernels, finish(): pl.pallas_call(finish_kernel, out_shape=shaped(*front.shape), in_specs=[S...  7.58 us
    pallas_call x1, Pallas kernels, panels(): call(panel_kernel, (shaped(rows, B), shaped(rows, B)), 6, flops=2 * 10 **...  5.15 us
    ppermute x6, waiting for transfers between devices, ring(): return [x] + [lax.ppermute(x, 'prow', shift(step)) for step in (1, -1, 2)]  3.91 us
    all_to_all x1, starting transfers between devices, body(): w_first = lax.all_to_all(send_first, 'prow', 0, 0, tiled=True)  3.74 us
  transfers between devices with their start and end apart: 14, of which 7 were waited for; matrix products, arithmetic and copies ran while one was open for 1% of the time, Pallas kernels for 15%

profile of v14, /device:TPU:65, one launch (start us, length us, event | category | flops | bytes accessed | tf_op | source)
XLA Modules:
  0.0 102.4 jit_solution(7561106802699184554)
XLA Ops:
  0.0 0.1 pad_add_fusion.place
  0.1 2.7 %shard_map.76 = f32[2176,128]{1,0:T(8,128)} custom-call(s32[3]{0:T(128)S(1)} %pad_add_fusion.place, f32[128,8,256]{2,1,0:T(8,128)} %bitcast.33, s32[8,128]{1,0:T(8,128)} %bitcast.34, s32[1,128]{1,0:T(1,128)} %counts_hbm.1), custom_call_target="tpu_custom_call" | custom-call | flops 1000000 | bytes 2000000 | tf_op jit(solution)/shard_map/pallas_call | solution.py:385
  2.8 10.4 %all-to-all-start.2 = ((f32[2176,1,128]{2,1,0:T(1,128)}), f32[2176,1,128]{2,1,0:T(1,128)S(1)}, u32[]{:S(2)}, u32[]{:S(2)}) async-start(f32[2176,1,128]{2,1,0:T(1,128)} %bitcast.31), calls=%async_computation.2 | async-start | bytes 2228224 | tf_op jit(solution)/shard_map/all_to_all | solution.py:401
  13.2 0.0 copy-start.13
  13.2 3.4 %shard_map.75 = (s32[512,128]{1,0:T(8,128)S(1)}, f32[2,512,128]{2,1,0:T(8,128)}, s32[48,128]{1,0:T(8,128)S(1)}, bf16[512,768]{1,0:T(8,128)(2,1)S(1)}, bf16[512,768]{1,0:T(8,128)(2,1)}, /*index=5*/s32[1]{0:T(128)}) custom-call(s32[3]{0:T(128)S(1)} %pad_add_fusion.place, s32[2,16,256]{2,1,0:T(8,128)S(1)} %copy-done.6, s32[2,4,16,256]{3,2,1,0:T(8,128)S(1)} %copy-done.5, ...), custom_call_target="tpu_custom_call" | custom-call | flops 1000000000 | bytes 1000000 | tf_op jit(solution)/shard_map/pallas_call | solution.py:405
  16.6 0.0 copy-done.13
  16.6 0.5 copy.11
  17.1 0.0 copy-start.8
  17.1 1.3 %copy-done.8 = f32[64,8,4,256]{3,1,2,0:T(8,128)} copy-done((f32[64,8,4,256]{3,1,2,0:T(8,128)}, f32[64,8,4,256]{3,1,2,0:T(8,128)S(1)}, u32[]{:S(2)}) %copy-start.8) | copy-done | bytes 2097176
  18.4 0.6 shard_map.78.front_rows
  18.9 11.2 %all-to-all-done.2 = f32[2176,1,128]{2,1,0:T(1,128)S(1)} async-done(((f32[2176,1,128]{2,1,0:T(1,128)}), f32[2176,1,128]{2,1,0:T(1,128)S(1)}, u32[]{:S(2)}, u32[]{:S(2)}) %all-to-all-start.2) | async-done | bytes 1114144 | tf_op jit(solution)/shard_map/all_to_all | solution.py:401
  30.1 1.4 %shard_map.79 = (f32[768,256]{1,0:T(8,128)}, f32[48,768]{1,0:T(8,128)S(1)}) custom-call(f32[2176,128]{1,0:T(8,128)S(1)} %bitcast.27, f32[192,256]{1,0:T(8,128)S(1)} %shard_map.78.front_rows, s32[48,128]{1,0:T(8,128)S(1)} %get-tuple-element.117.give), custom_call_target="tpu_custom_call" | custom-call | flops 100000000 | bytes 2000000 | tf_op jit(solution)/shard_map/pallas_call | solution.py:426
  31.5 3.7 %all-to-all-start.3 = ((f32[16,48,256]{2,1,0:T(8,128)}), f32[16,48,256]{2,1,0:T(8,128)S(1)}, u32[]{:S(2)}, u32[]{:S(2)}) async-start(f32[16,48,256]{2,1,0:T(8,128)} %bitcast.12), calls=%async_computation.3 | async-start | bytes 1572864 | tf_op jit(solution)/shard_map/all_to_all | solution.py:429
  35.2 0.0 copy-start.9
  35.3 2.2 %shard_map.77 = f32[512,256]{1,0:T(8,128)S(1)} custom-call(f32[2176,128]{1,0:T(8,128)} %bitcast.28, f32[512,1024]{1,0:T(8,128)} %bitcast.24), custom_call_target="tpu_custom_call" | custom-call | flops 1000000000 | bytes 2000000 | tf_op jit(solution)/shard_map/pallas_call | solution.py:431
  37.5 1.2 %collective-permute-start.11 = (f32[512,256]{1,0:T(8,128)S(1)}, f32[512,256]{1,0:T(8,128)S(1)}, u32[]{:S(2)}, u32[]{:S(2)}) collective-permute-start(f32[512,256]{1,0:T(8,128)S(1)} %shard_map.77), channel_id=1, source_target_pairs={{0,1},{1,0},{2,3},{3,2},{4,5},{5,4},{6,7},{7,6},{8,9},{9,8},{10,11... | collective-permute-start | bytes 1572872 | tf_op jit(solution)/shard_map/ppermute | solution.py:353
  38.7 3.2 %collective-permute-start.14 = (f32[48,768]{1,0:T(8,128)S(1)}, f32[48,768]{1,0:T(8,128)S(1)}, u32[]{:S(2)}, u32[]{:S(2)}) collective-permute-start(f32[48,768]{1,0:T(8,128)S(1)} %get-tuple-element.129.a0), channel_id=1, source_target_pairs={{0,16},{8,24},{16,0},{24,8},{32,48},{40,56},{48,32},{56,40},{64,80... | collective-permute-start | bytes 442376 | tf_op jit(solution)/shard_map/ppermute | solution.py:365
  41.9 0.9 collective-permute-start.13
  42.7 0.6 collective-permute-start.12
  43.3 3.0 %shard_map.81 = (f32[512,768]{1,0:T(8,128)}, f32[8,128]{1,0:T(8,128)S(1)}) custom-call(f32[2176,128]{1,0:T(8,128)S(1)} %bitcast.30, f32[512,1024]{1,0:T(8,128)S(1)} %bitcast.25), custom_call_target="tpu_custom_call" | custom-call | flops 4000000000 | bytes 6000000 | tf_op jit(solution)/shard_map/pallas_call | solution.py:441
  46.3 0.0 collective-permute-done.11.r_done
  46.4 1.9 %all-to-all-done.3 = f32[16,48,256]{2,1,0:T(8,128)S(1)} async-done(((f32[16,48,256]{2,1,0:T(8,128)}), f32[16,48,256]{2,1,0:T(8,128)S(1)}, u32[]{:S(2)}, u32[]{:S(2)}) %all-to-all-start.3) | async-done | bytes 786464 | tf_op jit(solution)/shard_map/all_to_all | solution.py:429
  48.3 1.4 %shard_map.80 = (f32[512,256]{1,0:T(8,128)}, f32[8,128]{1,0:T(8,128)S(1)}) custom-call(f32[512,256]{1,0:T(8,128)S(1)} %collective-permute-done.11.r_done, bf16[512,768]{1,0:T(8,128)(2,1)S(1)} %get-tuple-element.116.slot, f32[768,256]{1,0:T(8,128)S(1)} %bitcast.21), custom_call_target="tpu_custom_call" | custom-call | flops 100000000 | bytes 1000000 | tf_op jit(solution)/shard_map/pallas_call | solution.py:449
  49.7 0.0 collective-permute-done.14.a3
  49.7 1.6 %collective-permute-done.13.a2 = f32[48,768]{1,0:T(8,128)S(1)} collective-permute-done((f32[48,768]{1,0:T(8,128)S(1)}, f32[48,768]{1,0:T(8,128)S(1)}, u32[]{:S(2)}, u32[]{:S(2)}) %collective-permute-start.13) | collective-permute-done | bytes 147488 | tf_op jit(solution)/shard_map/ppermute | solution.py:365
  51.3 2.2 %collective-permute-done.12.a1 = f32[48,768]{1,0:T(8,128)S(1)} collective-permute-done((f32[48,768]{1,0:T(8,128)S(1)}, f32[48,768]{1,0:T(8,128)S(1)}, u32[]{:S(2)}, u32[]{:S(2)}) %collective-permute-start.12) | collective-permute-done | bytes 147488 | tf_op jit(solution)/shard_map/ppermute | solution.py:365
  53.6 2.8 %collective-permute-start.17 = (f32[192,768]{1,0:T(8,128)S(1)}, f32[192,768]{1,0:T(8,128)}, u32[]{:S(2)}, u32[]{:S(2)}) collective-permute-start(f32[192,768]{1,0:T(8,128)S(1)} %shard_map.82), channel_id=1, source_target_pairs={{0,64},{8,72},{16,80},{24,88},{32,96},{40,104},{48,112},{56,120},{... | collective-permute-start | bytes 1769480 | tf_op jit(solution)/shard_map/ppermute | solution.py:365
  56.4 0.9 collective-permute-start.16
  57.3 0.6 collective-permute-start.15
  58.4 0.0 copy-start.10
  58.4 36.0 %conditional.2 = (f32[512,256]{1,0:T(8,128)}, f32[512,256]{1,0:T(8,128)}, f32[512,256]{1,0:T(8,128)}, f32[512,256]{1,0:T(8,128)}, f32[512,256]{1,0:T(8,128)}) conditional(s32[]{:T(128)} %bitcast.5, () %tuple.22, (s32[]{:T(128)}, f32[512,256]{1,0:T(8,128)}, s32[3]{0:T(128)S(1)}, f32[512,256]{1,0:T(8,128)S(1)}, f32[512,256]{1,0:T(8,128)}, ...), branch_computations={%region_0.0_spmd, %region_1.2_spmd} | conditional | flops 2000131072 | bytes 16058886 | solution.py:473
  58.4 1.8 %collective-permute-start = (f32[512,256]{1,0:T(8,128)}, f32[512,256]{1,0:T(8,128)S(1)}, u32[]{:S(2)}, u32[]{:S(2)}) collective-permute-start(f32[512,256]{1,0:T(8,128)} %get-tuple-element.62.w_own), channel_id=1, source_target_pairs={{0,1},{1,0},{2,3},{3,2},{4,5},{5,4},{6,7},{7,6},{8,9},{9,8},{10,11... | collective-permute-start | bytes 1572872 | tf_op jit(solution)/shard_map/cond/branch_1_fun/ppermute | solution.py:353
  60.2 1.7 %collective-permute-done.w_other = f32[512,256]{1,0:T(8,128)S(1)} collective-permute-done((f32[512,256]{1,0:T(8,128)}, f32[512,256]{1,0:T(8,128)S(1)}, u32[]{:S(2)}, u32[]{:S(2)}) %collective-permute-start) | collective-permute-done | bytes 524320 | tf_op jit(solution)/shard_map/cond/branch_1_fun/ppermute | solution.py:353
  61.9 5.1 %branch_1_fun.2 = (f32[512,256]{1,0:T(8,128)S(1)}, f32[512,256]{1,0:T(8,128)}) custom-call(s32[3]{0:T(128)S(1)} %get-tuple-element.61.place, f32[512,256]{1,0:T(8,128)} %get-tuple-element.62.w_own, f32[512,256]{1,0:T(8,128)S(1)} %collective-permute-done.w_other, f32[512,256]{1,0:T(8,128)S(1)} %get-tuple-element.63.r_own, ...), custom_call_target="tpu_custom_call" | custom-call | flops 2000000000 | bytes 4000000 | tf_op jit(solution)/shard_map/cond/branch_1_fun/pallas_call | solution.py:459
  67.1 1.5 %collective-permute-start.1 = (f32[512,256]{1,0:T(8,128)S(1)}, f32[512,256]{1,0:T(8,128)}, u32[]{:S(2)}, u32[]{:S(2)}) collective-permute-start(f32[512,256]{1,0:T(8,128)S(1)} %get-tuple-element.66), channel_id=1, source_target_pairs={{0,2},{1,7},{8,10},{9,15},{16,18},{17,23},{24,26},{25,31},{32,34},... | collective-permute-start | bytes 1572872 | tf_op jit(solution)/shard_map/cond/branch_1_fun/ppermute | solution.py:463
  68.6 0.0 collective-permute-done.1
  68.6 0.9 broadcast_select_fusion
  69.4 1.3 %collective-permute-start.2 = (f32[512,256]{1,0:T(8,128)}, f32[512,256]{1,0:T(8,128)}, u32[]{:S(2)}, u32[]{:S(2)}) collective-permute-start(f32[512,256]{1,0:T(8,128)} %broadcast_select_fusion), channel_id=1, source_target_pairs={{1,3},{0,6},{2,4},{7,5},{9,11},{8,14},{10,12},{15,13},{17,19},{16,... | collective-permute-start | bytes 1572872 | tf_op jit(solution)/shard_map/cond/branch_1_fun/ppermute | solution.py:465
  70.7 1.5 %collective-permute-start.3 = (f32[512,256]{1,0:T(8,128)}, f32[512,256]{1,0:T(8,128)}, u32[]{:S(2)}, u32[]{:S(2)}) collective-permute-start(f32[512,256]{1,0:T(8,128)} %broadcast_select_fusion), channel_id=1, source_target_pairs={{0,1},{1,0},{2,3},{7,6},{8,9},{9,8},{10,11},{15,14},{16,17},{17,16... | collective-permute-start | bytes 1572872 | tf_op jit(solution)/shard_map/cond/branch_1_fun/ppermute | solution.py:466
  72.2 17.6 %collective-permute-done.2 = f32[512,256]{1,0:T(8,128)} collective-permute-done((f32[512,256]{1,0:T(8,128)}, f32[512,256]{1,0:T(8,128)}, u32[]{:S(2)}, u32[]{:S(2)}) %collective-permute-start.2) | collective-permute-done | bytes 524320 | tf_op jit(solution)/shard_map/cond/branch_1_fun/ppermute | solution.py:465
  89.7 2.8 %collective-permute-start.4 = (f32[512,256]{1,0:T(8,128)}, f32[512,256]{1,0:T(8,128)}, u32[]{:S(2)}, u32[]{:S(2)}) collective-permute-start(f32[512,256]{1,0:T(8,128)} %collective-permute-done.2), channel_id=1, source_target_pairs={{3,2},{6,7},{4,5},{5,4},{11,10},{14,15},{12,13},{13,12},{19,18},{2... | collective-permute-start | bytes 1572872 | tf_op jit(solution)/shard_map/cond/branch_1_fun/ppermute | solution.py:467
  92.6 0.0 collective-permute-done.3
  92.6 1.8 %collective-permute-done.4 = f32[512,256]{1,0:T(8,128)} collective-permute-done((f32[512,256]{1,0:T(8,128)}, f32[512,256]{1,0:T(8,128)}, u32[]{:S(2)}, u32[]{:S(2)}) %collective-permute-start.4) | collective-permute-done | bytes 524320 | tf_op jit(solution)/shard_map/cond/branch_1_fun/ppermute | solution.py:467
  94.4 0.0 collective-permute-done.17
  94.4 0.0 collective-permute-done.16
  94.4 0.0 collective-permute-done.15
  94.4 7.8 %conditional.3 = (f32[2,256,4,256]{3,2,1,0:T(4,128)}) conditional(s32[]{:T(128)} %bitcast.5, (f32[2176,128]{1,0:T(8,128)}, f32[512,1024]{1,0:T(8,128)S(1)}, s32[512,128]{1,0:T(8,128)S(1)}, s32[]{:T(128)}, s32[3]{0:T(128)S(1)}, /*index=5*/f32[2,512,128]{2,1,0:T(8,128)}) %tuple.32, (s32[3]{0:T(128)S(1)}, f32[512,256]{1,0:T(8,128)}, ...), branch_computations={%region_2.4_spmd, %region_4.5_spmd} | conditional | flops 8000884736 | bytes 85798736 | solution.py:517
  94.7 7.6 %branch_1_fun.3 = f32[2,256,4,256]{3,2,1,0:T(4,128)} custom-call(s32[3]{0:T(128)S(1)} %get-tuple-element.78.place, f32[512,256]{1,0:T(8,128)} %get-tuple-element.79.n_early, f32[512,256]{1,0:T(8,128)} %get-tuple-element.80.n_late, f32[512,256]{1,0:T(8,128)} %get-tuple-element.81.o_early, f32[512,256]{1,0:T(8,128)} %get-tuple-element.82.o_late, ...), custom_call_target="tpu_custom_call" | custom-call | flops 4000000000 | bytes 8000000 | tf_op jit(solution)/shard_map/cond/branch_1_fun/pallas_call | solution.py:476
  (19 shorter events, 0.1 us)
Async XLA Ops:
  0.1 13.1 %copy-start.5 = (s32[2,4,16,256]{3,2,1,0:T(8,128)S(1)}, s32[2,4,16,256]{3,2,1,0:T(8,128)}, u32[]{:S(2)}) copy-start(s32[2,4,16,256]{3,2,1,0:T(8,128)} %level_picks.1) | copy-start | bytes 393220
  0.1 13.1 %copy-start.6 = (s32[2,16,256]{2,1,0:T(8,128)S(1)}, s32[2,16,256]{2,1,0:T(8,128)}, u32[]{:S(2)}) copy-start(s32[2,16,256]{2,1,0:T(8,128)} %local_picks.1) | copy-start | bytes 98308
  0.1 13.1 %copy-start.7 = (s32[2,256]{1,0:T(2,128)S(1)}, s32[2,256]{1,0:T(2,128)}, u32[]{:S(2)}) copy-start(s32[2,256]{1,0:T(2,128)} %order.1) | copy-start | bytes 6148
  2.8 27.3 %all-to-all-start.2 = ((f32[2176,1,128]{2,1,0:T(1,128)}), f32[2176,1,128]{2,1,0:T(1,128)S(1)}, u32[]{:S(2)}, u32[]{:S(2)}) async-start(f32[2176,1,128]{2,1,0:T(1,128)} %bitcast.31), calls=%async_computation.2 | async-start | bytes 2228224 | tf_op jit(solution)/shard_map/all_to_all | solution.py:401
  13.2 3.4 %copy-start.13 = (f32[2,256,4,256]{3,2,1,0:T(4,128)S(1)}, f32[2,256,4,256]{3,2,1,0:T(4,128)}, u32[]{:S(2)}) copy-start(f32[2,256,4,256]{3,2,1,0:T(4,128)} %param.11) | copy-start | bytes 6291460
  17.1 1.3 %copy-start.8 = (f32[64,8,4,256]{3,1,2,0:T(8,128)}, f32[64,8,4,256]{3,1,2,0:T(8,128)S(1)}, u32[]{:S(2)}) copy-start(f32[64,8,4,256]{3,1,2,0:T(8,128)S(1)} %copy.11) | copy-start | bytes 6291460
  30.1 1.4 %copy-start.11 = (f32[2176,1,128]{2,1,0:T(1,128)}, f32[2176,1,128]{2,1,0:T(1,128)S(1)}, u32[]{:S(2)}) copy-start(f32[2176,1,128]{2,1,0:T(1,128)S(1)} %all-to-all-done.2) | copy-start | bytes 3342340
  31.5 16.8 %all-to-all-start.3 = ((f32[16,48,256]{2,1,0:T(8,128)}), f32[16,48,256]{2,1,0:T(8,128)S(1)}, u32[]{:S(2)}, u32[]{:S(2)}) async-start(f32[16,48,256]{2,1,0:T(8,128)} %bitcast.12), calls=%async_computation.3 | async-start | bytes 1572864 | tf_op jit(solution)/shard_map/all_to_all | solution.py:429
  35.2 8.1 %copy-start.9 = (f32[64,8,4,256]{3,1,2,0:T(8,128)S(1)}, f32[64,8,4,256]{3,1,2,0:T(8,128)}, u32[]{:S(2)}) copy-start(f32[64,8,4,256]{3,1,2,0:T(8,128)} %copy-done.8) | copy-start | bytes 6291460
  35.2 8.1 %copy-start.12 = (f32[2176,1,128]{2,1,0:T(1,128)S(1)}, f32[2176,1,128]{2,1,0:T(1,128)}, u32[]{:S(2)}) copy-start(f32[2176,1,128]{2,1,0:T(1,128)} %copy-done.11) | copy-start | bytes 3342340
  37.5 8.8 %copy-start.14 = (f32[512,256]{1,0:T(8,128)}, f32[512,256]{1,0:T(8,128)S(1)}, u32[]{:S(2)}) copy-start(f32[512,256]{1,0:T(8,128)S(1)} %shard_map.77) | copy-start | bytes 1572868
  37.5 8.8 %collective-permute-start.11 = (f32[512,256]{1,0:T(8,128)S(1)}, f32[512,256]{1,0:T(8,128)S(1)}, u32[]{:S(2)}, u32[]{:S(2)}) collective-permute-start(f32[512,256]{1,0:T(8,128)S(1)} %shard_map.77), channel_id=1, source_target_pairs={{0,1},{1,0},{2,3},{3,2},{4,5},{5,4},{6,7},{7,6},{8,9},{9,8},{10,11... | collective-permute-start | bytes 1572872 | tf_op jit(solution)/shard_map/ppermute | solution.py:353
  38.7 11.0 %collective-permute-start.14 = (f32[48,768]{1,0:T(8,128)S(1)}, f32[48,768]{1,0:T(8,128)S(1)}, u32[]{:S(2)}, u32[]{:S(2)}) collective-permute-start(f32[48,768]{1,0:T(8,128)S(1)} %get-tuple-element.129.a0), channel_id=1, source_target_pairs={{0,16},{8,24},{16,0},{24,8},{32,48},{40,56},{48,32},{56,40},{64,80... | collective-permute-start | bytes 442376 | tf_op jit(solution)/shard_map/ppermute | solution.py:365
  41.9 9.4 %collective-permute-start.13 = (f32[48,768]{1,0:T(8,128)S(1)}, f32[48,768]{1,0:T(8,128)S(1)}, u32[]{:S(2)}, u32[]{:S(2)}) collective-permute-start(f32[48,768]{1,0:T(8,128)S(1)} %get-tuple-element.129.a0), channel_id=1, source_target_pairs={{0,24},{8,0},{16,8},{24,16},{32,56},{40,32},{48,40},{56,48},{64,88... | collective-permute-start | bytes 442376 | tf_op jit(solution)/shard_map/ppermute | solution.py:365
  42.7 10.8 %collective-permute-start.12 = (f32[48,768]{1,0:T(8,128)S(1)}, f32[48,768]{1,0:T(8,128)S(1)}, u32[]{:S(2)}, u32[]{:S(2)}) collective-permute-start(f32[48,768]{1,0:T(8,128)S(1)} %get-tuple-element.129.a0), channel_id=1, source_target_pairs={{0,8},{8,16},{16,24},{24,0},{32,40},{40,48},{48,56},{56,32},{64,72... | collective-permute-start | bytes 442376 | tf_op jit(solution)/shard_map/ppermute | solution.py:365
  46.4 7.2 %copy-start.16 = (f32[512,256]{1,0:T(8,128)}, f32[512,256]{1,0:T(8,128)S(1)}, u32[]{:S(2)}) copy-start(f32[512,256]{1,0:T(8,128)S(1)} %collective-permute-done.11.r_done) | copy-start | bytes 1572868
  48.3 10.1 %copy-start.15 = (f32[512,256]{1,0:T(8,128)S(1)}, f32[512,256]{1,0:T(8,128)}, u32[]{:S(2)}) copy-start(f32[512,256]{1,0:T(8,128)} %copy-done.14) | copy-start | bytes 1572868
  53.6 40.8 %collective-permute-start.17 = (f32[192,768]{1,0:T(8,128)S(1)}, f32[192,768]{1,0:T(8,128)}, u32[]{:S(2)}, u32[]{:S(2)}) collective-permute-start(f32[192,768]{1,0:T(8,128)S(1)} %shard_map.82), channel_id=1, source_target_pairs={{0,64},{8,72},{16,80},{24,88},{32,96},{40,104},{48,112},{56,120},{... | collective-permute-start | bytes 1769480 | tf_op jit(solution)/shard_map/ppermute | solution.py:365
  56.4 38.1 %collective-permute-start.16 = (f32[192,768]{1,0:T(8,128)S(1)}, f32[192,768]{1,0:T(8,128)}, u32[]{:S(2)}, u32[]{:S(2)}) collective-permute-start(f32[192,768]{1,0:T(8,128)S(1)} %shard_map.82), channel_id=1, source_target_pairs={{0,96},{8,104},{16,112},{24,120},{32,0},{40,8},{48,16},{56,24},{64... | collective-permute-start | bytes 1769480 | tf_op jit(solution)/shard_map/ppermute | solution.py:365
  57.3 37.2 %collective-permute-start.15 = (f32[192,768]{1,0:T(8,128)S(1)}, f32[192,768]{1,0:T(8,128)}, u32[]{:S(2)}, u32[]{:S(2)}) collective-permute-start(f32[192,768]{1,0:T(8,128)S(1)} %shard_map.82), channel_id=1, source_target_pairs={{0,32},{8,40},{16,48},{24,56},{32,64},{40,72},{48,80},{56,88},{64,... | collective-permute-start | bytes 1769480 | tf_op jit(solution)/shard_map/ppermute | solution.py:365
  58.4 36.0 %copy-start.10 = (f32[64,8,4,256]{3,1,2,0:T(8,128)S(1)}, f32[64,8,4,256]{3,1,2,0:T(8,128)}, u32[]{:S(2)}) copy-start(f32[64,8,4,256]{3,1,2,0:T(8,128)} %copy-done.8) | copy-start | bytes 6291460
  58.4 3.5 %collective-permute-start = (f32[512,256]{1,0:T(8,128)}, f32[512,256]{1,0:T(8,128)S(1)}, u32[]{:S(2)}, u32[]{:S(2)}) collective-permute-start(f32[512,256]{1,0:T(8,128)} %get-tuple-element.62.w_own), channel_id=1, source_target_pairs={{0,1},{1,0},{2,3},{3,2},{4,5},{5,4},{6,7},{7,6},{8,9},{9,8},{10,11... | collective-permute-start | bytes 1572872 | tf_op jit(solution)/shard_map/cond/branch_1_fun/ppermute | solution.py:353
  67.1 1.5 %collective-permute-start.1 = (f32[512,256]{1,0:T(8,128)S(1)}, f32[512,256]{1,0:T(8,128)}, u32[]{:S(2)}, u32[]{:S(2)}) collective-permute-start(f32[512,256]{1,0:T(8,128)S(1)} %get-tuple-element.66), channel_id=1, source_target_pairs={{0,2},{1,7},{8,10},{9,15},{16,18},{17,23},{24,26},{25,31},{32,34},... | collective-permute-start | bytes 1572872 | tf_op jit(solution)/shard_map/cond/branch_1_fun/ppermute | solution.py:463
  69.4 20.3 %collective-permute-start.2 = (f32[512,256]{1,0:T(8,128)}, f32[512,256]{1,0:T(8,128)}, u32[]{:S(2)}, u32[]{:S(2)}) collective-permute-start(f32[512,256]{1,0:T(8,128)} %broadcast_select_fusion), channel_id=1, source_target_pairs={{1,3},{0,6},{2,4},{7,5},{9,11},{8,14},{10,12},{15,13},{17,19},{16,... | collective-permute-start | bytes 1572872 | tf_op jit(solution)/shard_map/cond/branch_1_fun/ppermute | solution.py:465
  70.7 21.8 %collective-permute-start.3 = (f32[512,256]{1,0:T(8,128)}, f32[512,256]{1,0:T(8,128)}, u32[]{:S(2)}, u32[]{:S(2)}) collective-permute-start(f32[512,256]{1,0:T(8,128)} %broadcast_select_fusion), channel_id=1, source_target_pairs={{0,1},{1,0},{2,3},{7,6},{8,9},{9,8},{10,11},{15,14},{16,17},{17,16... | collective-permute-start | bytes 1572872 | tf_op jit(solution)/shard_map/cond/branch_1_fun/ppermute | solution.py:466
  89.7 4.7 %collective-permute-start.4 = (f32[512,256]{1,0:T(8,128)}, f32[512,256]{1,0:T(8,128)}, u32[]{:S(2)}, u32[]{:S(2)}) collective-permute-start(f32[512,256]{1,0:T(8,128)} %collective-permute-done.2), channel_id=1, source_target_pairs={{3,2},{6,7},{4,5},{5,4},{11,10},{14,15},{12,13},{13,12},{19,18},{2... | collective-permute-start | bytes 1572872 | tf_op jit(solution)/shard_map/cond/branch_1_fun/ppermute | solution.py:467

commit v15 on v14

--- a/solution.py
+++ b/solution.py
@@ -286,15 +286,23 @@
         copy(xy_hbm, xy, sems.at[2]),
         copy(w_first_hbm, w_first, sems.at[3]),
         copy(first_hbm, first, sems.at[4]),
-        copy(tile_hbm, tile, sems.at[5]),
         copy(a0, w_rest.at[:size], sems.at[6]),
         copy(a1, w_rest.at[size : 2 * size], sems.at[7]),
         copy(a2, w_rest.at[2 * size : 3 * size], sems.at[8]),
         copy(a3, w_rest.at[3 * size :], sems.at[9]),
         copy(rest_hbm, rest, sems.at[10]),
     ]
-    for move in moves:
+    for move in moves[:2] + moves[3:]:
         move.start()
+
+    @pl.when(q < 2)
+    def _():
+        copy(tile_hbm, first, sems.at[4]).start()
+
+    @pl.when(q >= 2)
+    def _():
+        moves[2].start()
+
     copy(n_early, n_own, sems.at[0]).wait()
     copy(o_early, n_other, sems.at[1]).wait()
     h0, l0 = halves(jnp.where(even, n_own[...], n_other[...]))
@@ -308,13 +316,12 @@
     hot = xy[...]
     high = dot(n_high, hot).astype(BF16)
     low = dot(n_low, hot).astype(BF16)
-    for move in moves[1:4]:
+    for move in moves[1:3]:
         move.wait()
-    new = first[...] - dot3((n_high, n_low), halves(w_first[...]))
-    new = jnp.where(q < 2, tile[...], new)
+    new = first[...] - jnp.where(q < 2, 0.0, dot3((n_high, n_low), halves(w_first[...])))
     for t in range(rows // half):
         out[t, :, 0, :] = new[t * half : (t + 1) * half]
-    for move in moves[4:]:
+    for move in moves[3:]:
         move.wait()
     w = [halves(w_rest[:, u * B : (u + 1) * B]) for u in range(3)]
     sent = []

time: 103 us -> 103 us (level)
  no operation moved by 1% of the time
where the time goes in v15:
time: 103 us
  waiting for transfers between devices  38.1 us (37%)
  starting transfers between devices  32.9 us (32%)
  Pallas kernels  27.6 us (27%)
  local copies, waits for them, and re-layouts  1.83 us (2%)
    ppermute x1, waiting for transfers between devices, panels(): n_late = lax.ppermute(n_early, 'pcol', [(1, 3), (0, 6), (2, 4), (7, 5)])  17.6 us
    all_to_all x1, waiting for transfers between devices, body(): lax.all_to_all(payload, ('prow', 'pcol'), 0, 0, tiled=True)  11.2 us
    all_to_all x1, starting transfers between devices, body(): lax.all_to_all(payload, ('prow', 'pcol'), 0, 0, tiled=True)  10.4 us
    ppermute x6, starting transfers between devices, ring(): return [x] + [lax.ppermute(x, 'prow', shift(step)) for step in (1, -1, 2)]  8.87 us
    pallas_call x1, Pallas kernels, finish(): pl.pallas_call(finish_kernel, out_shape=shaped(*front.shape), in_specs=[S...  7.81 us
    pallas_call x1, Pallas kernels, panels(): call(panel_kernel, (shaped(rows, B), shaped(rows, B)), 6, flops=2 * 10 **...  5.15 us
    ppermute x6, waiting for transfers between devices, ring(): return [x] + [lax.ppermute(x, 'prow', shift(step)) for step in (1, -1, 2)]  3.91 us
    all_to_all x1, starting transfers between devices, body(): w_first = lax.all_to_all(send_first, 'prow', 0, 0, tiled=True)  3.74 us
  transfers between devices with their start and end apart: 14, of which 7 were waited for; matrix products, arithmetic and copies ran while one was open for 1% of the time, Pallas kernels for 15%

profile of v15, /device:TPU:65, one launch (start us, length us, event | category | flops | bytes accessed | tf_op | source)
XLA Modules:
  0.0 102.7 jit_solution(4275185646675582693)
XLA Ops:
  0.0 0.1 pad_add_fusion.place
  0.1 2.7 %shard_map.76 = f32[2176,128]{1,0:T(8,128)} custom-call(s32[3]{0:T(128)S(1)} %pad_add_fusion.place, f32[128,8,256]{2,1,0:T(8,128)} %bitcast.33, s32[8,128]{1,0:T(8,128)} %bitcast.34, s32[1,128]{1,0:T(1,128)} %counts_hbm.1), custom_call_target="tpu_custom_call" | custom-call | flops 1000000 | bytes 2000000 | tf_op jit(solution)/shard_map/pallas_call | solution.py:392
  2.8 10.4 %all-to-all-start.2 = ((f32[2176,1,128]{2,1,0:T(1,128)}), f32[2176,1,128]{2,1,0:T(1,128)S(1)}, u32[]{:S(2)}, u32[]{:S(2)}) async-start(f32[2176,1,128]{2,1,0:T(1,128)} %bitcast.31), calls=%async_computation.2 | async-start | bytes 2228224 | tf_op jit(solution)/shard_map/all_to_all | solution.py:408
  13.2 0.0 copy-start.13
  13.2 3.4 %shard_map.75 = (s32[512,128]{1,0:T(8,128)S(1)}, f32[2,512,128]{2,1,0:T(8,128)}, s32[48,128]{1,0:T(8,128)S(1)}, bf16[512,768]{1,0:T(8,128)(2,1)S(1)}, bf16[512,768]{1,0:T(8,128)(2,1)}, /*index=5*/s32[1]{0:T(128)}) custom-call(s32[3]{0:T(128)S(1)} %pad_add_fusion.place, s32[2,16,256]{2,1,0:T(8,128)S(1)} %copy-done.6, s32[2,4,16,256]{3,2,1,0:T(8,128)S(1)} %copy-done.5, ...), custom_call_target="tpu_custom_call" | custom-call | flops 1000000000 | bytes 1000000 | tf_op jit(solution)/shard_map/pallas_call | solution.py:412
  16.6 0.5 copy.11
  17.1 0.0 copy-start.8
  17.1 1.3 %copy-done.8 = f32[64,8,4,256]{3,1,2,0:T(8,128)} copy-done((f32[64,8,4,256]{3,1,2,0:T(8,128)}, f32[64,8,4,256]{3,1,2,0:T(8,128)S(1)}, u32[]{:S(2)}) %copy-start.8) | copy-done | bytes 2097176
  18.4 0.6 shard_map.78.front_rows
  18.9 11.2 %all-to-all-done.2 = f32[2176,1,128]{2,1,0:T(1,128)S(1)} async-done(((f32[2176,1,128]{2,1,0:T(1,128)}), f32[2176,1,128]{2,1,0:T(1,128)S(1)}, u32[]{:S(2)}, u32[]{:S(2)}) %all-to-all-start.2) | async-done | bytes 1114144 | tf_op jit(solution)/shard_map/all_to_all | solution.py:408
  30.1 1.4 %shard_map.79 = (f32[768,256]{1,0:T(8,128)}, f32[48,768]{1,0:T(8,128)S(1)}) custom-call(f32[2176,128]{1,0:T(8,128)S(1)} %bitcast.27, f32[192,256]{1,0:T(8,128)S(1)} %shard_map.78.front_rows, s32[48,128]{1,0:T(8,128)S(1)} %get-tuple-element.117.give), custom_call_target="tpu_custom_call" | custom-call | flops 100000000 | bytes 2000000 | tf_op jit(solution)/shard_map/pallas_call | solution.py:433
  31.5 3.7 %all-to-all-start.3 = ((f32[16,48,256]{2,1,0:T(8,128)}), f32[16,48,256]{2,1,0:T(8,128)S(1)}, u32[]{:S(2)}, u32[]{:S(2)}) async-start(f32[16,48,256]{2,1,0:T(8,128)} %bitcast.12), calls=%async_computation.3 | async-start | bytes 1572864 | tf_op jit(solution)/shard_map/all_to_all | solution.py:436
  35.2 0.0 copy-start.9
  35.3 2.2 %shard_map.77 = f32[512,256]{1,0:T(8,128)S(1)} custom-call(f32[2176,128]{1,0:T(8,128)} %bitcast.28, f32[512,1024]{1,0:T(8,128)} %bitcast.24), custom_call_target="tpu_custom_call" | custom-call | flops 1000000000 | bytes 2000000 | tf_op jit(solution)/shard_map/pallas_call | solution.py:438
  37.5 1.2 %collective-permute-start.11 = (f32[512,256]{1,0:T(8,128)S(1)}, f32[512,256]{1,0:T(8,128)S(1)}, u32[]{:S(2)}, u32[]{:S(2)}) collective-permute-start(f32[512,256]{1,0:T(8,128)S(1)} %shard_map.77), channel_id=1, source_target_pairs={{0,1},{1,0},{2,3},{3,2},{4,5},{5,4},{6,7},{7,6},{8,9},{9,8},{10,11... | collective-permute-start | bytes 1572872 | tf_op jit(solution)/shard_map/ppermute | solution.py:360
  38.7 3.2 %collective-permute-start.14 = (f32[48,768]{1,0:T(8,128)S(1)}, f32[48,768]{1,0:T(8,128)S(1)}, u32[]{:S(2)}, u32[]{:S(2)}) collective-permute-start(f32[48,768]{1,0:T(8,128)S(1)} %get-tuple-element.129.a0), channel_id=1, source_target_pairs={{0,16},{8,24},{16,0},{24,8},{32,48},{40,56},{48,32},{56,40},{64,80... | collective-permute-start | bytes 442376 | tf_op jit(solution)/shard_map/ppermute | solution.py:372
  41.9 0.9 collective-permute-start.13
  42.7 0.6 collective-permute-start.12
  43.3 0.0 copy-done.9
  43.3 3.0 %shard_map.81 = (f32[512,768]{1,0:T(8,128)}, f32[8,128]{1,0:T(8,128)S(1)}) custom-call(f32[2176,128]{1,0:T(8,128)S(1)} %bitcast.30, f32[512,1024]{1,0:T(8,128)S(1)} %bitcast.25), custom_call_target="tpu_custom_call" | custom-call | flops 4000000000 | bytes 6000000 | tf_op jit(solution)/shard_map/pallas_call | solution.py:448
  46.3 0.0 collective-permute-done.11.r_done
  46.4 1.9 %all-to-all-done.3 = f32[16,48,256]{2,1,0:T(8,128)S(1)} async-done(((f32[16,48,256]{2,1,0:T(8,128)}), f32[16,48,256]{2,1,0:T(8,128)S(1)}, u32[]{:S(2)}, u32[]{:S(2)}) %all-to-all-start.3) | async-done | bytes 786464 | tf_op jit(solution)/shard_map/all_to_all | solution.py:436
  48.3 1.4 %shard_map.80 = (f32[512,256]{1,0:T(8,128)}, f32[8,128]{1,0:T(8,128)S(1)}) custom-call(f32[512,256]{1,0:T(8,128)S(1)} %collective-permute-done.11.r_done, bf16[512,768]{1,0:T(8,128)(2,1)S(1)} %get-tuple-element.116.slot, f32[768,256]{1,0:T(8,128)S(1)} %bitcast.21), custom_call_target="tpu_custom_call" | custom-call | flops 100000000 | bytes 1000000 | tf_op jit(solution)/shard_map/pallas_call | solution.py:456
  49.7 0.0 collective-permute-done.14.a3
  49.7 1.6 %collective-permute-done.13.a2 = f32[48,768]{1,0:T(8,128)S(1)} collective-permute-done((f32[48,768]{1,0:T(8,128)S(1)}, f32[48,768]{1,0:T(8,128)S(1)}, u32[]{:S(2)}, u32[]{:S(2)}) %collective-permute-start.13) | collective-permute-done | bytes 147488 | tf_op jit(solution)/shard_map/ppermute | solution.py:372
  51.3 2.2 %collective-permute-done.12.a1 = f32[48,768]{1,0:T(8,128)S(1)} collective-permute-done((f32[48,768]{1,0:T(8,128)S(1)}, f32[48,768]{1,0:T(8,128)S(1)}, u32[]{:S(2)}, u32[]{:S(2)}) %collective-permute-start.12) | collective-permute-done | bytes 147488 | tf_op jit(solution)/shard_map/ppermute | solution.py:372
  53.6 2.8 %collective-permute-start.17 = (f32[192,768]{1,0:T(8,128)S(1)}, f32[192,768]{1,0:T(8,128)}, u32[]{:S(2)}, u32[]{:S(2)}) collective-permute-start(f32[192,768]{1,0:T(8,128)S(1)} %shard_map.82), channel_id=1, source_target_pairs={{0,64},{8,72},{16,80},{24,88},{32,96},{40,104},{48,112},{56,120},{... | collective-permute-start | bytes 1769480 | tf_op jit(solution)/shard_map/ppermute | solution.py:372
  56.4 0.9 collective-permute-start.16
  57.3 0.6 collective-permute-start.15
  58.4 0.0 copy-start.10
  58.4 36.0 %conditional.2 = (f32[512,256]{1,0:T(8,128)}, f32[512,256]{1,0:T(8,128)}, f32[512,256]{1,0:T(8,128)}, f32[512,256]{1,0:T(8,128)}, f32[512,256]{1,0:T(8,128)}) conditional(s32[]{:T(128)} %bitcast.5, () %tuple.22, (s32[]{:T(128)}, f32[512,256]{1,0:T(8,128)}, s32[3]{0:T(128)S(1)}, f32[512,256]{1,0:T(8,128)S(1)}, f32[512,256]{1,0:T(8,128)}, ...), branch_computations={%region_0.0_spmd, %region_1.2_spmd} | conditional | flops 2000131072 | bytes 16058886 | solution.py:480
  58.4 1.8 %collective-permute-start = (f32[512,256]{1,0:T(8,128)}, f32[512,256]{1,0:T(8,128)S(1)}, u32[]{:S(2)}, u32[]{:S(2)}) collective-permute-start(f32[512,256]{1,0:T(8,128)} %get-tuple-element.62.w_own), channel_id=1, source_target_pairs={{0,1},{1,0},{2,3},{3,2},{4,5},{5,4},{6,7},{7,6},{8,9},{9,8},{10,11... | collective-permute-start | bytes 1572872 | tf_op jit(solution)/shard_map/cond/branch_1_fun/ppermute | solution.py:360
  60.2 1.7 %collective-permute-done.w_other = f32[512,256]{1,0:T(8,128)S(1)} collective-permute-done((f32[512,256]{1,0:T(8,128)}, f32[512,256]{1,0:T(8,128)S(1)}, u32[]{:S(2)}, u32[]{:S(2)}) %collective-permute-start) | collective-permute-done | bytes 524320 | tf_op jit(solution)/shard_map/cond/branch_1_fun/ppermute | solution.py:360
  61.9 5.1 %branch_1_fun.2 = (f32[512,256]{1,0:T(8,128)S(1)}, f32[512,256]{1,0:T(8,128)}) custom-call(s32[3]{0:T(128)S(1)} %get-tuple-element.61.place, f32[512,256]{1,0:T(8,128)} %get-tuple-element.62.w_own, f32[512,256]{1,0:T(8,128)S(1)} %collective-permute-done.w_other, f32[512,256]{1,0:T(8,128)S(1)} %get-tuple-element.63.r_own, ...), custom_call_target="tpu_custom_call" | custom-call | flops 2000000000 | bytes 4000000 | tf_op jit(solution)/shard_map/cond/branch_1_fun/pallas_call | solution.py:466
  67.1 1.5 %collective-permute-start.1 = (f32[512,256]{1,0:T(8,128)S(1)}, f32[512,256]{1,0:T(8,128)}, u32[]{:S(2)}, u32[]{:S(2)}) collective-permute-start(f32[512,256]{1,0:T(8,128)S(1)} %get-tuple-element.66), channel_id=1, source_target_pairs={{0,2},{1,7},{8,10},{9,15},{16,18},{17,23},{24,26},{25,31},{32,34},... | collective-permute-start | bytes 1572872 | tf_op jit(solution)/shard_map/cond/branch_1_fun/ppermute | solution.py:470
  68.6 0.0 collective-permute-done.1
  68.6 0.9 broadcast_select_fusion
  69.4 1.3 %collective-permute-start.2 = (f32[512,256]{1,0:T(8,128)}, f32[512,256]{1,0:T(8,128)}, u32[]{:S(2)}, u32[]{:S(2)}) collective-permute-start(f32[512,256]{1,0:T(8,128)} %broadcast_select_fusion), channel_id=1, source_target_pairs={{1,3},{0,6},{2,4},{7,5},{9,11},{8,14},{10,12},{15,13},{17,19},{16,... | collective-permute-start | bytes 1572872 | tf_op jit(solution)/shard_map/cond/branch_1_fun/ppermute | solution.py:472
  70.7 1.5 %collective-permute-start.3 = (f32[512,256]{1,0:T(8,128)}, f32[512,256]{1,0:T(8,128)}, u32[]{:S(2)}, u32[]{:S(2)}) collective-permute-start(f32[512,256]{1,0:T(8,128)} %broadcast_select_fusion), channel_id=1, source_target_pairs={{0,1},{1,0},{2,3},{7,6},{8,9},{9,8},{10,11},{15,14},{16,17},{17,16... | collective-permute-start | bytes 1572872 | tf_op jit(solution)/shard_map/cond/branch_1_fun/ppermute | solution.py:473
  72.2 17.6 %collective-permute-done.2 = f32[512,256]{1,0:T(8,128)} collective-permute-done((f32[512,256]{1,0:T(8,128)}, f32[512,256]{1,0:T(8,128)}, u32[]{:S(2)}, u32[]{:S(2)}) %collective-permute-start.2) | collective-permute-done | bytes 524320 | tf_op jit(solution)/shard_map/cond/branch_1_fun/ppermute | solution.py:472
  89.7 2.8 %collective-permute-start.4 = (f32[512,256]{1,0:T(8,128)}, f32[512,256]{1,0:T(8,128)}, u32[]{:S(2)}, u32[]{:S(2)}) collective-permute-start(f32[512,256]{1,0:T(8,128)} %collective-permute-done.2), channel_id=1, source_target_pairs={{3,2},{6,7},{4,5},{5,4},{11,10},{14,15},{12,13},{13,12},{19,18},{2... | collective-permute-start | bytes 1572872 | tf_op jit(solution)/shard_map/cond/branch_1_fun/ppermute | solution.py:474
  92.6 0.0 collective-permute-done.3
  92.6 1.8 %collective-permute-done.4 = f32[512,256]{1,0:T(8,128)} collective-permute-done((f32[512,256]{1,0:T(8,128)}, f32[512,256]{1,0:T(8,128)}, u32[]{:S(2)}, u32[]{:S(2)}) %collective-permute-start.4) | collective-permute-done | bytes 524320 | tf_op jit(solution)/shard_map/cond/branch_1_fun/ppermute | solution.py:474
  94.4 0.0 collective-permute-done.17
  94.4 0.0 collective-permute-done.16
  94.4 0.0 collective-permute-done.15
  94.4 8.1 %conditional.3 = (f32[2,256,4,256]{3,2,1,0:T(4,128)}) conditional(s32[]{:T(128)} %bitcast.5, (f32[2176,128]{1,0:T(8,128)}, f32[512,1024]{1,0:T(8,128)S(1)}, s32[512,128]{1,0:T(8,128)S(1)}, s32[]{:T(128)}, s32[3]{0:T(128)S(1)}, /*index=5*/f32[2,512,128]{2,1,0:T(8,128)}) %tuple.32, (s32[3]{0:T(128)S(1)}, f32[512,256]{1,0:T(8,128)}, ...), branch_computations={%region_2.4_spmd, %region_4.5_spmd} | conditional | flops 8000884736 | bytes 85798736 | solution.py:524
  94.7 7.8 %branch_1_fun.3 = f32[2,256,4,256]{3,2,1,0:T(4,128)} custom-call(s32[3]{0:T(128)S(1)} %get-tuple-element.78.place, f32[512,256]{1,0:T(8,128)} %get-tuple-element.79.n_early, f32[512,256]{1,0:T(8,128)} %get-tuple-element.80.n_late, f32[512,256]{1,0:T(8,128)} %get-tuple-element.81.o_early, f32[512,256]{1,0:T(8,128)} %get-tuple-element.82.o_late, ...), custom_call_target="tpu_custom_call" | custom-call | flops 4000000000 | bytes 8000000 | tf_op jit(solution)/shard_map/cond/branch_1_fun/pallas_call | solution.py:483
  (19 shorter events, 0.1 us)
Async XLA Ops:
  0.1 13.1 %copy-start.5 = (s32[2,4,16,256]{3,2,1,0:T(8,128)S(1)}, s32[2,4,16,256]{3,2,1,0:T(8,128)}, u32[]{:S(2)}) copy-start(s32[2,4,16,256]{3,2,1,0:T(8,128)} %level_picks.1) | copy-start | bytes 393220
  0.1 13.1 %copy-start.6 = (s32[2,16,256]{2,1,0:T(8,128)S(1)}, s32[2,16,256]{2,1,0:T(8,128)}, u32[]{:S(2)}) copy-start(s32[2,16,256]{2,1,0:T(8,128)} %local_picks.1) | copy-start | bytes 98308
  0.1 13.1 %copy-start.7 = (s32[2,256]{1,0:T(2,128)S(1)}, s32[2,256]{1,0:T(2,128)}, u32[]{:S(2)}) copy-start(s32[2,256]{1,0:T(2,128)} %order.1) | copy-start | bytes 6148
  2.8 27.3 %all-to-all-start.2 = ((f32[2176,1,128]{2,1,0:T(1,128)}), f32[2176,1,128]{2,1,0:T(1,128)S(1)}, u32[]{:S(2)}, u32[]{:S(2)}) async-start(f32[2176,1,128]{2,1,0:T(1,128)} %bitcast.31), calls=%async_computation.2 | async-start | bytes 2228224 | tf_op jit(solution)/shard_map/all_to_all | solution.py:408
  13.2 3.4 %copy-start.13 = (f32[2,256,4,256]{3,2,1,0:T(4,128)S(1)}, f32[2,256,4,256]{3,2,1,0:T(4,128)}, u32[]{:S(2)}) copy-start(f32[2,256,4,256]{3,2,1,0:T(4,128)} %param.11) | copy-start | bytes 6291460
  17.1 1.3 %copy-start.8 = (f32[64,8,4,256]{3,1,2,0:T(8,128)}, f32[64,8,4,256]{3,1,2,0:T(8,128)S(1)}, u32[]{:S(2)}) copy-start(f32[64,8,4,256]{3,1,2,0:T(8,128)S(1)} %copy.11) | copy-start | bytes 6291460
  30.1 1.4 %copy-start.11 = (f32[2176,1,128]{2,1,0:T(1,128)}, f32[2176,1,128]{2,1,0:T(1,128)S(1)}, u32[]{:S(2)}) copy-start(f32[2176,1,128]{2,1,0:T(1,128)S(1)} %all-to-all-done.2) | copy-start | bytes 3342340
  31.5 16.8 %all-to-all-start.3 = ((f32[16,48,256]{2,1,0:T(8,128)}), f32[16,48,256]{2,1,0:T(8,128)S(1)}, u32[]{:S(2)}, u32[]{:S(2)}) async-start(f32[16,48,256]{2,1,0:T(8,128)} %bitcast.12), calls=%async_computation.3 | async-start | bytes 1572864 | tf_op jit(solution)/shard_map/all_to_all | solution.py:436
  35.2 8.1 %copy-start.9 = (f32[64,8,4,256]{3,1,2,0:T(8,128)S(1)}, f32[64,8,4,256]{3,1,2,0:T(8,128)}, u32[]{:S(2)}) copy-start(f32[64,8,4,256]{3,1,2,0:T(8,128)} %copy-done.8) | copy-start | bytes 6291460
  35.2 8.1 %copy-start.12 = (f32[2176,1,128]{2,1,0:T(1,128)S(1)}, f32[2176,1,128]{2,1,0:T(1,128)}, u32[]{:S(2)}) copy-start(f32[2176,1,128]{2,1,0:T(1,128)} %copy-done.11) | copy-start | bytes 3342340
  37.5 8.8 %copy-start.14 = (f32[512,256]{1,0:T(8,128)}, f32[512,256]{1,0:T(8,128)S(1)}, u32[]{:S(2)}) copy-start(f32[512,256]{1,0:T(8,128)S(1)} %shard_map.77) | copy-start | bytes 1572868
  37.5 8.8 %collective-permute-start.11 = (f32[512,256]{1,0:T(8,128)S(1)}, f32[512,256]{1,0:T(8,128)S(1)}, u32[]{:S(2)}, u32[]{:S(2)}) collective-permute-start(f32[512,256]{1,0:T(8,128)S(1)} %shard_map.77), channel_id=1, source_target_pairs={{0,1},{1,0},{2,3},{3,2},{4,5},{5,4},{6,7},{7,6},{8,9},{9,8},{10,11... | collective-permute-start | bytes 1572872 | tf_op jit(solution)/shard_map/ppermute | solution.py:360
  38.7 11.0 %collective-permute-start.14 = (f32[48,768]{1,0:T(8,128)S(1)}, f32[48,768]{1,0:T(8,128)S(1)}, u32[]{:S(2)}, u32[]{:S(2)}) collective-permute-start(f32[48,768]{1,0:T(8,128)S(1)} %get-tuple-element.129.a0), channel_id=1, source_target_pairs={{0,16},{8,24},{16,0},{24,8},{32,48},{40,56},{48,32},{56,40},{64,80... | collective-permute-start | bytes 442376 | tf_op jit(solution)/shard_map/ppermute | solution.py:372
  41.9 9.4 %collective-permute-start.13 = (f32[48,768]{1,0:T(8,128)S(1)}, f32[48,768]{1,0:T(8,128)S(1)}, u32[]{:S(2)}, u32[]{:S(2)}) collective-permute-start(f32[48,768]{1,0:T(8,128)S(1)} %get-tuple-element.129.a0), channel_id=1, source_target_pairs={{0,24},{8,0},{16,8},{24,16},{32,56},{40,32},{48,40},{56,48},{64,88... | collective-permute-start | bytes 442376 | tf_op jit(solution)/shard_map/ppermute | solution.py:372
  42.7 10.8 %collective-permute-start.12 = (f32[48,768]{1,0:T(8,128)S(1)}, f32[48,768]{1,0:T(8,128)S(1)}, u32[]{:S(2)}, u32[]{:S(2)}) collective-permute-start(f32[48,768]{1,0:T(8,128)S(1)} %get-tuple-element.129.a0), channel_id=1, source_target_pairs={{0,8},{8,16},{16,24},{24,0},{32,40},{40,48},{48,56},{56,32},{64,72... | collective-permute-start | bytes 442376 | tf_op jit(solution)/shard_map/ppermute | solution.py:372
  46.4 7.2 %copy-start.16 = (f32[512,256]{1,0:T(8,128)}, f32[512,256]{1,0:T(8,128)S(1)}, u32[]{:S(2)}) copy-start(f32[512,256]{1,0:T(8,128)S(1)} %collective-permute-done.11.r_done) | copy-start | bytes 1572868
  48.3 10.1 %copy-start.15 = (f32[512,256]{1,0:T(8,128)S(1)}, f32[512,256]{1,0:T(8,128)}, u32[]{:S(2)}) copy-start(f32[512,256]{1,0:T(8,128)} %copy-done.14) | copy-start | bytes 1572868
  53.6 40.8 %collective-permute-start.17 = (f32[192,768]{1,0:T(8,128)S(1)}, f32[192,768]{1,0:T(8,128)}, u32[]{:S(2)}, u32[]{:S(2)}) collective-permute-start(f32[192,768]{1,0:T(8,128)S(1)} %shard_map.82), channel_id=1, source_target_pairs={{0,64},{8,72},{16,80},{24,88},{32,96},{40,104},{48,112},{56,120},{... | collective-permute-start | bytes 1769480 | tf_op jit(solution)/shard_map/ppermute | solution.py:372
  56.4 38.1 %collective-permute-start.16 = (f32[192,768]{1,0:T(8,128)S(1)}, f32[192,768]{1,0:T(8,128)}, u32[]{:S(2)}, u32[]{:S(2)}) collective-permute-start(f32[192,768]{1,0:T(8,128)S(1)} %shard_map.82), channel_id=1, source_target_pairs={{0,96},{8,104},{16,112},{24,120},{32,0},{40,8},{48,16},{56,24},{64... | collective-permute-start | bytes 1769480 | tf_op jit(solution)/shard_map/ppermute | solution.py:372
  57.3 37.2 %collective-permute-start.15 = (f32[192,768]{1,0:T(8,128)S(1)}, f32[192,768]{1,0:T(8,128)}, u32[]{:S(2)}, u32[]{:S(2)}) collective-permute-start(f32[192,768]{1,0:T(8,128)S(1)} %shard_map.82), channel_id=1, source_target_pairs={{0,32},{8,40},{16,48},{24,56},{32,64},{40,72},{48,80},{56,88},{64,... | collective-permute-start | bytes 1769480 | tf_op jit(solution)/shard_map/ppermute | solution.py:372
  58.4 36.0 %copy-start.10 = (f32[64,8,4,256]{3,1,2,0:T(8,128)S(1)}, f32[64,8,4,256]{3,1,2,0:T(8,128)}, u32[]{:S(2)}) copy-start(f32[64,8,4,256]{3,1,2,0:T(8,128)} %copy-done.8) | copy-start | bytes 6291460
  58.4 3.5 %collective-permute-start = (f32[512,256]{1,0:T(8,128)}, f32[512,256]{1,0:T(8,128)S(1)}, u32[]{:S(2)}, u32[]{:S(2)}) collective-permute-start(f32[512,256]{1,0:T(8,128)} %get-tuple-element.62.w_own), channel_id=1, source_target_pairs={{0,1},{1,0},{2,3},{3,2},{4,5},{5,4},{6,7},{7,6},{8,9},{9,8},{10,11... | collective-permute-start | bytes 1572872 | tf_op jit(solution)/shard_map/cond/branch_1_fun/ppermute | solution.py:360
  67.1 1.5 %collective-permute-start.1 = (f32[512,256]{1,0:T(8,128)S(1)}, f32[512,256]{1,0:T(8,128)}, u32[]{:S(2)}, u32[]{:S(2)}) collective-permute-start(f32[512,256]{1,0:T(8,128)S(1)} %get-tuple-element.66), channel_id=1, source_target_pairs={{0,2},{1,7},{8,10},{9,15},{16,18},{17,23},{24,26},{25,31},{32,34},... | collective-permute-start | bytes 1572872 | tf_op jit(solution)/shard_map/cond/branch_1_fun/ppermute | solution.py:470
  69.4 20.3 %collective-permute-start.2 = (f32[512,256]{1,0:T(8,128)}, f32[512,256]{1,0:T(8,128)}, u32[]{:S(2)}, u32[]{:S(2)}) collective-permute-start(f32[512,256]{1,0:T(8,128)} %broadcast_select_fusion), channel_id=1, source_target_pairs={{1,3},{0,6},{2,4},{7,5},{9,11},{8,14},{10,12},{15,13},{17,19},{16,... | collective-permute-start | bytes 1572872 | tf_op jit(solution)/shard_map/cond/branch_1_fun/ppermute | solution.py:472
  70.7 21.8 %collective-permute-start.3 = (f32[512,256]{1,0:T(8,128)}, f32[512,256]{1,0:T(8,128)}, u32[]{:S(2)}, u32[]{:S(2)}) collective-permute-start(f32[512,256]{1,0:T(8,128)} %broadcast_select_fusion), channel_id=1, source_target_pairs={{0,1},{1,0},{2,3},{7,6},{8,9},{9,8},{10,11},{15,14},{16,17},{17,16... | collective-permute-start | bytes 1572872 | tf_op jit(solution)/shard_map/cond/branch_1_fun/ppermute | solution.py:473
  89.7 4.7 %collective-permute-start.4 = (f32[512,256]{1,0:T(8,128)}, f32[512,256]{1,0:T(8,128)}, u32[]{:S(2)}, u32[]{:S(2)}) collective-permute-start(f32[512,256]{1,0:T(8,128)} %collective-permute-done.2), channel_id=1, source_target_pairs={{3,2},{6,7},{4,5},{5,4},{11,10},{14,15},{12,13},{13,12},{19,18},{2... | collective-permute-start | bytes 1572872 | tf_op jit(solution)/shard_map/cond/branch_1_fun/ppermute | solution.py:474
